TPU v7x, 32 devices: a whole 2x2x4 slice. The times are simulated.
32 devices in a mesh: dp: 4 (over y, x), expert: 8 (over z, core).
Axes of the slice: x: 2, y: 2, z: 4, core: 2. Of those that a mesh axis runs over, the one named last changes fastest.
Arguments:
- tokens: bfloat16 [4096, 3584], P('expert', 'dp'), may hold values from -6 to 6
- grad_out: bfloat16 [4096, 3584], P('expert', 'dp'), may hold values from -1.796875 to 1.796875
- expert_ids: int32 [4096, 8], P('expert'), may hold values from 0 to 255, as said below
- gates: float32 [4096, 8], P('expert'), may hold values from 0.25 to 2.5
- w_gate: bfloat16 [8, 3584, 1024], P('expert', 'dp'), may hold values from -0.09375 to 0.09375
- w_up: bfloat16 [8, 3584, 1024], P('expert', 'dp'), may hold values from -0.09375 to 0.09375
- w_down: bfloat16 [8, 1024, 3584], P('expert', None, 'dp'), may hold values from -0.1875 to 0.1875
Outputs:
- mixed: bfloat16 [4096, 3584], P('expert', 'dp')
- grad_tokens: bfloat16 [4096, 3584], P('expert', 'dp')
- grad_gate: bfloat16 [8, 3584, 1024], P('expert', 'dp')
- grad_up: bfloat16 [8, 3584, 1024], P('expert', 'dp')
- grad_down: bfloat16 [8, 1024, 3584], P('expert', None, 'dp')
Inputs may be any that keep to these rules, and one draw needn't show every extreme that they name: `expert_ids`: each row names 8 different experts, at most one of them below 8. Within each aligned block of 512 rows no expert below 8 is named by more than 32 rows, and one such expert, the same in every block, is named by exactly 32 rows of every block.
All inputs are finite; a program needn't handle non-finite values.
Results may differ from a plain program's by a relative error of at most 0.029.
Values may be sent and summed in bfloat16 or wider, within the bound.
No kernel may reach another device: no remote copies, remote signals or barrier semaphores. Data moves between devices by JAX's collectives and lax.ppermute only.
A program may use at most 64 MiB of HBM per device.

v0:
```python
import jax
import jax.numpy as jnp
from jax import lax
from jax.sharding import PartitionSpec as P


def swish_gate(value):
    return value * jax.nn.sigmoid(value)


def swish_slope(value):
    logistic = jax.nn.sigmoid(value)
    return logistic * (1.0 + value * (1.0 - logistic))


def contract_rows(left, right):
    return lax.dot_general(
        left, right, (((0,), (0,)), ((), ())), preferred_element_type=jnp.float32
    )


def contract_cols(left, right):
    return lax.dot_general(
        left, right, (((1,), (1,)), ((), ())), preferred_element_type=jnp.float32
    )


def body(tokens, grad_out, expert_ids, gates, w_gate, w_up, w_down):
    experts = lax.axis_size("expert")
    tok_rows, features = tokens.shape
    capacity = tok_rows // 16
    slot_count = experts * capacity
    in_window = expert_ids < experts
    routed = jnp.any(in_window, axis=1)
    chosen = jnp.sum(jnp.where(in_window, expert_ids, 0), axis=1)
    weight_tok = jnp.sum(jnp.where(in_window, gates, jnp.zeros_like(gates)), axis=1)
    one_hot = (
        (chosen[:, None] == jnp.arange(experts, dtype=jnp.int32)[None, :]) & routed[:, None]
    ).astype(jnp.int32)
    position = jnp.sum((jnp.cumsum(one_hot, axis=0) - one_hot) * one_hot, axis=1)
    slot_index = jnp.where(routed, chosen * capacity + position, slot_count)
    source_row = jnp.full((slot_count,), tok_rows, jnp.int32)
    source_row = source_row.at[slot_index].set(jnp.arange(tok_rows, dtype=jnp.int32), mode="drop")
    scaled = (weight_tok[:, None] * grad_out.astype(jnp.float32)).astype(jnp.bfloat16)
    send_tokens = jnp.take(tokens, source_row, axis=0, mode="fill", fill_value=0).reshape(
        experts, capacity, features
    )
    send_grads = jnp.take(scaled, source_row, axis=0, mode="fill", fill_value=0).reshape(
        experts, capacity, features
    )
    arrived_tokens, arrived_grads = (
        lax.all_to_all(send_tokens, "expert", split_axis=0, concat_axis=0, tiled=True),
        lax.all_to_all(send_grads, "expert", split_axis=0, concat_axis=0, tiled=True),
    )
    expert_rows = arrived_tokens.reshape(slot_count, features)
    grad_rows_in = arrived_grads.reshape(slot_count, features)
    gate_mat = w_gate[0]
    up_mat = w_up[0]
    down_mat = w_down[0]
    part_gate = jnp.dot(expert_rows, gate_mat, preferred_element_type=jnp.float32)
    part_up = jnp.dot(expert_rows, up_mat, preferred_element_type=jnp.float32)
    gate_pre, up_pre = (
        lax.psum(part_gate.astype(jnp.bfloat16), "dp").astype(jnp.float32),
        lax.psum(part_up.astype(jnp.bfloat16), "dp").astype(jnp.float32),
    )
    full_act = (swish_gate(gate_pre) * up_pre).astype(jnp.bfloat16)
    expert_out = jnp.dot(full_act, down_mat, preferred_element_type=jnp.float32).astype(
        jnp.bfloat16
    )
    out_blocks = expert_out.reshape(experts, capacity, features)
    back_out = lax.all_to_all(out_blocks, "expert", split_axis=0, concat_axis=0, tiled=True)
    grad_down = contract_rows(full_act, grad_rows_in).astype(jnp.bfloat16)
    part_act = contract_cols(grad_rows_in, down_mat)
    grad_act = lax.psum(part_act.astype(jnp.bfloat16), "dp").astype(jnp.float32)
    grad_gate_pre = (grad_act * up_pre * swish_slope(gate_pre)).astype(jnp.bfloat16)
    grad_up_pre = (grad_act * swish_gate(gate_pre)).astype(jnp.bfloat16)
    grad_gate = contract_rows(expert_rows, grad_gate_pre).astype(jnp.bfloat16)
    grad_up = contract_rows(expert_rows, grad_up_pre).astype(jnp.bfloat16)
    row_grad = (contract_cols(grad_gate_pre, gate_mat) + contract_cols(grad_up_pre, up_mat)).astype(
        jnp.bfloat16
    )
    grad_blocks = row_grad.reshape(experts, capacity, features)
    back_grad = lax.all_to_all(grad_blocks, "expert", split_axis=0, concat_axis=0, tiled=True)
    token_out = jnp.take(
        back_out.reshape(slot_count, features), slot_index, axis=0, mode="fill", fill_value=0
    )
    mixed = (weight_tok[:, None] * token_out.astype(jnp.float32)).astype(jnp.bfloat16)
    grad_tokens = jnp.take(
        back_grad.reshape(slot_count, features), slot_index, axis=0, mode="fill", fill_value=0
    )
    return (mixed, grad_tokens, grad_gate[None], grad_up[None], grad_down[None])


def solution(mesh):
    placed = (
        P("expert", "dp"),
        P("expert", "dp"),
        P("expert", None),
        P("expert", None),
        P("expert", "dp", None),
        P("expert", "dp", None),
        P("expert", None, "dp"),
    )
    return jax.shard_map(
        body,
        mesh=mesh,
        in_specs=placed,
        out_specs=(
            P("expert", "dp"),
            P("expert", "dp"),
            P("expert", "dp", None),
            P("expert", "dp", None),
            P("expert", None, "dp"),
        ),
        check_vma=False,
    )
```

profile of v0, /device:TPU:0, one launch (start us, length us, event | category | flops | bytes accessed | tf_op | source)
XLA Modules:
  0.0 174.0 jit_solution(11299956101417143384)
XLA Ops:
  10.3 2.4 %scatter_custom_fusion = s32[256]{0:T(256)S(1)} fusion(s32[512]{0:T(512)S(1)} %bitcast.72, s32[512]{0:T(512)S(1)} %iota.11, s32[]{:T(128)} %constant.26.clone.1), kind=kCustom, calls=%fused_computation.66 | custom fusion | bytes 1028 | tf_op jit(solution)/shard_map/scatter | solution.py:43
  13.6 1.4 multiply_convert_fusion
  16.2 2.8 %gather_fusion = bf16[256,896]{1,0:T(8,128)(2,1)S(1)} fusion(bf16[512,896]{1,0:T(8,128)(2,1)} %param.11, s32[1024]{0:T(1024)S(1)} %pad_clamp_fusion.1), kind=kCustom, calls=%fused_computation.clone | custom fusion | bytes 918528 | tf_op jit(solution)/shard_map/jit(_take)/gather | solution.py:45
  19.9 20.1 %all_to_all.20 = bf16[8,32,896]{2,1,0:T(8,128)(2,1)S(1)} all-to-all(bf16[8,32,896]{2,1,0:T(8,128)(2,1)S(1)} %bitcast.61), channel_id=1, replica_groups=mesh['dp'=4,'expert'=8] {'expert'}, dimensions={0} | all-to-all | bytes 917504 | tf_op jit(solution)/shard_map/all_to_all | solution.py:52
  40.0 3.5 %all-to-all-start.2 = ((bf16[8,32,896]{2,1,0:T(8,128)(2,1)}), bf16[8,32,896]{2,1,0:T(8,128)(2,1)S(1)}, u32[]{:S(2)}, u32[]{:S(2)}) async-start(bf16[8,32,896]{2,1,0:T(8,128)(2,1)} %bitcast.13), calls=%async_computation.2 | async-start | bytes 917504 | tf_op jit(solution)/shard_map/all_to_all | solution.py:53
  43.5 3.0 %fusion.15 = bf16[256,1024]{1,0:T(8,128)(2,1)} fusion(bf16[256,896]{1,0:T(8,128)(2,1)S(1)} %bitcast.62, bf16[1,896,1024]{2,1,0:T(8,128)(2,1)} %param.15), kind=kOutput, calls=%fused_computation.29 | convolution fusion | flops 470024192 | bytes 2818048 | tf_op jit(solution)/shard_map/dot_general | solution.py:60
  46.5 1.5 fusion.18
  48.0 9.3 %all-to-all-done.2 = bf16[8,32,896]{2,1,0:T(8,128)(2,1)S(1)} async-done(((bf16[8,32,896]{2,1,0:T(8,128)(2,1)}), bf16[8,32,896]{2,1,0:T(8,128)(2,1)S(1)}, u32[]{:S(2)}, u32[]{:S(2)}) %all-to-all-start.2) | async-done | bytes 458784 | tf_op jit(solution)/shard_map/all_to_all | solution.py:53
  57.3 3.2 %fusion.21 = bf16[256,1024]{1,0:T(8,128)(2,1)} fusion(bf16[256,896]{1,0:T(8,128)(2,1)S(1)} %bitcast.66, bf16[1,1024,896]{2,1,0:T(8,128)(2,1)} %param.17), kind=kOutput, calls=%fused_computation.31 | convolution fusion | flops 470024192 | bytes 2818048 | tf_op jit(solution)/shard_map/dot_general | solution.py:23
  60.6 60.3 %all-reduce.3.cloned.1.call-done = (bf16[256,1024]{1,0:T(8,128)(2,1)}, bf16[256,1024]{1,0:T(8,128)(2,1)}, bf16[256,1024]{1,0:T(8,128)(2,1)}) async-done(((bf16[256,1024]{1,0:T(8,128)(2,1)}, bf16[256,1024]{1,0:T(8,128)(2,1)}, bf16[256,1024]{1,0:T(8,128)(2,1)}), (bf16[256,1024]{1,0:T(8,128)(2,1)}, bf16[256,1024]{1,0:T(8,128)(2,1)}, bf16[256,1024]{1,0:T(8,128)(2,1)})) %all-reduce.3.cloned.1.call-update) | async-done | bytes 1572880 | tf_op jit(solution)/shard_map/psum | solution.py:64
  120.9 2.2 %fusion.4 = f32[256,896]{1,0:T(8,128)S(1)} fusion(bf16[1,896,1024]{2,1,0:T(8,128)(2,1)S(1)} %copy-done, bf16[256,1024]{1,0:T(8,128)(2,1)} %get-tuple-element.9, bf16[256,1024]{1,0:T(8,128)(2,1)} %get-tuple-element.8), kind=kOutput, calls=%fused_computation.9 | convolution fusion | flops 471859200 | bytes 3801088 | tf_op jit(solution)/shard_map/dot_general | solution.py:23
  123.2 1.8 %fusion.24 = bf16[256,896]{1,0:T(8,128)(2,1)} fusion(f32[256,896]{1,0:T(8,128)S(1)} %fusion.4, bf16[1,896,1024]{2,1,0:T(8,128)(2,1)S(1)} %copy-done.4, bf16[256,1024]{1,0:T(8,128)(2,1)S(1)} %copy-done.5, bf16[256,1024]{1,0:T(8,128)(2,1)S(1)} %copy-done.9, bf16[256,1024]{1,0:T(8,128)(2,1)S(1)} %copy-done.7), kind=kOutput, calls=%fused_computation.32 | convolution fusion | flops 473628672 | bytes 4784128 | tf_op jit(solution)/shard_map/dot_general | solution.py:23
  124.9 4.6 %all-to-all-start.3 = ((bf16[8,32,896]{2,1,0:T(8,128)(2,1)}), bf16[8,32,896]{2,1,0:T(8,128)(2,1)S(1)}, u32[]{:S(2)}, u32[]{:S(2)}) async-start(bf16[8,32,896]{2,1,0:T(8,128)(2,1)} %bitcast.15), calls=%async_computation.3 | async-start | bytes 917504 | tf_op jit(solution)/shard_map/all_to_all | solution.py:83
  129.6 3.4 %fusion.27 = bf16[256,896]{1,0:T(8,128)(2,1)} fusion(bf16[1,1024,896]{2,1,0:T(8,128)(2,1)} %param.17, bf16[256,1024]{1,0:T(8,128)(2,1)} %get-tuple-element.7, bf16[256,1024]{1,0:T(8,128)(2,1)} %get-tuple-element.8), kind=kOutput, calls=%fused_computation.33 | convolution fusion | flops 472088576 | bytes 3342336 | tf_op jit(solution)/shard_map/dot_general | solution.py:67
  133.0 10.5 %all-to-all-done.3 = bf16[8,32,896]{2,1,0:T(8,128)(2,1)S(1)} async-done(((bf16[8,32,896]{2,1,0:T(8,128)(2,1)}), bf16[8,32,896]{2,1,0:T(8,128)(2,1)S(1)}, u32[]{:S(2)}, u32[]{:S(2)}) %all-to-all-start.3) | async-done | bytes 458784 | tf_op jit(solution)/shard_map/all_to_all | solution.py:83
  143.5 3.7 %all-to-all-start.1 = ((bf16[8,32,896]{2,1,0:T(8,128)(2,1)}), bf16[8,32,896]{2,1,0:T(8,128)(2,1)S(1)}, u32[]{:S(2)}, u32[]{:S(2)}) async-start(bf16[8,32,896]{2,1,0:T(8,128)(2,1)} %bitcast.68), calls=%async_computation.1 | async-start | bytes 917504 | tf_op jit(solution)/shard_map/all_to_all | solution.py:71
  147.2 3.3 %convert_bitcast_fusion.1 = bf16[1,896,1024]{2,1,0:T(8,128)(2,1)} fusion(bf16[256,896]{1,0:T(8,128)(2,1)S(1)} %bitcast.64, bf16[256,1024]{1,0:T(8,128)(2,1)} %get-tuple-element.9, bf16[256,1024]{1,0:T(8,128)(2,1)} %get-tuple-element.8), kind=kOutput, calls=%fused_computation.18 | convolution fusion | flops 472776704 | bytes 3342336 | tf_op jit(solution)/shard_map/dot_general | solution.py:17
  150.6 2.1 %convert_bitcast_fusion = bf16[1,1024,896]{2,1,0:T(8,128)(2,1)} fusion(bf16[256,896]{1,0:T(8,128)(2,1)S(1)} %bitcast.67, bf16[256,1024]{1,0:T(8,128)(2,1)S(1)} %copy-done.6, bf16[256,1024]{1,0:T(8,128)(2,1)S(1)} %copy-done.8), kind=kOutput, calls=%fused_computation.17 | convolution fusion | flops 472776704 | bytes 3342336 | tf_op jit(solution)/shard_map/dot_general | solution.py:17
  152.7 2.1 %convert_bitcast_fusion.2 = bf16[1,896,1024]{2,1,0:T(8,128)(2,1)} fusion(bf16[256,896]{1,0:T(8,128)(2,1)S(1)} %bitcast.65, bf16[256,1024]{1,0:T(8,128)(2,1)S(1)} %copy-done.6, bf16[256,1024]{1,0:T(8,128)(2,1)S(1)} %copy-done.10, bf16[256,1024]{1,0:T(8,128)(2,1)S(1)} %copy-done.8), kind=kOutput, calls=%fused_computation.19 | convolution fusion | flops 474087424 | bytes 3866624 | tf_op jit(solution)/shard_map/dot_general | solution.py:17
  154.8 2.7 %gather_fusion.3 = bf16[512,896]{1,0:T(8,128)(2,1)} fusion(bf16[256,896]{1,0:T(8,128)(2,1)S(1)} %bitcast.59, s32[1024]{0:T(1024)S(1)} %pad_clamp_fusion), kind=kCustom, calls=%fused_computation.3.clone | custom fusion | bytes 1837056 | tf_op jit(solution)/shard_map/jit(_take)/gather | solution.py:88
  157.5 3.4 %all-to-all-done.1 = bf16[8,32,896]{2,1,0:T(8,128)(2,1)S(1)} async-done(((bf16[8,32,896]{2,1,0:T(8,128)(2,1)}), bf16[8,32,896]{2,1,0:T(8,128)(2,1)S(1)}, u32[]{:S(2)}, u32[]{:S(2)}) %all-to-all-start.1) | async-done | bytes 458784 | tf_op jit(solution)/shard_map/all_to_all | solution.py:71
  160.9 2.7 %gather_fusion.1 = bf16[512,896]{1,0:T(8,128)(2,1)} fusion(bf16[256,896]{1,0:T(8,128)(2,1)S(1)} %bitcast.60, s32[1024]{0:T(1024)S(1)} %pad_clamp_fusion), kind=kCustom, calls=%fused_computation.1.clone | custom fusion | bytes 1837056 | tf_op jit(solution)/shard_map/jit(_take)/gather | solution.py:84
  163.6 2.4 %broadcast_select_fusion = bf16[512,896]{1,0:T(8,128)(2,1)} fusion(bf16[512,896]{1,0:T(8,128)(2,1)} %gather_fusion.3, pred[512]{0:T(512)(128)(4,1)S(1)} %get-tuple-element.10), kind=kLoop, calls=%fused_computation.43 | loop fusion | flops 458752 | bytes 1835520 | tf_op jit(solution)/shard_map/jit(_take)/select_n | solution.py:88
  166.0 1.2 multiply_convert_fusion.1
  (43 shorter events, 6.1 us)
Async XLA Ops:
  7.2 39.4 %copy-start = (bf16[1,896,1024]{2,1,0:T(8,128)(2,1)S(1)}, bf16[1,896,1024]{2,1,0:T(8,128)(2,1)}, u32[]{:S(2)}) copy-start(bf16[1,896,1024]{2,1,0:T(8,128)(2,1)} %param.16) | copy-start | bytes 5505028
  40.0 17.4 %all-to-all-start.2 = ((bf16[8,32,896]{2,1,0:T(8,128)(2,1)}), bf16[8,32,896]{2,1,0:T(8,128)(2,1)S(1)}, u32[]{:S(2)}, u32[]{:S(2)}) async-start(bf16[8,32,896]{2,1,0:T(8,128)(2,1)} %bitcast.13), calls=%async_computation.2 | async-start | bytes 917504 | tf_op jit(solution)/shard_map/all_to_all | solution.py:53
  43.5 77.5 %all-reduce.3.cloned.1.call-start = ((), (), s32[]{:S(2)}) async-start(), calls=%async_computation.4 | async-start | bytes 3145728 | tf_op jit(solution)/shard_map/psum | solution.py:64
  57.3 3.2 %copy-start.2 = (bf16[8,32,896]{2,1,0:T(8,128)(2,1)}, bf16[8,32,896]{2,1,0:T(8,128)(2,1)S(1)}, u32[]{:S(2)}) copy-start(bf16[8,32,896]{2,1,0:T(8,128)(2,1)S(1)} %all-to-all-done.2) | copy-start | bytes 1376260
  120.9 2.2 %copy-start.4 = (bf16[1,896,1024]{2,1,0:T(8,128)(2,1)S(1)}, bf16[1,896,1024]{2,1,0:T(8,128)(2,1)}, u32[]{:S(2)}) copy-start(bf16[1,896,1024]{2,1,0:T(8,128)(2,1)} %param.15) | copy-start | bytes 5505028
  120.9 2.2 %copy-start.5 = (bf16[256,1024]{1,0:T(8,128)(2,1)S(1)}, bf16[256,1024]{1,0:T(8,128)(2,1)}, u32[]{:S(2)}) copy-start(bf16[256,1024]{1,0:T(8,128)(2,1)} %get-tuple-element.7) | copy-start | bytes 1572868
  120.9 2.2 %copy-start.7 = (bf16[256,1024]{1,0:T(8,128)(2,1)S(1)}, bf16[256,1024]{1,0:T(8,128)(2,1)}, u32[]{:S(2)}) copy-start(bf16[256,1024]{1,0:T(8,128)(2,1)} %get-tuple-element.8) | copy-start | bytes 1572868
  120.9 2.2 %copy-start.9 = (bf16[256,1024]{1,0:T(8,128)(2,1)S(1)}, bf16[256,1024]{1,0:T(8,128)(2,1)}, u32[]{:S(2)}) copy-start(bf16[256,1024]{1,0:T(8,128)(2,1)} %get-tuple-element.9) | copy-start | bytes 1572868
  124.9 18.6 %all-to-all-start.3 = ((bf16[8,32,896]{2,1,0:T(8,128)(2,1)}), bf16[8,32,896]{2,1,0:T(8,128)(2,1)S(1)}, u32[]{:S(2)}, u32[]{:S(2)}) async-start(bf16[8,32,896]{2,1,0:T(8,128)(2,1)} %bitcast.15), calls=%async_computation.3 | async-start | bytes 917504 | tf_op jit(solution)/shard_map/all_to_all | solution.py:83
  143.5 17.4 %all-to-all-start.1 = ((bf16[8,32,896]{2,1,0:T(8,128)(2,1)}), bf16[8,32,896]{2,1,0:T(8,128)(2,1)S(1)}, u32[]{:S(2)}, u32[]{:S(2)}) async-start(bf16[8,32,896]{2,1,0:T(8,128)(2,1)} %bitcast.68), calls=%async_computation.1 | async-start | bytes 917504 | tf_op jit(solution)/shard_map/all_to_all | solution.py:71
  147.2 3.4 %copy-start.3 = (bf16[8,32,896]{2,1,0:T(8,128)(2,1)S(1)}, bf16[8,32,896]{2,1,0:T(8,128)(2,1)}, u32[]{:S(2)}) copy-start(bf16[8,32,896]{2,1,0:T(8,128)(2,1)} %copy-done.2) | copy-start | bytes 1376260
  147.2 3.4 %copy-start.6 = (bf16[256,1024]{1,0:T(8,128)(2,1)S(1)}, bf16[256,1024]{1,0:T(8,128)(2,1)}, u32[]{:S(2)}) copy-start(bf16[256,1024]{1,0:T(8,128)(2,1)} %get-tuple-element.7) | copy-start | bytes 1572868
  147.2 3.4 %copy-start.8 = (bf16[256,1024]{1,0:T(8,128)(2,1)S(1)}, bf16[256,1024]{1,0:T(8,128)(2,1)}, u32[]{:S(2)}) copy-start(bf16[256,1024]{1,0:T(8,128)(2,1)} %get-tuple-element.8) | copy-start | bytes 1572868
  150.5 2.1 %copy-start.10 = (bf16[256,1024]{1,0:T(8,128)(2,1)S(1)}, bf16[256,1024]{1,0:T(8,128)(2,1)}, u32[]{:S(2)}) copy-start(bf16[256,1024]{1,0:T(8,128)(2,1)} %get-tuple-element.9) | copy-start | bytes 1572868
  163.6 2.4 %copy-start.1 = (bf16[512,896]{1,0:T(8,128)(2,1)S(1)}, bf16[512,896]{1,0:T(8,128)(2,1)}, u32[]{:S(2)}) copy-start(bf16[512,896]{1,0:T(8,128)(2,1)} %gather_fusion.1) | copy-start | bytes 2752516
Sparse Core Ops, SparseCore 0:
  60.7 60.1 all-reduce.2
where the time goes:
time: 175 us; the launch traced here: 174 us
  waiting for transfers between devices  83.6 us (48%)
  matrix products  22.6 us (13%)
  blocking collectives  20.1 us (11%)
  between operations  14.2 us (8%)
  local copies, waits for them, and re-layouts  12.2 us (7%)
  starting transfers between devices  11.8 us (7%)
  other arithmetic  9.6 us (5%)
    psum x1, waiting for transfers between devices, body(): lax.psum(part_up.astype(jnp.bfloat16), 'dp').astype(jnp.float32)  60.3 us
    all_to_all x1, blocking collectives, body(): lax.all_to_all(send_tokens, 'expert', split_axis=0, concat_axis=0, tiled=...  20.1 us
    all_to_all x1, waiting for transfers between devices, body(): lax.all_to_all(grad_blocks, 'expert', split_axis=0, concat_axis=0, tiled=...  10.5 us
    all_to_all x1, waiting for transfers between devices, body(): lax.all_to_all(send_grads, 'expert', split_axis=0, concat_axis=0, tiled=T...  9.31 us
    dot_general x3, matrix products, contract_rows(): lax.dot_general(left, right, (((0,), (0,)), ((), ())), preferred_element_...  7.55 us
    dot_general x3, matrix products, contract_cols(): lax.dot_general(left, right, (((1,), (1,)), ((), ())), preferred_element_...  7.16 us
    all_to_all x1, starting transfers between devices, body(): lax.all_to_all(grad_blocks, 'expert', split_axis=0, concat_axis=0, tiled=...  4.6 us
    all_to_all x1, starting transfers between devices, body(): lax.all_to_all(out_blocks, 'expert', split_axis=0, concat_axis=0, tiled=T...  3.65 us
  transfers between devices with their start and end apart: 4, of which 4 were waited for; matrix products, arithmetic and copies ran while one was open for 10% of the time, Pallas kernels for 0%

commit v1 on v0

v1 whole, which is shorter than its diff:
```python
import functools

import jax
import jax.numpy as jnp
from jax import lax
from jax.experimental import pallas as pl
from jax.experimental.pallas import tpu as pltpu
from jax.sharding import PartitionSpec as P

F32 = jnp.float32
BF16 = jnp.bfloat16
VMEM_LIMIT = 24 * 1024 * 1024


def mm(left, right, dims):
    return lax.dot_general(left, right, (dims, ((), ())), preferred_element_type=F32)


def call(kernel, out_shape, flops=0, moved=0, **kwargs):
    return pl.pallas_call(
        kernel,
        out_shape=out_shape,
        cost_estimate=pl.CostEstimate(flops=flops, bytes_accessed=moved, transcendentals=0),
        compiler_params=pltpu.CompilerParams(vmem_limit_bytes=VMEM_LIMIT),
        **kwargs,
    )


def route_kernel(experts, capacity, ids_ref, gates_ref, tokens_ref, pick_ref, weight_ref, send_ref):
    ids = ids_ref[...]
    tok_rows = ids.shape[1]
    slots = pick_ref.shape[0]
    inside = ids < experts
    routed = jnp.max(inside.astype(jnp.int32), axis=0, keepdims=True)
    chosen = jnp.sum(jnp.where(inside, ids, 0), axis=0, keepdims=True)
    weight = jnp.sum(jnp.where(inside, gates_ref[...], 0.0), axis=0, keepdims=True)
    key = jnp.where(routed > 0, chosen, experts)
    hot = lax.broadcasted_iota(jnp.int32, (experts, tok_rows), 0) == key
    earlier = lax.broadcasted_iota(jnp.int32, (tok_rows, tok_rows), 0) < lax.broadcasted_iota(
        jnp.int32, (tok_rows, tok_rows), 1
    )
    before = mm(hot.astype(F32).astype(BF16), earlier.astype(F32).astype(BF16), ((1,), (0,)))
    position = jnp.sum(jnp.where(hot, before, 0.0), axis=0, keepdims=True).astype(jnp.int32)
    slot = jnp.where(routed > 0, chosen * capacity + position, slots)
    pick = lax.broadcasted_iota(jnp.int32, (slots, tok_rows), 0) == slot
    weight_ref[...] = jnp.sum(jnp.where(pick, weight, 0.0), axis=1, keepdims=True)
    pick = pick.astype(F32).astype(BF16)
    pick_ref[...] = pick
    send_ref[...] = mm(pick, tokens_ref[...], ((1,), (0,))).astype(BF16)


def gather_scaled_kernel(pick_ref, weight_ref, grad_ref, send_ref):
    rows = mm(pick_ref[...], grad_ref[...], ((1,), (0,)))
    send_ref[...] = (weight_ref[...] * rows).astype(BF16)


def gate_up_kernel(rows_ref, gate_ref, up_ref, out_ref):
    rows = rows_ref[...]
    dp, _, chunk, cols = out_ref.shape
    for at, mat in enumerate((gate_ref, up_ref)):
        part = mm(rows, mat[...], ((1,), (0,))).astype(BF16)
        out_ref[:, at] = part.reshape(dp, chunk, cols)


def grad_act_kernel(grads_ref, down_ref, out_ref):
    dp, chunk, cols = out_ref.shape
    part = mm(grads_ref[...], down_ref[...], ((1,), (1,))).astype(BF16)
    out_ref[...] = part.reshape(dp, chunk, cols)


def group_sum(ref, *at):
    total = ref[(0, *at)].astype(F32)
    for group in range(1, ref.shape[0]):
        total = total + ref[(group, *at)].astype(F32)
    return total


def logistic(value):
    return 1.0 / (1.0 + jnp.exp(-value))


def act_kernel(sums_ref, act_ref):
    gate = group_sum(sums_ref, 0)
    up = group_sum(sums_ref, 1)
    act_ref[...] = (gate * logistic(gate) * up).astype(BF16)


def grad_pre_kernel(sums_ref, grad_ref, out_ref):
    gate = group_sum(sums_ref, 0)
    up = group_sum(sums_ref, 1)
    grad = group_sum(grad_ref)
    soft = logistic(gate)
    out_ref[0] = (grad * up * (soft * (1.0 + gate * (1.0 - soft)))).astype(BF16)
    out_ref[1] = (grad * (gate * soft)).astype(BF16)


def expert_out_kernel(act_ref, down_ref, out_ref):
    dp, chunk, hidden = act_ref.shape
    act = act_ref[...].reshape(dp * chunk, hidden)
    out_ref[...] = mm(act, down_ref[...], ((1,), (0,))).astype(BF16)


def row_grad_kernel(pre_ref, gate_ref, up_ref, out_ref):
    dp, _, chunk, hidden = pre_ref.shape
    gate_pre = pre_ref[:, 0].reshape(dp * chunk, hidden)
    up_pre = pre_ref[:, 1].reshape(dp * chunk, hidden)
    total = mm(gate_pre, gate_ref[...], ((1,), (1,))) + mm(up_pre, up_ref[...], ((1,), (1,)))
    out_ref[...] = total.astype(BF16)


def scatter_scaled_kernel(pick_ref, weight_ref, back_ref, out_ref):
    scaled = (weight_ref[...] * back_ref[...].astype(F32)).astype(BF16)
    out_ref[...] = mm(pick_ref[...], scaled, ((0,), (0,))).astype(BF16)


def scatter_kernel(pick_ref, back_ref, out_ref):
    out_ref[...] = mm(pick_ref[...], back_ref[...], ((0,), (0,))).astype(BF16)


def exchange(value, axis):
    return lax.all_to_all(value, axis, split_axis=0, concat_axis=0, tiled=True)


def spread(value, axis):
    size = lax.axis_size(axis)
    return exchange(jnp.broadcast_to(value[None], (size, *value.shape)), axis)


def body(tokens, grad_out, expert_ids, gates, w_gate, w_up, w_down):
    experts = lax.axis_size("expert")
    dp = lax.axis_size("dp")
    tok_rows, features = tokens.shape
    capacity = tok_rows // 16
    slots = experts * capacity
    hidden = w_gate.shape[2]
    chunk = slots // dp
    gate_mat, up_mat, down_mat = w_gate[0], w_up[0], w_down[0]
    shape = jax.ShapeDtypeStruct
    product = 2 * slots * features * hidden
    weights = 2 * features * hidden

    pick, weight, send_tokens = call(
        functools.partial(route_kernel, experts, capacity),
        (
            shape((slots, tok_rows), BF16),
            shape((slots, 1), F32),
            shape((slots, features), BF16),
        ),
        2 * slots * tok_rows * features,
        4 * tok_rows * features,
    )(expert_ids.T, gates.T, tokens)
    rows = exchange(send_tokens.reshape(experts, capacity, features), "expert")
    rows = rows.reshape(slots, features)
    send_grads = call(
        gather_scaled_kernel,
        shape((slots, features), BF16),
        2 * slots * tok_rows * features,
        4 * tok_rows * features,
    )(pick, weight, grad_out)
    grads = exchange(send_grads.reshape(experts, capacity, features), "expert")
    grads = grads.reshape(slots, features)

    tiles = 4 if hidden % 512 == 0 else 1
    cols = hidden // tiles
    part_pre = call(
        gate_up_kernel,
        shape((dp, 2, chunk, hidden), BF16),
        2 * product,
        2 * weights,
        grid=(tiles,),
        in_specs=[
            pl.BlockSpec((slots, features), lambda i: (0, 0)),
            pl.BlockSpec((features, cols), lambda i: (0, i)),
            pl.BlockSpec((features, cols), lambda i: (0, i)),
        ],
        out_specs=pl.BlockSpec((dp, 2, chunk, cols), lambda i: (0, 0, 0, i)),
    )(rows, gate_mat, up_mat)
    sums = exchange(part_pre, "dp")
    part_grad = call(
        grad_act_kernel,
        shape((dp, chunk, hidden), BF16),
        product,
        weights,
        grid=(tiles,),
        in_specs=[
            pl.BlockSpec((slots, features), lambda i: (0, 0)),
            pl.BlockSpec((cols, features), lambda i: (i, 0)),
        ],
        out_specs=pl.BlockSpec((dp, chunk, cols), lambda i: (0, 0, i)),
    )(grads, down_mat)
    act_mine = call(act_kernel, shape((chunk, hidden), BF16), 0, 4 * dp * chunk * hidden)(sums)
    act = spread(act_mine, "dp")
    grad_sums = exchange(part_grad, "dp")
    expert_out = call(
        expert_out_kernel, shape((slots, features), BF16), product, weights
    )(act, down_mat)
    back_out = exchange(expert_out.reshape(experts, capacity, features), "expert")
    pre_mine = call(
        grad_pre_kernel, shape((2, chunk, hidden), BF16), 0, 6 * dp * chunk * hidden
    )(sums, grad_sums)
    pre = spread(pre_mine, "dp")
    row_grad = call(
        row_grad_kernel, shape((slots, features), BF16), 2 * product, 2 * weights
    )(pre, gate_mat, up_mat)
    back_grad = exchange(row_grad.reshape(experts, capacity, features), "expert")

    act_rows = act.reshape(slots, hidden)
    grad_down = mm(act_rows, grads, ((0,), (0,))).astype(BF16)
    grad_gate = mm(rows, pre[:, 0].reshape(slots, hidden), ((0,), (0,))).astype(BF16)
    grad_up = mm(rows, pre[:, 1].reshape(slots, hidden), ((0,), (0,))).astype(BF16)

    full = shape((tok_rows, features), BF16)
    mixed = call(
        scatter_scaled_kernel, full, 2 * slots * tok_rows * features, 4 * tok_rows * features
    )(pick, weight, back_out.reshape(slots, features))
    grad_tokens = call(
        scatter_kernel, full, 2 * slots * tok_rows * features, 4 * tok_rows * features
    )(pick, back_grad.reshape(slots, features))
    return (mixed, grad_tokens, grad_gate[None], grad_up[None], grad_down[None])


def solution(mesh):
    placed = (
        P("expert", "dp"),
        P("expert", "dp"),
        P("expert", None),
        P("expert", None),
        P("expert", "dp", None),
        P("expert", "dp", None),
        P("expert", None, "dp"),
    )
    return jax.shard_map(
        body,
        mesh=mesh,
        in_specs=placed,
        out_specs=(
            P("expert", "dp"),
            P("expert", "dp"),
            P("expert", "dp", None),
            P("expert", "dp", None),
            P("expert", None, "dp"),
        ),
        check_vma=False,
    )
```

time: 175 us -> 139 us (0.79)
  starting transfers between devices: 11.8 us -> 32.4 us
  blocking collectives: 20.1 us -> 0 us
  waiting for transfers between devices: 83.6 us -> 66.1 us
  matrix products: 22.6 us -> 6.84 us
  Pallas kernels: 0 us -> 13.9 us
  between operations: 14.2 us -> 0.84 us
  other arithmetic: 9.6 us -> 0 us
  local copies, waits for them, and re-layouts: 12.2 us -> 17.5 us
    psum x1 -> x0, waiting for transfers between devices: 60.3 us -> none  [body(): lax.psum(part_up.astype(jnp.bfloat16), 'dp').astype(jnp.float32)]
    all_to_all x3 -> x8, waiting for transfers between devices: 23.2 us -> 66.1 us  [exchange(): return lax.all_to_all(value, axis, split_axis=0, concat_axis=0, tiled=True)]
    all_to_all x3 -> x8, starting transfers between devices: 11.7 us -> 32.4 us  [exchange(): return lax.all_to_all(value, axis, split_axis=0, concat_axis=0, tiled=True)]
    all_to_all x1 -> x0, blocking collectives: 20.1 us -> none  [body(): lax.all_to_all(send_tokens, 'expert', split_axis=0, concat_axis=0, tiled=...]
    dot_general x9 -> x3, matrix products: 22.6 us -> 6.84 us  [mm(): lax.dot_general(left, right, (dims, ((), ())), preferred_element_type=F32)]
    unnamed x22 -> x44, local copies, waits for them, and re-layouts: 0.05 us -> 14.5 us
    pallas_call x0 -> x10, Pallas kernels: none -> 13.9 us  [the longest x1 2.36 us: body(): call(gate_up_kernel, shape((dp, 2, chunk, hidden), BF16), 2 * product, 2...]
    gather x4 -> x0, local copies, waits for them, and re-layouts: 9.46 us -> none  [the longest x1 2.8 us: body(): jnp.take(tokens, source_row, axis=0, mode='fill', fill_value=0)]
  transfers between devices with their start and end apart: 4 -> 8, of which waited for: 4 -> 8; matrix products, arithmetic and copies ran while one was open for 10% -> 5% of each run, Pallas kernels for 0% -> 9%
where the time goes in v1:
time: 139 us; the launch traced here: 138 us
  waiting for transfers between devices  66.1 us (48%)
  starting transfers between devices  32.4 us (23%)
  local copies, waits for them, and re-layouts  17.5 us (13%)
  Pallas kernels  13.9 us (10%)
  matrix products  6.84 us (5%)
    all_to_all x8, waiting for transfers between devices, exchange(): return lax.all_to_all(value, axis, split_axis=0, concat_axis=0, tiled=True)  66.1 us
    all_to_all x8, starting transfers between devices, exchange(): return lax.all_to_all(value, axis, split_axis=0, concat_axis=0, tiled=True)  32.4 us
    unnamed x44, local copies, waits for them, and re-layouts  14.5 us
    dot_general x3, matrix products, mm(): lax.dot_general(left, right, (dims, ((), ())), preferred_element_type=F32)  6.84 us
    broadcast_in_dim x2, local copies, waits for them, and re-layouts, spread(): return exchange(jnp.broadcast_to(value[None], (size, *value.shape)), axis)  2.9 us
  transfers between devices with their start and end apart: 8, of which 8 were waited for; matrix products, arithmetic and copies ran while one was open for 5% of the time, Pallas kernels for 9%

profile of v1, /device:TPU:0, one launch (start us, length us, event | category | flops | bytes accessed | tf_op | source)
XLA Modules:
  0.0 137.5 jit_solution(5731349263398350839)
XLA Ops:
  5.4 6.5 %all-to-all-start = ((bf16[8,32,896]{2,1,0:T(8,128)(2,1)}), bf16[8,32,896]{2,1,0:T(8,128)(2,1)S(1)}, u32[]{:S(2)}, u32[]{:S(2)}) async-start(bf16[8,32,896]{2,1,0:T(8,128)(2,1)} %bitcast.42), calls=%async_computation | async-start | bytes 917504 | tf_op jit(solution)/shard_map/all_to_all | solution.py:121
  14.0 11.8 %all-to-all-done = bf16[8,32,896]{2,1,0:T(8,128)(2,1)S(1)} async-done(((bf16[8,32,896]{2,1,0:T(8,128)(2,1)}), bf16[8,32,896]{2,1,0:T(8,128)(2,1)S(1)}, u32[]{:S(2)}, u32[]{:S(2)}) %all-to-all-start) | async-done | bytes 458784 | tf_op jit(solution)/shard_map/all_to_all | solution.py:121
  25.8 3.5 %all-to-all-start.4 = ((bf16[8,32,896]{2,1,0:T(8,128)(2,1)}), bf16[8,32,896]{2,1,0:T(8,128)(2,1)S(1)}, u32[]{:S(2)}, u32[]{:S(2)}) async-start(bf16[8,32,896]{2,1,0:T(8,128)(2,1)} %bitcast.9), calls=%async_computation.4 | async-start | bytes 917504 | tf_op jit(solution)/shard_map/all_to_all | solution.py:121
  30.8 2.4 %shard_map.111 = bf16[4,2,64,1024]{3,2,1,0:T(8,128)(2,1)S(1)} custom-call(bf16[256,896]{1,0:T(8,128)(2,1)S(1)} %bitcast.28, bf16[896,1024]{1,0:T(8,128)(2,1)S(1)} %bitcast.33, bf16[896,1024]{1,0:T(8,128)(2,1)S(1)} %bitcast.35), custom_call_target="tpu_custom_call" | custom-call | flops 939524096 | bytes 3670016 | tf_op jit(solution)/shard_map/pallas_call | solution.py:165
  34.2 9.0 %all-to-all-done.4 = bf16[8,32,896]{2,1,0:T(8,128)(2,1)S(1)} async-done(((bf16[8,32,896]{2,1,0:T(8,128)(2,1)}), bf16[8,32,896]{2,1,0:T(8,128)(2,1)S(1)}, u32[]{:S(2)}, u32[]{:S(2)}) %all-to-all-start.4) | async-done | bytes 458784 | tf_op jit(solution)/shard_map/all_to_all | solution.py:121
  44.0 3.7 %all-to-all-start.1 = ((bf16[4,2,64,1024]{3,2,1,0:T(8,128)(2,1)}), bf16[4,2,64,1024]{3,2,1,0:T(8,128)(2,1)S(1)}, u32[]{:S(2)}, u32[]{:S(2)}) async-start(bf16[4,2,64,1024]{3,2,1,0:T(8,128)(2,1)} %copy-done.5), calls=%async_computation.1 | async-start | bytes 2097152 | tf_op jit(solution)/shard_map/all_to_all | solution.py:121
  50.9 10.2 %all-to-all-done.1.sums_ref = bf16[4,2,64,1024]{3,2,1,0:T(8,128)(2,1)S(1)} async-done(((bf16[4,2,64,1024]{3,2,1,0:T(8,128)(2,1)}), bf16[4,2,64,1024]{3,2,1,0:T(8,128)(2,1)S(1)}, u32[]{:S(2)}, u32[]{:S(2)}) %all-to-all-start.1) | async-done | bytes 1048608 | tf_op jit(solution)/shard_map/all_to_all | solution.py:121
  61.2 4.1 %all-to-all-start.5 = ((bf16[4,64,1024]{2,1,0:T(8,128)(2,1)}), bf16[4,64,1024]{2,1,0:T(8,128)(2,1)}, u32[]{:S(2)}, u32[]{:S(2)}) async-start(bf16[4,64,1024]{2,1,0:T(8,128)(2,1)} %copy-done.11), calls=%async_computation.5 | async-start | bytes 1048576 | tf_op jit(solution)/shard_map/all_to_all | solution.py:121
  65.5 7.3 %all-to-all-done.5.grad_ref = bf16[4,64,1024]{2,1,0:T(8,128)(2,1)} async-done(((bf16[4,64,1024]{2,1,0:T(8,128)(2,1)}), bf16[4,64,1024]{2,1,0:T(8,128)(2,1)}, u32[]{:S(2)}, u32[]{:S(2)}) %all-to-all-start.5) | async-done | bytes 524320 | tf_op jit(solution)/shard_map/all_to_all | solution.py:121
  73.7 4.1 %all-to-all-start.2 = ((bf16[4,64,1024]{2,1,0:T(8,128)(2,1)}), bf16[4,64,1024]{2,1,0:T(8,128)(2,1)}, u32[]{:S(2)}, u32[]{:S(2)}) async-start(bf16[4,64,1024]{2,1,0:T(8,128)(2,1)} %broadcast_in_dim.10), calls=%async_computation.2 | async-start | bytes 1048576 | tf_op jit(solution)/shard_map/all_to_all | solution.py:121
  79.9 4.6 %all-to-all-done.2.act_ref = bf16[4,64,1024]{2,1,0:T(8,128)(2,1)} async-done(((bf16[4,64,1024]{2,1,0:T(8,128)(2,1)}), bf16[4,64,1024]{2,1,0:T(8,128)(2,1)}, u32[]{:S(2)}, u32[]{:S(2)}) %all-to-all-start.2) | async-done | bytes 524320 | tf_op jit(solution)/shard_map/all_to_all | solution.py:121
  84.5 2.0 %broadcast_in_dim.22 = bf16[4,2,64,1024]{3,2,1,0:T(8,128)(2,1)} broadcast(bf16[2,64,1024]{2,1,0:T(8,128)(2,1)} %copy-done.13), dimensions={1,2,3} | broadcast | bytes 1310720 | tf_op jit(solution)/shard_map/broadcast_in_dim | solution.py:126
  86.6 3.5 %all-to-all-start.6 = ((bf16[4,2,64,1024]{3,2,1,0:T(8,128)(2,1)}), bf16[4,2,64,1024]{3,2,1,0:T(8,128)(2,1)S(1)}, u32[]{:S(2)}, u32[]{:S(2)}) async-start(bf16[4,2,64,1024]{3,2,1,0:T(8,128)(2,1)} %broadcast_in_dim.22), calls=%async_computation.6 | async-start | bytes 2097152 | tf_op jit(solution)/shard_map/all_to_all | solution.py:121
  90.1 1.8 %shard_map.113 = bf16[256,896]{1,0:T(8,128)(2,1)S(1)} custom-call(bf16[4,64,1024]{2,1,0:T(8,128)(2,1)} %all-to-all-done.2.act_ref, bf16[1024,896]{1,0:T(8,128)(2,1)S(1)} %bitcast.32), custom_call_target="tpu_custom_call" | custom-call | flops 469762048 | bytes 1835008 | tf_op jit(solution)/shard_map/pallas_call | solution.py:194
  92.6 8.8 %all-to-all-done.6.pre_ref = bf16[4,2,64,1024]{3,2,1,0:T(8,128)(2,1)S(1)} async-done(((bf16[4,2,64,1024]{3,2,1,0:T(8,128)(2,1)}), bf16[4,2,64,1024]{3,2,1,0:T(8,128)(2,1)S(1)}, u32[]{:S(2)}, u32[]{:S(2)}) %all-to-all-start.6) | async-done | bytes 1048608 | tf_op jit(solution)/shard_map/all_to_all | solution.py:121
  101.4 3.5 %all-to-all-start.3 = ((bf16[8,32,896]{2,1,0:T(8,128)(2,1)}), bf16[8,32,896]{2,1,0:T(8,128)(2,1)S(1)}, u32[]{:S(2)}, u32[]{:S(2)}) async-start(bf16[8,32,896]{2,1,0:T(8,128)(2,1)} %bitcast.41), calls=%async_computation.3 | async-start | bytes 917504 | tf_op jit(solution)/shard_map/all_to_all | solution.py:121
  106.4 1.5 %copy-done.4 = bf16[1,896,1024]{2,1,0:T(8,128)(2,1)S(1)} copy-done((bf16[1,896,1024]{2,1,0:T(8,128)(2,1)S(1)}, bf16[1,896,1024]{2,1,0:T(8,128)(2,1)}, u32[]{:S(2)}) %copy-start.4) | copy-done | bytes 1835032
  107.9 2.1 %shard_map.118 = bf16[256,896]{1,0:T(8,128)(2,1)} custom-call(bf16[4,2,64,1024]{3,2,1,0:T(8,128)(2,1)S(1)} %all-to-all-done.6.pre_ref, bf16[896,1024]{1,0:T(8,128)(2,1)S(1)} %bitcast.34, bf16[896,1024]{1,0:T(8,128)(2,1)S(1)} %bitcast.36), custom_call_target="tpu_custom_call" | custom-call | flops 939524096 | bytes 3670016 | tf_op jit(solution)/shard_map/pallas_call | solution.py:202
  110.0 8.8 %all-to-all-done.3 = bf16[8,32,896]{2,1,0:T(8,128)(2,1)S(1)} async-done(((bf16[8,32,896]{2,1,0:T(8,128)(2,1)}), bf16[8,32,896]{2,1,0:T(8,128)(2,1)S(1)}, u32[]{:S(2)}, u32[]{:S(2)}) %all-to-all-start.3) | async-done | bytes 458784 | tf_op jit(solution)/shard_map/all_to_all | solution.py:121
  118.8 3.5 %all-to-all-start.7 = ((bf16[8,32,896]{2,1,0:T(8,128)(2,1)}), bf16[8,32,896]{2,1,0:T(8,128)(2,1)S(1)}, u32[]{:S(2)}, u32[]{:S(2)}) async-start(bf16[8,32,896]{2,1,0:T(8,128)(2,1)} %bitcast.11), calls=%async_computation.7 | async-start | bytes 917504 | tf_op jit(solution)/shard_map/all_to_all | solution.py:121
  122.3 3.0 %convert_bitcast_fusion = bf16[1,1024,896]{2,1,0:T(8,128)(2,1)} fusion(bf16[256,1024]{1,0:T(8,128)(2,1)} %bitcast.17, bf16[256,896]{1,0:T(8,128)(2,1)S(1)} %bitcast.38), kind=kOutput, calls=%fused_computation | convolution fusion | flops 470679552 | bytes 2818048 | tf_op jit(solution)/shard_map/dot_general | solution.py:16
  125.4 1.9 %convert_bitcast_fusion.1 = bf16[1,896,1024]{2,1,0:T(8,128)(2,1)} fusion(bf16[256,896]{1,0:T(8,128)(2,1)S(1)} %bitcast.29, bf16[256,1024]{1,0:T(8,128)(2,1)S(1)} %bitcast.46), kind=kOutput, calls=%fused_computation.1 | convolution fusion | flops 470679552 | bytes 2818048 | tf_op jit(solution)/shard_map/dot_general | solution.py:16
  127.3 1.9 %convert_bitcast_fusion.2 = bf16[1,896,1024]{2,1,0:T(8,128)(2,1)} fusion(bf16[256,896]{1,0:T(8,128)(2,1)S(1)} %bitcast.30, bf16[256,1024]{1,0:T(8,128)(2,1)S(1)} %bitcast.45), kind=kOutput, calls=%fused_computation.2 | convolution fusion | flops 470679552 | bytes 2818048 | tf_op jit(solution)/shard_map/dot_general | solution.py:16
  130.7 5.5 %all-to-all-done.7 = bf16[8,32,896]{2,1,0:T(8,128)(2,1)S(1)} async-done(((bf16[8,32,896]{2,1,0:T(8,128)(2,1)}), bf16[8,32,896]{2,1,0:T(8,128)(2,1)S(1)}, u32[]{:S(2)}, u32[]{:S(2)}) %all-to-all-start.7) | async-done | bytes 458784 | tf_op jit(solution)/shard_map/all_to_all | solution.py:121
  (52 shorter events, 21.6 us)
Async XLA Ops:
  0.6 11.3 %copy-start.14 = (bf16[512,896]{1,0:T(8,128)(2,1)S(1)}, bf16[512,896]{1,0:T(8,128)(2,1)}, u32[]{:S(2)}) copy-start(bf16[512,896]{1,0:T(8,128)(2,1)} %grad_ref.1) | copy-start | bytes 2752516
  0.6 1.3 copy-start.15
  5.4 20.4 %copy-start.9 = (bf16[256,512]{1,0:T(8,128)(2,1)}, bf16[256,512]{1,0:T(8,128)(2,1)S(1)}, u32[]{:S(2)}) copy-start(bf16[256,512]{1,0:T(8,128)(2,1)S(1)} %get-tuple-element.8.pick_ref) | copy-start | bytes 786436
  5.4 23.9 %copy-start.1 = (bf16[1,896,1024]{2,1,0:T(8,128)(2,1)S(1)}, bf16[1,896,1024]{2,1,0:T(8,128)(2,1)}, u32[]{:S(2)}) copy-start(bf16[1,896,1024]{2,1,0:T(8,128)(2,1)} %param.11) | copy-start | bytes 5505028
  5.4 20.4 %all-to-all-start = ((bf16[8,32,896]{2,1,0:T(8,128)(2,1)}), bf16[8,32,896]{2,1,0:T(8,128)(2,1)S(1)}, u32[]{:S(2)}, u32[]{:S(2)}) async-start(bf16[8,32,896]{2,1,0:T(8,128)(2,1)} %bitcast.42), calls=%async_computation | async-start | bytes 917504 | tf_op jit(solution)/shard_map/all_to_all | solution.py:121
  11.9 0.9 copy-start.17
  25.8 17.4 %all-to-all-start.4 = ((bf16[8,32,896]{2,1,0:T(8,128)(2,1)}), bf16[8,32,896]{2,1,0:T(8,128)(2,1)S(1)}, u32[]{:S(2)}, u32[]{:S(2)}) async-start(bf16[8,32,896]{2,1,0:T(8,128)(2,1)} %bitcast.9), calls=%async_computation.4 | async-start | bytes 917504 | tf_op jit(solution)/shard_map/all_to_all | solution.py:121
  29.3 1.5 %copy-start.3 = (bf16[1,896,1024]{2,1,0:T(8,128)(2,1)S(1)}, bf16[1,896,1024]{2,1,0:T(8,128)(2,1)}, u32[]{:S(2)}) copy-start(bf16[1,896,1024]{2,1,0:T(8,128)(2,1)} %param.12) | copy-start | bytes 5505028
  33.2 1.0 copy-start.5
  34.2 13.5 %copy-start = (bf16[1,1024,896]{2,1,0:T(8,128)(2,1)S(1)}, bf16[1,1024,896]{2,1,0:T(8,128)(2,1)}, u32[]{:S(2)}) copy-start(bf16[1,1024,896]{2,1,0:T(8,128)(2,1)} %param.13) | copy-start | bytes 5505028
  44.0 17.2 %all-to-all-start.1 = ((bf16[4,2,64,1024]{3,2,1,0:T(8,128)(2,1)}), bf16[4,2,64,1024]{3,2,1,0:T(8,128)(2,1)S(1)}, u32[]{:S(2)}, u32[]{:S(2)}) async-start(bf16[4,2,64,1024]{3,2,1,0:T(8,128)(2,1)} %copy-done.5), calls=%async_computation.1 | async-start | bytes 2097152 | tf_op jit(solution)/shard_map/all_to_all | solution.py:121
  47.7 1.0 copy-start.7
  50.1 0.8 copy-start.11
  61.2 11.7 %all-to-all-start.5 = ((bf16[4,64,1024]{2,1,0:T(8,128)(2,1)}), bf16[4,64,1024]{2,1,0:T(8,128)(2,1)}, u32[]{:S(2)}, u32[]{:S(2)}) async-start(bf16[4,64,1024]{2,1,0:T(8,128)(2,1)} %copy-done.11), calls=%async_computation.5 | async-start | bytes 1048576 | tf_op jit(solution)/shard_map/all_to_all | solution.py:121
  73.7 10.8 %all-to-all-start.2 = ((bf16[4,64,1024]{2,1,0:T(8,128)(2,1)}), bf16[4,64,1024]{2,1,0:T(8,128)(2,1)}, u32[]{:S(2)}, u32[]{:S(2)}) async-start(bf16[4,64,1024]{2,1,0:T(8,128)(2,1)} %broadcast_in_dim.10), calls=%async_computation.2 | async-start | bytes 1048576 | tf_op jit(solution)/shard_map/all_to_all | solution.py:121
  86.6 14.8 %all-to-all-start.6 = ((bf16[4,2,64,1024]{3,2,1,0:T(8,128)(2,1)}), bf16[4,2,64,1024]{3,2,1,0:T(8,128)(2,1)S(1)}, u32[]{:S(2)}, u32[]{:S(2)}) async-start(bf16[4,2,64,1024]{3,2,1,0:T(8,128)(2,1)} %broadcast_in_dim.22), calls=%async_computation.6 | async-start | bytes 2097152 | tf_op jit(solution)/shard_map/all_to_all | solution.py:121
  91.9 0.8 copy-start.12
  101.4 17.4 %all-to-all-start.3 = ((bf16[8,32,896]{2,1,0:T(8,128)(2,1)}), bf16[8,32,896]{2,1,0:T(8,128)(2,1)S(1)}, u32[]{:S(2)}, u32[]{:S(2)}) async-start(bf16[8,32,896]{2,1,0:T(8,128)(2,1)} %bitcast.41), calls=%async_computation.3 | async-start | bytes 917504 | tf_op jit(solution)/shard_map/all_to_all | solution.py:121
  104.9 1.5 %copy-start.2 = (bf16[1,896,1024]{2,1,0:T(8,128)(2,1)S(1)}, bf16[1,896,1024]{2,1,0:T(8,128)(2,1)}, u32[]{:S(2)}) copy-start(bf16[1,896,1024]{2,1,0:T(8,128)(2,1)} %param.11) | copy-start | bytes 5505028
  106.4 1.5 %copy-start.4 = (bf16[1,896,1024]{2,1,0:T(8,128)(2,1)S(1)}, bf16[1,896,1024]{2,1,0:T(8,128)(2,1)}, u32[]{:S(2)}) copy-start(bf16[1,896,1024]{2,1,0:T(8,128)(2,1)} %param.12) | copy-start | bytes 5505028
  107.9 14.4 %copy-start.8 = (bf16[8,32,896]{2,1,0:T(8,128)(2,1)S(1)}, bf16[8,32,896]{2,1,0:T(8,128)(2,1)}, u32[]{:S(2)}) copy-start(bf16[8,32,896]{2,1,0:T(8,128)(2,1)} %copy-done.6) | copy-start | bytes 1376260
  118.8 17.4 %all-to-all-start.7 = ((bf16[8,32,896]{2,1,0:T(8,128)(2,1)}), bf16[8,32,896]{2,1,0:T(8,128)(2,1)S(1)}, u32[]{:S(2)}, u32[]{:S(2)}) async-start(bf16[8,32,896]{2,1,0:T(8,128)(2,1)} %bitcast.11), calls=%async_computation.7 | async-start | bytes 917504 | tf_op jit(solution)/shard_map/all_to_all | solution.py:121
  127.3 1.9 %copy-start.10 = (bf16[256,512]{1,0:T(8,128)(2,1)S(1)}, bf16[256,512]{1,0:T(8,128)(2,1)}, u32[]{:S(2)}) copy-start(bf16[256,512]{1,0:T(8,128)(2,1)} %copy-done.9) | copy-start | bytes 786436
  127.3 1.9 %copy-start.18 = (f32[256,1]{1,0:T(8,128)S(1)}, f32[256,1]{1,0:T(8,128)}, u32[]{:S(2)}) copy-start(f32[256,1]{1,0:T(8,128)} %copy-done.16) | copy-start | bytes 3076
  (6 other events, 4.3 us)

commit v2 on v1

--- a/solution.py
+++ b/solution.py
@@ -54,24 +54,37 @@
     send_ref[...] = (weight_ref[...] * rows).astype(BF16)
 
 
-def gate_up_kernel(rows_ref, gate_ref, up_ref, out_ref):
-    rows = rows_ref[...]
-    dp, _, chunk, cols = out_ref.shape
+def local_order(ref, chunks):
+    mine = lax.axis_index("dp")
+    chunk = ref.shape[0] // chunks
+    return [
+        ref[pl.ds(pl.multiple_of((mine ^ k) * chunk, chunk), chunk), :] for k in range(chunks)
+    ]
+
+
+def gate_up_kernel(dp, rows_ref, gate_ref, up_ref, local_ref, *out_refs):
+    rows = jnp.concatenate(local_order(rows_ref, dp), axis=0)
+    local_ref[...] = rows
+    chunk = rows.shape[0] // dp
     for at, mat in enumerate((gate_ref, up_ref)):
         part = mm(rows, mat[...], ((1,), (0,))).astype(BF16)
-        out_ref[:, at] = part.reshape(dp, chunk, cols)
-
-
-def grad_act_kernel(grads_ref, down_ref, out_ref):
-    dp, chunk, cols = out_ref.shape
-    part = mm(grads_ref[...], down_ref[...], ((1,), (1,))).astype(BF16)
-    out_ref[...] = part.reshape(dp, chunk, cols)
-
-
-def group_sum(ref, *at):
-    total = ref[(0, *at)].astype(F32)
-    for group in range(1, ref.shape[0]):
-        total = total + ref[(group, *at)].astype(F32)
+        for k, out_ref in enumerate(out_refs):
+            out_ref[at] = part[k * chunk : (k + 1) * chunk]
+
+
+def grad_act_kernel(dp, grads_ref, down_ref, local_ref, *out_refs):
+    rows = jnp.concatenate(local_order(grads_ref, dp), axis=0)
+    local_ref[...] = rows
+    chunk = rows.shape[0] // dp
+    part = mm(rows, down_ref[...], ((1,), (1,))).astype(BF16)
+    for k, out_ref in enumerate(out_refs):
+        out_ref[...] = part[k * chunk : (k + 1) * chunk]
+
+
+def group_sum(refs, *at):
+    total = refs[0][at].astype(F32)
+    for ref in refs[1:]:
+        total = total + ref[at].astype(F32)
     return total
 
 
@@ -79,33 +92,46 @@
     return 1.0 / (1.0 + jnp.exp(-value))
 
 
-def act_kernel(sums_ref, act_ref):
-    gate = group_sum(sums_ref, 0)
-    up = group_sum(sums_ref, 1)
-    act_ref[...] = (gate * logistic(gate) * up).astype(BF16)
-
-
-def grad_pre_kernel(sums_ref, grad_ref, out_ref):
-    gate = group_sum(sums_ref, 0)
-    up = group_sum(sums_ref, 1)
-    grad = group_sum(grad_ref)
+def act_kernel(dp, *refs):
+    gate = group_sum(refs[:dp], 0)
+    up = group_sum(refs[:dp], 1)
+    refs[dp][...] = (gate * logistic(gate) * up).astype(BF16)
+
+
+def grad_pre_kernel(dp, *refs):
+    gate = group_sum(refs[:dp], 0)
+    up = group_sum(refs[:dp], 1)
+    grad = group_sum(refs[dp : 2 * dp], Ellipsis)
+    out_ref = refs[2 * dp]
     soft = logistic(gate)
     out_ref[0] = (grad * up * (soft * (1.0 + gate * (1.0 - soft)))).astype(BF16)
     out_ref[1] = (grad * (gate * soft)).astype(BF16)
 
 
-def expert_out_kernel(act_ref, down_ref, out_ref):
-    dp, chunk, hidden = act_ref.shape
-    act = act_ref[...].reshape(dp * chunk, hidden)
-    out_ref[...] = mm(act, down_ref[...], ((1,), (0,))).astype(BF16)
-
-
-def row_grad_kernel(pre_ref, gate_ref, up_ref, out_ref):
-    dp, _, chunk, hidden = pre_ref.shape
-    gate_pre = pre_ref[:, 0].reshape(dp * chunk, hidden)
-    up_pre = pre_ref[:, 1].reshape(dp * chunk, hidden)
+def store_natural(out_ref, rows, dp):
+    mine = lax.axis_index("dp")
+    chunk = rows.shape[0] // dp
+    for k in range(dp):
+        out_ref[pl.ds(pl.multiple_of((mine ^ k) * chunk, chunk), chunk), :] = rows[
+            k * chunk : (k + 1) * chunk
+        ]
+
+
+def expert_out_kernel(dp, *refs):
+    down_ref, act_ref, out_ref = refs[dp:]
+    act = jnp.concatenate([ref[...] for ref in refs[:dp]], axis=0)
+    act_ref[...] = act
+    store_natural(out_ref, mm(act, down_ref[...], ((1,), (0,))).astype(BF16), dp)
+
+
+def row_grad_kernel(dp, *refs):
+    gate_ref, up_ref, gate_pre_ref, up_pre_ref, out_ref = refs[dp:]
+    gate_pre = jnp.concatenate([ref[0] for ref in refs[:dp]], axis=0)
+    up_pre = jnp.concatenate([ref[1] for ref in refs[:dp]], axis=0)
+    gate_pre_ref[...] = gate_pre
+    up_pre_ref[...] = up_pre
     total = mm(gate_pre, gate_ref[...], ((1,), (1,))) + mm(up_pre, up_ref[...], ((1,), (1,)))
-    out_ref[...] = total.astype(BF16)
+    store_natural(out_ref, total.astype(BF16), dp)
 
 
 def scatter_scaled_kernel(pick_ref, weight_ref, back_ref, out_ref):
@@ -121,9 +147,11 @@
     return lax.all_to_all(value, axis, split_axis=0, concat_axis=0, tiled=True)
 
 
-def spread(value, axis):
-    size = lax.axis_size(axis)
-    return exchange(jnp.broadcast_to(value[None], (size, *value.shape)), axis)
+def trade(values):
+    size = lax.axis_size("dp")
+    return [values[0]] + [
+        lax.ppermute(values[k], "dp", [(i, i ^ k) for i in range(size)]) for k in range(1, size)
+    ]
 
 
 def body(tokens, grad_out, expert_ids, gates, w_gate, w_up, w_down):
@@ -160,54 +188,53 @@
     grads = exchange(send_grads.reshape(experts, capacity, features), "expert")
     grads = grads.reshape(slots, features)
 
-    tiles = 4 if hidden % 512 == 0 else 1
-    cols = hidden // tiles
-    part_pre = call(
-        gate_up_kernel,
-        shape((dp, 2, chunk, hidden), BF16),
+    sized = shape((slots, features), BF16)
+    rows, *part_pre = call(
+        functools.partial(gate_up_kernel, dp),
+        (sized, *[shape((2, chunk, hidden), BF16)] * dp),
         2 * product,
         2 * weights,
-        grid=(tiles,),
-        in_specs=[
-            pl.BlockSpec((slots, features), lambda i: (0, 0)),
-            pl.BlockSpec((features, cols), lambda i: (0, i)),
-            pl.BlockSpec((features, cols), lambda i: (0, i)),
-        ],
-        out_specs=pl.BlockSpec((dp, 2, chunk, cols), lambda i: (0, 0, 0, i)),
     )(rows, gate_mat, up_mat)
-    sums = exchange(part_pre, "dp")
-    part_grad = call(
-        grad_act_kernel,
-        shape((dp, chunk, hidden), BF16),
+    sums = trade(part_pre)
+    grads, *part_grad = call(
+        functools.partial(grad_act_kernel, dp),
+        (sized, *[shape((chunk, hidden), BF16)] * dp),
         product,
         weights,
-        grid=(tiles,),
-        in_specs=[
-            pl.BlockSpec((slots, features), lambda i: (0, 0)),
-            pl.BlockSpec((cols, features), lambda i: (i, 0)),
-        ],
-        out_specs=pl.BlockSpec((dp, chunk, cols), lambda i: (0, 0, i)),
     )(grads, down_mat)
-    act_mine = call(act_kernel, shape((chunk, hidden), BF16), 0, 4 * dp * chunk * hidden)(sums)
-    act = spread(act_mine, "dp")
-    grad_sums = exchange(part_grad, "dp")
-    expert_out = call(
-        expert_out_kernel, shape((slots, features), BF16), product, weights
-    )(act, down_mat)
+    act_mine = call(
+        functools.partial(act_kernel, dp),
+        shape((chunk, hidden), BF16),
+        0,
+        4 * dp * chunk * hidden,
+    )(*sums)
+    acts = trade([act_mine] * dp)
+    grad_sums = trade(part_grad)
+    act, expert_out = call(
+        functools.partial(expert_out_kernel, dp),
+        (shape((slots, hidden), BF16), sized),
+        product,
+        weights,
+    )(*acts, down_mat)
     back_out = exchange(expert_out.reshape(experts, capacity, features), "expert")
     pre_mine = call(
-        grad_pre_kernel, shape((2, chunk, hidden), BF16), 0, 6 * dp * chunk * hidden
-    )(sums, grad_sums)
-    pre = spread(pre_mine, "dp")
-    row_grad = call(
-        row_grad_kernel, shape((slots, features), BF16), 2 * product, 2 * weights
-    )(pre, gate_mat, up_mat)
+        functools.partial(grad_pre_kernel, dp),
+        shape((2, chunk, hidden), BF16),
+        0,
+        6 * dp * chunk * hidden,
+    )(*sums, *grad_sums)
+    pre = trade([pre_mine] * dp)
+    gate_pre, up_pre, row_grad = call(
+        functools.partial(row_grad_kernel, dp),
+        (*[shape((slots, hidden), BF16)] * 2, sized),
+        2 * product,
+        2 * weights,
+    )(*pre, gate_mat, up_mat)
     back_grad = exchange(row_grad.reshape(experts, capacity, features), "expert")
 
-    act_rows = act.reshape(slots, hidden)
-    grad_down = mm(act_rows, grads, ((0,), (0,))).astype(BF16)
-    grad_gate = mm(rows, pre[:, 0].reshape(slots, hidden), ((0,), (0,))).astype(BF16)
-    grad_up = mm(rows, pre[:, 1].reshape(slots, hidden), ((0,), (0,))).astype(BF16)
+    grad_down = mm(act, grads, ((0,), (0,))).astype(BF16)
+    grad_gate = mm(rows, gate_pre, ((0,), (0,))).astype(BF16)
+    grad_up = mm(rows, up_pre, ((0,), (0,))).astype(BF16)
 
     full = shape((tok_rows, features), BF16)
     mixed = call(

time: 139 us -> 118 us (0.85)
  waiting for transfers between devices: 66.1 us -> 51.6 us
  Pallas kernels: 13.9 us -> 9.18 us
  local copies, waits for them, and re-layouts: 17.5 us -> 16 us
    all_to_all x8 -> x4, waiting for transfers between devices: 66.1 us -> 17.4 us  [exchange(): return lax.all_to_all(value, axis, split_axis=0, concat_axis=0, tiled=True)]
    ppermute x0 -> x12, waiting for transfers between devices: none -> 34.2 us  [trade(): lax.ppermute(values[k], 'dp', [(i, i ^ k) for i in range(size)])]
    ppermute x0 -> x12, starting transfers between devices: none -> 14.1 us  [trade(): lax.ppermute(values[k], 'dp', [(i, i ^ k) for i in range(size)])]
    all_to_all x8 -> x4, starting transfers between devices: 32.4 us -> 18.8 us  [exchange(): return lax.all_to_all(value, axis, split_axis=0, concat_axis=0, tiled=True)]
    pallas_call x6, Pallas kernels: 9.15 us -> 4.47 us  [the longest x1 1.28 us: body(): call(functools.partial(row_grad_kernel, dp), (*[shape((slots, hidden), BF...]
    broadcast_in_dim x2 -> x0, local copies, waits for them, and re-layouts: 2.9 us -> none  [spread(): return exchange(jnp.broadcast_to(value[None], (size, *value.shape)), axis)]
    unnamed x44 -> x58, local copies, waits for them, and re-layouts: 14.5 us -> 16 us
  transfers between devices with their start and end apart: 8 -> 16, of which waited for: 8 -> 11; matrix products, arithmetic and copies ran while one was open for 5% -> 6% of each run, Pallas kernels for 9% -> 6%
where the time goes in v2:
time: 118 us
  waiting for transfers between devices  51.6 us (44%)
  starting transfers between devices  33 us (28%)
  local copies, waits for them, and re-layouts  16 us (14%)
  Pallas kernels  9.18 us (8%)
  matrix products  6.95 us (6%)
    ppermute x12, waiting for transfers between devices, trade(): lax.ppermute(values[k], 'dp', [(i, i ^ k) for i in range(size)])  34.2 us
    all_to_all x4, starting transfers between devices, exchange(): return lax.all_to_all(value, axis, split_axis=0, concat_axis=0, tiled=True)  18.8 us
    all_to_all x4, waiting for transfers between devices, exchange(): return lax.all_to_all(value, axis, split_axis=0, concat_axis=0, tiled=True)  17.4 us
    unnamed x58, local copies, waits for them, and re-layouts  16 us
    ppermute x12, starting transfers between devices, trade(): lax.ppermute(values[k], 'dp', [(i, i ^ k) for i in range(size)])  14.1 us
    dot_general x3, matrix products, mm(): lax.dot_general(left, right, (dims, ((), ())), preferred_element_type=F32)  6.95 us
  transfers between devices with their start and end apart: 16, of which 11 were waited for; matrix products, arithmetic and copies ran while one was open for 6% of the time, Pallas kernels for 6%

profile of v2, /device:TPU:0, one launch (start us, length us, event | category | flops | bytes accessed | tf_op | source)
XLA Modules:
  0.0 117.5 jit_solution(14103304685060282252)
XLA Ops:
  5.4 6.3 %all-to-all-start = ((bf16[8,32,896]{2,1,0:T(8,128)(2,1)}), bf16[8,32,896]{2,1,0:T(8,128)(2,1)S(1)}, u32[]{:S(2)}, u32[]{:S(2)}) async-start(bf16[8,32,896]{2,1,0:T(8,128)(2,1)} %bitcast.37), calls=%async_computation | async-start | bytes 917504 | tf_op jit(solution)/shard_map/all_to_all | solution.py:147
  13.9 11.8 %all-to-all-done = bf16[8,32,896]{2,1,0:T(8,128)(2,1)S(1)} async-done(((bf16[8,32,896]{2,1,0:T(8,128)(2,1)}), bf16[8,32,896]{2,1,0:T(8,128)(2,1)S(1)}, u32[]{:S(2)}, u32[]{:S(2)}) %all-to-all-start) | async-done | bytes 458784 | tf_op jit(solution)/shard_map/all_to_all | solution.py:147
  25.7 3.5 %all-to-all-start.2 = ((bf16[8,32,896]{2,1,0:T(8,128)(2,1)}), bf16[8,32,896]{2,1,0:T(8,128)(2,1)S(1)}, u32[]{:S(2)}, u32[]{:S(2)}) async-start(bf16[8,32,896]{2,1,0:T(8,128)(2,1)} %bitcast.9), calls=%async_computation.2 | async-start | bytes 917504 | tf_op jit(solution)/shard_map/all_to_all | solution.py:147
  29.2 1.5 %copy-done.1 = bf16[1,896,1024]{2,1,0:T(8,128)(2,1)S(1)} copy-done((bf16[1,896,1024]{2,1,0:T(8,128)(2,1)S(1)}, bf16[1,896,1024]{2,1,0:T(8,128)(2,1)}, u32[]{:S(2)}) %copy-start.1) | copy-done | bytes 1835032
  31.9 1.6 %collective-permute-start = (bf16[2,64,1024]{2,1,0:T(8,128)(2,1)S(1)}, bf16[2,64,1024]{2,1,0:T(8,128)(2,1)S(1)}, u32[]{:S(2)}, u32[]{:S(2)}) collective-permute-start(bf16[2,64,1024]{2,1,0:T(8,128)(2,1)S(1)} %get-tuple-element.27), channel_id=1, source_target_pairs={{0,8},{8,0},{16,24},{24,16},{1,9},{9,1},{17,25},{25,17},{2,10},{10... | collective-permute-start | bytes 786440 | tf_op jit(solution)/shard_map/ppermute | solution.py:153
  33.5 1.5 %collective-permute-start.1 = (bf16[2,64,1024]{2,1,0:T(8,128)(2,1)S(1)}, bf16[2,64,1024]{2,1,0:T(8,128)(2,1)S(1)}, u32[]{:S(2)}, u32[]{:S(2)}) collective-permute-start(bf16[2,64,1024]{2,1,0:T(8,128)(2,1)S(1)} %get-tuple-element.28), channel_id=1, source_target_pairs={{0,16},{8,24},{16,0},{24,8},{1,17},{9,25},{17,1},{25,9},{2,18},{10... | collective-permute-start | bytes 786440 | tf_op jit(solution)/shard_map/ppermute | solution.py:153
  35.5 5.6 %collective-permute-done.refs_1_ = bf16[2,64,1024]{2,1,0:T(8,128)(2,1)S(1)} collective-permute-done((bf16[2,64,1024]{2,1,0:T(8,128)(2,1)S(1)}, bf16[2,64,1024]{2,1,0:T(8,128)(2,1)S(1)}, u32[]{:S(2)}, u32[]{:S(2)}) %collective-permute-start) | collective-permute-done | bytes 262176 | tf_op jit(solution)/shard_map/ppermute | solution.py:153
  41.1 6.3 %collective-permute-done.1.refs_2_ = bf16[2,64,1024]{2,1,0:T(8,128)(2,1)S(1)} collective-permute-done((bf16[2,64,1024]{2,1,0:T(8,128)(2,1)S(1)}, bf16[2,64,1024]{2,1,0:T(8,128)(2,1)S(1)}, u32[]{:S(2)}, u32[]{:S(2)}) %collective-permute-start.1) | collective-permute-done | bytes 262176 | tf_op jit(solution)/shard_map/ppermute | solution.py:153
  50.9 1.4 %collective-permute-start.5 = (bf16[64,1024]{1,0:T(8,128)(2,1)S(1)}, bf16[64,1024]{1,0:T(8,128)(2,1)S(1)}, u32[]{:S(2)}, u32[]{:S(2)}) collective-permute-start(bf16[64,1024]{1,0:T(8,128)(2,1)S(1)} %shard_map.112.refs_0_), channel_id=1, source_target_pairs={{0,24},{8,16},{16,8},{24,0},{1,25},{9,17},{17,9},{25,1},{2,26},{10... | collective-permute-start | bytes 393224 | tf_op jit(solution)/shard_map/ppermute | solution.py:153
  52.3 2.6 %collective-permute-done.3.refs_1_ = bf16[64,1024]{1,0:T(8,128)(2,1)S(1)} collective-permute-done((bf16[64,1024]{1,0:T(8,128)(2,1)S(1)}, bf16[64,1024]{1,0:T(8,128)(2,1)S(1)}, u32[]{:S(2)}, u32[]{:S(2)}) %collective-permute-start.3) | collective-permute-done | bytes 131104 | tf_op jit(solution)/shard_map/ppermute | solution.py:153
  59.5 4.5 %all-to-all-start.1 = ((bf16[8,32,896]{2,1,0:T(8,128)(2,1)}), bf16[8,32,896]{2,1,0:T(8,128)(2,1)S(1)}, u32[]{:S(2)}, u32[]{:S(2)}) async-start(bf16[8,32,896]{2,1,0:T(8,128)(2,1)} %bitcast.35), calls=%async_computation.1 | async-start | bytes 917504 | tf_op jit(solution)/shard_map/all_to_all | solution.py:147
  64.1 1.5 %copy-done.4 = bf16[1,1024,896]{2,1,0:T(8,128)(2,1)S(1)} copy-done((bf16[1,1024,896]{2,1,0:T(8,128)(2,1)S(1)}, bf16[1,1024,896]{2,1,0:T(8,128)(2,1)}, u32[]{:S(2)}) %copy-start.4) | copy-done | bytes 1835032
  66.3 1.6 %collective-permute-start.6 = (bf16[64,1024]{1,0:T(8,128)(2,1)S(1)}, bf16[64,1024]{1,0:T(8,128)(2,1)S(1)}, u32[]{:S(2)}, u32[]{:S(2)}) collective-permute-start(bf16[64,1024]{1,0:T(8,128)(2,1)S(1)} %get-tuple-element.32), channel_id=1, source_target_pairs={{0,8},{8,0},{16,24},{24,16},{1,9},{9,1},{17,25},{25,17},{2,10},{10... | collective-permute-start | bytes 393224 | tf_op jit(solution)/shard_map/ppermute | solution.py:153
  69.9 2.7 %collective-permute-done.6.refs_5_ = bf16[64,1024]{1,0:T(8,128)(2,1)S(1)} collective-permute-done((bf16[64,1024]{1,0:T(8,128)(2,1)S(1)}, bf16[64,1024]{1,0:T(8,128)(2,1)S(1)}, u32[]{:S(2)}, u32[]{:S(2)}) %collective-permute-start.6) | collective-permute-done | bytes 131104 | tf_op jit(solution)/shard_map/ppermute | solution.py:153
  72.6 3.8 %collective-permute-done.7.refs_6_ = bf16[64,1024]{1,0:T(8,128)(2,1)S(1)} collective-permute-done((bf16[64,1024]{1,0:T(8,128)(2,1)S(1)}, bf16[64,1024]{1,0:T(8,128)(2,1)S(1)}, u32[]{:S(2)}, u32[]{:S(2)}) %collective-permute-start.7) | collective-permute-done | bytes 131104 | tf_op jit(solution)/shard_map/ppermute | solution.py:153
  81.7 1.4 %collective-permute-start.9 = (bf16[2,64,1024]{2,1,0:T(8,128)(2,1)S(1)}, bf16[2,64,1024]{2,1,0:T(8,128)(2,1)S(1)}, u32[]{:S(2)}, u32[]{:S(2)}) collective-permute-start(bf16[2,64,1024]{2,1,0:T(8,128)(2,1)S(1)} %shard_map.117.refs_0_), channel_id=1, source_target_pairs={{0,8},{8,0},{16,24},{24,16},{1,9},{9,1},{17,25},{25,17},{2,10},{10... | collective-permute-start | bytes 786440 | tf_op jit(solution)/shard_map/ppermute | solution.py:153
  83.1 9.6 %collective-permute-done.10.refs_2_ = bf16[2,64,1024]{2,1,0:T(8,128)(2,1)S(1)} collective-permute-done((bf16[2,64,1024]{2,1,0:T(8,128)(2,1)S(1)}, bf16[2,64,1024]{2,1,0:T(8,128)(2,1)S(1)}, u32[]{:S(2)}, u32[]{:S(2)}) %collective-permute-start.10) | collective-permute-done | bytes 262176 | tf_op jit(solution)/shard_map/ppermute | solution.py:153
  97.7 4.5 %all-to-all-start.3 = ((bf16[8,32,896]{2,1,0:T(8,128)(2,1)}), bf16[8,32,896]{2,1,0:T(8,128)(2,1)S(1)}, u32[]{:S(2)}, u32[]{:S(2)}) async-start(bf16[8,32,896]{2,1,0:T(8,128)(2,1)} %bitcast.36), calls=%async_computation.3 | async-start | bytes 917504 | tf_op jit(solution)/shard_map/all_to_all | solution.py:147
  102.2 3.2 %convert_bitcast_fusion = bf16[1,1024,896]{2,1,0:T(8,128)(2,1)} fusion(bf16[256,1024]{1,0:T(8,128)(2,1)} %copy-done.18, bf16[256,896]{1,0:T(8,128)(2,1)} %copy-done.26), kind=kOutput, calls=%fused_computation | convolution fusion | flops 470679552 | bytes 2818048 | tf_op jit(solution)/shard_map/dot_general | solution.py:16
  105.3 1.9 %convert_bitcast_fusion.1 = bf16[1,896,1024]{2,1,0:T(8,128)(2,1)} fusion(bf16[256,896]{1,0:T(8,128)(2,1)S(1)} %get-tuple-element.36, bf16[256,1024]{1,0:T(8,128)(2,1)S(1)} %copy-done.22), kind=kOutput, calls=%fused_computation.1 | convolution fusion | flops 470679552 | bytes 2818048 | tf_op jit(solution)/shard_map/dot_general | solution.py:16
  107.2 1.9 %convert_bitcast_fusion.2 = bf16[1,896,1024]{2,1,0:T(8,128)(2,1)} fusion(bf16[256,896]{1,0:T(8,128)(2,1)S(1)} %get-tuple-element.36, bf16[256,1024]{1,0:T(8,128)(2,1)S(1)} %copy-done.20), kind=kOutput, calls=%fused_computation.2 | convolution fusion | flops 470679552 | bytes 2818048 | tf_op jit(solution)/shard_map/dot_general | solution.py:16
  109.1 1.5 %shard_map.114 = bf16[512,896]{1,0:T(8,128)(2,1)} custom-call(bf16[256,512]{1,0:T(8,128)(2,1)S(1)} %get-tuple-element.23.pick_ref, f32[256,1]{1,0:T(8,128)S(1)} %copy-done.17, bf16[256,896]{1,0:T(8,128)(2,1)S(1)} %bitcast.31), custom_call_target="tpu_custom_call" | custom-call | flops 234881024 | bytes 1835008 | tf_op jit(solution)/shard_map/pallas_call | solution.py:240
  110.6 5.5 %all-to-all-done.3 = bf16[8,32,896]{2,1,0:T(8,128)(2,1)S(1)} async-done(((bf16[8,32,896]{2,1,0:T(8,128)(2,1)}), bf16[8,32,896]{2,1,0:T(8,128)(2,1)S(1)}, u32[]{:S(2)}, u32[]{:S(2)}) %all-to-all-start.3) | async-done | bytes 458784 | tf_op jit(solution)/shard_map/all_to_all | solution.py:147
  116.1 1.4 %shard_map.119 = bf16[512,896]{1,0:T(8,128)(2,1)} custom-call(bf16[256,512]{1,0:T(8,128)(2,1)S(1)} %get-tuple-element.23.pick_ref, bf16[256,896]{1,0:T(8,128)(2,1)S(1)} %bitcast.32), custom_call_target="tpu_custom_call" | custom-call | flops 234881024 | bytes 1835008 | tf_op jit(solution)/shard_map/pallas_call | solution.py:243
  (79 shorter events, 29.5 us)
Async XLA Ops:
  0.6 11.1 %copy-start.13 = (bf16[512,896]{1,0:T(8,128)(2,1)S(1)}, bf16[512,896]{1,0:T(8,128)(2,1)}, u32[]{:S(2)}) copy-start(bf16[512,896]{1,0:T(8,128)(2,1)} %grad_ref.1) | copy-start | bytes 2752516
  4.6 24.5 %copy-start = (bf16[1,896,1024]{2,1,0:T(8,128)(2,1)S(1)}, bf16[1,896,1024]{2,1,0:T(8,128)(2,1)}, u32[]{:S(2)}) copy-start(bf16[1,896,1024]{2,1,0:T(8,128)(2,1)} %param.11) | copy-start | bytes 5505028
  5.4 20.3 %all-to-all-start = ((bf16[8,32,896]{2,1,0:T(8,128)(2,1)}), bf16[8,32,896]{2,1,0:T(8,128)(2,1)S(1)}, u32[]{:S(2)}, u32[]{:S(2)}) async-start(bf16[8,32,896]{2,1,0:T(8,128)(2,1)} %bitcast.37), calls=%async_computation | async-start | bytes 917504 | tf_op jit(solution)/shard_map/all_to_all | solution.py:147
  25.7 33.8 %all-to-all-start.2 = ((bf16[8,32,896]{2,1,0:T(8,128)(2,1)}), bf16[8,32,896]{2,1,0:T(8,128)(2,1)S(1)}, u32[]{:S(2)}, u32[]{:S(2)}) async-start(bf16[8,32,896]{2,1,0:T(8,128)(2,1)} %bitcast.9), calls=%async_computation.2 | async-start | bytes 917504 | tf_op jit(solution)/shard_map/all_to_all | solution.py:147
  30.7 26.6 %copy-start.3 = (bf16[1,1024,896]{2,1,0:T(8,128)(2,1)S(1)}, bf16[1,1024,896]{2,1,0:T(8,128)(2,1)}, u32[]{:S(2)}) copy-start(bf16[1,1024,896]{2,1,0:T(8,128)(2,1)} %param.13) | copy-start | bytes 5505028
  31.9 9.2 %collective-permute-start = (bf16[2,64,1024]{2,1,0:T(8,128)(2,1)S(1)}, bf16[2,64,1024]{2,1,0:T(8,128)(2,1)S(1)}, u32[]{:S(2)}, u32[]{:S(2)}) collective-permute-start(bf16[2,64,1024]{2,1,0:T(8,128)(2,1)S(1)} %get-tuple-element.27), channel_id=1, source_target_pairs={{0,8},{8,0},{16,24},{24,16},{1,9},{9,1},{17,25},{25,17},{2,10},{10... | collective-permute-start | bytes 786440 | tf_op jit(solution)/shard_map/ppermute | solution.py:153
  33.5 13.9 %collective-permute-start.1 = (bf16[2,64,1024]{2,1,0:T(8,128)(2,1)S(1)}, bf16[2,64,1024]{2,1,0:T(8,128)(2,1)S(1)}, u32[]{:S(2)}, u32[]{:S(2)}) collective-permute-start(bf16[2,64,1024]{2,1,0:T(8,128)(2,1)S(1)} %get-tuple-element.28), channel_id=1, source_target_pairs={{0,16},{8,24},{16,0},{24,8},{1,17},{9,25},{17,1},{25,9},{2,18},{10... | collective-permute-start | bytes 786440 | tf_op jit(solution)/shard_map/ppermute | solution.py:153
  35.1 12.4 %collective-permute-start.2 = (bf16[2,64,1024]{2,1,0:T(8,128)(2,1)S(1)}, bf16[2,64,1024]{2,1,0:T(8,128)(2,1)S(1)}, u32[]{:S(2)}, u32[]{:S(2)}) collective-permute-start(bf16[2,64,1024]{2,1,0:T(8,128)(2,1)S(1)} %get-tuple-element.29), channel_id=1, source_target_pairs={{0,24},{8,16},{16,8},{24,0},{1,25},{9,17},{17,9},{25,1},{2,26},{10... | collective-permute-start | bytes 786440 | tf_op jit(solution)/shard_map/ppermute | solution.py:153
  41.1 18.4 %copy-start.7 = (bf16[2,64,1024]{2,1,0:T(8,128)(2,1)}, bf16[2,64,1024]{2,1,0:T(8,128)(2,1)S(1)}, u32[]{:S(2)}) copy-start(bf16[2,64,1024]{2,1,0:T(8,128)(2,1)S(1)} %collective-permute-done.refs_1_) | copy-start | bytes 786436
  47.5 9.8 %copy-start.11 = (bf16[2,64,1024]{2,1,0:T(8,128)(2,1)}, bf16[2,64,1024]{2,1,0:T(8,128)(2,1)S(1)}, u32[]{:S(2)}) copy-start(bf16[2,64,1024]{2,1,0:T(8,128)(2,1)S(1)} %collective-permute-done.2.refs_3_) | copy-start | bytes 786436
  48.8 6.1 %collective-permute-start.3 = (bf16[64,1024]{1,0:T(8,128)(2,1)S(1)}, bf16[64,1024]{1,0:T(8,128)(2,1)S(1)}, u32[]{:S(2)}, u32[]{:S(2)}) collective-permute-start(bf16[64,1024]{1,0:T(8,128)(2,1)S(1)} %shard_map.112.refs_0_), channel_id=1, source_target_pairs={{0,8},{8,0},{16,24},{24,16},{1,9},{9,1},{17,25},{25,17},{2,10},{10... | collective-permute-start | bytes 393224 | tf_op jit(solution)/shard_map/ppermute | solution.py:153
  49.6 6.5 %collective-permute-start.4 = (bf16[64,1024]{1,0:T(8,128)(2,1)S(1)}, bf16[64,1024]{1,0:T(8,128)(2,1)S(1)}, u32[]{:S(2)}, u32[]{:S(2)}) collective-permute-start(bf16[64,1024]{1,0:T(8,128)(2,1)S(1)} %shard_map.112.refs_0_), channel_id=1, source_target_pairs={{0,16},{8,24},{16,0},{24,8},{1,17},{9,25},{17,1},{25,9},{2,18},{10... | collective-permute-start | bytes 393224 | tf_op jit(solution)/shard_map/ppermute | solution.py:153
  50.9 6.4 %collective-permute-start.5 = (bf16[64,1024]{1,0:T(8,128)(2,1)S(1)}, bf16[64,1024]{1,0:T(8,128)(2,1)S(1)}, u32[]{:S(2)}, u32[]{:S(2)}) collective-permute-start(bf16[64,1024]{1,0:T(8,128)(2,1)S(1)} %shard_map.112.refs_0_), channel_id=1, source_target_pairs={{0,24},{8,16},{16,8},{24,0},{1,25},{9,17},{17,9},{25,1},{2,26},{10... | collective-permute-start | bytes 393224 | tf_op jit(solution)/shard_map/ppermute | solution.py:153
  59.5 38.1 %all-to-all-start.1 = ((bf16[8,32,896]{2,1,0:T(8,128)(2,1)}), bf16[8,32,896]{2,1,0:T(8,128)(2,1)S(1)}, u32[]{:S(2)}, u32[]{:S(2)}) async-start(bf16[8,32,896]{2,1,0:T(8,128)(2,1)} %bitcast.35), calls=%async_computation.1 | async-start | bytes 917504 | tf_op jit(solution)/shard_map/all_to_all | solution.py:147
  65.6 10.8 %copy-start.6 = (bf16[2,64,1024]{2,1,0:T(8,128)(2,1)S(1)}, bf16[2,64,1024]{2,1,0:T(8,128)(2,1)}, u32[]{:S(2)}) copy-start(bf16[2,64,1024]{2,1,0:T(8,128)(2,1)} %copy-done.5) | copy-start | bytes 786436
  65.6 28.4 %copy-start.2 = (bf16[1,896,1024]{2,1,0:T(8,128)(2,1)S(1)}, bf16[1,896,1024]{2,1,0:T(8,128)(2,1)}, u32[]{:S(2)}) copy-start(bf16[1,896,1024]{2,1,0:T(8,128)(2,1)} %param.12) | copy-start | bytes 5505028
  66.3 27.7 %copy-start.26 = (bf16[256,896]{1,0:T(8,128)(2,1)}, bf16[256,896]{1,0:T(8,128)(2,1)S(1)}, u32[]{:S(2)}) copy-start(bf16[256,896]{1,0:T(8,128)(2,1)S(1)} %get-tuple-element.40) | copy-start | bytes 1376260
  66.3 6.3 %collective-permute-start.6 = (bf16[64,1024]{1,0:T(8,128)(2,1)S(1)}, bf16[64,1024]{1,0:T(8,128)(2,1)S(1)}, u32[]{:S(2)}, u32[]{:S(2)}) collective-permute-start(bf16[64,1024]{1,0:T(8,128)(2,1)S(1)} %get-tuple-element.32), channel_id=1, source_target_pairs={{0,8},{8,0},{16,24},{24,16},{1,9},{9,1},{17,25},{25,17},{2,10},{10... | collective-permute-start | bytes 393224 | tf_op jit(solution)/shard_map/ppermute | solution.py:153
  68.0 8.4 %collective-permute-start.7 = (bf16[64,1024]{1,0:T(8,128)(2,1)S(1)}, bf16[64,1024]{1,0:T(8,128)(2,1)S(1)}, u32[]{:S(2)}, u32[]{:S(2)}) collective-permute-start(bf16[64,1024]{1,0:T(8,128)(2,1)S(1)} %get-tuple-element.33), channel_id=1, source_target_pairs={{0,16},{8,24},{16,0},{24,8},{1,17},{9,25},{17,1},{25,9},{2,18},{10... | collective-permute-start | bytes 393224 | tf_op jit(solution)/shard_map/ppermute | solution.py:153
  68.9 7.5 %collective-permute-start.8 = (bf16[64,1024]{1,0:T(8,128)(2,1)S(1)}, bf16[64,1024]{1,0:T(8,128)(2,1)S(1)}, u32[]{:S(2)}, u32[]{:S(2)}) collective-permute-start(bf16[64,1024]{1,0:T(8,128)(2,1)S(1)} %get-tuple-element.34), channel_id=1, source_target_pairs={{0,24},{8,16},{16,8},{24,0},{1,25},{9,17},{17,9},{25,1},{2,26},{10... | collective-permute-start | bytes 393224 | tf_op jit(solution)/shard_map/ppermute | solution.py:153
  79.6 13.2 %collective-permute-start.10 = (bf16[2,64,1024]{2,1,0:T(8,128)(2,1)S(1)}, bf16[2,64,1024]{2,1,0:T(8,128)(2,1)S(1)}, u32[]{:S(2)}, u32[]{:S(2)}) collective-permute-start(bf16[2,64,1024]{2,1,0:T(8,128)(2,1)S(1)} %shard_map.117.refs_0_), channel_id=1, source_target_pairs={{0,16},{8,24},{16,0},{24,8},{1,17},{9,25},{17,1},{25,9},{2,18},{10... | collective-permute-start | bytes 786440 | tf_op jit(solution)/shard_map/ppermute | solution.py:153
  80.6 12.2 %collective-permute-start.11 = (bf16[2,64,1024]{2,1,0:T(8,128)(2,1)S(1)}, bf16[2,64,1024]{2,1,0:T(8,128)(2,1)S(1)}, u32[]{:S(2)}, u32[]{:S(2)}) collective-permute-start(bf16[2,64,1024]{2,1,0:T(8,128)(2,1)S(1)} %shard_map.117.refs_0_), channel_id=1, source_target_pairs={{0,24},{8,16},{16,8},{24,0},{1,25},{9,17},{17,9},{25,1},{2,26},{10... | collective-permute-start | bytes 786440 | tf_op jit(solution)/shard_map/ppermute | solution.py:153
  81.7 12.2 %collective-permute-start.9 = (bf16[2,64,1024]{2,1,0:T(8,128)(2,1)S(1)}, bf16[2,64,1024]{2,1,0:T(8,128)(2,1)S(1)}, u32[]{:S(2)}, u32[]{:S(2)}) collective-permute-start(bf16[2,64,1024]{2,1,0:T(8,128)(2,1)S(1)} %shard_map.117.refs_0_), channel_id=1, source_target_pairs={{0,8},{8,0},{16,24},{24,16},{1,9},{9,1},{17,25},{25,17},{2,10},{10... | collective-permute-start | bytes 786440 | tf_op jit(solution)/shard_map/ppermute | solution.py:153
  97.7 18.5 %all-to-all-start.3 = ((bf16[8,32,896]{2,1,0:T(8,128)(2,1)}), bf16[8,32,896]{2,1,0:T(8,128)(2,1)S(1)}, u32[]{:S(2)}, u32[]{:S(2)}) async-start(bf16[8,32,896]{2,1,0:T(8,128)(2,1)} %bitcast.36), calls=%async_computation.3 | async-start | bytes 917504 | tf_op jit(solution)/shard_map/all_to_all | solution.py:147
  (21 other events, 27.7 us)

commit v3 on v2

v3 whole, which is shorter than its diff:
```python
import functools

import jax
import jax.numpy as jnp
from jax import lax
from jax.experimental import pallas as pl
from jax.experimental.pallas import tpu as pltpu
from jax.sharding import PartitionSpec as P

F32 = jnp.float32
BF16 = jnp.bfloat16
VMEM_LIMIT = 24 * 1024 * 1024


def mm(left, right, dims):
    return lax.dot_general(left, right, (dims, ((), ())), preferred_element_type=F32)


def call(kernel, out_shape, flops=0, moved=0, **kwargs):
    return pl.pallas_call(
        kernel,
        out_shape=out_shape,
        cost_estimate=pl.CostEstimate(flops=flops, bytes_accessed=moved, transcendentals=0),
        compiler_params=pltpu.CompilerParams(vmem_limit_bytes=VMEM_LIMIT),
        **kwargs,
    )


def split_rows(refs, value):
    rows = value.shape[0] // len(refs)
    for k, ref in enumerate(refs):
        ref[...] = value[k * rows : (k + 1) * rows]


def join_rows(refs):
    return jnp.concatenate([ref[...] for ref in refs], axis=0)


def route_kernel(experts, ids_ref, gates_ref, tokens_ref, pick_ref, weight_ref, *send_refs):
    ids = ids_ref[...]
    tok_rows = ids.shape[1]
    slots = pick_ref.shape[0]
    inside = ids < experts
    routed = jnp.max(inside.astype(jnp.int32), axis=0, keepdims=True)
    chosen = jnp.sum(jnp.where(inside, ids, 0), axis=0, keepdims=True)
    weight = jnp.sum(jnp.where(inside, gates_ref[...], 0.0), axis=0, keepdims=True)
    key = jnp.where(routed > 0, chosen ^ lax.axis_index("expert"), experts)
    hot = lax.broadcasted_iota(jnp.int32, (experts, tok_rows), 0) == key
    earlier = lax.broadcasted_iota(jnp.int32, (tok_rows, tok_rows), 0) < lax.broadcasted_iota(
        jnp.int32, (tok_rows, tok_rows), 1
    )
    before = mm(hot.astype(F32).astype(BF16), earlier.astype(F32).astype(BF16), ((1,), (0,)))
    position = jnp.sum(jnp.where(hot, before, 0.0), axis=0, keepdims=True).astype(jnp.int32)
    slot = jnp.where(routed > 0, key * (slots // experts) + position, slots)
    pick = lax.broadcasted_iota(jnp.int32, (slots, tok_rows), 0) == slot
    weight_ref[...] = jnp.sum(jnp.where(pick, weight, 0.0), axis=1, keepdims=True)
    pick = pick.astype(F32).astype(BF16)
    pick_ref[...] = pick
    split_rows(send_refs, mm(pick, tokens_ref[...], ((1,), (0,))).astype(BF16))


def gather_scaled_kernel(pick_ref, weight_ref, grad_ref, *send_refs):
    rows = mm(pick_ref[...], grad_ref[...], ((1,), (0,)))
    split_rows(send_refs, (weight_ref[...] * rows).astype(BF16))


def chunk_rows(rows, dp, k):
    chunk = rows // dp
    mine = lax.axis_index("dp")
    return pl.ds(pl.multiple_of((mine ^ k) * chunk, chunk), chunk)


def local_order(refs, scratch, dp):
    scratch[...] = join_rows(refs)
    rows = scratch.shape[0]
    return jnp.concatenate([scratch[chunk_rows(rows, dp, k), :] for k in range(dp)], axis=0)


def gate_up_kernel(dp, experts, *refs):
    gate_ref, up_ref, local_ref = refs[experts : experts + 3]
    out_refs = refs[experts + 3 : experts + 3 + dp]
    rows = local_order(refs[:experts], refs[-1], dp)
    local_ref[...] = rows
    chunk = rows.shape[0] // dp
    for at, mat in enumerate((gate_ref, up_ref)):
        part = mm(rows, mat[...], ((1,), (0,))).astype(BF16)
        for k, out_ref in enumerate(out_refs):
            out_ref[at] = part[k * chunk : (k + 1) * chunk]


def grad_act_kernel(dp, experts, *refs):
    down_ref, local_ref = refs[experts : experts + 2]
    out_refs = refs[experts + 2 : experts + 2 + dp]
    rows = local_order(refs[:experts], refs[-1], dp)
    local_ref[...] = rows
    split_rows(out_refs, mm(rows, down_ref[...], ((1,), (1,))).astype(BF16))


def group_sum(refs, *at):
    total = refs[0][at].astype(F32)
    for ref in refs[1:]:
        total = total + ref[at].astype(F32)
    return total


def logistic(value):
    return 1.0 / (1.0 + jnp.exp(-value))


def act_kernel(dp, *refs):
    gate = group_sum(refs[:dp], 0)
    up = group_sum(refs[:dp], 1)
    refs[dp][...] = (gate * logistic(gate) * up).astype(BF16)


def grad_pre_kernel(dp, *refs):
    gate = group_sum(refs[:dp], 0)
    up = group_sum(refs[:dp], 1)
    grad = group_sum(refs[dp : 2 * dp], Ellipsis)
    out_ref = refs[2 * dp]
    soft = logistic(gate)
    out_ref[0] = (grad * up * (soft * (1.0 + gate * (1.0 - soft)))).astype(BF16)
    out_ref[1] = (grad * (gate * soft)).astype(BF16)


def send_back(out_refs, scratch, rows, dp):
    chunk = rows.shape[0] // dp
    for k in range(dp):
        scratch[chunk_rows(rows.shape[0], dp, k), :] = rows[k * chunk : (k + 1) * chunk]
    split_rows(out_refs, scratch[...])


def expert_out_kernel(dp, *refs):
    down_ref, act_ref, *out_refs, scratch = refs[dp:]
    act = join_rows(refs[:dp])
    act_ref[...] = act
    send_back(out_refs, scratch, mm(act, down_ref[...], ((1,), (0,))).astype(BF16), dp)


def row_grad_kernel(dp, *refs):
    gate_ref, up_ref, gate_pre_ref, up_pre_ref, *out_refs, scratch = refs[dp:]
    gate_pre = jnp.concatenate([ref[0] for ref in refs[:dp]], axis=0)
    up_pre = jnp.concatenate([ref[1] for ref in refs[:dp]], axis=0)
    gate_pre_ref[...] = gate_pre
    up_pre_ref[...] = up_pre
    total = mm(gate_pre, gate_ref[...], ((1,), (1,))) + mm(up_pre, up_ref[...], ((1,), (1,)))
    send_back(out_refs, scratch, total.astype(BF16), dp)


def scatter_scaled_kernel(pick_ref, weight_ref, *refs):
    scaled = (weight_ref[...] * join_rows(refs[:-1]).astype(F32)).astype(BF16)
    refs[-1][...] = mm(pick_ref[...], scaled, ((0,), (0,))).astype(BF16)


def scatter_kernel(pick_ref, *refs):
    refs[-1][...] = mm(pick_ref[...], join_rows(refs[:-1]), ((0,), (0,))).astype(BF16)


def trade(values, axis):
    size = lax.axis_size(axis)
    return [values[0]] + [
        lax.ppermute(values[k], axis, [(i, i ^ k) for i in range(size)]) for k in range(1, size)
    ]


def body(tokens, grad_out, expert_ids, gates, w_gate, w_up, w_down):
    experts = lax.axis_size("expert")
    dp = lax.axis_size("dp")
    tok_rows, features = tokens.shape
    capacity = tok_rows // 16
    slots = experts * capacity
    hidden = w_gate.shape[2]
    chunk = slots // dp
    gate_mat, up_mat, down_mat = w_gate[0], w_up[0], w_down[0]
    shape = jax.ShapeDtypeStruct
    product = 2 * slots * features * hidden
    weights = 2 * features * hidden

    blocks = [shape((capacity, features), BF16)] * experts
    sized = shape((slots, features), BF16)
    wide = shape((slots, hidden), BF16)
    in_order = [pltpu.VMEM((slots, features), BF16)]

    pick, weight, *send_tokens = call(
        functools.partial(route_kernel, experts),
        (shape((slots, tok_rows), BF16), shape((slots, 1), F32), *blocks),
        2 * slots * tok_rows * features,
        4 * tok_rows * features,
    )(expert_ids.T, gates.T, tokens)
    rows = trade(send_tokens, "expert")
    send_grads = call(
        gather_scaled_kernel,
        blocks,
        2 * slots * tok_rows * features,
        4 * tok_rows * features,
    )(pick, weight, grad_out)
    grads = trade(send_grads, "expert")

    rows, *part_pre = call(
        functools.partial(gate_up_kernel, dp, experts),
        (sized, *[shape((2, chunk, hidden), BF16)] * dp),
        2 * product,
        2 * weights,
        scratch_shapes=in_order,
    )(*rows, gate_mat, up_mat)
    sums = trade(part_pre, "dp")
    grads, *part_grad = call(
        functools.partial(grad_act_kernel, dp, experts),
        (sized, *[shape((chunk, hidden), BF16)] * dp),
        product,
        weights,
        scratch_shapes=in_order,
    )(*grads, down_mat)
    grad_sums = trade(part_grad, "dp")
    sums, part_grad = lax.optimization_barrier((sums, part_grad))
    act_mine = call(
        functools.partial(act_kernel, dp),
        shape((chunk, hidden), BF16),
        0,
        4 * dp * chunk * hidden,
    )(*sums)
    acts = trade([act_mine] * dp, "dp")
    pre_mine = call(
        functools.partial(grad_pre_kernel, dp),
        shape((2, chunk, hidden), BF16),
        0,
        6 * dp * chunk * hidden,
    )(*sums, *grad_sums)
    pre = trade([pre_mine] * dp, "dp")
    act, *expert_out = call(
        functools.partial(expert_out_kernel, dp),
        (wide, *blocks),
        product,
        weights,
        scratch_shapes=in_order,
    )(*acts, down_mat)
    back_out = trade(expert_out, "expert")
    gate_pre, up_pre, *row_grad = call(
        functools.partial(row_grad_kernel, dp),
        (wide, wide, *blocks),
        2 * product,
        2 * weights,
        scratch_shapes=in_order,
    )(*pre, gate_mat, up_mat)
    back_grad = trade(row_grad, "expert")

    grad_down = mm(act, grads, ((0,), (0,))).astype(BF16)
    grad_gate = mm(rows, gate_pre, ((0,), (0,))).astype(BF16)
    grad_up = mm(rows, up_pre, ((0,), (0,))).astype(BF16)

    full = shape((tok_rows, features), BF16)
    mixed = call(
        scatter_scaled_kernel, full, 2 * slots * tok_rows * features, 4 * tok_rows * features
    )(pick, weight, *back_out)
    grad_tokens = call(
        scatter_kernel, full, 2 * slots * tok_rows * features, 4 * tok_rows * features
    )(pick, *back_grad)
    return (mixed, grad_tokens, grad_gate[None], grad_up[None], grad_down[None])


def solution(mesh):
    placed = (
        P("expert", "dp"),
        P("expert", "dp"),
        P("expert", None),
        P("expert", None),
        P("expert", "dp", None),
        P("expert", "dp", None),
        P("expert", None, "dp"),
    )
    return jax.shard_map(
        body,
        mesh=mesh,
        in_specs=placed,
        out_specs=(
            P("expert", "dp"),
            P("expert", "dp"),
            P("expert", "dp", None),
            P("expert", "dp", None),
            P("expert", None, "dp"),
        ),
        check_vma=False,
    )
```

time: 118 us -> 98.7 us (0.84)
  waiting for transfers between devices: 51.6 us -> 28.8 us
  starting transfers between devices: 33 us -> 49.1 us
  local copies, waits for them, and re-layouts: 16 us -> 5.43 us
  matrix products: 6.95 us -> 5.77 us
    ppermute x12 -> x40, starting transfers between devices: 14.1 us -> 49.1 us  [trade(): lax.ppermute(values[k], axis, [(i, i ^ k) for i in range(size)])]
    all_to_all x4 -> x0, starting transfers between devices: 18.8 us -> none  [exchange(): return lax.all_to_all(value, axis, split_axis=0, concat_axis=0, tiled=True)]
    all_to_all x4 -> x0, waiting for transfers between devices: 17.4 us -> none  [exchange(): return lax.all_to_all(value, axis, split_axis=0, concat_axis=0, tiled=True)]
    unnamed x58 -> x16, local copies, waits for them, and re-layouts: 16 us -> 5.43 us
    ppermute x12 -> x40, waiting for transfers between devices: 34.2 us -> 28.8 us  [trade(): lax.ppermute(values[k], axis, [(i, i ^ k) for i in range(size)])]
    dot_general x3, matrix products: 6.95 us -> 5.77 us  [mm(): lax.dot_general(left, right, (dims, ((), ())), preferred_element_type=F32)]
  transfers between devices with their start and end apart: 16 -> 40, of which waited for: 11 -> 15; matrix products, arithmetic and copies ran while one was open for 6% -> 6% of each run, Pallas kernels for 6% -> 5%
where the time goes in v3:
time: 98.7 us; the launch traced here: 98.4 us
  starting transfers between devices  49.1 us (50%)
  waiting for transfers between devices  28.8 us (29%)
  Pallas kernels  8.53 us (9%)
  matrix products  5.77 us (6%)
  local copies, waits for them, and re-layouts  5.43 us (6%)
    ppermute x40, starting transfers between devices, trade(): lax.ppermute(values[k], axis, [(i, i ^ k) for i in range(size)])  49.1 us
    ppermute x40, waiting for transfers between devices, trade(): lax.ppermute(values[k], axis, [(i, i ^ k) for i in range(size)])  28.8 us
    dot_general x3, matrix products, mm(): lax.dot_general(left, right, (dims, ((), ())), preferred_element_type=F32)  5.77 us
    unnamed x16, local copies, waits for them, and re-layouts  5.43 us
  transfers between devices with their start and end apart: 40, of which 15 were waited for; matrix products, arithmetic and copies ran while one was open for 6% of the time, Pallas kernels for 5%

profile of v3, /device:TPU:0, one launch (start us, length us, event | category | flops | bytes accessed | tf_op | source)
XLA Modules:
  0.0 98.4 jit_solution(9968215257799746291)
XLA Ops:
  4.6 2.6 %collective-permute-start.1 = (bf16[32,896]{1,0:T(8,128)(2,1)S(1)}, bf16[32,896]{1,0:T(8,128)(2,1)S(1)}, u32[]{:S(2)}, u32[]{:S(2)}) collective-permute-start(bf16[32,896]{1,0:T(8,128)(2,1)S(1)} %get-tuple-element.60), channel_id=1, source_target_pairs={{0,2},{1,3},{2,0},{3,1},{4,6},{5,7},{6,4},{7,5},{8,10},{9,11},{10,... | collective-permute-start | bytes 172040 | tf_op jit(solution)/shard_map/ppermute | solution.py:162
  7.3 2.7 %collective-permute-start.3 = (bf16[32,896]{1,0:T(8,128)(2,1)S(1)}, bf16[32,896]{1,0:T(8,128)(2,1)S(1)}, u32[]{:S(2)}, u32[]{:S(2)}) collective-permute-start(bf16[32,896]{1,0:T(8,128)(2,1)S(1)} %get-tuple-element.62), channel_id=1, source_target_pairs={{0,4},{1,5},{2,6},{3,7},{4,0},{5,1},{6,2},{7,3},{8,12},{9,13},{10,... | collective-permute-start | bytes 172040 | tf_op jit(solution)/shard_map/ppermute | solution.py:162
  10.0 3.6 %collective-permute-start.5 = (bf16[32,896]{1,0:T(8,128)(2,1)S(1)}, bf16[32,896]{1,0:T(8,128)(2,1)S(1)}, u32[]{:S(2)}, u32[]{:S(2)}) collective-permute-start(bf16[32,896]{1,0:T(8,128)(2,1)S(1)} %get-tuple-element.64), channel_id=1, source_target_pairs={{0,6},{1,7},{2,4},{3,5},{4,2},{5,3},{6,0},{7,1},{8,14},{9,15},{10,... | collective-permute-start | bytes 172040 | tf_op jit(solution)/shard_map/ppermute | solution.py:162
  15.8 2.6 %collective-permute-done.4.refs_5_ = bf16[32,896]{1,0:T(8,128)(2,1)S(1)} collective-permute-done((bf16[32,896]{1,0:T(8,128)(2,1)S(1)}, bf16[32,896]{1,0:T(8,128)(2,1)S(1)}, u32[]{:S(2)}, u32[]{:S(2)}) %collective-permute-start.4) | collective-permute-done | bytes 57376 | tf_op jit(solution)/shard_map/ppermute | solution.py:162
  25.8 3.2 %collective-permute-start.11 = (bf16[32,896]{1,0:T(8,128)(2,1)S(1)}, bf16[32,896]{1,0:T(8,128)(2,1)S(1)}, u32[]{:S(2)}, u32[]{:S(2)}) collective-permute-start(bf16[32,896]{1,0:T(8,128)(2,1)S(1)} %get-tuple-element.72), channel_id=1, source_target_pairs={{0,2},{1,3},{2,0},{3,1},{4,6},{5,7},{6,4},{7,5},{8,10},{9,11},{10,... | collective-permute-start | bytes 172040 | tf_op jit(solution)/shard_map/ppermute | solution.py:162
  28.9 2.1 %collective-permute-done.11.refs_2_ = bf16[32,896]{1,0:T(8,128)(2,1)S(1)} collective-permute-done((bf16[32,896]{1,0:T(8,128)(2,1)S(1)}, bf16[32,896]{1,0:T(8,128)(2,1)S(1)}, u32[]{:S(2)}, u32[]{:S(2)}) %collective-permute-start.11) | collective-permute-done | bytes 57376 | tf_op jit(solution)/shard_map/ppermute | solution.py:162
  31.1 3.1 %collective-permute-start.13 = (bf16[32,896]{1,0:T(8,128)(2,1)S(1)}, bf16[32,896]{1,0:T(8,128)(2,1)S(1)}, u32[]{:S(2)}, u32[]{:S(2)}) collective-permute-start(bf16[32,896]{1,0:T(8,128)(2,1)S(1)} %get-tuple-element.74), channel_id=1, source_target_pairs={{0,4},{1,5},{2,6},{3,7},{4,0},{5,1},{6,2},{7,3},{8,12},{9,13},{10,... | collective-permute-start | bytes 172040 | tf_op jit(solution)/shard_map/ppermute | solution.py:162
  34.6 1.8 %collective-permute-done.13.refs_4_ = bf16[32,896]{1,0:T(8,128)(2,1)S(1)} collective-permute-done((bf16[32,896]{1,0:T(8,128)(2,1)S(1)}, bf16[32,896]{1,0:T(8,128)(2,1)S(1)}, u32[]{:S(2)}, u32[]{:S(2)}) %collective-permute-start.13) | collective-permute-done | bytes 57376 | tf_op jit(solution)/shard_map/ppermute | solution.py:162
  36.4 2.3 %collective-permute-start.15 = (bf16[32,896]{1,0:T(8,128)(2,1)S(1)}, bf16[32,896]{1,0:T(8,128)(2,1)S(1)}, u32[]{:S(2)}, u32[]{:S(2)}) collective-permute-start(bf16[32,896]{1,0:T(8,128)(2,1)S(1)} %get-tuple-element.76), channel_id=1, source_target_pairs={{0,6},{1,7},{2,4},{3,5},{4,2},{5,3},{6,0},{7,1},{8,14},{9,15},{10,... | collective-permute-start | bytes 172040 | tf_op jit(solution)/shard_map/ppermute | solution.py:162
  42.5 3.1 %collective-permute-done.16.refs_7_ = bf16[32,896]{1,0:T(8,128)(2,1)S(1)} collective-permute-done((bf16[32,896]{1,0:T(8,128)(2,1)S(1)}, bf16[32,896]{1,0:T(8,128)(2,1)S(1)}, u32[]{:S(2)}, u32[]{:S(2)}) %collective-permute-start.16) | collective-permute-done | bytes 57376 | tf_op jit(solution)/shard_map/ppermute | solution.py:162
  53.1 2.3 %collective-permute-start.29 = (bf16[64,1024]{1,0:T(8,128)(2,1)S(1)}, bf16[64,1024]{1,0:T(8,128)(2,1)S(1)}, u32[]{:S(2)}, u32[]{:S(2)}) collective-permute-start(bf16[64,1024]{1,0:T(8,128)(2,1)S(1)} %get-tuple-element.81), channel_id=1, source_target_pairs={{0,24},{8,16},{16,8},{24,0},{1,25},{9,17},{17,9},{25,1},{2,26},{10... | collective-permute-start | bytes 393224 | tf_op jit(solution)/shard_map/ppermute | solution.py:162
  55.4 2.1 %collective-permute-done.18.refs_2_ = bf16[64,1024]{1,0:T(8,128)(2,1)S(1)} collective-permute-done((bf16[64,1024]{1,0:T(8,128)(2,1)S(1)}, bf16[64,1024]{1,0:T(8,128)(2,1)S(1)}, u32[]{:S(2)}, u32[]{:S(2)}) %collective-permute-start.18) | collective-permute-done | bytes 131104 | tf_op jit(solution)/shard_map/ppermute | solution.py:162
  58.6 1.6 %collective-permute-start.22 = (bf16[32,896]{1,0:T(8,128)(2,1)S(1)}, bf16[32,896]{1,0:T(8,128)(2,1)S(1)}, u32[]{:S(2)}, u32[]{:S(2)}) collective-permute-start(bf16[32,896]{1,0:T(8,128)(2,1)S(1)} %get-tuple-element.89), channel_id=1, source_target_pairs={{0,3},{1,2},{2,1},{3,0},{4,7},{5,6},{6,5},{7,4},{8,11},{9,10},{10,... | collective-permute-start | bytes 172040 | tf_op jit(solution)/shard_map/ppermute | solution.py:162
  63.0 2.3 %collective-permute-start.32 = (bf16[2,64,1024]{2,1,0:T(8,128)(2,1)S(1)}, bf16[2,64,1024]{2,1,0:T(8,128)(2,1)S(1)}, u32[]{:S(2)}, u32[]{:S(2)}) collective-permute-start(bf16[2,64,1024]{2,1,0:T(8,128)(2,1)S(1)} %shard_map.117.refs_0_), channel_id=1, source_target_pairs={{0,24},{8,16},{16,8},{24,0},{1,25},{9,17},{17,9},{25,1},{2,26},{10... | collective-permute-start | bytes 786440 | tf_op jit(solution)/shard_map/ppermute | solution.py:162
  65.9 6.8 %collective-permute-done.23.refs_4_ = bf16[32,896]{1,0:T(8,128)(2,1)S(1)} collective-permute-done((bf16[32,896]{1,0:T(8,128)(2,1)S(1)}, bf16[32,896]{1,0:T(8,128)(2,1)S(1)}, u32[]{:S(2)}, u32[]{:S(2)}) %collective-permute-start.23) | collective-permute-done | bytes 57376 | tf_op jit(solution)/shard_map/ppermute | solution.py:162
  74.9 2.0 %convert_bitcast_fusion = bf16[1,1024,896]{2,1,0:T(8,128)(2,1)} fusion(bf16[256,1024]{1,0:T(8,128)(2,1)S(1)} %get-tuple-element.105, bf16[256,896]{1,0:T(8,128)(2,1)S(1)} %get-tuple-element.106), kind=kOutput, calls=%fused_computation | convolution fusion | flops 470679552 | bytes 2818048 | tf_op jit(solution)/shard_map/dot_general | solution.py:16
  76.9 1.8 %collective-permute-done.25.refs_6_ = bf16[32,896]{1,0:T(8,128)(2,1)S(1)} collective-permute-done((bf16[32,896]{1,0:T(8,128)(2,1)S(1)}, bf16[32,896]{1,0:T(8,128)(2,1)S(1)}, u32[]{:S(2)}, u32[]{:S(2)}) %collective-permute-start.25) | collective-permute-done | bytes 57376 | tf_op jit(solution)/shard_map/ppermute | solution.py:162
  83.0 1.7 %collective-permute-start.35 = (bf16[32,896]{1,0:T(8,128)(2,1)S(1)}, bf16[32,896]{1,0:T(8,128)(2,1)S(1)}, u32[]{:S(2)}, u32[]{:S(2)}) collective-permute-start(bf16[32,896]{1,0:T(8,128)(2,1)S(1)} %get-tuple-element.97), channel_id=1, source_target_pairs={{0,3},{1,2},{2,1},{3,0},{4,7},{5,6},{6,5},{7,4},{8,11},{9,10},{10,... | collective-permute-start | bytes 172040 | tf_op jit(solution)/shard_map/ppermute | solution.py:162
  85.5 1.9 %collective-permute-start.37 = (bf16[32,896]{1,0:T(8,128)(2,1)S(1)}, bf16[32,896]{1,0:T(8,128)(2,1)S(1)}, u32[]{:S(2)}, u32[]{:S(2)}) collective-permute-start(bf16[32,896]{1,0:T(8,128)(2,1)S(1)} %get-tuple-element.99), channel_id=1, source_target_pairs={{0,5},{1,4},{2,7},{3,6},{4,1},{5,0},{6,3},{7,2},{8,13},{9,12},{10,... | collective-permute-start | bytes 172040 | tf_op jit(solution)/shard_map/ppermute | solution.py:162
  87.4 1.9 %convert_bitcast_fusion.1 = bf16[1,896,1024]{2,1,0:T(8,128)(2,1)} fusion(bf16[256,896]{1,0:T(8,128)(2,1)S(1)} %get-tuple-element.102, bf16[256,1024]{1,0:T(8,128)(2,1)S(1)} %get-tuple-element.104), kind=kOutput, calls=%fused_computation.1 | convolution fusion | flops 470679552 | bytes 2818048 | tf_op jit(solution)/shard_map/dot_general | solution.py:16
  89.3 1.9 %collective-permute-start.38 = (bf16[32,896]{1,0:T(8,128)(2,1)S(1)}, bf16[32,896]{1,0:T(8,128)(2,1)S(1)}, u32[]{:S(2)}, u32[]{:S(2)}) collective-permute-start(bf16[32,896]{1,0:T(8,128)(2,1)S(1)} %get-tuple-element.100), channel_id=1, source_target_pairs={{0,6},{1,7},{2,4},{3,5},{4,2},{5,3},{6,0},{7,1},{8,14},{9,15},{10,... | collective-permute-start | bytes 172040 | tf_op jit(solution)/shard_map/ppermute | solution.py:162
  91.2 1.6 %collective-permute-start.39 = (bf16[32,896]{1,0:T(8,128)(2,1)S(1)}, bf16[32,896]{1,0:T(8,128)(2,1)S(1)}, u32[]{:S(2)}, u32[]{:S(2)}) collective-permute-start(bf16[32,896]{1,0:T(8,128)(2,1)S(1)} %get-tuple-element.101), channel_id=1, source_target_pairs={{0,7},{1,6},{2,5},{3,4},{4,3},{5,2},{6,1},{7,0},{8,15},{9,14},{10,... | collective-permute-start | bytes 172040 | tf_op jit(solution)/shard_map/ppermute | solution.py:162
  92.8 1.9 %convert_bitcast_fusion.2 = bf16[1,896,1024]{2,1,0:T(8,128)(2,1)} fusion(bf16[256,896]{1,0:T(8,128)(2,1)S(1)} %get-tuple-element.102, bf16[256,1024]{1,0:T(8,128)(2,1)S(1)} %get-tuple-element.103), kind=kOutput, calls=%fused_computation.2 | convolution fusion | flops 470679552 | bytes 2818048 | tf_op jit(solution)/shard_map/dot_general | solution.py:16
  95.4 1.6 %collective-permute-done.39.refs_7_ = bf16[32,896]{1,0:T(8,128)(2,1)S(1)} collective-permute-done((bf16[32,896]{1,0:T(8,128)(2,1)S(1)}, bf16[32,896]{1,0:T(8,128)(2,1)S(1)}, u32[]{:S(2)}, u32[]{:S(2)}) %collective-permute-start.39) | collective-permute-done | bytes 57376 | tf_op jit(solution)/shard_map/ppermute | solution.py:162
  (85 shorter events, 39.0 us)
Async XLA Ops:
  4.6 9.1 %collective-permute-start.1 = (bf16[32,896]{1,0:T(8,128)(2,1)S(1)}, bf16[32,896]{1,0:T(8,128)(2,1)S(1)}, u32[]{:S(2)}, u32[]{:S(2)}) collective-permute-start(bf16[32,896]{1,0:T(8,128)(2,1)S(1)} %get-tuple-element.60), channel_id=1, source_target_pairs={{0,2},{1,3},{2,0},{3,1},{4,6},{5,7},{6,4},{7,5},{8,10},{9,11},{10,... | collective-permute-start | bytes 172040 | tf_op jit(solution)/shard_map/ppermute | solution.py:162
  7.2 8.2 %collective-permute-start.2 = (bf16[32,896]{1,0:T(8,128)(2,1)S(1)}, bf16[32,896]{1,0:T(8,128)(2,1)S(1)}, u32[]{:S(2)}, u32[]{:S(2)}) collective-permute-start(bf16[32,896]{1,0:T(8,128)(2,1)S(1)} %get-tuple-element.61), channel_id=1, source_target_pairs={{0,3},{1,2},{2,1},{3,0},{4,7},{5,6},{6,5},{7,4},{8,11},{9,10},{10,... | collective-permute-start | bytes 172040 | tf_op jit(solution)/shard_map/ppermute | solution.py:162
  7.3 8.5 %collective-permute-start.3 = (bf16[32,896]{1,0:T(8,128)(2,1)S(1)}, bf16[32,896]{1,0:T(8,128)(2,1)S(1)}, u32[]{:S(2)}, u32[]{:S(2)}) collective-permute-start(bf16[32,896]{1,0:T(8,128)(2,1)S(1)} %get-tuple-element.62), channel_id=1, source_target_pairs={{0,4},{1,5},{2,6},{3,7},{4,0},{5,1},{6,2},{7,3},{8,12},{9,13},{10,... | collective-permute-start | bytes 172040 | tf_op jit(solution)/shard_map/ppermute | solution.py:162
  10.0 8.3 %collective-permute-start.4 = (bf16[32,896]{1,0:T(8,128)(2,1)S(1)}, bf16[32,896]{1,0:T(8,128)(2,1)S(1)}, u32[]{:S(2)}, u32[]{:S(2)}) collective-permute-start(bf16[32,896]{1,0:T(8,128)(2,1)S(1)} %get-tuple-element.63), channel_id=1, source_target_pairs={{0,5},{1,4},{2,7},{3,6},{4,1},{5,0},{6,3},{7,2},{8,13},{9,12},{10,... | collective-permute-start | bytes 172040 | tf_op jit(solution)/shard_map/ppermute | solution.py:162
  10.0 8.3 %collective-permute-start.5 = (bf16[32,896]{1,0:T(8,128)(2,1)S(1)}, bf16[32,896]{1,0:T(8,128)(2,1)S(1)}, u32[]{:S(2)}, u32[]{:S(2)}) collective-permute-start(bf16[32,896]{1,0:T(8,128)(2,1)S(1)} %get-tuple-element.64), channel_id=1, source_target_pairs={{0,6},{1,7},{2,4},{3,5},{4,2},{5,3},{6,0},{7,1},{8,14},{9,15},{10,... | collective-permute-start | bytes 172040 | tf_op jit(solution)/shard_map/ppermute | solution.py:162
  15.4 13.6 %collective-permute-start.10 = (bf16[32,896]{1,0:T(8,128)(2,1)S(1)}, bf16[32,896]{1,0:T(8,128)(2,1)S(1)}, u32[]{:S(2)}, u32[]{:S(2)}) collective-permute-start(bf16[32,896]{1,0:T(8,128)(2,1)S(1)} %get-tuple-element.71), channel_id=1, source_target_pairs={{0,1},{1,0},{2,3},{3,2},{4,5},{5,4},{6,7},{7,6},{8,9},{9,8},{10,11... | collective-permute-start | bytes 172040 | tf_op jit(solution)/shard_map/ppermute | solution.py:162
  22.2 24.1 %collective-permute-start.7 = (bf16[2,64,1024]{2,1,0:T(8,128)(2,1)S(1)}, bf16[2,64,1024]{2,1,0:T(8,128)(2,1)S(1)}, u32[]{:S(2)}, u32[]{:S(2)}) collective-permute-start(bf16[2,64,1024]{2,1,0:T(8,128)(2,1)S(1)} %get-tuple-element.67), channel_id=1, source_target_pairs={{0,8},{8,0},{16,24},{24,16},{1,9},{9,1},{17,25},{25,17},{2,10},{10... | collective-permute-start | bytes 786440 | tf_op jit(solution)/shard_map/ppermute | solution.py:162
  23.8 22.6 %collective-permute-start.8 = (bf16[2,64,1024]{2,1,0:T(8,128)(2,1)S(1)}, bf16[2,64,1024]{2,1,0:T(8,128)(2,1)S(1)}, u32[]{:S(2)}, u32[]{:S(2)}) collective-permute-start(bf16[2,64,1024]{2,1,0:T(8,128)(2,1)S(1)} %get-tuple-element.68), channel_id=1, source_target_pairs={{0,16},{8,24},{16,0},{24,8},{1,17},{9,25},{17,1},{25,9},{2,18},{10... | collective-permute-start | bytes 786440 | tf_op jit(solution)/shard_map/ppermute | solution.py:162
  25.3 21.1 %collective-permute-start.9 = (bf16[2,64,1024]{2,1,0:T(8,128)(2,1)S(1)}, bf16[2,64,1024]{2,1,0:T(8,128)(2,1)S(1)}, u32[]{:S(2)}, u32[]{:S(2)}) collective-permute-start(bf16[2,64,1024]{2,1,0:T(8,128)(2,1)S(1)} %get-tuple-element.69), channel_id=1, source_target_pairs={{0,24},{8,16},{16,8},{24,0},{1,25},{9,17},{17,9},{25,1},{2,26},{10... | collective-permute-start | bytes 786440 | tf_op jit(solution)/shard_map/ppermute | solution.py:162
  48.1 9.4 %collective-permute-start.18 = (bf16[64,1024]{1,0:T(8,128)(2,1)S(1)}, bf16[64,1024]{1,0:T(8,128)(2,1)S(1)}, u32[]{:S(2)}, u32[]{:S(2)}) collective-permute-start(bf16[64,1024]{1,0:T(8,128)(2,1)S(1)} %shard_map.114.refs_0_), channel_id=1, source_target_pairs={{0,16},{8,24},{16,0},{24,8},{1,17},{9,25},{17,1},{25,9},{2,18},{10... | collective-permute-start | bytes 393224 | tf_op jit(solution)/shard_map/ppermute | solution.py:162
  49.6 7.9 %collective-permute-start.19 = (bf16[64,1024]{1,0:T(8,128)(2,1)S(1)}, bf16[64,1024]{1,0:T(8,128)(2,1)S(1)}, u32[]{:S(2)}, u32[]{:S(2)}) collective-permute-start(bf16[64,1024]{1,0:T(8,128)(2,1)S(1)} %shard_map.114.refs_0_), channel_id=1, source_target_pairs={{0,24},{8,16},{16,8},{24,0},{1,25},{9,17},{17,9},{25,1},{2,26},{10... | collective-permute-start | bytes 393224 | tf_op jit(solution)/shard_map/ppermute | solution.py:162
  50.1 8.5 %collective-permute-start.27 = (bf16[64,1024]{1,0:T(8,128)(2,1)S(1)}, bf16[64,1024]{1,0:T(8,128)(2,1)S(1)}, u32[]{:S(2)}, u32[]{:S(2)}) collective-permute-start(bf16[64,1024]{1,0:T(8,128)(2,1)S(1)} %get-tuple-element.79), channel_id=1, source_target_pairs={{0,8},{8,0},{16,24},{24,16},{1,9},{9,1},{17,25},{25,17},{2,10},{10... | collective-permute-start | bytes 393224 | tf_op jit(solution)/shard_map/ppermute | solution.py:162
  51.6 9.8 %collective-permute-start.28 = (bf16[64,1024]{1,0:T(8,128)(2,1)S(1)}, bf16[64,1024]{1,0:T(8,128)(2,1)S(1)}, u32[]{:S(2)}, u32[]{:S(2)}) collective-permute-start(bf16[64,1024]{1,0:T(8,128)(2,1)S(1)} %get-tuple-element.80), channel_id=1, source_target_pairs={{0,16},{8,24},{16,0},{24,8},{1,17},{9,25},{17,1},{25,9},{2,18},{10... | collective-permute-start | bytes 393224 | tf_op jit(solution)/shard_map/ppermute | solution.py:162
  53.1 8.3 %collective-permute-start.29 = (bf16[64,1024]{1,0:T(8,128)(2,1)S(1)}, bf16[64,1024]{1,0:T(8,128)(2,1)S(1)}, u32[]{:S(2)}, u32[]{:S(2)}) collective-permute-start(bf16[64,1024]{1,0:T(8,128)(2,1)S(1)} %get-tuple-element.81), channel_id=1, source_target_pairs={{0,24},{8,16},{16,8},{24,0},{1,25},{9,17},{17,9},{25,1},{2,26},{10... | collective-permute-start | bytes 393224 | tf_op jit(solution)/shard_map/ppermute | solution.py:162
  58.6 6.9 %collective-permute-start.22 = (bf16[32,896]{1,0:T(8,128)(2,1)S(1)}, bf16[32,896]{1,0:T(8,128)(2,1)S(1)}, u32[]{:S(2)}, u32[]{:S(2)}) collective-permute-start(bf16[32,896]{1,0:T(8,128)(2,1)S(1)} %get-tuple-element.89), channel_id=1, source_target_pairs={{0,3},{1,2},{2,1},{3,0},{4,7},{5,6},{6,5},{7,4},{8,11},{9,10},{10,... | collective-permute-start | bytes 172040 | tf_op jit(solution)/shard_map/ppermute | solution.py:162
  61.7 19.7 %collective-permute-start.30 = (bf16[2,64,1024]{2,1,0:T(8,128)(2,1)S(1)}, bf16[2,64,1024]{2,1,0:T(8,128)(2,1)S(1)}, u32[]{:S(2)}, u32[]{:S(2)}) collective-permute-start(bf16[2,64,1024]{2,1,0:T(8,128)(2,1)S(1)} %shard_map.117.refs_0_), channel_id=1, source_target_pairs={{0,8},{8,0},{16,24},{24,16},{1,9},{9,1},{17,25},{25,17},{2,10},{10... | collective-permute-start | bytes 786440 | tf_op jit(solution)/shard_map/ppermute | solution.py:162
  62.2 19.2 %collective-permute-start.31 = (bf16[2,64,1024]{2,1,0:T(8,128)(2,1)S(1)}, bf16[2,64,1024]{2,1,0:T(8,128)(2,1)S(1)}, u32[]{:S(2)}, u32[]{:S(2)}) collective-permute-start(bf16[2,64,1024]{2,1,0:T(8,128)(2,1)S(1)} %shard_map.117.refs_0_), channel_id=1, source_target_pairs={{0,16},{8,24},{16,0},{24,8},{1,17},{9,25},{17,1},{25,9},{2,18},{10... | collective-permute-start | bytes 786440 | tf_op jit(solution)/shard_map/ppermute | solution.py:162
  63.0 18.4 %collective-permute-start.32 = (bf16[2,64,1024]{2,1,0:T(8,128)(2,1)S(1)}, bf16[2,64,1024]{2,1,0:T(8,128)(2,1)S(1)}, u32[]{:S(2)}, u32[]{:S(2)}) collective-permute-start(bf16[2,64,1024]{2,1,0:T(8,128)(2,1)S(1)} %shard_map.117.refs_0_), channel_id=1, source_target_pairs={{0,24},{8,16},{16,8},{24,0},{1,25},{9,17},{17,9},{25,1},{2,26},{10... | collective-permute-start | bytes 786440 | tf_op jit(solution)/shard_map/ppermute | solution.py:162
  65.3 7.4 %collective-permute-start.23 = (bf16[32,896]{1,0:T(8,128)(2,1)S(1)}, bf16[32,896]{1,0:T(8,128)(2,1)S(1)}, u32[]{:S(2)}, u32[]{:S(2)}) collective-permute-start(bf16[32,896]{1,0:T(8,128)(2,1)S(1)} %get-tuple-element.90), channel_id=1, source_target_pairs={{0,4},{1,5},{2,6},{3,7},{4,0},{5,1},{6,2},{7,3},{8,12},{9,13},{10,... | collective-permute-start | bytes 172040 | tf_op jit(solution)/shard_map/ppermute | solution.py:162
  65.5 8.8 %collective-permute-start.24 = (bf16[32,896]{1,0:T(8,128)(2,1)S(1)}, bf16[32,896]{1,0:T(8,128)(2,1)S(1)}, u32[]{:S(2)}, u32[]{:S(2)}) collective-permute-start(bf16[32,896]{1,0:T(8,128)(2,1)S(1)} %get-tuple-element.91), channel_id=1, source_target_pairs={{0,5},{1,4},{2,7},{3,6},{4,1},{5,0},{6,3},{7,2},{8,13},{9,12},{10,... | collective-permute-start | bytes 172040 | tf_op jit(solution)/shard_map/ppermute | solution.py:162
  83.0 8.2 %collective-permute-start.34 = (bf16[32,896]{1,0:T(8,128)(2,1)S(1)}, bf16[32,896]{1,0:T(8,128)(2,1)S(1)}, u32[]{:S(2)}, u32[]{:S(2)}) collective-permute-start(bf16[32,896]{1,0:T(8,128)(2,1)S(1)} %get-tuple-element.96), channel_id=1, source_target_pairs={{0,2},{1,3},{2,0},{3,1},{4,6},{5,7},{6,4},{7,5},{8,10},{9,11},{10,... | collective-permute-start | bytes 172040 | tf_op jit(solution)/shard_map/ppermute | solution.py:162
  83.0 11.7 %collective-permute-start.35 = (bf16[32,896]{1,0:T(8,128)(2,1)S(1)}, bf16[32,896]{1,0:T(8,128)(2,1)S(1)}, u32[]{:S(2)}, u32[]{:S(2)}) collective-permute-start(bf16[32,896]{1,0:T(8,128)(2,1)S(1)} %get-tuple-element.97), channel_id=1, source_target_pairs={{0,3},{1,2},{2,1},{3,0},{4,7},{5,6},{6,5},{7,4},{8,11},{9,10},{10,... | collective-permute-start | bytes 172040 | tf_op jit(solution)/shard_map/ppermute | solution.py:162
  84.7 10.0 %collective-permute-start.36 = (bf16[32,896]{1,0:T(8,128)(2,1)S(1)}, bf16[32,896]{1,0:T(8,128)(2,1)S(1)}, u32[]{:S(2)}, u32[]{:S(2)}) collective-permute-start(bf16[32,896]{1,0:T(8,128)(2,1)S(1)} %get-tuple-element.98), channel_id=1, source_target_pairs={{0,4},{1,5},{2,6},{3,7},{4,0},{5,1},{6,2},{7,3},{8,12},{9,13},{10,... | collective-permute-start | bytes 172040 | tf_op jit(solution)/shard_map/ppermute | solution.py:162
  85.5 9.2 %collective-permute-start.37 = (bf16[32,896]{1,0:T(8,128)(2,1)S(1)}, bf16[32,896]{1,0:T(8,128)(2,1)S(1)}, u32[]{:S(2)}, u32[]{:S(2)}) collective-permute-start(bf16[32,896]{1,0:T(8,128)(2,1)S(1)} %get-tuple-element.99), channel_id=1, source_target_pairs={{0,5},{1,4},{2,7},{3,6},{4,1},{5,0},{6,3},{7,2},{8,13},{9,12},{10,... | collective-permute-start | bytes 172040 | tf_op jit(solution)/shard_map/ppermute | solution.py:162
  (24 other events, 148.8 us)

commit v4 on v3

v4 whole, which is shorter than its diff:
```python
import functools

import jax
import jax.numpy as jnp
from jax import lax
from jax.experimental import pallas as pl
from jax.experimental.pallas import tpu as pltpu
from jax.sharding import PartitionSpec as P

F32 = jnp.float32
BF16 = jnp.bfloat16
MIB = 1024 * 1024
VMEM_LIMIT = 24 * MIB
ROUTE_LIMIT = 59 * MIB


def mm(left, right, dims):
    return lax.dot_general(left, right, (dims, ((), ())), preferred_element_type=F32)


def call(kernel, out_shape, flops=0, moved=0, limit=VMEM_LIMIT, **kwargs):
    return pl.pallas_call(
        kernel,
        out_shape=out_shape,
        cost_estimate=pl.CostEstimate(flops=flops, bytes_accessed=moved, transcendentals=0),
        compiler_params=pltpu.CompilerParams(vmem_limit_bytes=limit),
        **kwargs,
    )


def split_rows(refs, value):
    rows = value.shape[0] // len(refs)
    for k, ref in enumerate(refs):
        ref[...] = value[k * rows : (k + 1) * rows]


def join_rows(refs):
    return jnp.concatenate([ref[...] for ref in refs], axis=0)


def split_cores(keep_ref, swap_ref, value, *at):
    half, rows = keep_ref.shape[-3:-1]
    for k in range(half):
        keep_ref[(*at, k)] = value[2 * k * rows : (2 * k + 1) * rows]
        swap_ref[(*at, k)] = value[(2 * k + 1) * rows : (2 * k + 2) * rows]


def route_kernel(
    experts, ids_ref, gates_ref, tokens_ref, grad_ref, pick_ref, weight_ref, keep_ref, swap_ref
):
    ids = ids_ref[...]
    tok_rows = ids.shape[1]
    slots = pick_ref.shape[0]
    inside = ids < experts
    routed = jnp.max(inside.astype(jnp.int32), axis=0, keepdims=True)
    chosen = jnp.sum(jnp.where(inside, ids, 0), axis=0, keepdims=True)
    weight = jnp.sum(jnp.where(inside, gates_ref[...], 0.0), axis=0, keepdims=True)
    key = jnp.where(routed > 0, chosen ^ lax.axis_index("expert"), experts)
    hot = lax.broadcasted_iota(jnp.int32, (experts, tok_rows), 0) == key
    earlier = lax.broadcasted_iota(jnp.int32, (tok_rows, tok_rows), 0) < lax.broadcasted_iota(
        jnp.int32, (tok_rows, tok_rows), 1
    )
    before = mm(hot.astype(F32).astype(BF16), earlier.astype(F32).astype(BF16), ((1,), (0,)))
    position = jnp.sum(jnp.where(hot, before, 0.0), axis=0, keepdims=True).astype(jnp.int32)
    slot = jnp.where(routed > 0, key * (slots // experts) + position, slots)
    pick = lax.broadcasted_iota(jnp.int32, (slots, tok_rows), 0) == slot
    slot_weight = jnp.sum(jnp.where(pick, weight, 0.0), axis=1, keepdims=True)
    weight_ref[...] = slot_weight
    pick = pick.astype(F32).astype(BF16)
    pick_ref[...] = pick
    rows = mm(pick, tokens_ref[...], ((1,), (0,))).astype(BF16)
    split_cores(keep_ref, swap_ref, rows, 0)
    rows = (slot_weight * mm(pick, grad_ref[...], ((1,), (0,)))).astype(BF16)
    split_cores(keep_ref, swap_ref, rows, 1)


def load_kernel(from_ref, to_ref):
    to_ref[...] = from_ref[...]


def pack_kernel(half, keep_ref, swap_ref, near_ref, *far_refs):
    for at in range(2):
        near_ref[at, 0] = keep_ref[at, 1]
        near_ref[at, 1] = swap_ref[at, 1]
        for k in range(2, half):
            far_refs[at * (half - 2) + k - 2][0] = keep_ref[at, k]
            far_refs[at * (half - 2) + k - 2][1] = swap_ref[at, k]


def pack_out_kernel(keep_ref, swap_ref, *far_refs):
    for k, far_ref in enumerate(far_refs):
        far_ref[0] = keep_ref[k + 2]
        far_ref[1] = swap_ref[k + 2]


def pack_last_kernel(out_keep_ref, out_swap_ref, keep_ref, swap_ref, near_ref, *far_refs):
    near_ref[0, 0] = out_keep_ref[1]
    near_ref[0, 1] = out_swap_ref[1]
    near_ref[1, 0] = keep_ref[1]
    near_ref[1, 1] = swap_ref[1]
    pack_out_kernel(keep_ref, swap_ref, *far_refs)


def pieces(at, keep_ref, swap_ref, near_ref, far_refs):
    found = [keep_ref[at + (0,)], swap_ref[at + (0,)]]
    found += [near_ref[at + (0,)], near_ref[at + (1,)]]
    for ref in far_refs:
        found += [ref[0], ref[1]]
    return found


def chunk_rows(rows, dp, k):
    chunk = rows // dp
    mine = lax.axis_index("dp")
    return pl.ds(pl.multiple_of((mine ^ k) * chunk, chunk), chunk)


def local_order(found, scratch, dp):
    scratch[...] = jnp.concatenate(found, axis=0)
    rows = scratch.shape[0]
    return jnp.concatenate([scratch[chunk_rows(rows, dp, k), :] for k in range(dp)], axis=0)


def gate_up_kernel(half, keep_ref, swap_ref, near_ref, *refs):
    far_refs, refs = refs[: half - 2], refs[half - 2 :]
    gate_ref, up_ref, local_ref, *out_refs, scratch = refs
    dp = len(out_refs)
    rows = local_order(pieces((0,), keep_ref, swap_ref, near_ref, far_refs), scratch, dp)
    local_ref[...] = rows
    chunk = rows.shape[0] // dp
    for at, mat in enumerate((gate_ref, up_ref)):
        part = mm(rows, mat[...], ((1,), (0,))).astype(BF16)
        for k, out_ref in enumerate(out_refs):
            out_ref[at] = part[k * chunk : (k + 1) * chunk]


def grad_act_kernel(half, keep_ref, swap_ref, near_ref, *refs):
    far_refs, refs = refs[: half - 2], refs[half - 2 :]
    down_ref, local_ref, *out_refs, scratch = refs
    dp = len(out_refs)
    rows = local_order(pieces((1,), keep_ref, swap_ref, near_ref, far_refs), scratch, dp)
    local_ref[...] = rows
    split_rows(out_refs, mm(rows, down_ref[...], ((1,), (1,))).astype(BF16))


def group_sum(refs, *at):
    total = refs[0][at].astype(F32)
    for ref in refs[1:]:
        total = total + ref[at].astype(F32)
    return total


def logistic(value):
    return 1.0 / (1.0 + jnp.exp(-value))


def act_kernel(dp, *refs):
    gate = group_sum(refs[:dp], 0)
    up = group_sum(refs[:dp], 1)
    refs[dp][...] = (gate * logistic(gate) * up).astype(BF16)


def grad_pre_kernel(dp, *refs):
    gate = group_sum(refs[:dp], 0)
    up = group_sum(refs[:dp], 1)
    grad = group_sum(refs[dp : 2 * dp], Ellipsis)
    out_ref = refs[2 * dp]
    soft = logistic(gate)
    out_ref[0] = (grad * up * (soft * (1.0 + gate * (1.0 - soft)))).astype(BF16)
    out_ref[1] = (grad * (gate * soft)).astype(BF16)


def send_back(keep_ref, swap_ref, scratch, rows, dp):
    chunk = rows.shape[0] // dp
    for k in range(dp):
        scratch[chunk_rows(rows.shape[0], dp, k), :] = rows[k * chunk : (k + 1) * chunk]
    split_cores(keep_ref, swap_ref, scratch[...])


def expert_out_kernel(dp, *refs):
    down_ref, act_ref, keep_ref, swap_ref, scratch = refs[dp:]
    act = join_rows(refs[:dp])
    act_ref[...] = act
    rows = mm(act, down_ref[...], ((1,), (0,))).astype(BF16)
    send_back(keep_ref, swap_ref, scratch, rows, dp)


def row_grad_kernel(dp, *refs):
    gate_ref, up_ref, gate_pre_ref, up_pre_ref, keep_ref, swap_ref, scratch = refs[dp:]
    gate_pre = jnp.concatenate([ref[0] for ref in refs[:dp]], axis=0)
    up_pre = jnp.concatenate([ref[1] for ref in refs[:dp]], axis=0)
    gate_pre_ref[...] = gate_pre
    up_pre_ref[...] = up_pre
    total = mm(gate_pre, gate_ref[...], ((1,), (1,))) + mm(up_pre, up_ref[...], ((1,), (1,)))
    send_back(keep_ref, swap_ref, scratch, total.astype(BF16), dp)


def scatter_scaled_kernel(pick_ref, weight_ref, keep_ref, swap_ref, near_ref, *refs):
    found = [keep_ref[0], swap_ref[0], near_ref[0, 0], near_ref[0, 1]]
    for ref in refs[:-1]:
        found += [ref[0], ref[1]]
    back = jnp.concatenate(found, axis=0).astype(F32)
    scaled = (weight_ref[...] * back).astype(BF16)
    refs[-1][...] = mm(pick_ref[...], scaled, ((0,), (0,))).astype(BF16)


def scatter_kernel(pick_ref, keep_ref, swap_ref, near_ref, *refs):
    found = [keep_ref[0], swap_ref[0], near_ref[1, 0], near_ref[1, 1]]
    for ref in refs[:-1]:
        found += [ref[0], ref[1]]
    back = jnp.concatenate(found, axis=0)
    refs[-1][...] = mm(pick_ref[...], back, ((0,), (0,))).astype(BF16)


def partner(value, axis, k):
    size = lax.axis_size(axis)
    return lax.ppermute(value, axis, [(i, i ^ k) for i in range(size)])


def trade(values):
    return [values[0]] + [partner(value, "dp", k + 1) for k, value in enumerate(values[1:])]


def whole(array):
    return pl.BlockSpec(array.shape, lambda i: (0,) * len(array.shape))


def body(tokens, grad_out, expert_ids, gates, w_gate, w_up, w_down):
    experts = lax.axis_size("expert")
    dp = lax.axis_size("dp")
    tok_rows, features = tokens.shape
    capacity = tok_rows // 16
    slots = experts * capacity
    hidden = w_gate.shape[2]
    chunk = slots // dp
    gate_mat, up_mat, down_mat = w_gate[0], w_up[0], w_down[0]
    shape = jax.ShapeDtypeStruct
    product = 2 * slots * features * hidden
    weights = 2 * features * hidden

    half = experts // 2
    sized = shape((slots, features), BF16)
    wide = shape((slots, hidden), BF16)
    both = shape((2, half, capacity, features), BF16)
    one = shape((half, capacity, features), BF16)
    near = shape((2, 2, capacity, features), BF16)
    far = [shape((2, capacity, features), BF16)] * (half - 2)
    in_order = [pltpu.VMEM((slots, features), BF16)]

    ins = (expert_ids.T, gates.T, tokens, grad_out)
    outs = (shape((slots, tok_rows), BF16), shape((slots, 1), F32), both, both)
    pick, weight, keep, swap = call(
        functools.partial(route_kernel, experts),
        outs,
        4 * slots * tok_rows * features,
        8 * tok_rows * features,
        limit=ROUTE_LIMIT,
        grid=(1,),
        in_specs=[whole(array) for array in ins],
        out_specs=tuple(whole(array) for array in outs),
    )(*ins)
    swap_to, up_mat = lax.optimization_barrier((swap, up_mat))
    swap = partner(swap_to, "expert", 1)
    up_mat = call(load_kernel, shape(up_mat.shape, BF16), 0, 2 * weights)(up_mat)
    swap, up_mat = lax.optimization_barrier((swap, up_mat))
    near_to, *far_to = call(functools.partial(pack_kernel, half), (near, *far, *far), 0, 8 * slots)(
        keep, swap
    )
    near_in = partner(near_to, "expert", 2)
    far_in = [
        partner(value, "expert", 2 * (2 + k % (half - 2))) for k, value in enumerate(far_to)
    ]
    rows, *part_pre = call(
        functools.partial(gate_up_kernel, half),
        (sized, *[shape((2, chunk, hidden), BF16)] * dp),
        2 * product,
        2 * weights,
        scratch_shapes=in_order,
    )(keep, swap, near_in, *far_in[: half - 2], gate_mat, up_mat)
    sums = trade(part_pre)
    grads, *part_grad = call(
        functools.partial(grad_act_kernel, half),
        (sized, *[shape((chunk, hidden), BF16)] * dp),
        product,
        weights,
        scratch_shapes=in_order,
    )(keep, swap, near_in, *far_in[half - 2 :], down_mat)
    grad_sums = trade(part_grad)
    sums, part_grad = lax.optimization_barrier((sums, part_grad))
    act_mine = call(
        functools.partial(act_kernel, dp),
        shape((chunk, hidden), BF16),
        0,
        4 * dp * chunk * hidden,
    )(*sums)
    acts = trade([act_mine] * dp)
    pre_mine = call(
        functools.partial(grad_pre_kernel, dp),
        shape((2, chunk, hidden), BF16),
        0,
        6 * dp * chunk * hidden,
    )(*sums, *grad_sums)
    pre = trade([pre_mine] * dp)
    act, out_keep, out_swap = call(
        functools.partial(expert_out_kernel, dp),
        (wide, one, one),
        product,
        weights,
        scratch_shapes=in_order,
    )(*acts, down_mat)
    out_swap = partner(out_swap, "expert", 1)
    out_far = call(pack_out_kernel, far, 0, 8 * slots)(out_keep, out_swap)
    out_far = [partner(value, "expert", 2 * (2 + k)) for k, value in enumerate(out_far)]
    gate_pre, up_pre, grad_keep, grad_swap = call(
        functools.partial(row_grad_kernel, dp),
        (wide, wide, one, one),
        2 * product,
        2 * weights,
        scratch_shapes=in_order,
    )(*pre, gate_mat, up_mat)
    grad_swap = partner(grad_swap, "expert", 1)
    grad_swap, out_far = lax.optimization_barrier((grad_swap, out_far))
    near_back, *grad_far = call(pack_last_kernel, (near, *far), 0, 8 * slots)(
        out_keep, out_swap, grad_keep, grad_swap
    )
    near_back = partner(near_back, "expert", 2)
    grad_far = [partner(value, "expert", 2 * (2 + k)) for k, value in enumerate(grad_far)]

    grad_down = mm(act, grads, ((0,), (0,))).astype(BF16)
    grad_gate = mm(rows, gate_pre, ((0,), (0,))).astype(BF16)
    grad_up = mm(rows, up_pre, ((0,), (0,))).astype(BF16)

    full = shape((tok_rows, features), BF16)
    mixed = call(
        scatter_scaled_kernel, full, 2 * slots * tok_rows * features, 4 * tok_rows * features
    )(pick, weight, out_keep, out_swap, near_back, *out_far)
    grad_tokens = call(
        scatter_kernel, full, 2 * slots * tok_rows * features, 4 * tok_rows * features
    )(pick, grad_keep, grad_swap, near_back, *grad_far)
    return (mixed, grad_tokens, grad_gate[None], grad_up[None], grad_down[None])


def solution(mesh):
    placed = (
        P("expert", "dp"),
        P("expert", "dp"),
        P("expert", None),
        P("expert", None),
        P("expert", "dp", None),
        P("expert", "dp", None),
        P("expert", None, "dp"),
    )
    return jax.shard_map(
        body,
        mesh=mesh,
        in_specs=placed,
        out_specs=(
            P("expert", "dp"),
            P("expert", "dp"),
            P("expert", "dp", None),
            P("expert", "dp", None),
            P("expert", None, "dp"),
        ),
        check_vma=False,
    )
```

time: 98.7 us -> 95.7 us (0.970)
  waiting for transfers between devices: 28.8 us -> 42.7 us
  starting transfers between devices: 49.1 us -> 35.2 us
  local copies, waits for them, and re-layouts: 5.43 us -> 0.02 us
  Pallas kernels: 8.53 us -> 11.1 us
    ppermute x40 -> x25, starting transfers between devices: 49.1 us -> 35.2 us  [partner(): return lax.ppermute(value, axis, [(i, i ^ k) for i in range(size)])]
    ppermute x40 -> x25, waiting for transfers between devices: 28.8 us -> 42.7 us  [partner(): return lax.ppermute(value, axis, [(i, i ^ k) for i in range(size)])]
    unnamed x16 -> x12, local copies, waits for them, and re-layouts: 5.43 us -> 0.02 us
    pallas_call x6 -> x9, Pallas kernels: 5.18 us -> 7.77 us  [the longest x1 3.46 us: body(): call(functools.partial(route_kernel, experts), outs, 4 * slots * tok_rows...]
  transfers between devices with their start and end apart: 40 -> 25, of which waited for: 15 -> 10; matrix products, arithmetic and copies ran while one was open for 6% -> 6% of each run, Pallas kernels for 5% -> 4%
where the time goes in v4:
time: 95.7 us; the launch traced here: 95.6 us
  waiting for transfers between devices  42.7 us (45%)
  starting transfers between devices  35.2 us (37%)
  Pallas kernels  11.1 us (12%)
  matrix products  5.77 us (6%)
    ppermute x25, waiting for transfers between devices, partner(): return lax.ppermute(value, axis, [(i, i ^ k) for i in range(size)])  42.7 us
    ppermute x25, starting transfers between devices, partner(): return lax.ppermute(value, axis, [(i, i ^ k) for i in range(size)])  35.2 us
    dot_general x3, matrix products, mm(): lax.dot_general(left, right, (dims, ((), ())), preferred_element_type=F32)  5.77 us
    pallas_call x1, Pallas kernels, body(): call(functools.partial(route_kernel, experts), outs, 4 * slots * tok_rows...  3.46 us
  transfers between devices with their start and end apart: 25, of which 10 were waited for; matrix products, arithmetic and copies ran while one was open for 6% of the time, Pallas kernels for 4%

profile of v4, /device:TPU:0, one launch (start us, length us, event | category | flops | bytes accessed | tf_op | source)
XLA Modules:
  0.0 95.6 jit_solution(17538486606850309884)
XLA Ops:
  0.6 3.5 %shard_map.110 = (bf16[256,512]{1,0:T(8,128)(2,1)}, f32[256,1]{1,0:T(8,128)}, bf16[2,4,32,896]{3,2,1,0:T(8,128)(2,1)}, bf16[2,4,32,896]{3,2,1,0:T(8,128)(2,1)}) custom-call(s32[8,512]{1,0:T(8,128)} %bitcast.22, f32[8,512]{1,0:T(8,128)} %bitcast.23, bf16[512,896]{1,0:T(8,128)(2,1)} %tokens_ref.1, bf16[512,896]{1,0:T(8,128)(2,1)} %grad_ref.1), custom_call_target="tpu_custom_call" | custom-call | flops 469762048 | bytes 3670016 | tf_op jit(solution)/shard_map/pallas_call | solution.py:252
  4.7 1.5 %collective-permute-done.swap_ref = bf16[2,4,32,896]{3,2,1,0:T(8,128)(2,1)S(1)} collective-permute-done((bf16[2,4,32,896]{3,2,1,0:T(8,128)(2,1)}, bf16[2,4,32,896]{3,2,1,0:T(8,128)(2,1)S(1)}, u32[]{:S(2)}, u32[]{:S(2)}) %collective-permute-start) | collective-permute-done | bytes 458784 | tf_op jit(solution)/shard_map/ppermute | solution.py:217
  6.3 3.0 %collective-permute-start.1 = (bf16[2,2,32,896]{3,2,1,0:T(8,128)(2,1)S(1)}, bf16[2,2,32,896]{3,2,1,0:T(8,128)(2,1)S(1)}, u32[]{:S(2)}, u32[]{:S(2)}) collective-permute-start(bf16[2,2,32,896]{3,2,1,0:T(8,128)(2,1)S(1)} %get-tuple-element.54), channel_id=1, source_target_pairs={{0,2},{1,3},{2,0},{3,1},{4,6},{5,7},{6,4},{7,5},{8,10},{9,11},{10,... | collective-permute-start | bytes 688136 | tf_op jit(solution)/shard_map/ppermute | solution.py:217
  9.3 2.6 %collective-permute-start.2 = (bf16[2,32,896]{2,1,0:T(8,128)(2,1)S(1)}, bf16[2,32,896]{2,1,0:T(8,128)(2,1)S(1)}, u32[]{:S(2)}, u32[]{:S(2)}) collective-permute-start(bf16[2,32,896]{2,1,0:T(8,128)(2,1)S(1)} %get-tuple-element.55), channel_id=1, source_target_pairs={{0,4},{1,5},{2,6},{3,7},{4,0},{5,1},{6,2},{7,3},{8,12},{9,13},{10,... | collective-permute-start | bytes 344072 | tf_op jit(solution)/shard_map/ppermute | solution.py:217
  11.9 5.9 %collective-permute-done.2.refs_0_ = bf16[2,32,896]{2,1,0:T(8,128)(2,1)S(1)} collective-permute-done((bf16[2,32,896]{2,1,0:T(8,128)(2,1)S(1)}, bf16[2,32,896]{2,1,0:T(8,128)(2,1)S(1)}, u32[]{:S(2)}, u32[]{:S(2)}) %collective-permute-start.2) | collective-permute-done | bytes 114720 | tf_op jit(solution)/shard_map/ppermute | solution.py:217
  17.8 4.6 %collective-permute-done.3.refs_1_ = bf16[2,32,896]{2,1,0:T(8,128)(2,1)S(1)} collective-permute-done((bf16[2,32,896]{2,1,0:T(8,128)(2,1)S(1)}, bf16[2,32,896]{2,1,0:T(8,128)(2,1)S(1)}, u32[]{:S(2)}, u32[]{:S(2)}) %collective-permute-start.3) | collective-permute-done | bytes 114720 | tf_op jit(solution)/shard_map/ppermute | solution.py:217
  23.7 1.6 %collective-permute-start.4 = (bf16[2,64,1024]{2,1,0:T(8,128)(2,1)S(1)}, bf16[2,64,1024]{2,1,0:T(8,128)(2,1)S(1)}, u32[]{:S(2)}, u32[]{:S(2)}) collective-permute-start(bf16[2,64,1024]{2,1,0:T(8,128)(2,1)S(1)} %get-tuple-element.59), channel_id=1, source_target_pairs={{0,8},{8,0},{16,24},{24,16},{1,9},{9,1},{17,25},{25,17},{2,10},{10... | collective-permute-start | bytes 786440 | tf_op jit(solution)/shard_map/ppermute | solution.py:217
  27.2 1.7 %collective-permute-start.7 = (bf16[2,32,896]{2,1,0:T(8,128)(2,1)S(1)}, bf16[2,32,896]{2,1,0:T(8,128)(2,1)S(1)}, u32[]{:S(2)}, u32[]{:S(2)}) collective-permute-start(bf16[2,32,896]{2,1,0:T(8,128)(2,1)S(1)} %get-tuple-element.62), channel_id=1, source_target_pairs={{0,4},{1,5},{2,6},{3,7},{4,0},{5,1},{6,2},{7,3},{8,12},{9,13},{10,... | collective-permute-start | bytes 344072 | tf_op jit(solution)/shard_map/ppermute | solution.py:217
  30.3 6.2 %collective-permute-done.7.refs_0_ = bf16[2,32,896]{2,1,0:T(8,128)(2,1)S(1)} collective-permute-done((bf16[2,32,896]{2,1,0:T(8,128)(2,1)S(1)}, bf16[2,32,896]{2,1,0:T(8,128)(2,1)S(1)}, u32[]{:S(2)}, u32[]{:S(2)}) %collective-permute-start.7) | collective-permute-done | bytes 114720 | tf_op jit(solution)/shard_map/ppermute | solution.py:217
  37.3 1.6 %collective-permute-start.13 = (bf16[64,1024]{1,0:T(8,128)(2,1)S(1)}, bf16[64,1024]{1,0:T(8,128)(2,1)S(1)}, u32[]{:S(2)}, u32[]{:S(2)}) collective-permute-start(bf16[64,1024]{1,0:T(8,128)(2,1)S(1)} %get-tuple-element.65), channel_id=1, source_target_pairs={{0,8},{8,0},{16,24},{24,16},{1,9},{9,1},{17,25},{25,17},{2,10},{10... | collective-permute-start | bytes 393224 | tf_op jit(solution)/shard_map/ppermute | solution.py:217
  38.8 1.5 %collective-permute-start.14 = (bf16[64,1024]{1,0:T(8,128)(2,1)S(1)}, bf16[64,1024]{1,0:T(8,128)(2,1)S(1)}, u32[]{:S(2)}, u32[]{:S(2)}) collective-permute-start(bf16[64,1024]{1,0:T(8,128)(2,1)S(1)} %get-tuple-element.66), channel_id=1, source_target_pairs={{0,16},{8,24},{16,0},{24,8},{1,17},{9,25},{17,1},{25,9},{2,18},{10... | collective-permute-start | bytes 393224 | tf_op jit(solution)/shard_map/ppermute | solution.py:217
  41.0 2.5 %collective-permute-start.11 = (bf16[64,1024]{1,0:T(8,128)(2,1)S(1)}, bf16[64,1024]{1,0:T(8,128)(2,1)S(1)}, u32[]{:S(2)}, u32[]{:S(2)}) collective-permute-start(bf16[64,1024]{1,0:T(8,128)(2,1)S(1)} %shard_map.115.refs_0_), channel_id=1, source_target_pairs={{0,24},{8,16},{16,8},{24,0},{1,25},{9,17},{17,9},{25,1},{2,26},{10... | collective-permute-start | bytes 393224 | tf_op jit(solution)/shard_map/ppermute | solution.py:217
  45.1 5.8 %collective-permute-done.14.refs_6_ = bf16[64,1024]{1,0:T(8,128)(2,1)S(1)} collective-permute-done((bf16[64,1024]{1,0:T(8,128)(2,1)S(1)}, bf16[64,1024]{1,0:T(8,128)(2,1)S(1)}, u32[]{:S(2)}, u32[]{:S(2)}) %collective-permute-start.14) | collective-permute-done | bytes 131104 | tf_op jit(solution)/shard_map/ppermute | solution.py:217
  52.5 2.3 %collective-permute-start.16 = (bf16[2,64,1024]{2,1,0:T(8,128)(2,1)S(1)}, bf16[2,64,1024]{2,1,0:T(8,128)(2,1)S(1)}, u32[]{:S(2)}, u32[]{:S(2)}) collective-permute-start(bf16[2,64,1024]{2,1,0:T(8,128)(2,1)S(1)} %shard_map.117.refs_0_), channel_id=1, source_target_pairs={{0,8},{8,0},{16,24},{24,16},{1,9},{9,1},{17,25},{25,17},{2,10},{10... | collective-permute-start | bytes 786440 | tf_op jit(solution)/shard_map/ppermute | solution.py:217
  55.7 3.0 %collective-permute-done.18.refs_3_ = bf16[2,64,1024]{2,1,0:T(8,128)(2,1)S(1)} collective-permute-done((bf16[2,64,1024]{2,1,0:T(8,128)(2,1)S(1)}, bf16[2,64,1024]{2,1,0:T(8,128)(2,1)S(1)}, u32[]{:S(2)}, u32[]{:S(2)}) %collective-permute-start.18) | collective-permute-done | bytes 262176 | tf_op jit(solution)/shard_map/ppermute | solution.py:217
  58.7 2.2 %collective-permute-done.17.refs_2_ = bf16[2,64,1024]{2,1,0:T(8,128)(2,1)S(1)} collective-permute-done((bf16[2,64,1024]{2,1,0:T(8,128)(2,1)S(1)}, bf16[2,64,1024]{2,1,0:T(8,128)(2,1)S(1)}, u32[]{:S(2)}, u32[]{:S(2)}) %collective-permute-start.17) | collective-permute-done | bytes 262176 | tf_op jit(solution)/shard_map/ppermute | solution.py:217
  62.5 5.2 %collective-permute-start.20 = (bf16[2,32,896]{2,1,0:T(8,128)(2,1)S(1)}, bf16[2,32,896]{2,1,0:T(8,128)(2,1)S(1)}, u32[]{:S(2)}, u32[]{:S(2)}) collective-permute-start(bf16[2,32,896]{2,1,0:T(8,128)(2,1)S(1)} %get-tuple-element.76), channel_id=1, source_target_pairs={{0,4},{1,5},{2,6},{3,7},{4,0},{5,1},{6,2},{7,3},{8,12},{9,13},{10,... | collective-permute-start | bytes 344072 | tf_op jit(solution)/shard_map/ppermute | solution.py:217
  68.5 2.0 %convert_bitcast_fusion = bf16[1,1024,896]{2,1,0:T(8,128)(2,1)} fusion(bf16[256,1024]{1,0:T(8,128)(2,1)S(1)} %get-tuple-element.87, bf16[256,896]{1,0:T(8,128)(2,1)S(1)} %get-tuple-element.88), kind=kOutput, calls=%fused_computation | convolution fusion | flops 470679552 | bytes 2818048 | tf_op jit(solution)/shard_map/dot_general | solution.py:18
  70.4 6.2 %collective-permute-done.20.refs_0_ = bf16[2,32,896]{2,1,0:T(8,128)(2,1)S(1)} collective-permute-done((bf16[2,32,896]{2,1,0:T(8,128)(2,1)S(1)}, bf16[2,32,896]{2,1,0:T(8,128)(2,1)S(1)}, u32[]{:S(2)}, u32[]{:S(2)}) %collective-permute-start.20) | collective-permute-done | bytes 114720 | tf_op jit(solution)/shard_map/ppermute | solution.py:217
  76.7 2.9 %collective-permute-start.22 = (bf16[2,2,32,896]{3,2,1,0:T(8,128)(2,1)S(1)}, bf16[2,2,32,896]{3,2,1,0:T(8,128)(2,1)S(1)}, u32[]{:S(2)}, u32[]{:S(2)}) collective-permute-start(bf16[2,2,32,896]{3,2,1,0:T(8,128)(2,1)S(1)} %get-tuple-element.79), channel_id=1, source_target_pairs={{0,2},{1,3},{2,0},{3,1},{4,6},{5,7},{6,4},{7,5},{8,10},{9,11},{10,... | collective-permute-start | bytes 688136 | tf_op jit(solution)/shard_map/ppermute | solution.py:217
  79.6 1.9 %convert_bitcast_fusion.2 = bf16[1,896,1024]{2,1,0:T(8,128)(2,1)} fusion(bf16[256,896]{1,0:T(8,128)(2,1)S(1)} %get-tuple-element.84, bf16[256,1024]{1,0:T(8,128)(2,1)S(1)} %get-tuple-element.85), kind=kOutput, calls=%fused_computation.2 | convolution fusion | flops 470679552 | bytes 2818048 | tf_op jit(solution)/shard_map/dot_general | solution.py:18
  81.5 2.4 %collective-permute-start.24 = (bf16[2,32,896]{2,1,0:T(8,128)(2,1)S(1)}, bf16[2,32,896]{2,1,0:T(8,128)(2,1)S(1)}, u32[]{:S(2)}, u32[]{:S(2)}) collective-permute-start(bf16[2,32,896]{2,1,0:T(8,128)(2,1)S(1)} %get-tuple-element.83), channel_id=1, source_target_pairs={{0,6},{1,7},{2,4},{3,5},{4,2},{5,3},{6,0},{7,1},{8,14},{9,15},{10,... | collective-permute-start | bytes 344072 | tf_op jit(solution)/shard_map/ppermute | solution.py:217
  83.9 1.9 %convert_bitcast_fusion.1 = bf16[1,896,1024]{2,1,0:T(8,128)(2,1)} fusion(bf16[256,896]{1,0:T(8,128)(2,1)S(1)} %get-tuple-element.84, bf16[256,1024]{1,0:T(8,128)(2,1)S(1)} %get-tuple-element.86), kind=kOutput, calls=%fused_computation.1 | convolution fusion | flops 470679552 | bytes 2818048 | tf_op jit(solution)/shard_map/dot_general | solution.py:18
  85.8 6.9 %collective-permute-done.23.refs_0_ = bf16[2,32,896]{2,1,0:T(8,128)(2,1)S(1)} collective-permute-done((bf16[2,32,896]{2,1,0:T(8,128)(2,1)S(1)}, bf16[2,32,896]{2,1,0:T(8,128)(2,1)S(1)}, u32[]{:S(2)}, u32[]{:S(2)}) %collective-permute-start.23) | collective-permute-done | bytes 114720 | tf_op jit(solution)/shard_map/ppermute | solution.py:217
  (54 shorter events, 15.8 us)
Async XLA Ops:
  6.3 16.1 %collective-permute-start.1 = (bf16[2,2,32,896]{3,2,1,0:T(8,128)(2,1)S(1)}, bf16[2,2,32,896]{3,2,1,0:T(8,128)(2,1)S(1)}, u32[]{:S(2)}, u32[]{:S(2)}) collective-permute-start(bf16[2,2,32,896]{3,2,1,0:T(8,128)(2,1)S(1)} %get-tuple-element.54), channel_id=1, source_target_pairs={{0,2},{1,3},{2,0},{3,1},{4,6},{5,7},{6,4},{7,5},{8,10},{9,11},{10,... | collective-permute-start | bytes 688136 | tf_op jit(solution)/shard_map/ppermute | solution.py:217
  9.3 8.5 %collective-permute-start.2 = (bf16[2,32,896]{2,1,0:T(8,128)(2,1)S(1)}, bf16[2,32,896]{2,1,0:T(8,128)(2,1)S(1)}, u32[]{:S(2)}, u32[]{:S(2)}) collective-permute-start(bf16[2,32,896]{2,1,0:T(8,128)(2,1)S(1)} %get-tuple-element.55), channel_id=1, source_target_pairs={{0,4},{1,5},{2,6},{3,7},{4,0},{5,1},{6,2},{7,3},{8,12},{9,13},{10,... | collective-permute-start | bytes 344072 | tf_op jit(solution)/shard_map/ppermute | solution.py:217
  11.9 10.5 %collective-permute-start.3 = (bf16[2,32,896]{2,1,0:T(8,128)(2,1)S(1)}, bf16[2,32,896]{2,1,0:T(8,128)(2,1)S(1)}, u32[]{:S(2)}, u32[]{:S(2)}) collective-permute-start(bf16[2,32,896]{2,1,0:T(8,128)(2,1)S(1)} %get-tuple-element.56), channel_id=1, source_target_pairs={{0,6},{1,7},{2,4},{3,5},{4,2},{5,3},{6,0},{7,1},{8,14},{9,15},{10,... | collective-permute-start | bytes 344072 | tf_op jit(solution)/shard_map/ppermute | solution.py:217
  23.7 16.7 %collective-permute-start.4 = (bf16[2,64,1024]{2,1,0:T(8,128)(2,1)S(1)}, bf16[2,64,1024]{2,1,0:T(8,128)(2,1)S(1)}, u32[]{:S(2)}, u32[]{:S(2)}) collective-permute-start(bf16[2,64,1024]{2,1,0:T(8,128)(2,1)S(1)} %get-tuple-element.59), channel_id=1, source_target_pairs={{0,8},{8,0},{16,24},{24,16},{1,9},{9,1},{17,25},{25,17},{2,10},{10... | collective-permute-start | bytes 786440 | tf_op jit(solution)/shard_map/ppermute | solution.py:217
  25.3 15.6 %collective-permute-start.5 = (bf16[2,64,1024]{2,1,0:T(8,128)(2,1)S(1)}, bf16[2,64,1024]{2,1,0:T(8,128)(2,1)S(1)}, u32[]{:S(2)}, u32[]{:S(2)}) collective-permute-start(bf16[2,64,1024]{2,1,0:T(8,128)(2,1)S(1)} %get-tuple-element.60), channel_id=1, source_target_pairs={{0,16},{8,24},{16,0},{24,8},{1,17},{9,25},{17,1},{25,9},{2,18},{10... | collective-permute-start | bytes 786440 | tf_op jit(solution)/shard_map/ppermute | solution.py:217
  26.8 14.1 %collective-permute-start.6 = (bf16[2,64,1024]{2,1,0:T(8,128)(2,1)S(1)}, bf16[2,64,1024]{2,1,0:T(8,128)(2,1)S(1)}, u32[]{:S(2)}, u32[]{:S(2)}) collective-permute-start(bf16[2,64,1024]{2,1,0:T(8,128)(2,1)S(1)} %get-tuple-element.61), channel_id=1, source_target_pairs={{0,24},{8,16},{16,8},{24,0},{1,25},{9,17},{17,9},{25,1},{2,26},{10... | collective-permute-start | bytes 786440 | tf_op jit(solution)/shard_map/ppermute | solution.py:217
  27.2 9.3 %collective-permute-start.7 = (bf16[2,32,896]{2,1,0:T(8,128)(2,1)S(1)}, bf16[2,32,896]{2,1,0:T(8,128)(2,1)S(1)}, u32[]{:S(2)}, u32[]{:S(2)}) collective-permute-start(bf16[2,32,896]{2,1,0:T(8,128)(2,1)S(1)} %get-tuple-element.62), channel_id=1, source_target_pairs={{0,4},{1,5},{2,6},{3,7},{4,0},{5,1},{6,2},{7,3},{8,12},{9,13},{10,... | collective-permute-start | bytes 344072 | tf_op jit(solution)/shard_map/ppermute | solution.py:217
  28.9 7.6 %collective-permute-start.8 = (bf16[2,32,896]{2,1,0:T(8,128)(2,1)S(1)}, bf16[2,32,896]{2,1,0:T(8,128)(2,1)S(1)}, u32[]{:S(2)}, u32[]{:S(2)}) collective-permute-start(bf16[2,32,896]{2,1,0:T(8,128)(2,1)S(1)} %get-tuple-element.63), channel_id=1, source_target_pairs={{0,6},{1,7},{2,4},{3,5},{4,2},{5,3},{6,0},{7,1},{8,14},{9,15},{10,... | collective-permute-start | bytes 344072 | tf_op jit(solution)/shard_map/ppermute | solution.py:217
  37.3 6.8 %collective-permute-start.13 = (bf16[64,1024]{1,0:T(8,128)(2,1)S(1)}, bf16[64,1024]{1,0:T(8,128)(2,1)S(1)}, u32[]{:S(2)}, u32[]{:S(2)}) collective-permute-start(bf16[64,1024]{1,0:T(8,128)(2,1)S(1)} %get-tuple-element.65), channel_id=1, source_target_pairs={{0,8},{8,0},{16,24},{24,16},{1,9},{9,1},{17,25},{25,17},{2,10},{10... | collective-permute-start | bytes 393224 | tf_op jit(solution)/shard_map/ppermute | solution.py:217
  38.8 12.1 %collective-permute-start.14 = (bf16[64,1024]{1,0:T(8,128)(2,1)S(1)}, bf16[64,1024]{1,0:T(8,128)(2,1)S(1)}, u32[]{:S(2)}, u32[]{:S(2)}) collective-permute-start(bf16[64,1024]{1,0:T(8,128)(2,1)S(1)} %get-tuple-element.66), channel_id=1, source_target_pairs={{0,16},{8,24},{16,0},{24,8},{1,17},{9,25},{17,1},{25,9},{2,18},{10... | collective-permute-start | bytes 393224 | tf_op jit(solution)/shard_map/ppermute | solution.py:217
  40.4 10.6 %collective-permute-start.15 = (bf16[64,1024]{1,0:T(8,128)(2,1)S(1)}, bf16[64,1024]{1,0:T(8,128)(2,1)S(1)}, u32[]{:S(2)}, u32[]{:S(2)}) collective-permute-start(bf16[64,1024]{1,0:T(8,128)(2,1)S(1)} %get-tuple-element.67), channel_id=1, source_target_pairs={{0,24},{8,16},{16,8},{24,0},{1,25},{9,17},{17,9},{25,1},{2,26},{10... | collective-permute-start | bytes 393224 | tf_op jit(solution)/shard_map/ppermute | solution.py:217
  41.0 11.5 %collective-permute-start.11 = (bf16[64,1024]{1,0:T(8,128)(2,1)S(1)}, bf16[64,1024]{1,0:T(8,128)(2,1)S(1)}, u32[]{:S(2)}, u32[]{:S(2)}) collective-permute-start(bf16[64,1024]{1,0:T(8,128)(2,1)S(1)} %shard_map.115.refs_0_), channel_id=1, source_target_pairs={{0,24},{8,16},{16,8},{24,0},{1,25},{9,17},{17,9},{25,1},{2,26},{10... | collective-permute-start | bytes 393224 | tf_op jit(solution)/shard_map/ppermute | solution.py:217
  43.6 11.2 %collective-permute-start.10 = (bf16[64,1024]{1,0:T(8,128)(2,1)S(1)}, bf16[64,1024]{1,0:T(8,128)(2,1)S(1)}, u32[]{:S(2)}, u32[]{:S(2)}) collective-permute-start(bf16[64,1024]{1,0:T(8,128)(2,1)S(1)} %shard_map.115.refs_0_), channel_id=1, source_target_pairs={{0,16},{8,24},{16,0},{24,8},{1,17},{9,25},{17,1},{25,9},{2,18},{10... | collective-permute-start | bytes 393224 | tf_op jit(solution)/shard_map/ppermute | solution.py:217
  44.1 10.7 %collective-permute-start.9 = (bf16[64,1024]{1,0:T(8,128)(2,1)S(1)}, bf16[64,1024]{1,0:T(8,128)(2,1)S(1)}, u32[]{:S(2)}, u32[]{:S(2)}) collective-permute-start(bf16[64,1024]{1,0:T(8,128)(2,1)S(1)} %shard_map.115.refs_0_), channel_id=1, source_target_pairs={{0,8},{8,0},{16,24},{24,16},{1,9},{9,1},{17,25},{25,17},{2,10},{10... | collective-permute-start | bytes 393224 | tf_op jit(solution)/shard_map/ppermute | solution.py:217
  51.2 7.4 %collective-permute-start.18 = (bf16[2,64,1024]{2,1,0:T(8,128)(2,1)S(1)}, bf16[2,64,1024]{2,1,0:T(8,128)(2,1)S(1)}, u32[]{:S(2)}, u32[]{:S(2)}) collective-permute-start(bf16[2,64,1024]{2,1,0:T(8,128)(2,1)S(1)} %shard_map.117.refs_0_), channel_id=1, source_target_pairs={{0,24},{8,16},{16,8},{24,0},{1,25},{9,17},{17,9},{25,1},{2,26},{10... | collective-permute-start | bytes 786440 | tf_op jit(solution)/shard_map/ppermute | solution.py:217
  51.3 9.6 %collective-permute-start.17 = (bf16[2,64,1024]{2,1,0:T(8,128)(2,1)S(1)}, bf16[2,64,1024]{2,1,0:T(8,128)(2,1)S(1)}, u32[]{:S(2)}, u32[]{:S(2)}) collective-permute-start(bf16[2,64,1024]{2,1,0:T(8,128)(2,1)S(1)} %shard_map.117.refs_0_), channel_id=1, source_target_pairs={{0,16},{8,24},{16,0},{24,8},{1,17},{9,25},{17,1},{25,9},{2,18},{10... | collective-permute-start | bytes 786440 | tf_op jit(solution)/shard_map/ppermute | solution.py:217
  52.5 8.6 %collective-permute-start.16 = (bf16[2,64,1024]{2,1,0:T(8,128)(2,1)S(1)}, bf16[2,64,1024]{2,1,0:T(8,128)(2,1)S(1)}, u32[]{:S(2)}, u32[]{:S(2)}) collective-permute-start(bf16[2,64,1024]{2,1,0:T(8,128)(2,1)S(1)} %shard_map.117.refs_0_), channel_id=1, source_target_pairs={{0,8},{8,0},{16,24},{24,16},{1,9},{9,1},{17,25},{25,17},{2,10},{10... | collective-permute-start | bytes 786440 | tf_op jit(solution)/shard_map/ppermute | solution.py:217
  55.6 6.9 %collective-permute-start.12 = (bf16[4,32,896]{2,1,0:T(8,128)(2,1)S(1)}, bf16[4,32,896]{2,1,0:T(8,128)(2,1)S(1)}, u32[]{:S(2)}, u32[]{:S(2)}) collective-permute-start(bf16[4,32,896]{2,1,0:T(8,128)(2,1)S(1)} %get-tuple-element.73), channel_id=1, source_target_pairs={{0,1},{1,0},{2,3},{3,2},{4,5},{5,4},{6,7},{7,6},{8,9},{9,8},{10,11... | collective-permute-start | bytes 688136 | tf_op jit(solution)/shard_map/ppermute | solution.py:217
  62.4 14.3 %collective-permute-start.19 = (bf16[4,32,896]{2,1,0:T(8,128)(2,1)S(1)}, bf16[4,32,896]{2,1,0:T(8,128)(2,1)S(1)}, u32[]{:S(2)}, u32[]{:S(2)}) collective-permute-start(bf16[4,32,896]{2,1,0:T(8,128)(2,1)S(1)} %get-tuple-element.75), channel_id=1, source_target_pairs={{0,1},{1,0},{2,3},{3,2},{4,5},{5,4},{6,7},{7,6},{8,9},{9,8},{10,11... | collective-permute-start | bytes 688136 | tf_op jit(solution)/shard_map/ppermute | solution.py:217
  62.5 14.1 %collective-permute-start.20 = (bf16[2,32,896]{2,1,0:T(8,128)(2,1)S(1)}, bf16[2,32,896]{2,1,0:T(8,128)(2,1)S(1)}, u32[]{:S(2)}, u32[]{:S(2)}) collective-permute-start(bf16[2,32,896]{2,1,0:T(8,128)(2,1)S(1)} %get-tuple-element.76), channel_id=1, source_target_pairs={{0,4},{1,5},{2,6},{3,7},{4,0},{5,1},{6,2},{7,3},{8,12},{9,13},{10,... | collective-permute-start | bytes 344072 | tf_op jit(solution)/shard_map/ppermute | solution.py:217
  67.7 8.9 %collective-permute-start.21 = (bf16[2,32,896]{2,1,0:T(8,128)(2,1)S(1)}, bf16[2,32,896]{2,1,0:T(8,128)(2,1)S(1)}, u32[]{:S(2)}, u32[]{:S(2)}) collective-permute-start(bf16[2,32,896]{2,1,0:T(8,128)(2,1)S(1)} %get-tuple-element.77), channel_id=1, source_target_pairs={{0,6},{1,7},{2,4},{3,5},{4,2},{5,3},{6,0},{7,1},{8,14},{9,15},{10,... | collective-permute-start | bytes 344072 | tf_op jit(solution)/shard_map/ppermute | solution.py:217
  76.7 16.0 %collective-permute-start.22 = (bf16[2,2,32,896]{3,2,1,0:T(8,128)(2,1)S(1)}, bf16[2,2,32,896]{3,2,1,0:T(8,128)(2,1)S(1)}, u32[]{:S(2)}, u32[]{:S(2)}) collective-permute-start(bf16[2,2,32,896]{3,2,1,0:T(8,128)(2,1)S(1)} %get-tuple-element.79), channel_id=1, source_target_pairs={{0,2},{1,3},{2,0},{3,1},{4,6},{5,7},{6,4},{7,5},{8,10},{9,11},{10,... | collective-permute-start | bytes 688136 | tf_op jit(solution)/shard_map/ppermute | solution.py:217
  81.5 11.2 %collective-permute-start.23 = (bf16[2,32,896]{2,1,0:T(8,128)(2,1)S(1)}, bf16[2,32,896]{2,1,0:T(8,128)(2,1)S(1)}, u32[]{:S(2)}, u32[]{:S(2)}) collective-permute-start(bf16[2,32,896]{2,1,0:T(8,128)(2,1)S(1)} %get-tuple-element.82), channel_id=1, source_target_pairs={{0,4},{1,5},{2,6},{3,7},{4,0},{5,1},{6,2},{7,3},{8,12},{9,13},{10,... | collective-permute-start | bytes 344072 | tf_op jit(solution)/shard_map/ppermute | solution.py:217
  81.5 11.2 %collective-permute-start.24 = (bf16[2,32,896]{2,1,0:T(8,128)(2,1)S(1)}, bf16[2,32,896]{2,1,0:T(8,128)(2,1)S(1)}, u32[]{:S(2)}, u32[]{:S(2)}) collective-permute-start(bf16[2,32,896]{2,1,0:T(8,128)(2,1)S(1)} %get-tuple-element.83), channel_id=1, source_target_pairs={{0,6},{1,7},{2,4},{3,5},{4,2},{5,3},{6,0},{7,1},{8,14},{9,15},{10,... | collective-permute-start | bytes 344072 | tf_op jit(solution)/shard_map/ppermute | solution.py:217
  (7 other events, 62.0 us)

commit v5 on v4

--- a/solution.py
+++ b/solution.py
@@ -87,18 +87,10 @@
             far_refs[at * (half - 2) + k - 2][1] = swap_ref[at, k]
 
 
-def pack_out_kernel(keep_ref, swap_ref, *far_refs):
-    for k, far_ref in enumerate(far_refs):
-        far_ref[0] = keep_ref[k + 2]
-        far_ref[1] = swap_ref[k + 2]
-
-
-def pack_last_kernel(out_keep_ref, out_swap_ref, keep_ref, swap_ref, near_ref, *far_refs):
-    near_ref[0, 0] = out_keep_ref[1]
-    near_ref[0, 1] = out_swap_ref[1]
-    near_ref[1, 0] = keep_ref[1]
-    near_ref[1, 1] = swap_ref[1]
-    pack_out_kernel(keep_ref, swap_ref, *far_refs)
+def pack_back_kernel(keep_ref, swap_ref, *out_refs):
+    for k, out_ref in enumerate(out_refs):
+        out_ref[0] = keep_ref[k + 1]
+        out_ref[1] = swap_ref[k + 1]
 
 
 def pieces(at, keep_ref, swap_ref, near_ref, far_refs):
@@ -195,20 +187,21 @@
     send_back(keep_ref, swap_ref, scratch, total.astype(BF16), dp)
 
 
-def scatter_scaled_kernel(pick_ref, weight_ref, keep_ref, swap_ref, near_ref, *refs):
-    found = [keep_ref[0], swap_ref[0], near_ref[0, 0], near_ref[0, 1]]
-    for ref in refs[:-1]:
+def returned(keep_ref, swap_ref, refs):
+    found = [keep_ref[0], swap_ref[0]]
+    for ref in refs:
         found += [ref[0], ref[1]]
-    back = jnp.concatenate(found, axis=0).astype(F32)
+    return jnp.concatenate(found, axis=0)
+
+
+def scatter_scaled_kernel(pick_ref, weight_ref, keep_ref, swap_ref, *refs):
+    back = returned(keep_ref, swap_ref, refs[:-1]).astype(F32)
     scaled = (weight_ref[...] * back).astype(BF16)
     refs[-1][...] = mm(pick_ref[...], scaled, ((0,), (0,))).astype(BF16)
 
 
-def scatter_kernel(pick_ref, keep_ref, swap_ref, near_ref, *refs):
-    found = [keep_ref[0], swap_ref[0], near_ref[1, 0], near_ref[1, 1]]
-    for ref in refs[:-1]:
-        found += [ref[0], ref[1]]
-    back = jnp.concatenate(found, axis=0)
+def scatter_kernel(pick_ref, keep_ref, swap_ref, *refs):
+    back = returned(keep_ref, swap_ref, refs[:-1])
     refs[-1][...] = mm(pick_ref[...], back, ((0,), (0,))).astype(BF16)
 
 
@@ -266,27 +259,17 @@
     near_to, *far_to = call(functools.partial(pack_kernel, half), (near, *far, *far), 0, 8 * slots)(
         keep, swap
     )
+    far_rows = [partner(far_to[k], "expert", 2 * (2 + k)) for k in reversed(range(half - 2))][::-1]
     near_in = partner(near_to, "expert", 2)
-    far_in = [
-        partner(value, "expert", 2 * (2 + k % (half - 2))) for k, value in enumerate(far_to)
-    ]
+    far_grads = [partner(far_to[half - 2 + k], "expert", 2 * (2 + k)) for k in range(half - 2)]
     rows, *part_pre = call(
         functools.partial(gate_up_kernel, half),
         (sized, *[shape((2, chunk, hidden), BF16)] * dp),
         2 * product,
         2 * weights,
         scratch_shapes=in_order,
-    )(keep, swap, near_in, *far_in[: half - 2], gate_mat, up_mat)
+    )(keep, swap, near_in, *far_rows, gate_mat, up_mat)
     sums = trade(part_pre)
-    grads, *part_grad = call(
-        functools.partial(grad_act_kernel, half),
-        (sized, *[shape((chunk, hidden), BF16)] * dp),
-        product,
-        weights,
-        scratch_shapes=in_order,
-    )(keep, swap, near_in, *far_in[half - 2 :], down_mat)
-    grad_sums = trade(part_grad)
-    sums, part_grad = lax.optimization_barrier((sums, part_grad))
     act_mine = call(
         functools.partial(act_kernel, dp),
         shape((chunk, hidden), BF16),
@@ -294,6 +277,15 @@
         4 * dp * chunk * hidden,
     )(*sums)
     acts = trade([act_mine] * dp)
+    far_grads, act_mine = lax.optimization_barrier((far_grads, act_mine))
+    grads, *part_grad = call(
+        functools.partial(grad_act_kernel, half),
+        (sized, *[shape((chunk, hidden), BF16)] * dp),
+        product,
+        weights,
+        scratch_shapes=in_order,
+    )(keep, swap, near_in, *far_grads, down_mat)
+    grad_sums = trade(part_grad)
     pre_mine = call(
         functools.partial(grad_pre_kernel, dp),
         shape((2, chunk, hidden), BF16),
@@ -308,9 +300,11 @@
         weights,
         scratch_shapes=in_order,
     )(*acts, down_mat)
+    back = [far[0]] * (half - 1)
     out_swap = partner(out_swap, "expert", 1)
-    out_far = call(pack_out_kernel, far, 0, 8 * slots)(out_keep, out_swap)
+    out_near, *out_far = call(pack_back_kernel, back, 0, 8 * slots)(out_keep, out_swap)
     out_far = [partner(value, "expert", 2 * (2 + k)) for k, value in enumerate(out_far)]
+    pre, out_far = lax.optimization_barrier((pre, out_far))
     gate_pre, up_pre, grad_keep, grad_swap = call(
         functools.partial(row_grad_kernel, dp),
         (wide, wide, one, one),
@@ -318,13 +312,13 @@
         2 * weights,
         scratch_shapes=in_order,
     )(*pre, gate_mat, up_mat)
+    grad_swap, out_near = lax.optimization_barrier((grad_swap, out_near))
     grad_swap = partner(grad_swap, "expert", 1)
-    grad_swap, out_far = lax.optimization_barrier((grad_swap, out_far))
-    near_back, *grad_far = call(pack_last_kernel, (near, *far), 0, 8 * slots)(
-        out_keep, out_swap, grad_keep, grad_swap
-    )
-    near_back = partner(near_back, "expert", 2)
-    grad_far = [partner(value, "expert", 2 * (2 + k)) for k, value in enumerate(grad_far)]
+    out_near = partner(out_near, "expert", 2)
+    grad_back = call(pack_back_kernel, back, 0, 8 * slots)(grad_keep, grad_swap)
+    grad_back = [
+        partner(grad_back[k], "expert", 2 * (1 + k)) for k in reversed(range(half - 1))
+    ][::-1]
 
     grad_down = mm(act, grads, ((0,), (0,))).astype(BF16)
     grad_gate = mm(rows, gate_pre, ((0,), (0,))).astype(BF16)
@@ -333,10 +327,10 @@
     full = shape((tok_rows, features), BF16)
     mixed = call(
         scatter_scaled_kernel, full, 2 * slots * tok_rows * features, 4 * tok_rows * features
-    )(pick, weight, out_keep, out_swap, near_back, *out_far)
+    )(pick, weight, out_keep, out_swap, out_near, *out_far)
     grad_tokens = call(
         scatter_kernel, full, 2 * slots * tok_rows * features, 4 * tok_rows * features
-    )(pick, grad_keep, grad_swap, near_back, *grad_far)
+    )(pick, grad_keep, grad_swap, *grad_back)
     return (mixed, grad_tokens, grad_gate[None], grad_up[None], grad_down[None])
 
 

time: 95.7 us -> 85.8 us (0.90)
  starting transfers between devices: 35.2 us -> 29.6 us
  waiting for transfers between devices: 42.7 us -> 38.4 us
    ppermute x25 -> x26, starting transfers between devices: 35.2 us -> 29.6 us  [partner(): return lax.ppermute(value, axis, [(i, i ^ k) for i in range(size)])]
    ppermute x25 -> x26, waiting for transfers between devices: 42.7 us -> 38.4 us  [partner(): return lax.ppermute(value, axis, [(i, i ^ k) for i in range(size)])]
  transfers between devices with their start and end apart: 25 -> 26, of which waited for: 10 -> 13; matrix products, arithmetic and copies ran while one was open for 6% -> 7% of each run, Pallas kernels for 4% -> 4%
where the time goes in v5:
time: 85.8 us; the launch traced here: 85.6 us
  waiting for transfers between devices  38.4 us (45%)
  starting transfers between devices  29.6 us (34%)
  Pallas kernels  11.1 us (13%)
  matrix products  5.78 us (7%)
    ppermute x26, waiting for transfers between devices, partner(): return lax.ppermute(value, axis, [(i, i ^ k) for i in range(size)])  38.4 us
    ppermute x26, starting transfers between devices, partner(): return lax.ppermute(value, axis, [(i, i ^ k) for i in range(size)])  29.6 us
    dot_general x3, matrix products, mm(): lax.dot_general(left, right, (dims, ((), ())), preferred_element_type=F32)  5.78 us
    pallas_call x1, Pallas kernels, body(): call(functools.partial(route_kernel, experts), outs, 4 * slots * tok_rows...  3.46 us
  transfers between devices with their start and end apart: 26, of which 13 were waited for; matrix products, arithmetic and copies ran while one was open for 7% of the time, Pallas kernels for 4%

profile of v5, /device:TPU:0, one launch (start us, length us, event | category | flops | bytes accessed | tf_op | source)
XLA Modules:
  0.0 85.6 jit_solution(16360615228643030477)
XLA Ops:
  0.6 3.5 %shard_map.110 = (bf16[256,512]{1,0:T(8,128)(2,1)}, f32[256,1]{1,0:T(8,128)}, bf16[2,4,32,896]{3,2,1,0:T(8,128)(2,1)}, bf16[2,4,32,896]{3,2,1,0:T(8,128)(2,1)}) custom-call(s32[8,512]{1,0:T(8,128)} %bitcast.22, f32[8,512]{1,0:T(8,128)} %bitcast.23, bf16[512,896]{1,0:T(8,128)(2,1)} %tokens_ref.1, bf16[512,896]{1,0:T(8,128)(2,1)} %grad_ref.1), custom_call_target="tpu_custom_call" | custom-call | flops 469762048 | bytes 3670016 | tf_op jit(solution)/shard_map/pallas_call | solution.py:245
  4.7 1.5 %collective-permute-done.swap_ref = bf16[2,4,32,896]{3,2,1,0:T(8,128)(2,1)S(1)} collective-permute-done((bf16[2,4,32,896]{3,2,1,0:T(8,128)(2,1)}, bf16[2,4,32,896]{3,2,1,0:T(8,128)(2,1)S(1)}, u32[]{:S(2)}, u32[]{:S(2)}) %collective-permute-start) | collective-permute-done | bytes 458784 | tf_op jit(solution)/shard_map/ppermute | solution.py:210
  6.3 3.0 %collective-permute-start.1 = (bf16[2,2,32,896]{3,2,1,0:T(8,128)(2,1)S(1)}, bf16[2,2,32,896]{3,2,1,0:T(8,128)(2,1)S(1)}, u32[]{:S(2)}, u32[]{:S(2)}) collective-permute-start(bf16[2,2,32,896]{3,2,1,0:T(8,128)(2,1)S(1)} %get-tuple-element.58), channel_id=1, source_target_pairs={{0,2},{1,3},{2,0},{3,1},{4,6},{5,7},{6,4},{7,5},{8,10},{9,11},{10,... | collective-permute-start | bytes 688136 | tf_op jit(solution)/shard_map/ppermute | solution.py:210
  9.3 2.6 %collective-permute-start.2 = (bf16[2,32,896]{2,1,0:T(8,128)(2,1)S(1)}, bf16[2,32,896]{2,1,0:T(8,128)(2,1)S(1)}, u32[]{:S(2)}, u32[]{:S(2)}) collective-permute-start(bf16[2,32,896]{2,1,0:T(8,128)(2,1)S(1)} %get-tuple-element.59), channel_id=1, source_target_pairs={{0,4},{1,5},{2,6},{3,7},{4,0},{5,1},{6,2},{7,3},{8,12},{9,13},{10,... | collective-permute-start | bytes 344072 | tf_op jit(solution)/shard_map/ppermute | solution.py:210
  11.9 5.9 %collective-permute-done.2.refs_0_ = bf16[2,32,896]{2,1,0:T(8,128)(2,1)S(1)} collective-permute-done((bf16[2,32,896]{2,1,0:T(8,128)(2,1)S(1)}, bf16[2,32,896]{2,1,0:T(8,128)(2,1)S(1)}, u32[]{:S(2)}, u32[]{:S(2)}) %collective-permute-start.2) | collective-permute-done | bytes 114720 | tf_op jit(solution)/shard_map/ppermute | solution.py:210
  17.8 4.6 %collective-permute-done.3.refs_1_ = bf16[2,32,896]{2,1,0:T(8,128)(2,1)S(1)} collective-permute-done((bf16[2,32,896]{2,1,0:T(8,128)(2,1)S(1)}, bf16[2,32,896]{2,1,0:T(8,128)(2,1)S(1)}, u32[]{:S(2)}, u32[]{:S(2)}) %collective-permute-start.3) | collective-permute-done | bytes 114720 | tf_op jit(solution)/shard_map/ppermute | solution.py:210
  23.7 1.6 %collective-permute-start.4 = (bf16[2,64,1024]{2,1,0:T(8,128)(2,1)S(1)}, bf16[2,64,1024]{2,1,0:T(8,128)(2,1)S(1)}, u32[]{:S(2)}, u32[]{:S(2)}) collective-permute-start(bf16[2,64,1024]{2,1,0:T(8,128)(2,1)S(1)} %get-tuple-element.63), channel_id=1, source_target_pairs={{0,8},{8,0},{16,24},{24,16},{1,9},{9,1},{17,25},{25,17},{2,10},{10... | collective-permute-start | bytes 786440 | tf_op jit(solution)/shard_map/ppermute | solution.py:210
  25.3 1.5 %collective-permute-start.5 = (bf16[2,64,1024]{2,1,0:T(8,128)(2,1)S(1)}, bf16[2,64,1024]{2,1,0:T(8,128)(2,1)S(1)}, u32[]{:S(2)}, u32[]{:S(2)}) collective-permute-start(bf16[2,64,1024]{2,1,0:T(8,128)(2,1)S(1)} %get-tuple-element.64), channel_id=1, source_target_pairs={{0,16},{8,24},{16,0},{24,8},{1,17},{9,25},{17,1},{25,9},{2,18},{10... | collective-permute-start | bytes 786440 | tf_op jit(solution)/shard_map/ppermute | solution.py:210
  27.2 1.7 %collective-permute-start.11 = (bf16[2,32,896]{2,1,0:T(8,128)(2,1)S(1)}, bf16[2,32,896]{2,1,0:T(8,128)(2,1)S(1)}, u32[]{:S(2)}, u32[]{:S(2)}) collective-permute-start(bf16[2,32,896]{2,1,0:T(8,128)(2,1)S(1)} %get-tuple-element.68), channel_id=1, source_target_pairs={{0,4},{1,5},{2,6},{3,7},{4,0},{5,1},{6,2},{7,3},{8,12},{9,13},{10,... | collective-permute-start | bytes 344072 | tf_op jit(solution)/shard_map/ppermute | solution.py:210
  30.3 2.7 %collective-permute-done.4.refs_1_ = bf16[2,64,1024]{2,1,0:T(8,128)(2,1)S(1)} collective-permute-done((bf16[2,64,1024]{2,1,0:T(8,128)(2,1)S(1)}, bf16[2,64,1024]{2,1,0:T(8,128)(2,1)S(1)}, u32[]{:S(2)}, u32[]{:S(2)}) %collective-permute-start.4) | collective-permute-done | bytes 262176 | tf_op jit(solution)/shard_map/ppermute | solution.py:210
  33.0 5.0 %collective-permute-done.5.refs_2_ = bf16[2,64,1024]{2,1,0:T(8,128)(2,1)S(1)} collective-permute-done((bf16[2,64,1024]{2,1,0:T(8,128)(2,1)S(1)}, bf16[2,64,1024]{2,1,0:T(8,128)(2,1)S(1)}, u32[]{:S(2)}, u32[]{:S(2)}) %collective-permute-start.5) | collective-permute-done | bytes 262176 | tf_op jit(solution)/shard_map/ppermute | solution.py:210
  38.2 1.6 %collective-permute-start.9 = (bf16[64,1024]{1,0:T(8,128)(2,1)S(1)}, bf16[64,1024]{1,0:T(8,128)(2,1)S(1)}, u32[]{:S(2)}, u32[]{:S(2)}) collective-permute-start(bf16[64,1024]{1,0:T(8,128)(2,1)S(1)} %shard_map.114.refs_0_), channel_id=1, source_target_pairs={{0,24},{8,16},{16,8},{24,0},{1,25},{9,17},{17,9},{25,1},{2,26},{10... | collective-permute-start | bytes 393224 | tf_op jit(solution)/shard_map/ppermute | solution.py:210
  46.6 2.0 %collective-permute-done.8.refs_2_ = bf16[64,1024]{1,0:T(8,128)(2,1)S(1)} collective-permute-done((bf16[64,1024]{1,0:T(8,128)(2,1)S(1)}, bf16[64,1024]{1,0:T(8,128)(2,1)S(1)}, u32[]{:S(2)}, u32[]{:S(2)}) %collective-permute-start.8) | collective-permute-done | bytes 131104 | tf_op jit(solution)/shard_map/ppermute | solution.py:210
  50.1 1.5 %collective-permute-done.15.refs_7_ = bf16[64,1024]{1,0:T(8,128)(2,1)S(1)} collective-permute-done((bf16[64,1024]{1,0:T(8,128)(2,1)S(1)}, bf16[64,1024]{1,0:T(8,128)(2,1)S(1)}, u32[]{:S(2)}, u32[]{:S(2)}) %collective-permute-start.15) | collective-permute-done | bytes 131104 | tf_op jit(solution)/shard_map/ppermute | solution.py:210
  53.1 1.5 %collective-permute-start.17 = (bf16[2,64,1024]{2,1,0:T(8,128)(2,1)S(1)}, bf16[2,64,1024]{2,1,0:T(8,128)(2,1)S(1)}, u32[]{:S(2)}, u32[]{:S(2)}) collective-permute-start(bf16[2,64,1024]{2,1,0:T(8,128)(2,1)S(1)} %shard_map.117.refs_0_), channel_id=1, source_target_pairs={{0,16},{8,24},{16,0},{24,8},{1,17},{9,25},{17,1},{25,9},{2,18},{10... | collective-permute-start | bytes 786440 | tf_op jit(solution)/shard_map/ppermute | solution.py:210
  55.5 1.6 %collective-permute-start.19 = (bf16[2,32,896]{2,1,0:T(8,128)(2,1)S(1)}, bf16[2,32,896]{2,1,0:T(8,128)(2,1)S(1)}, u32[]{:S(2)}, u32[]{:S(2)}) collective-permute-start(bf16[2,32,896]{2,1,0:T(8,128)(2,1)S(1)} %get-tuple-element.76), channel_id=1, source_target_pairs={{0,4},{1,5},{2,6},{3,7},{4,0},{5,1},{6,2},{7,3},{8,12},{9,13},{10,... | collective-permute-start | bytes 344072 | tf_op jit(solution)/shard_map/ppermute | solution.py:210
  57.1 5.1 %collective-permute-done.18.refs_3_ = bf16[2,64,1024]{2,1,0:T(8,128)(2,1)S(1)} collective-permute-done((bf16[2,64,1024]{2,1,0:T(8,128)(2,1)S(1)}, bf16[2,64,1024]{2,1,0:T(8,128)(2,1)S(1)}, u32[]{:S(2)}, u32[]{:S(2)}) %collective-permute-start.18) | collective-permute-done | bytes 262176 | tf_op jit(solution)/shard_map/ppermute | solution.py:210
  62.1 2.8 %collective-permute-done.17.refs_2_ = bf16[2,64,1024]{2,1,0:T(8,128)(2,1)S(1)} collective-permute-done((bf16[2,64,1024]{2,1,0:T(8,128)(2,1)S(1)}, bf16[2,64,1024]{2,1,0:T(8,128)(2,1)S(1)}, u32[]{:S(2)}, u32[]{:S(2)}) %collective-permute-start.17) | collective-permute-done | bytes 262176 | tf_op jit(solution)/shard_map/ppermute | solution.py:210
  66.4 2.0 %convert_bitcast_fusion = bf16[1,1024,896]{2,1,0:T(8,128)(2,1)} fusion(bf16[256,1024]{1,0:T(8,128)(2,1)S(1)} %get-tuple-element.95, bf16[256,896]{1,0:T(8,128)(2,1)S(1)} %get-tuple-element.96), kind=kOutput, calls=%fused_computation | convolution fusion | flops 470679552 | bytes 2818048 | tf_op jit(solution)/shard_map/dot_general | solution.py:18
  69.1 1.9 %convert_bitcast_fusion.2 = bf16[1,896,1024]{2,1,0:T(8,128)(2,1)} fusion(bf16[256,896]{1,0:T(8,128)(2,1)S(1)} %get-tuple-element.92, bf16[256,1024]{1,0:T(8,128)(2,1)S(1)} %get-tuple-element.93), kind=kOutput, calls=%fused_computation.2 | convolution fusion | flops 470679552 | bytes 2818048 | tf_op jit(solution)/shard_map/dot_general | solution.py:18
  72.4 1.9 %collective-permute-start.24 = (bf16[2,32,896]{2,1,0:T(8,128)(2,1)S(1)}, bf16[2,32,896]{2,1,0:T(8,128)(2,1)S(1)}, u32[]{:S(2)}, u32[]{:S(2)}) collective-permute-start(bf16[2,32,896]{2,1,0:T(8,128)(2,1)S(1)} %get-tuple-element.90), channel_id=1, source_target_pairs={{0,4},{1,5},{2,6},{3,7},{4,0},{5,1},{6,2},{7,3},{8,12},{9,13},{10,... | collective-permute-start | bytes 344072 | tf_op jit(solution)/shard_map/ppermute | solution.py:210
  75.5 1.9 %convert_bitcast_fusion.1 = bf16[1,896,1024]{2,1,0:T(8,128)(2,1)} fusion(bf16[256,896]{1,0:T(8,128)(2,1)S(1)} %get-tuple-element.92, bf16[256,1024]{1,0:T(8,128)(2,1)S(1)} %get-tuple-element.94), kind=kOutput, calls=%fused_computation.1 | convolution fusion | flops 470679552 | bytes 2818048 | tf_op jit(solution)/shard_map/dot_general | solution.py:18
  77.4 1.5 %shard_map.120 = bf16[512,896]{1,0:T(8,128)(2,1)} custom-call(bf16[256,512]{1,0:T(8,128)(2,1)S(1)} %copy-done.4, f32[256,1]{1,0:T(8,128)S(1)} %copy-done.5, bf16[4,32,896]{2,1,0:T(8,128)(2,1)S(1)} %get-tuple-element.66.keep_ref, bf16[4,32,896]{2,1,0:T(8,128)(2,1)S(1)} %collective-permute-done.10.swap_ref, ...), custom_call_target="tpu_custom_call" | custom-call | flops 234881024 | bytes 1835008 | tf_op jit(solution)/shard_map/pallas_call | solution.py:328
  78.9 5.4 %collective-permute-done.24.refs_1_ = bf16[2,32,896]{2,1,0:T(8,128)(2,1)S(1)} collective-permute-done((bf16[2,32,896]{2,1,0:T(8,128)(2,1)S(1)}, bf16[2,32,896]{2,1,0:T(8,128)(2,1)S(1)}, u32[]{:S(2)}, u32[]{:S(2)}) %collective-permute-start.24) | collective-permute-done | bytes 114720 | tf_op jit(solution)/shard_map/ppermute | solution.py:210
  (56 shorter events, 20.7 us)
Async XLA Ops:
  6.3 16.1 %collective-permute-start.1 = (bf16[2,2,32,896]{3,2,1,0:T(8,128)(2,1)S(1)}, bf16[2,2,32,896]{3,2,1,0:T(8,128)(2,1)S(1)}, u32[]{:S(2)}, u32[]{:S(2)}) collective-permute-start(bf16[2,2,32,896]{3,2,1,0:T(8,128)(2,1)S(1)} %get-tuple-element.58), channel_id=1, source_target_pairs={{0,2},{1,3},{2,0},{3,1},{4,6},{5,7},{6,4},{7,5},{8,10},{9,11},{10,... | collective-permute-start | bytes 688136 | tf_op jit(solution)/shard_map/ppermute | solution.py:210
  9.3 8.5 %collective-permute-start.2 = (bf16[2,32,896]{2,1,0:T(8,128)(2,1)S(1)}, bf16[2,32,896]{2,1,0:T(8,128)(2,1)S(1)}, u32[]{:S(2)}, u32[]{:S(2)}) collective-permute-start(bf16[2,32,896]{2,1,0:T(8,128)(2,1)S(1)} %get-tuple-element.59), channel_id=1, source_target_pairs={{0,4},{1,5},{2,6},{3,7},{4,0},{5,1},{6,2},{7,3},{8,12},{9,13},{10,... | collective-permute-start | bytes 344072 | tf_op jit(solution)/shard_map/ppermute | solution.py:210
  11.9 10.5 %collective-permute-start.3 = (bf16[2,32,896]{2,1,0:T(8,128)(2,1)S(1)}, bf16[2,32,896]{2,1,0:T(8,128)(2,1)S(1)}, u32[]{:S(2)}, u32[]{:S(2)}) collective-permute-start(bf16[2,32,896]{2,1,0:T(8,128)(2,1)S(1)} %get-tuple-element.60), channel_id=1, source_target_pairs={{0,6},{1,7},{2,4},{3,5},{4,2},{5,3},{6,0},{7,1},{8,14},{9,15},{10,... | collective-permute-start | bytes 344072 | tf_op jit(solution)/shard_map/ppermute | solution.py:210
  23.7 9.3 %collective-permute-start.4 = (bf16[2,64,1024]{2,1,0:T(8,128)(2,1)S(1)}, bf16[2,64,1024]{2,1,0:T(8,128)(2,1)S(1)}, u32[]{:S(2)}, u32[]{:S(2)}) collective-permute-start(bf16[2,64,1024]{2,1,0:T(8,128)(2,1)S(1)} %get-tuple-element.63), channel_id=1, source_target_pairs={{0,8},{8,0},{16,24},{24,16},{1,9},{9,1},{17,25},{25,17},{2,10},{10... | collective-permute-start | bytes 786440 | tf_op jit(solution)/shard_map/ppermute | solution.py:210
  25.3 12.8 %collective-permute-start.5 = (bf16[2,64,1024]{2,1,0:T(8,128)(2,1)S(1)}, bf16[2,64,1024]{2,1,0:T(8,128)(2,1)S(1)}, u32[]{:S(2)}, u32[]{:S(2)}) collective-permute-start(bf16[2,64,1024]{2,1,0:T(8,128)(2,1)S(1)} %get-tuple-element.64), channel_id=1, source_target_pairs={{0,16},{8,24},{16,0},{24,8},{1,17},{9,25},{17,1},{25,9},{2,18},{10... | collective-permute-start | bytes 786440 | tf_op jit(solution)/shard_map/ppermute | solution.py:210
  26.8 11.3 %collective-permute-start.6 = (bf16[2,64,1024]{2,1,0:T(8,128)(2,1)S(1)}, bf16[2,64,1024]{2,1,0:T(8,128)(2,1)S(1)}, u32[]{:S(2)}, u32[]{:S(2)}) collective-permute-start(bf16[2,64,1024]{2,1,0:T(8,128)(2,1)S(1)} %get-tuple-element.65), channel_id=1, source_target_pairs={{0,24},{8,16},{16,8},{24,0},{1,25},{9,17},{17,9},{25,1},{2,26},{10... | collective-permute-start | bytes 786440 | tf_op jit(solution)/shard_map/ppermute | solution.py:210
  27.2 14.6 %collective-permute-start.11 = (bf16[2,32,896]{2,1,0:T(8,128)(2,1)S(1)}, bf16[2,32,896]{2,1,0:T(8,128)(2,1)S(1)}, u32[]{:S(2)}, u32[]{:S(2)}) collective-permute-start(bf16[2,32,896]{2,1,0:T(8,128)(2,1)S(1)} %get-tuple-element.68), channel_id=1, source_target_pairs={{0,4},{1,5},{2,6},{3,7},{4,0},{5,1},{6,2},{7,3},{8,12},{9,13},{10,... | collective-permute-start | bytes 344072 | tf_op jit(solution)/shard_map/ppermute | solution.py:210
  28.9 12.9 %collective-permute-start.12 = (bf16[2,32,896]{2,1,0:T(8,128)(2,1)S(1)}, bf16[2,32,896]{2,1,0:T(8,128)(2,1)S(1)}, u32[]{:S(2)}, u32[]{:S(2)}) collective-permute-start(bf16[2,32,896]{2,1,0:T(8,128)(2,1)S(1)} %get-tuple-element.69), channel_id=1, source_target_pairs={{0,6},{1,7},{2,4},{3,5},{4,2},{5,3},{6,0},{7,1},{8,14},{9,15},{10,... | collective-permute-start | bytes 344072 | tf_op jit(solution)/shard_map/ppermute | solution.py:210
  38.2 7.5 %collective-permute-start.9 = (bf16[64,1024]{1,0:T(8,128)(2,1)S(1)}, bf16[64,1024]{1,0:T(8,128)(2,1)S(1)}, u32[]{:S(2)}, u32[]{:S(2)}) collective-permute-start(bf16[64,1024]{1,0:T(8,128)(2,1)S(1)} %shard_map.114.refs_0_), channel_id=1, source_target_pairs={{0,24},{8,16},{16,8},{24,0},{1,25},{9,17},{17,9},{25,1},{2,26},{10... | collective-permute-start | bytes 393224 | tf_op jit(solution)/shard_map/ppermute | solution.py:210
  39.8 8.8 %collective-permute-start.8 = (bf16[64,1024]{1,0:T(8,128)(2,1)S(1)}, bf16[64,1024]{1,0:T(8,128)(2,1)S(1)}, u32[]{:S(2)}, u32[]{:S(2)}) collective-permute-start(bf16[64,1024]{1,0:T(8,128)(2,1)S(1)} %shard_map.114.refs_0_), channel_id=1, source_target_pairs={{0,16},{8,24},{16,0},{24,8},{1,17},{9,25},{17,1},{25,9},{2,18},{10... | collective-permute-start | bytes 393224 | tf_op jit(solution)/shard_map/ppermute | solution.py:210
  41.0 7.6 %collective-permute-start.7 = (bf16[64,1024]{1,0:T(8,128)(2,1)S(1)}, bf16[64,1024]{1,0:T(8,128)(2,1)S(1)}, u32[]{:S(2)}, u32[]{:S(2)}) collective-permute-start(bf16[64,1024]{1,0:T(8,128)(2,1)S(1)} %shard_map.114.refs_0_), channel_id=1, source_target_pairs={{0,8},{8,0},{16,24},{24,16},{1,9},{9,1},{17,25},{25,17},{2,10},{10... | collective-permute-start | bytes 393224 | tf_op jit(solution)/shard_map/ppermute | solution.py:210
  42.6 7.2 %collective-permute-start.13 = (bf16[64,1024]{1,0:T(8,128)(2,1)S(1)}, bf16[64,1024]{1,0:T(8,128)(2,1)S(1)}, u32[]{:S(2)}, u32[]{:S(2)}) collective-permute-start(bf16[64,1024]{1,0:T(8,128)(2,1)S(1)} %get-tuple-element.73), channel_id=1, source_target_pairs={{0,8},{8,0},{16,24},{24,16},{1,9},{9,1},{17,25},{25,17},{2,10},{10... | collective-permute-start | bytes 393224 | tf_op jit(solution)/shard_map/ppermute | solution.py:210
  43.9 6.3 %collective-permute-start.14 = (bf16[64,1024]{1,0:T(8,128)(2,1)S(1)}, bf16[64,1024]{1,0:T(8,128)(2,1)S(1)}, u32[]{:S(2)}, u32[]{:S(2)}) collective-permute-start(bf16[64,1024]{1,0:T(8,128)(2,1)S(1)} %get-tuple-element.74), channel_id=1, source_target_pairs={{0,16},{8,24},{16,0},{24,8},{1,17},{9,25},{17,1},{25,9},{2,18},{10... | collective-permute-start | bytes 393224 | tf_op jit(solution)/shard_map/ppermute | solution.py:210
  45.7 5.9 %collective-permute-start.15 = (bf16[64,1024]{1,0:T(8,128)(2,1)S(1)}, bf16[64,1024]{1,0:T(8,128)(2,1)S(1)}, u32[]{:S(2)}, u32[]{:S(2)}) collective-permute-start(bf16[64,1024]{1,0:T(8,128)(2,1)S(1)} %get-tuple-element.75), channel_id=1, source_target_pairs={{0,24},{8,16},{16,8},{24,0},{1,25},{9,17},{17,9},{25,1},{2,26},{10... | collective-permute-start | bytes 393224 | tf_op jit(solution)/shard_map/ppermute | solution.py:210
  49.3 6.1 %collective-permute-start.10 = (bf16[4,32,896]{2,1,0:T(8,128)(2,1)S(1)}, bf16[4,32,896]{2,1,0:T(8,128)(2,1)S(1)}, u32[]{:S(2)}, u32[]{:S(2)}) collective-permute-start(bf16[4,32,896]{2,1,0:T(8,128)(2,1)S(1)} %get-tuple-element.67), channel_id=1, source_target_pairs={{0,1},{1,0},{2,3},{3,2},{4,5},{5,4},{6,7},{7,6},{8,9},{9,8},{10,11... | collective-permute-start | bytes 688136 | tf_op jit(solution)/shard_map/ppermute | solution.py:210
  51.9 10.2 %collective-permute-start.18 = (bf16[2,64,1024]{2,1,0:T(8,128)(2,1)S(1)}, bf16[2,64,1024]{2,1,0:T(8,128)(2,1)S(1)}, u32[]{:S(2)}, u32[]{:S(2)}) collective-permute-start(bf16[2,64,1024]{2,1,0:T(8,128)(2,1)S(1)} %shard_map.117.refs_0_), channel_id=1, source_target_pairs={{0,24},{8,16},{16,8},{24,0},{1,25},{9,17},{17,9},{25,1},{2,26},{10... | collective-permute-start | bytes 786440 | tf_op jit(solution)/shard_map/ppermute | solution.py:210
  53.1 11.9 %collective-permute-start.17 = (bf16[2,64,1024]{2,1,0:T(8,128)(2,1)S(1)}, bf16[2,64,1024]{2,1,0:T(8,128)(2,1)S(1)}, u32[]{:S(2)}, u32[]{:S(2)}) collective-permute-start(bf16[2,64,1024]{2,1,0:T(8,128)(2,1)S(1)} %shard_map.117.refs_0_), channel_id=1, source_target_pairs={{0,16},{8,24},{16,0},{24,8},{1,17},{9,25},{17,1},{25,9},{2,18},{10... | collective-permute-start | bytes 786440 | tf_op jit(solution)/shard_map/ppermute | solution.py:210
  54.6 10.4 %collective-permute-start.16 = (bf16[2,64,1024]{2,1,0:T(8,128)(2,1)S(1)}, bf16[2,64,1024]{2,1,0:T(8,128)(2,1)S(1)}, u32[]{:S(2)}, u32[]{:S(2)}) collective-permute-start(bf16[2,64,1024]{2,1,0:T(8,128)(2,1)S(1)} %shard_map.117.refs_0_), channel_id=1, source_target_pairs={{0,8},{8,0},{16,24},{24,16},{1,9},{9,1},{17,25},{25,17},{2,10},{10... | collective-permute-start | bytes 786440 | tf_op jit(solution)/shard_map/ppermute | solution.py:210
  55.5 9.5 %collective-permute-start.19 = (bf16[2,32,896]{2,1,0:T(8,128)(2,1)S(1)}, bf16[2,32,896]{2,1,0:T(8,128)(2,1)S(1)}, u32[]{:S(2)}, u32[]{:S(2)}) collective-permute-start(bf16[2,32,896]{2,1,0:T(8,128)(2,1)S(1)} %get-tuple-element.76), channel_id=1, source_target_pairs={{0,4},{1,5},{2,6},{3,7},{4,0},{5,1},{6,2},{7,3},{8,12},{9,13},{10,... | collective-permute-start | bytes 344072 | tf_op jit(solution)/shard_map/ppermute | solution.py:210
  57.0 7.9 %collective-permute-start.20 = (bf16[2,32,896]{2,1,0:T(8,128)(2,1)S(1)}, bf16[2,32,896]{2,1,0:T(8,128)(2,1)S(1)}, u32[]{:S(2)}, u32[]{:S(2)}) collective-permute-start(bf16[2,32,896]{2,1,0:T(8,128)(2,1)S(1)} %get-tuple-element.77), channel_id=1, source_target_pairs={{0,6},{1,7},{2,4},{3,5},{4,2},{5,3},{6,0},{7,1},{8,14},{9,15},{10,... | collective-permute-start | bytes 344072 | tf_op jit(solution)/shard_map/ppermute | solution.py:210
  68.4 9.0 %collective-permute-start.21 = (bf16[2,32,896]{2,1,0:T(8,128)(2,1)S(1)}, bf16[2,32,896]{2,1,0:T(8,128)(2,1)S(1)}, u32[]{:S(2)}, u32[]{:S(2)}) collective-permute-start(bf16[2,32,896]{2,1,0:T(8,128)(2,1)S(1)} %get-tuple-element.84), channel_id=1, source_target_pairs={{0,2},{1,3},{2,0},{3,1},{4,6},{5,7},{6,4},{7,5},{8,10},{9,11},{10,... | collective-permute-start | bytes 344072 | tf_op jit(solution)/shard_map/ppermute | solution.py:210
  71.0 7.8 %collective-permute-start.23 = (bf16[2,32,896]{2,1,0:T(8,128)(2,1)S(1)}, bf16[2,32,896]{2,1,0:T(8,128)(2,1)S(1)}, u32[]{:S(2)}, u32[]{:S(2)}) collective-permute-start(bf16[2,32,896]{2,1,0:T(8,128)(2,1)S(1)} %get-tuple-element.89), channel_id=1, source_target_pairs={{0,2},{1,3},{2,0},{3,1},{4,6},{5,7},{6,4},{7,5},{8,10},{9,11},{10,... | collective-permute-start | bytes 344072 | tf_op jit(solution)/shard_map/ppermute | solution.py:210
  72.4 11.8 %collective-permute-start.24 = (bf16[2,32,896]{2,1,0:T(8,128)(2,1)S(1)}, bf16[2,32,896]{2,1,0:T(8,128)(2,1)S(1)}, u32[]{:S(2)}, u32[]{:S(2)}) collective-permute-start(bf16[2,32,896]{2,1,0:T(8,128)(2,1)S(1)} %get-tuple-element.90), channel_id=1, source_target_pairs={{0,4},{1,5},{2,6},{3,7},{4,0},{5,1},{6,2},{7,3},{8,12},{9,13},{10,... | collective-permute-start | bytes 344072 | tf_op jit(solution)/shard_map/ppermute | solution.py:210
  74.3 9.9 %collective-permute-start.25 = (bf16[2,32,896]{2,1,0:T(8,128)(2,1)S(1)}, bf16[2,32,896]{2,1,0:T(8,128)(2,1)S(1)}, u32[]{:S(2)}, u32[]{:S(2)}) collective-permute-start(bf16[2,32,896]{2,1,0:T(8,128)(2,1)S(1)} %get-tuple-element.91), channel_id=1, source_target_pairs={{0,6},{1,7},{2,4},{3,5},{4,2},{5,3},{6,0},{7,1},{8,14},{9,15},{10,... | collective-permute-start | bytes 344072 | tf_op jit(solution)/shard_map/ppermute | solution.py:210
  (8 other events, 63.3 us)

commit v6 on v5

--- a/solution.py
+++ b/solution.py
@@ -45,9 +45,16 @@
         swap_ref[(*at, k)] = value[(2 * k + 1) * rows : (2 * k + 2) * rows]
 
 
-def route_kernel(
-    experts, ids_ref, gates_ref, tokens_ref, grad_ref, pick_ref, weight_ref, keep_ref, swap_ref
-):
+def route_kernel(experts, *refs):
+    pick_ref, weight_ref, keep_ref, swap_ref = refs[4:8]
+    ids_ref, gates_ref, tokens_ref, grad_ref, sems = refs[8:]
+    copies = [
+        pltpu.make_async_copy(refs[k], refs[8 + k], sems.at[k]) for k in range(4)
+    ]
+    for copy in copies:
+        copy.start()
+    copies[0].wait()
+    copies[1].wait()
     ids = ids_ref[...]
     tok_rows = ids.shape[1]
     slots = pick_ref.shape[0]
@@ -68,8 +75,10 @@
     weight_ref[...] = slot_weight
     pick = pick.astype(F32).astype(BF16)
     pick_ref[...] = pick
+    copies[2].wait()
     rows = mm(pick, tokens_ref[...], ((1,), (0,))).astype(BF16)
     split_cores(keep_ref, swap_ref, rows, 0)
+    copies[3].wait()
     rows = (slot_weight * mm(pick, grad_ref[...], ((1,), (0,)))).astype(BF16)
     split_cores(keep_ref, swap_ref, rows, 1)
 
@@ -211,11 +220,8 @@
 
 
 def trade(values):
-    return [values[0]] + [partner(value, "dp", k + 1) for k, value in enumerate(values[1:])]
-
-
-def whole(array):
-    return pl.BlockSpec(array.shape, lambda i: (0,) * len(array.shape))
+    far_first = reversed(range(1, len(values)))
+    return [values[0]] + [partner(values[k], "dp", k) for k in far_first][::-1]
 
 
 def body(tokens, grad_out, expert_ids, gates, w_gate, w_up, w_down):
@@ -248,9 +254,11 @@
         4 * slots * tok_rows * features,
         8 * tok_rows * features,
         limit=ROUTE_LIMIT,
-        grid=(1,),
-        in_specs=[whole(array) for array in ins],
-        out_specs=tuple(whole(array) for array in outs),
+        in_specs=[pl.BlockSpec(memory_space=pl.ANY)] * 4,
+        scratch_shapes=[
+            *[pltpu.VMEM(array.shape, array.dtype) for array in ins],
+            pltpu.SemaphoreType.DMA((4,)),
+        ],
     )(*ins)
     swap_to, up_mat = lax.optimization_barrier((swap, up_mat))
     swap = partner(swap_to, "expert", 1)
@@ -269,7 +277,7 @@
         2 * weights,
         scratch_shapes=in_order,
     )(keep, swap, near_in, *far_rows, gate_mat, up_mat)
-    sums = trade(part_pre)
+    sums = trade(part_pre)[::-1]
     act_mine = call(
         functools.partial(act_kernel, dp),
         shape((chunk, hidden), BF16),
@@ -285,7 +293,7 @@
         weights,
         scratch_shapes=in_order,
     )(keep, swap, near_in, *far_grads, down_mat)
-    grad_sums = trade(part_grad)
+    grad_sums = trade(part_grad)[::-1]
     pre_mine = call(
         functools.partial(grad_pre_kernel, dp),
         shape((2, chunk, hidden), BF16),
@@ -312,9 +320,9 @@
         2 * weights,
         scratch_shapes=in_order,
     )(*pre, gate_mat, up_mat)
-    grad_swap, out_near = lax.optimization_barrier((grad_swap, out_near))
     grad_swap = partner(grad_swap, "expert", 1)
     out_near = partner(out_near, "expert", 2)
+    grad_swap, gate_pre, up_pre = lax.optimization_barrier((grad_swap, gate_pre, up_pre))
     grad_back = call(pack_back_kernel, back, 0, 8 * slots)(grad_keep, grad_swap)
     grad_back = [
         partner(grad_back[k], "expert", 2 * (1 + k)) for k in reversed(range(half - 1))

time: 85.8 us -> 89.9 us (1.048)
  waiting for transfers between devices: 38.4 us -> 41.3 us
  starting transfers between devices: 29.6 us -> 31.1 us
    ppermute x26, waiting for transfers between devices: 38.4 us -> 41.3 us  [partner(): return lax.ppermute(value, axis, [(i, i ^ k) for i in range(size)])]
    ppermute x26, starting transfers between devices: 29.6 us -> 31.1 us  [partner(): return lax.ppermute(value, axis, [(i, i ^ k) for i in range(size)])]
  transfers between devices with their start and end apart: 26 -> 26, of which waited for: 13 -> 15; matrix products, arithmetic and copies ran while one was open for 7% -> 6% of each run, Pallas kernels for 4% -> 4%
where the time goes in v6:
time: 89.9 us; the launch traced here: 89.8 us
  waiting for transfers between devices  41.3 us (46%)
  starting transfers between devices  31.1 us (35%)
  Pallas kernels  10.9 us (12%)
  matrix products  5.77 us (6%)
    ppermute x26, waiting for transfers between devices, partner(): return lax.ppermute(value, axis, [(i, i ^ k) for i in range(size)])  41.3 us
    ppermute x26, starting transfers between devices, partner(): return lax.ppermute(value, axis, [(i, i ^ k) for i in range(size)])  31.1 us
    dot_general x3, matrix products, mm(): lax.dot_general(left, right, (dims, ((), ())), preferred_element_type=F32)  5.77 us
    pallas_call x1, Pallas kernels, body(): call(functools.partial(route_kernel, experts), outs, 4 * slots * tok_rows...  3.2 us
  transfers between devices with their start and end apart: 26, of which 15 were waited for; matrix products, arithmetic and copies ran while one was open for 6% of the time, Pallas kernels for 4%

profile of v6, /device:TPU:0, one launch (start us, length us, event | category | flops | bytes accessed | tf_op | source)
XLA Modules:
  0.0 89.8 jit_solution(11602332819923838552)
XLA Ops:
  0.6 3.2 %shard_map.110 = (bf16[256,512]{1,0:T(8,128)(2,1)}, f32[256,1]{1,0:T(8,128)}, bf16[2,4,32,896]{3,2,1,0:T(8,128)(2,1)}, bf16[2,4,32,896]{3,2,1,0:T(8,128)(2,1)}) custom-call(s32[8,512]{1,0:T(8,128)} %bitcast.22, f32[8,512]{1,0:T(8,128)} %bitcast.23, bf16[512,896]{1,0:T(8,128)(2,1)} %refs_2_.1, bf16[512,896]{1,0:T(8,128)(2,1)} %refs_3_.1), custom_call_target="tpu_custom_call" | custom-call | flops 469762048 | bytes 3670016 | tf_op jit(solution)/shard_map/pallas_call | solution.py:251
  4.5 1.5 %collective-permute-done.swap_ref = bf16[2,4,32,896]{3,2,1,0:T(8,128)(2,1)S(1)} collective-permute-done((bf16[2,4,32,896]{3,2,1,0:T(8,128)(2,1)}, bf16[2,4,32,896]{3,2,1,0:T(8,128)(2,1)S(1)}, u32[]{:S(2)}, u32[]{:S(2)}) %collective-permute-start) | collective-permute-done | bytes 458784 | tf_op jit(solution)/shard_map/ppermute | solution.py:219
  6.1 3.0 %collective-permute-start.1 = (bf16[2,2,32,896]{3,2,1,0:T(8,128)(2,1)S(1)}, bf16[2,2,32,896]{3,2,1,0:T(8,128)(2,1)S(1)}, u32[]{:S(2)}, u32[]{:S(2)}) collective-permute-start(bf16[2,2,32,896]{3,2,1,0:T(8,128)(2,1)S(1)} %get-tuple-element.59), channel_id=1, source_target_pairs={{0,2},{1,3},{2,0},{3,1},{4,6},{5,7},{6,4},{7,5},{8,10},{9,11},{10,... | collective-permute-start | bytes 688136 | tf_op jit(solution)/shard_map/ppermute | solution.py:219
  9.1 2.6 %collective-permute-start.2 = (bf16[2,32,896]{2,1,0:T(8,128)(2,1)S(1)}, bf16[2,32,896]{2,1,0:T(8,128)(2,1)S(1)}, u32[]{:S(2)}, u32[]{:S(2)}) collective-permute-start(bf16[2,32,896]{2,1,0:T(8,128)(2,1)S(1)} %get-tuple-element.60), channel_id=1, source_target_pairs={{0,4},{1,5},{2,6},{3,7},{4,0},{5,1},{6,2},{7,3},{8,12},{9,13},{10,... | collective-permute-start | bytes 344072 | tf_op jit(solution)/shard_map/ppermute | solution.py:219
  11.7 5.9 %collective-permute-done.2.refs_0_ = bf16[2,32,896]{2,1,0:T(8,128)(2,1)S(1)} collective-permute-done((bf16[2,32,896]{2,1,0:T(8,128)(2,1)S(1)}, bf16[2,32,896]{2,1,0:T(8,128)(2,1)S(1)}, u32[]{:S(2)}, u32[]{:S(2)}) %collective-permute-start.2) | collective-permute-done | bytes 114720 | tf_op jit(solution)/shard_map/ppermute | solution.py:219
  17.6 4.6 %collective-permute-done.3.refs_1_ = bf16[2,32,896]{2,1,0:T(8,128)(2,1)S(1)} collective-permute-done((bf16[2,32,896]{2,1,0:T(8,128)(2,1)S(1)}, bf16[2,32,896]{2,1,0:T(8,128)(2,1)S(1)}, u32[]{:S(2)}, u32[]{:S(2)}) %collective-permute-start.3) | collective-permute-done | bytes 114720 | tf_op jit(solution)/shard_map/ppermute | solution.py:219
  23.5 2.5 %collective-permute-start.4 = (bf16[2,64,1024]{2,1,0:T(8,128)(2,1)S(1)}, bf16[2,64,1024]{2,1,0:T(8,128)(2,1)S(1)}, u32[]{:S(2)}, u32[]{:S(2)}) collective-permute-start(bf16[2,64,1024]{2,1,0:T(8,128)(2,1)S(1)} %get-tuple-element.63), channel_id=1, source_target_pairs={{0,24},{8,16},{16,8},{24,0},{1,25},{9,17},{17,9},{25,1},{2,26},{10... | collective-permute-start | bytes 786440 | tf_op jit(solution)/shard_map/ppermute | solution.py:219
  27.1 1.7 %collective-permute-start.12 = (bf16[2,32,896]{2,1,0:T(8,128)(2,1)S(1)}, bf16[2,32,896]{2,1,0:T(8,128)(2,1)S(1)}, u32[]{:S(2)}, u32[]{:S(2)}) collective-permute-start(bf16[2,32,896]{2,1,0:T(8,128)(2,1)S(1)} %get-tuple-element.70), channel_id=1, source_target_pairs={{0,4},{1,5},{2,6},{3,7},{4,0},{5,1},{6,2},{7,3},{8,12},{9,13},{10,... | collective-permute-start | bytes 344072 | tf_op jit(solution)/shard_map/ppermute | solution.py:219
  30.1 3.7 %collective-permute-done.4.refs_0_ = bf16[2,64,1024]{2,1,0:T(8,128)(2,1)S(1)} collective-permute-done((bf16[2,64,1024]{2,1,0:T(8,128)(2,1)S(1)}, bf16[2,64,1024]{2,1,0:T(8,128)(2,1)S(1)}, u32[]{:S(2)}, u32[]{:S(2)}) %collective-permute-start.4) | collective-permute-done | bytes 262176 | tf_op jit(solution)/shard_map/ppermute | solution.py:219
  33.8 3.8 %collective-permute-done.5.refs_1_ = bf16[2,64,1024]{2,1,0:T(8,128)(2,1)S(1)} collective-permute-done((bf16[2,64,1024]{2,1,0:T(8,128)(2,1)S(1)}, bf16[2,64,1024]{2,1,0:T(8,128)(2,1)S(1)}, u32[]{:S(2)}, u32[]{:S(2)}) %collective-permute-start.5) | collective-permute-done | bytes 262176 | tf_op jit(solution)/shard_map/ppermute | solution.py:219
  37.9 1.7 %collective-permute-start.9 = (bf16[64,1024]{1,0:T(8,128)(2,1)S(1)}, bf16[64,1024]{1,0:T(8,128)(2,1)S(1)}, u32[]{:S(2)}, u32[]{:S(2)}) collective-permute-start(bf16[64,1024]{1,0:T(8,128)(2,1)S(1)} %shard_map.114.refs_0_), channel_id=1, source_target_pairs={{0,24},{8,16},{16,8},{24,0},{1,25},{9,17},{17,9},{25,1},{2,26},{10... | collective-permute-start | bytes 393224 | tf_op jit(solution)/shard_map/ppermute | solution.py:219
  42.2 1.7 %collective-permute-start.14 = (bf16[64,1024]{1,0:T(8,128)(2,1)S(1)}, bf16[64,1024]{1,0:T(8,128)(2,1)S(1)}, u32[]{:S(2)}, u32[]{:S(2)}) collective-permute-start(bf16[64,1024]{1,0:T(8,128)(2,1)S(1)} %get-tuple-element.74), channel_id=1, source_target_pairs={{0,24},{8,16},{16,8},{24,0},{1,25},{9,17},{17,9},{25,1},{2,26},{10... | collective-permute-start | bytes 393224 | tf_op jit(solution)/shard_map/ppermute | solution.py:219
  48.9 1.9 %collective-permute-done.14.refs_4_ = bf16[64,1024]{1,0:T(8,128)(2,1)S(1)} collective-permute-done((bf16[64,1024]{1,0:T(8,128)(2,1)S(1)}, bf16[64,1024]{1,0:T(8,128)(2,1)S(1)}, u32[]{:S(2)}, u32[]{:S(2)}) %collective-permute-start.14) | collective-permute-done | bytes 131104 | tf_op jit(solution)/shard_map/ppermute | solution.py:219
  50.8 1.7 %collective-permute-done.15.refs_5_ = bf16[64,1024]{1,0:T(8,128)(2,1)S(1)} collective-permute-done((bf16[64,1024]{1,0:T(8,128)(2,1)S(1)}, bf16[64,1024]{1,0:T(8,128)(2,1)S(1)}, u32[]{:S(2)}, u32[]{:S(2)}) %collective-permute-start.15) | collective-permute-done | bytes 131104 | tf_op jit(solution)/shard_map/ppermute | solution.py:219
  53.0 1.5 %collective-permute-start.19 = (bf16[2,64,1024]{2,1,0:T(8,128)(2,1)S(1)}, bf16[2,64,1024]{2,1,0:T(8,128)(2,1)S(1)}, u32[]{:S(2)}, u32[]{:S(2)}) collective-permute-start(bf16[2,64,1024]{2,1,0:T(8,128)(2,1)S(1)} %shard_map.118.refs_0_), channel_id=1, source_target_pairs={{0,24},{8,16},{16,8},{24,0},{1,25},{9,17},{17,9},{25,1},{2,26},{10... | collective-permute-start | bytes 786440 | tf_op jit(solution)/shard_map/ppermute | solution.py:219
  56.5 1.5 %collective-permute-start.20 = (bf16[2,32,896]{2,1,0:T(8,128)(2,1)S(1)}, bf16[2,32,896]{2,1,0:T(8,128)(2,1)S(1)}, u32[]{:S(2)}, u32[]{:S(2)}) collective-permute-start(bf16[2,32,896]{2,1,0:T(8,128)(2,1)S(1)} %get-tuple-element.78), channel_id=1, source_target_pairs={{0,4},{1,5},{2,6},{3,7},{4,0},{5,1},{6,2},{7,3},{8,12},{9,13},{10,... | collective-permute-start | bytes 344072 | tf_op jit(solution)/shard_map/ppermute | solution.py:219
  58.1 5.1 %collective-permute-done.19.refs_3_ = bf16[2,64,1024]{2,1,0:T(8,128)(2,1)S(1)} collective-permute-done((bf16[2,64,1024]{2,1,0:T(8,128)(2,1)S(1)}, bf16[2,64,1024]{2,1,0:T(8,128)(2,1)S(1)}, u32[]{:S(2)}, u32[]{:S(2)}) %collective-permute-start.19) | collective-permute-done | bytes 262176 | tf_op jit(solution)/shard_map/ppermute | solution.py:219
  63.1 4.5 %collective-permute-done.18.refs_2_ = bf16[2,64,1024]{2,1,0:T(8,128)(2,1)S(1)} collective-permute-done((bf16[2,64,1024]{2,1,0:T(8,128)(2,1)S(1)}, bf16[2,64,1024]{2,1,0:T(8,128)(2,1)S(1)}, u32[]{:S(2)}, u32[]{:S(2)}) %collective-permute-start.18) | collective-permute-done | bytes 262176 | tf_op jit(solution)/shard_map/ppermute | solution.py:219
  69.9 2.0 %convert_bitcast_fusion = bf16[1,1024,896]{2,1,0:T(8,128)(2,1)} fusion(bf16[256,1024]{1,0:T(8,128)(2,1)S(1)} %get-tuple-element.97, bf16[256,896]{1,0:T(8,128)(2,1)S(1)} %get-tuple-element.98), kind=kOutput, calls=%fused_computation | convolution fusion | flops 470679552 | bytes 2818048 | tf_op jit(solution)/shard_map/dot_general | solution.py:18
  71.8 3.0 %collective-permute-done.11.refs_0_ = bf16[2,32,896]{2,1,0:T(8,128)(2,1)S(1)} collective-permute-done((bf16[2,32,896]{2,1,0:T(8,128)(2,1)S(1)}, bf16[2,32,896]{2,1,0:T(8,128)(2,1)S(1)}, u32[]{:S(2)}, u32[]{:S(2)}) %collective-permute-start.11) | collective-permute-done | bytes 114720 | tf_op jit(solution)/shard_map/ppermute | solution.py:219
  78.3 2.4 %collective-permute-start.25 = (bf16[2,32,896]{2,1,0:T(8,128)(2,1)S(1)}, bf16[2,32,896]{2,1,0:T(8,128)(2,1)S(1)}, u32[]{:S(2)}, u32[]{:S(2)}) collective-permute-start(bf16[2,32,896]{2,1,0:T(8,128)(2,1)S(1)} %get-tuple-element.93), channel_id=1, source_target_pairs={{0,6},{1,7},{2,4},{3,5},{4,2},{5,3},{6,0},{7,1},{8,14},{9,15},{10,... | collective-permute-start | bytes 344072 | tf_op jit(solution)/shard_map/ppermute | solution.py:219
  80.8 1.9 %convert_bitcast_fusion.2 = bf16[1,896,1024]{2,1,0:T(8,128)(2,1)} fusion(bf16[256,896]{1,0:T(8,128)(2,1)S(1)} %get-tuple-element.94, bf16[256,1024]{1,0:T(8,128)(2,1)S(1)} %get-tuple-element.95), kind=kOutput, calls=%fused_computation.2 | convolution fusion | flops 470679552 | bytes 2818048 | tf_op jit(solution)/shard_map/dot_general | solution.py:18
  82.7 1.9 %convert_bitcast_fusion.1 = bf16[1,896,1024]{2,1,0:T(8,128)(2,1)} fusion(bf16[256,896]{1,0:T(8,128)(2,1)S(1)} %get-tuple-element.94, bf16[256,1024]{1,0:T(8,128)(2,1)S(1)} %get-tuple-element.96), kind=kOutput, calls=%fused_computation.1 | convolution fusion | flops 470679552 | bytes 2818048 | tf_op jit(solution)/shard_map/dot_general | solution.py:18
  84.6 3.8 %collective-permute-done.24.refs_1_ = bf16[2,32,896]{2,1,0:T(8,128)(2,1)S(1)} collective-permute-done((bf16[2,32,896]{2,1,0:T(8,128)(2,1)S(1)}, bf16[2,32,896]{2,1,0:T(8,128)(2,1)S(1)}, u32[]{:S(2)}, u32[]{:S(2)}) %collective-permute-start.24) | collective-permute-done | bytes 114720 | tf_op jit(solution)/shard_map/ppermute | solution.py:219
  (56 shorter events, 21.8 us)
Async XLA Ops:
  6.1 16.1 %collective-permute-start.1 = (bf16[2,2,32,896]{3,2,1,0:T(8,128)(2,1)S(1)}, bf16[2,2,32,896]{3,2,1,0:T(8,128)(2,1)S(1)}, u32[]{:S(2)}, u32[]{:S(2)}) collective-permute-start(bf16[2,2,32,896]{3,2,1,0:T(8,128)(2,1)S(1)} %get-tuple-element.59), channel_id=1, source_target_pairs={{0,2},{1,3},{2,0},{3,1},{4,6},{5,7},{6,4},{7,5},{8,10},{9,11},{10,... | collective-permute-start | bytes 688136 | tf_op jit(solution)/shard_map/ppermute | solution.py:219
  9.1 8.5 %collective-permute-start.2 = (bf16[2,32,896]{2,1,0:T(8,128)(2,1)S(1)}, bf16[2,32,896]{2,1,0:T(8,128)(2,1)S(1)}, u32[]{:S(2)}, u32[]{:S(2)}) collective-permute-start(bf16[2,32,896]{2,1,0:T(8,128)(2,1)S(1)} %get-tuple-element.60), channel_id=1, source_target_pairs={{0,4},{1,5},{2,6},{3,7},{4,0},{5,1},{6,2},{7,3},{8,12},{9,13},{10,... | collective-permute-start | bytes 344072 | tf_op jit(solution)/shard_map/ppermute | solution.py:219
  11.7 10.5 %collective-permute-start.3 = (bf16[2,32,896]{2,1,0:T(8,128)(2,1)S(1)}, bf16[2,32,896]{2,1,0:T(8,128)(2,1)S(1)}, u32[]{:S(2)}, u32[]{:S(2)}) collective-permute-start(bf16[2,32,896]{2,1,0:T(8,128)(2,1)S(1)} %get-tuple-element.61), channel_id=1, source_target_pairs={{0,6},{1,7},{2,4},{3,5},{4,2},{5,3},{6,0},{7,1},{8,14},{9,15},{10,... | collective-permute-start | bytes 344072 | tf_op jit(solution)/shard_map/ppermute | solution.py:219
  23.5 10.2 %collective-permute-start.4 = (bf16[2,64,1024]{2,1,0:T(8,128)(2,1)S(1)}, bf16[2,64,1024]{2,1,0:T(8,128)(2,1)S(1)}, u32[]{:S(2)}, u32[]{:S(2)}) collective-permute-start(bf16[2,64,1024]{2,1,0:T(8,128)(2,1)S(1)} %get-tuple-element.63), channel_id=1, source_target_pairs={{0,24},{8,16},{16,8},{24,0},{1,25},{9,17},{17,9},{25,1},{2,26},{10... | collective-permute-start | bytes 786440 | tf_op jit(solution)/shard_map/ppermute | solution.py:219
  26.0 11.5 %collective-permute-start.5 = (bf16[2,64,1024]{2,1,0:T(8,128)(2,1)S(1)}, bf16[2,64,1024]{2,1,0:T(8,128)(2,1)S(1)}, u32[]{:S(2)}, u32[]{:S(2)}) collective-permute-start(bf16[2,64,1024]{2,1,0:T(8,128)(2,1)S(1)} %get-tuple-element.64), channel_id=1, source_target_pairs={{0,16},{8,24},{16,0},{24,8},{1,17},{9,25},{17,1},{25,9},{2,18},{10... | collective-permute-start | bytes 786440 | tf_op jit(solution)/shard_map/ppermute | solution.py:219
  26.5 11.1 %collective-permute-start.6 = (bf16[2,64,1024]{2,1,0:T(8,128)(2,1)S(1)}, bf16[2,64,1024]{2,1,0:T(8,128)(2,1)S(1)}, u32[]{:S(2)}, u32[]{:S(2)}) collective-permute-start(bf16[2,64,1024]{2,1,0:T(8,128)(2,1)S(1)} %get-tuple-element.65), channel_id=1, source_target_pairs={{0,8},{8,0},{16,24},{24,16},{1,9},{9,1},{17,25},{25,17},{2,10},{10... | collective-permute-start | bytes 786440 | tf_op jit(solution)/shard_map/ppermute | solution.py:219
  27.1 14.3 %collective-permute-start.12 = (bf16[2,32,896]{2,1,0:T(8,128)(2,1)S(1)}, bf16[2,32,896]{2,1,0:T(8,128)(2,1)S(1)}, u32[]{:S(2)}, u32[]{:S(2)}) collective-permute-start(bf16[2,32,896]{2,1,0:T(8,128)(2,1)S(1)} %get-tuple-element.70), channel_id=1, source_target_pairs={{0,4},{1,5},{2,6},{3,7},{4,0},{5,1},{6,2},{7,3},{8,12},{9,13},{10,... | collective-permute-start | bytes 344072 | tf_op jit(solution)/shard_map/ppermute | solution.py:219
  28.8 12.7 %collective-permute-start.13 = (bf16[2,32,896]{2,1,0:T(8,128)(2,1)S(1)}, bf16[2,32,896]{2,1,0:T(8,128)(2,1)S(1)}, u32[]{:S(2)}, u32[]{:S(2)}) collective-permute-start(bf16[2,32,896]{2,1,0:T(8,128)(2,1)S(1)} %get-tuple-element.71), channel_id=1, source_target_pairs={{0,6},{1,7},{2,4},{3,5},{4,2},{5,3},{6,0},{7,1},{8,14},{9,15},{10,... | collective-permute-start | bytes 344072 | tf_op jit(solution)/shard_map/ppermute | solution.py:219
  37.9 7.4 %collective-permute-start.9 = (bf16[64,1024]{1,0:T(8,128)(2,1)S(1)}, bf16[64,1024]{1,0:T(8,128)(2,1)S(1)}, u32[]{:S(2)}, u32[]{:S(2)}) collective-permute-start(bf16[64,1024]{1,0:T(8,128)(2,1)S(1)} %shard_map.114.refs_0_), channel_id=1, source_target_pairs={{0,24},{8,16},{16,8},{24,0},{1,25},{9,17},{17,9},{25,1},{2,26},{10... | collective-permute-start | bytes 393224 | tf_op jit(solution)/shard_map/ppermute | solution.py:219
  39.6 8.5 %collective-permute-start.8 = (bf16[64,1024]{1,0:T(8,128)(2,1)S(1)}, bf16[64,1024]{1,0:T(8,128)(2,1)S(1)}, u32[]{:S(2)}, u32[]{:S(2)}) collective-permute-start(bf16[64,1024]{1,0:T(8,128)(2,1)S(1)} %shard_map.114.refs_0_), channel_id=1, source_target_pairs={{0,16},{8,24},{16,0},{24,8},{1,17},{9,25},{17,1},{25,9},{2,18},{10... | collective-permute-start | bytes 393224 | tf_op jit(solution)/shard_map/ppermute | solution.py:219
  40.9 7.2 %collective-permute-start.7 = (bf16[64,1024]{1,0:T(8,128)(2,1)S(1)}, bf16[64,1024]{1,0:T(8,128)(2,1)S(1)}, u32[]{:S(2)}, u32[]{:S(2)}) collective-permute-start(bf16[64,1024]{1,0:T(8,128)(2,1)S(1)} %shard_map.114.refs_0_), channel_id=1, source_target_pairs={{0,8},{8,0},{16,24},{24,16},{1,9},{9,1},{17,25},{25,17},{2,10},{10... | collective-permute-start | bytes 393224 | tf_op jit(solution)/shard_map/ppermute | solution.py:219
  42.2 8.7 %collective-permute-start.14 = (bf16[64,1024]{1,0:T(8,128)(2,1)S(1)}, bf16[64,1024]{1,0:T(8,128)(2,1)S(1)}, u32[]{:S(2)}, u32[]{:S(2)}) collective-permute-start(bf16[64,1024]{1,0:T(8,128)(2,1)S(1)} %get-tuple-element.74), channel_id=1, source_target_pairs={{0,24},{8,16},{16,8},{24,0},{1,25},{9,17},{17,9},{25,1},{2,26},{10... | collective-permute-start | bytes 393224 | tf_op jit(solution)/shard_map/ppermute | solution.py:219
  43.9 8.7 %collective-permute-start.15 = (bf16[64,1024]{1,0:T(8,128)(2,1)S(1)}, bf16[64,1024]{1,0:T(8,128)(2,1)S(1)}, u32[]{:S(2)}, u32[]{:S(2)}) collective-permute-start(bf16[64,1024]{1,0:T(8,128)(2,1)S(1)} %get-tuple-element.75), channel_id=1, source_target_pairs={{0,16},{8,24},{16,0},{24,8},{1,17},{9,25},{17,1},{25,9},{2,18},{10... | collective-permute-start | bytes 393224 | tf_op jit(solution)/shard_map/ppermute | solution.py:219
  45.2 7.4 %collective-permute-start.16 = (bf16[64,1024]{1,0:T(8,128)(2,1)S(1)}, bf16[64,1024]{1,0:T(8,128)(2,1)S(1)}, u32[]{:S(2)}, u32[]{:S(2)}) collective-permute-start(bf16[64,1024]{1,0:T(8,128)(2,1)S(1)} %get-tuple-element.76), channel_id=1, source_target_pairs={{0,8},{8,0},{16,24},{24,16},{1,9},{9,1},{17,25},{25,17},{2,10},{10... | collective-permute-start | bytes 393224 | tf_op jit(solution)/shard_map/ppermute | solution.py:219
  48.9 7.6 %collective-permute-start.10 = (bf16[4,32,896]{2,1,0:T(8,128)(2,1)S(1)}, bf16[4,32,896]{2,1,0:T(8,128)(2,1)S(1)}, u32[]{:S(2)}, u32[]{:S(2)}) collective-permute-start(bf16[4,32,896]{2,1,0:T(8,128)(2,1)S(1)} %get-tuple-element.68), channel_id=1, source_target_pairs={{0,1},{1,0},{2,3},{3,2},{4,5},{5,4},{6,7},{7,6},{8,9},{9,8},{10,11... | collective-permute-start | bytes 688136 | tf_op jit(solution)/shard_map/ppermute | solution.py:219
  53.0 10.2 %collective-permute-start.19 = (bf16[2,64,1024]{2,1,0:T(8,128)(2,1)S(1)}, bf16[2,64,1024]{2,1,0:T(8,128)(2,1)S(1)}, u32[]{:S(2)}, u32[]{:S(2)}) collective-permute-start(bf16[2,64,1024]{2,1,0:T(8,128)(2,1)S(1)} %shard_map.118.refs_0_), channel_id=1, source_target_pairs={{0,24},{8,16},{16,8},{24,0},{1,25},{9,17},{17,9},{25,1},{2,26},{10... | collective-permute-start | bytes 786440 | tf_op jit(solution)/shard_map/ppermute | solution.py:219
  54.4 13.3 %collective-permute-start.18 = (bf16[2,64,1024]{2,1,0:T(8,128)(2,1)S(1)}, bf16[2,64,1024]{2,1,0:T(8,128)(2,1)S(1)}, u32[]{:S(2)}, u32[]{:S(2)}) collective-permute-start(bf16[2,64,1024]{2,1,0:T(8,128)(2,1)S(1)} %shard_map.118.refs_0_), channel_id=1, source_target_pairs={{0,16},{8,24},{16,0},{24,8},{1,17},{9,25},{17,1},{25,9},{2,18},{10... | collective-permute-start | bytes 786440 | tf_op jit(solution)/shard_map/ppermute | solution.py:219
  55.9 11.9 %collective-permute-start.17 = (bf16[2,64,1024]{2,1,0:T(8,128)(2,1)S(1)}, bf16[2,64,1024]{2,1,0:T(8,128)(2,1)S(1)}, u32[]{:S(2)}, u32[]{:S(2)}) collective-permute-start(bf16[2,64,1024]{2,1,0:T(8,128)(2,1)S(1)} %shard_map.118.refs_0_), channel_id=1, source_target_pairs={{0,8},{8,0},{16,24},{24,16},{1,9},{9,1},{17,25},{25,17},{2,10},{10... | collective-permute-start | bytes 786440 | tf_op jit(solution)/shard_map/ppermute | solution.py:219
  56.5 11.2 %collective-permute-start.20 = (bf16[2,32,896]{2,1,0:T(8,128)(2,1)S(1)}, bf16[2,32,896]{2,1,0:T(8,128)(2,1)S(1)}, u32[]{:S(2)}, u32[]{:S(2)}) collective-permute-start(bf16[2,32,896]{2,1,0:T(8,128)(2,1)S(1)} %get-tuple-element.78), channel_id=1, source_target_pairs={{0,4},{1,5},{2,6},{3,7},{4,0},{5,1},{6,2},{7,3},{8,12},{9,13},{10,... | collective-permute-start | bytes 344072 | tf_op jit(solution)/shard_map/ppermute | solution.py:219
  58.1 9.7 %collective-permute-start.21 = (bf16[2,32,896]{2,1,0:T(8,128)(2,1)S(1)}, bf16[2,32,896]{2,1,0:T(8,128)(2,1)S(1)}, u32[]{:S(2)}, u32[]{:S(2)}) collective-permute-start(bf16[2,32,896]{2,1,0:T(8,128)(2,1)S(1)} %get-tuple-element.79), channel_id=1, source_target_pairs={{0,6},{1,7},{2,4},{3,5},{4,2},{5,3},{6,0},{7,1},{8,14},{9,15},{10,... | collective-permute-start | bytes 344072 | tf_op jit(solution)/shard_map/ppermute | solution.py:219
  69.1 7.1 %collective-permute-start.22 = (bf16[4,32,896]{2,1,0:T(8,128)(2,1)S(1)}, bf16[4,32,896]{2,1,0:T(8,128)(2,1)S(1)}, u32[]{:S(2)}, u32[]{:S(2)}) collective-permute-start(bf16[4,32,896]{2,1,0:T(8,128)(2,1)S(1)} %get-tuple-element.87), channel_id=1, source_target_pairs={{0,1},{1,0},{2,3},{3,2},{4,5},{5,4},{6,7},{7,6},{8,9},{9,8},{10,11... | collective-permute-start | bytes 688136 | tf_op jit(solution)/shard_map/ppermute | solution.py:219
  76.3 8.3 %collective-permute-start.23 = (bf16[2,32,896]{2,1,0:T(8,128)(2,1)S(1)}, bf16[2,32,896]{2,1,0:T(8,128)(2,1)S(1)}, u32[]{:S(2)}, u32[]{:S(2)}) collective-permute-start(bf16[2,32,896]{2,1,0:T(8,128)(2,1)S(1)} %get-tuple-element.91), channel_id=1, source_target_pairs={{0,2},{1,3},{2,0},{3,1},{4,6},{5,7},{6,4},{7,5},{8,10},{9,11},{10,... | collective-permute-start | bytes 344072 | tf_op jit(solution)/shard_map/ppermute | solution.py:219
  76.9 11.5 %collective-permute-start.24 = (bf16[2,32,896]{2,1,0:T(8,128)(2,1)S(1)}, bf16[2,32,896]{2,1,0:T(8,128)(2,1)S(1)}, u32[]{:S(2)}, u32[]{:S(2)}) collective-permute-start(bf16[2,32,896]{2,1,0:T(8,128)(2,1)S(1)} %get-tuple-element.92), channel_id=1, source_target_pairs={{0,4},{1,5},{2,6},{3,7},{4,0},{5,1},{6,2},{7,3},{8,12},{9,13},{10,... | collective-permute-start | bytes 344072 | tf_op jit(solution)/shard_map/ppermute | solution.py:219
  78.3 10.1 %collective-permute-start.25 = (bf16[2,32,896]{2,1,0:T(8,128)(2,1)S(1)}, bf16[2,32,896]{2,1,0:T(8,128)(2,1)S(1)}, u32[]{:S(2)}, u32[]{:S(2)}) collective-permute-start(bf16[2,32,896]{2,1,0:T(8,128)(2,1)S(1)} %get-tuple-element.93), channel_id=1, source_target_pairs={{0,6},{1,7},{2,4},{3,5},{4,2},{5,3},{6,0},{7,1},{8,14},{9,15},{10,... | collective-permute-start | bytes 344072 | tf_op jit(solution)/shard_map/ppermute | solution.py:219
  (8 other events, 62.6 us)

commit v7 on v6

v7 whole, which is shorter than its diff:
```python
import functools

import jax
import jax.numpy as jnp
from jax import lax
from jax.experimental import pallas as pl
from jax.experimental.pallas import tpu as pltpu
from jax.sharding import PartitionSpec as P

F32 = jnp.float32
BF16 = jnp.bfloat16
MIB = 1024 * 1024
ANY = pl.BlockSpec(memory_space=pl.ANY)
VMEM_LIMIT = 24 * MIB
ROUTE_LIMIT = 59 * MIB


def mm(left, right, dims):
    return lax.dot_general(left, right, (dims, ((), ())), preferred_element_type=F32)


def call(kernel, out_shape, flops=0, limit=VMEM_LIMIT, **kwargs):
    return pl.pallas_call(
        kernel,
        out_shape=out_shape,
        cost_estimate=pl.CostEstimate(flops=flops, bytes_accessed=flops // 256, transcendentals=0),
        compiler_params=pltpu.CompilerParams(vmem_limit_bytes=limit),
        **kwargs,
    )


def split_rows(refs, value):
    rows = value.shape[0] // len(refs)
    for k, ref in enumerate(refs):
        ref[...] = value[k * rows : (k + 1) * rows]


def join_rows(refs):
    return jnp.concatenate([ref[...] for ref in refs], axis=0)


def split_cores(keep_ref, swap_ref, value, *at):
    half, rows = keep_ref.shape[-3:-1]
    for k in range(half):
        keep_ref[(*at, k)] = value[2 * k * rows : (2 * k + 1) * rows]
        swap_ref[(*at, k)] = value[(2 * k + 1) * rows : (2 * k + 2) * rows]


def route_kernel(experts, *refs):
    pick_ref, weight_ref, keep_ref, swap_ref = refs[4:8]
    ids_ref, gates_ref, tokens_ref, grad_ref, sems = refs[8:]
    copies = [
        pltpu.make_async_copy(refs[k], refs[8 + k], sems.at[k]) for k in range(4)
    ]
    for copy in copies:
        copy.start()
    copies[0].wait()
    copies[1].wait()
    ids = ids_ref[...]
    tok_rows = ids.shape[1]
    slots = pick_ref.shape[0]
    inside = ids < experts
    routed = jnp.max(inside.astype(jnp.int32), axis=0, keepdims=True)
    chosen = jnp.sum(jnp.where(inside, ids, 0), axis=0, keepdims=True)
    weight = jnp.sum(jnp.where(inside, gates_ref[...], 0.0), axis=0, keepdims=True)
    key = jnp.where(routed > 0, chosen ^ lax.axis_index("expert"), experts)
    hot = lax.broadcasted_iota(jnp.int32, (experts, tok_rows), 0) == key
    earlier = lax.broadcasted_iota(jnp.int32, (tok_rows, tok_rows), 0) < lax.broadcasted_iota(
        jnp.int32, (tok_rows, tok_rows), 1
    )
    before = mm(hot.astype(F32).astype(BF16), earlier.astype(F32).astype(BF16), ((1,), (0,)))
    position = jnp.sum(jnp.where(hot, before, 0.0), axis=0, keepdims=True).astype(jnp.int32)
    slot = jnp.where(routed > 0, key * (slots // experts) + position, slots)
    pick = lax.broadcasted_iota(jnp.int32, (slots, tok_rows), 0) == slot
    slot_weight = jnp.sum(jnp.where(pick, weight, 0.0), axis=1, keepdims=True)
    weight_ref[...] = slot_weight
    pick = pick.astype(F32).astype(BF16)
    pick_ref[...] = pick
    copies[2].wait()
    rows = mm(pick, tokens_ref[...], ((1,), (0,))).astype(BF16)
    split_cores(keep_ref, swap_ref, rows, 0)
    copies[3].wait()
    rows = (slot_weight * mm(pick, grad_ref[...], ((1,), (0,)))).astype(BF16)
    split_cores(keep_ref, swap_ref, rows, 1)


def load_kernel(from_ref, to_ref):
    to_ref[...] = from_ref[...]


def pack_kernel(half, keep_ref, swap_ref, near_ref, *far_refs):
    for at in range(2):
        near_ref[at, 0] = keep_ref[at, 1]
        near_ref[at, 1] = swap_ref[at, 1]
        for k in range(2, half):
            far_refs[at * (half - 2) + k - 2][0] = keep_ref[at, k]
            far_refs[at * (half - 2) + k - 2][1] = swap_ref[at, k]


def pack_back_kernel(first, keep_ref, swap_ref, *refs):
    out_refs = refs[-(keep_ref.shape[0] - first) :]
    for k, out_ref in enumerate(out_refs):
        out_ref[0] = keep_ref[k + first]
        out_ref[1] = swap_ref[k + first]


def near_pieces(at, keep_ref, swap_ref, near_ref):
    return [keep_ref[at, 0], swap_ref[at, 0], near_ref[at, 0], near_ref[at, 1]]


def pair_pieces(refs):
    return [ref[k] for ref in refs for k in range(2)]


def part_rows(rows, dp, k):
    part = rows // dp
    mine = lax.axis_index("dp")
    return pl.ds(pl.multiple_of((mine ^ k) * part, part), part)


def local_order(found, scratch, dp):
    scratch[...] = jnp.concatenate(found, axis=0)
    rows = scratch.shape[0]
    return [scratch[part_rows(rows, dp, k), :] for k in range(dp)]


def natural_order(parts, scratch):
    for k, part in enumerate(parts):
        scratch[part_rows(scratch.shape[0], len(parts), k), :] = part
    return scratch[...]


def gate_up_kernel(dp, first, *refs):
    count = 1 if first else dp
    gate_ref, up_ref, local_ref, *out_refs, scratch = refs[-count - 4 :]
    refs = refs[: -count - 4]
    if first:
        found = near_pieces(0, *refs[:3]) + pair_pieces(refs[3:])
    else:
        found = pair_pieces(refs[1:])
    rows = jnp.concatenate(local_order(found, scratch, dp), axis=0)
    local_ref[...] = rows
    part = rows.shape[0] // dp
    for at, mat in enumerate((gate_ref, up_ref)):
        sums = mm(rows, mat[...], ((1,), (0,))).astype(BF16)
        for k in range(dp):
            if first:
                out_refs[0][lax.axis_index("dp") ^ k, at] = sums[k * part : (k + 1) * part]
            else:
                out_refs[k][at] = sums[k * part : (k + 1) * part]


def grad_act_kernel(dp, early, keep_ref, swap_ref, near_ref, *refs):
    down_ref, local_ref, *out_refs, early_scratch, late_scratch = refs[-dp - 4 :]
    far_refs = refs[: -dp - 4]
    found = near_pieces(1, keep_ref, swap_ref, near_ref) + pair_pieces(far_refs[:early])
    rows = local_order(found, early_scratch, dp)
    rows += local_order(pair_pieces(far_refs[early:]), late_scratch, dp)
    rows = jnp.concatenate(rows, axis=0)
    local_ref[...] = rows
    sums = mm(rows, down_ref[...], ((1,), (1,))).astype(BF16)
    part = sums.shape[0] // (2 * dp)
    for k, out_ref in enumerate(out_refs):
        out_ref[0] = sums[k * part : (k + 1) * part]
        out_ref[1] = sums[(dp + k) * part : (dp + k + 1) * part]


def group_sum(pieces):
    total = pieces[0].astype(F32)
    for piece in pieces[1:]:
        total = total + piece.astype(F32)
    return total


def received(refs, dp):
    if len(refs) == 1:
        return [refs[0].at[k] for k in range(dp)]
    return refs


def logistic(value):
    return 1.0 / (1.0 + jnp.exp(-value))


def act_kernel(dp, *refs):
    for at, sums in enumerate((refs[:1], refs[1 : dp + 1])):
        sums = received(sums, dp)
        gate = group_sum([ref[0] for ref in sums])
        up = group_sum([ref[1] for ref in sums])
        refs[-1][at] = (gate * logistic(gate) * up).astype(BF16)


def grad_pre_kernel(dp, at, count, *refs):
    sums = received(refs[:count], dp)
    out_ref = refs[-1]
    gate = group_sum([ref[0] for ref in sums])
    up = group_sum([ref[1] for ref in sums])
    grad = group_sum([ref[at] for ref in refs[count : count + dp]])
    soft = logistic(gate)
    gate_pre = (grad * up * (soft * (1.0 + gate * (1.0 - soft)))).astype(BF16)
    up_pre = (grad * (gate * soft)).astype(BF16)
    copies = [out_ref] if count > 1 else received([out_ref], dp)
    for copy in copies:
        copy[0] = gate_pre
        copy[1] = up_pre


def store_cores(keep_ref, swap_ref, value, first):
    rows = keep_ref.shape[1]
    for k in range(value.shape[0] // (2 * rows)):
        keep_ref[first + k] = value[2 * k * rows : (2 * k + 1) * rows]
        swap_ref[first + k] = value[(2 * k + 1) * rows : (2 * k + 2) * rows]


def expert_out_kernel(dp, *refs):
    down_ref = refs[dp]
    act_ref, keep_ref, swap_ref, early_scratch, late_scratch = refs[-5:]
    act = jnp.concatenate([ref[at] for at in range(2) for ref in refs[:dp]], axis=0)
    act_ref[...] = act
    rows = mm(act, down_ref[...], ((1,), (0,))).astype(BF16)
    part = rows.shape[0] // (2 * dp)
    parts = [rows[k * part : (k + 1) * part] for k in range(2 * dp)]
    store_cores(keep_ref, swap_ref, natural_order(parts[:dp], early_scratch), 0)
    half = keep_ref.shape[0] // 2
    store_cores(keep_ref, swap_ref, natural_order(parts[dp:], late_scratch), half)


def row_grad_kernel(dp, count, *refs):
    gate_ref, up_ref = refs[count : count + 2]
    gate_pre_ref, up_pre_ref, keep_ref, swap_ref, scratch = refs[-5:]
    if count > 1:
        pre = refs[:dp]
    else:
        pre = [refs[0].at[lax.axis_index("dp") ^ k] for k in range(dp)]
    gate_pre = jnp.concatenate([ref[0] for ref in pre], axis=0)
    up_pre = jnp.concatenate([ref[1] for ref in pre], axis=0)
    gate_pre_ref[...] = gate_pre
    up_pre_ref[...] = up_pre
    total = mm(gate_pre, gate_ref[...], ((1,), (1,))) + mm(up_pre, up_ref[...], ((1,), (1,)))
    rows = total.astype(BF16)
    part = rows.shape[0] // dp
    parts = [rows[k * part : (k + 1) * part] for k in range(dp)]
    store_cores(keep_ref, swap_ref, natural_order(parts, scratch), 0)


def grads_kernel(count, cuts, *refs):
    left_refs, refs = refs[:cuts], refs[cuts:]
    left = jnp.concatenate([ref[...] for ref in left_refs], axis=0).T
    right_refs, out_refs = refs[: -count], refs[-count:]
    each = len(right_refs) // count
    for k, out_ref in enumerate(out_refs):
        right = jnp.concatenate([ref[...] for ref in right_refs[k * each : (k + 1) * each]], axis=0)
        out_ref[...] = mm(left, right, ((1,), (0,))).astype(BF16)


def pairs_after(blocks, refs):
    return jnp.concatenate(blocks + pair_pieces(refs), axis=0)


def scatter_scaled_kernel(pick_ref, weight_ref, keep_ref, swap_ref, *refs):
    back = pairs_after([keep_ref[0], swap_ref[0]], refs[:-1])
    scaled = (weight_ref[...] * back.astype(F32)).astype(BF16)
    refs[-1][...] = mm(pick_ref[...], scaled, ((0,), (0,))).astype(BF16)


def scatter_kernel(pick_ref, keep_ref, swap_ref, *refs):
    back = pairs_after([keep_ref[0], swap_ref[0]], refs[:-1])
    refs[-1][...] = mm(pick_ref[...], back, ((0,), (0,))).astype(BF16)


def partner(value, axis, k):
    size = lax.axis_size(axis)
    return lax.ppermute(value, axis, [(i, i ^ k) for i in range(size)])


def exchange(value):
    return lax.all_to_all(value, "dp", split_axis=0, concat_axis=0, tiled=True)


def trade(values):
    far_first = reversed(range(1, len(values)))
    return [values[0]] + [partner(values[k], "dp", k) for k in far_first][::-1]


def body(tokens, grad_out, expert_ids, gates, w_gate, w_up, w_down):
    experts = lax.axis_size("expert")
    dp = lax.axis_size("dp")
    tok_rows, features = tokens.shape
    capacity = tok_rows // 16
    slots = experts * capacity
    hidden = w_gate.shape[2]
    chunk = slots // dp
    gate_mat, up_mat, down_mat = w_gate[0], w_up[0], w_down[0]
    shape = jax.ShapeDtypeStruct

    half = experts // 2
    early = half // 2 - 2
    part = slots // (2 * dp)
    product = 2 * slots * features * hidden
    sized = shape((slots, features), BF16)
    cut = shape((slots // 2, features), BF16)
    wide = shape((slots, hidden), BF16)
    cut_wide = shape((slots // 2, hidden), BF16)
    both = shape((2, half, capacity, features), BF16)
    one = shape((half, capacity, features), BF16)
    cut_one = shape((half // 2, capacity, features), BF16)
    near = shape((2, 2, capacity, features), BF16)
    pair = shape((2, capacity, features), BF16)
    far = [pair] * (half - 2)
    mine = shape((2, part, hidden), BF16)
    in_order = pltpu.VMEM((slots // 2, features), BF16)

    ins = (expert_ids.T, gates.T, tokens, grad_out)
    outs = (shape((slots, tok_rows), BF16), shape((slots, 1), F32), both, both)
    pick, weight, keep, swap = call(
        functools.partial(route_kernel, experts),
        outs,
        limit=ROUTE_LIMIT,
        in_specs=[ANY] * 4,
        scratch_shapes=[
            *[pltpu.VMEM(array.shape, array.dtype) for array in ins],
            pltpu.SemaphoreType.DMA((4,)),
        ],
    )(*ins)
    swap_to, up_mat = lax.optimization_barrier((swap, up_mat))
    swap = partner(swap_to, "expert", 1)
    up_mat = call(load_kernel, shape(up_mat.shape, BF16))(up_mat)
    swap, up_mat = lax.optimization_barrier((swap, up_mat))
    near_to, *far_to = call(functools.partial(pack_kernel, half), (near, *far, *far))(
        keep, swap
    )
    near_in = partner(near_to, "expert", 2)
    far_rows = [partner(far_to[k], "expert", 2 * (2 + k)) for k in range(half - 2)]
    far_grads = [partner(far_to[half - 2 + k], "expert", 2 * (2 + k)) for k in range(half - 2)]

    def gate_up(first, *found):
        return call(
            functools.partial(gate_up_kernel, dp, first),
            (cut, *([shape((dp, 2, part, hidden), BF16)] if first else [mine] * dp)),
            product,
            in_specs=[pl.BlockSpec() if first else ANY] + [pl.BlockSpec()] * (len(found) + 1),
            scratch_shapes=[in_order],
        )(*found, gate_mat, up_mat)

    rows_early, sums = gate_up(True, keep, swap, near_in, *far_rows[:early])
    sums_early = [exchange(sums)]
    rows_late, *sums = gate_up(False, rows_early, *far_rows[early:])
    sums_late = trade(sums)
    grads, *part_grad = call(
        functools.partial(grad_act_kernel, dp, early),
        (sized, *[shape((2, part, hidden), BF16)] * dp),
        product,
        scratch_shapes=[in_order, in_order],
    )(keep, swap, near_in, *far_grads, down_mat)
    grad_sums = trade(part_grad)
    act_mine = call(
        functools.partial(act_kernel, dp),
        shape((2, part, hidden), BF16),
        in_specs=[pl.BlockSpec()] * (dp + 1) + [ANY],
    )(*sums_early, *sums_late, grads)
    acts = trade([act_mine] * dp)
    act, out_keep, out_swap = call(
        functools.partial(expert_out_kernel, dp),
        (wide, one, one),
        product,
        in_specs=[pl.BlockSpec()] * (dp + 1) + [ANY] * (dp - 1),
        scratch_shapes=[in_order, in_order],
    )(*acts, down_mat, *grad_sums[1:])
    out_swap = partner(out_swap, "expert", 1)
    out_near_to, *out_far = call(functools.partial(pack_back_kernel, 1), [pair] * (half - 1))(
        out_keep, out_swap
    )
    out_far = [partner(value, "expert", 2 * (2 + k)) for k, value in enumerate(out_far)]

    def grad_pre(at, sums, *after):
        return call(
            functools.partial(grad_pre_kernel, dp, at, len(sums)),
            mine if at else shape((dp, 2, part, hidden), BF16),
            in_specs=[pl.BlockSpec()] * (len(sums) + dp) + [ANY] * len(after),
        )(*sums, *grad_sums, *after)

    def row_grad(pre, *after):
        return call(
            functools.partial(row_grad_kernel, dp, len(pre)),
            (cut_wide, cut_wide, cut_one, cut_one),
            product,
            in_specs=[pl.BlockSpec()] * (len(pre) + 2) + [ANY] * len(after),
            scratch_shapes=[in_order],
        )(*pre, gate_mat, up_mat, *after)

    pre_late = grad_pre(1, sums_late)
    pre_early = [exchange(grad_pre(0, sums_early, pre_late))]
    pre_late = trade([pre_late] * dp)
    gate_late, up_late, keep_late, swap_late = row_grad(pre_late, out_near_to)
    swap_late = partner(swap_late, "expert", 1)
    gate_early, up_early, keep_early, swap_early = row_grad(pre_early)
    late_to = call(
        functools.partial(pack_back_kernel, 0),
        [pair] * (half // 2),
        in_specs=[pl.BlockSpec()] * 2 + [ANY] * (len(out_far) + 1),
    )(keep_late, swap_late, *out_far, keep_early)
    late_back = [
        partner(value, "expert", 2 * (half // 2 + k)) for k, value in enumerate(late_to)
    ]
    swap_early = partner(swap_early, "expert", 1)
    out_near = partner(out_near_to, "expert", 2)
    early_to = call(functools.partial(pack_back_kernel, 1), [pair] * (half // 2 - 1))(
        keep_early, swap_early
    )
    early_back = [partner(value, "expert", 2 * (1 + k)) for k, value in enumerate(early_to)]

    (grad_down,) = call(
        functools.partial(grads_kernel, 1, 1), [shape((hidden, features), BF16)], product
    )(act, grads)
    grad_gate, grad_up = call(
        functools.partial(grads_kernel, 2, 2), [shape((features, hidden), BF16)] * 2, 2 * product
    )(rows_early, rows_late, gate_early, gate_late, up_early, up_late)

    full = shape((tok_rows, features), BF16)
    mixed = call(
        scatter_scaled_kernel, full
    )(pick, weight, out_keep, out_swap, out_near, *out_far)
    grad_tokens = call(
        scatter_kernel, full
    )(pick, keep_early, swap_early, *early_back, *late_back)
    return (mixed, grad_tokens, grad_gate[None], grad_up[None], grad_down[None])


def solution(mesh):
    placed = (
        P("expert", "dp"),
        P("expert", "dp"),
        P("expert", None),
        P("expert", None),
        P("expert", "dp", None),
        P("expert", "dp", None),
        P("expert", None, "dp"),
    )
    return jax.shard_map(
        body,
        mesh=mesh,
        in_specs=placed,
        out_specs=(
            P("expert", "dp"),
            P("expert", "dp"),
            P("expert", "dp", None),
            P("expert", "dp", None),
            P("expert", None, "dp"),
        ),
        check_vma=False,
    )
```

time: 89.9 us -> 110 us (1.22)
  local copies, waits for them, and re-layouts: 0.03 us -> 24.8 us
  waiting for transfers between devices: 41.3 us -> 18.9 us
  starting transfers between devices: 31.1 us -> 44.4 us
  Pallas kernels: 10.9 us -> 20.9 us
  matrix products: 5.77 us -> 0 us
    unnamed x12 -> x88, local copies, waits for them, and re-layouts: 0.03 us -> 24.8 us
    ppermute x26 -> x27, waiting for transfers between devices: 41.3 us -> 18.9 us  [partner(): return lax.ppermute(value, axis, [(i, i ^ k) for i in range(size)])]
    pallas_call x12 -> x18, Pallas kernels: 10.1 us -> 19.1 us  [the longest x2 3.22 us: row_grad(): call(functools.partial(row_grad_kernel, dp, len(pre)), (cut_wide, cut_wid...]
    all_to_all x0 -> x2, starting transfers between devices: none -> 7.69 us  [exchange(): return lax.all_to_all(value, 'dp', split_axis=0, concat_axis=0, tiled=True)]
    dot_general x3 -> x0, matrix products: 5.77 us -> none  [mm(): lax.dot_general(left, right, (dims, ((), ())), preferred_element_type=F32)]
    ppermute x26 -> x27, starting transfers between devices: 31.1 us -> 36.7 us  [partner(): return lax.ppermute(value, axis, [(i, i ^ k) for i in range(size)])]
  transfers between devices with their start and end apart: 26 -> 29, of which waited for: 15 -> 4; matrix products, arithmetic and copies ran while one was open for 6% -> 0% of each run, Pallas kernels for 4% -> 14%
where the time goes in v7:
time: 110 us
  starting transfers between devices  44.4 us (40%)
  local copies, waits for them, and re-layouts  24.8 us (23%)
  Pallas kernels  20.9 us (19%)
  waiting for transfers between devices  18.9 us (17%)
    ppermute x27, starting transfers between devices, partner(): return lax.ppermute(value, axis, [(i, i ^ k) for i in range(size)])  36.7 us
    unnamed x88, local copies, waits for them, and re-layouts  24.8 us
    ppermute x27, waiting for transfers between devices, partner(): return lax.ppermute(value, axis, [(i, i ^ k) for i in range(size)])  18.9 us
    all_to_all x2, starting transfers between devices, exchange(): return lax.all_to_all(value, 'dp', split_axis=0, concat_axis=0, tiled=True)  7.69 us
    pallas_call x2, Pallas kernels, row_grad(): call(functools.partial(row_grad_kernel, dp, len(pre)), (cut_wide, cut_wid...  3.22 us
    pallas_call x1, Pallas kernels, body(): call(functools.partial(route_kernel, experts), outs, limit=ROUTE_LIMIT, i...  3.06 us
    pallas_call x1, Pallas kernels, body(): call(functools.partial(grads_kernel, 2, 2), [shape((features, hidden), BF...  2.54 us
  transfers between devices with their start and end apart: 29, of which 4 were waited for; matrix products, arithmetic and copies ran while one was open for 0% of the time, Pallas kernels for 14%

profile of v7, /device:TPU:0, one launch (start us, length us, event | category | flops | bytes accessed | tf_op | source)
XLA Modules:
  0.0 109.9 jit_solution(12816872634777739370)
XLA Ops:
  0.6 3.1 %shard_map.110 = (bf16[256,512]{1,0:T(8,128)(2,1)}, f32[256,1]{1,0:T(8,128)}, bf16[2,4,32,896]{3,2,1,0:T(8,128)(2,1)}, bf16[2,4,32,896]{3,2,1,0:T(8,128)(2,1)}) custom-call(s32[8,512]{1,0:T(8,128)} %bitcast.16, f32[8,512]{1,0:T(8,128)} %bitcast.17, bf16[512,896]{1,0:T(8,128)(2,1)} %refs_2_.1, bf16[512,896]{1,0:T(8,128)(2,1)} %refs_3_.1), custom_call_target="tpu_custom_call" | custom-call | tf_op jit(solution)/shard_map/pallas_call | solution.py:315
  4.2 1.6 %copy-done.7 = bf16[1,896,1024]{2,1,0:T(8,128)(2,1)S(1)} copy-done((bf16[1,896,1024]{2,1,0:T(8,128)(2,1)S(1)}, bf16[1,896,1024]{2,1,0:T(8,128)(2,1)}, u32[]{:S(2)}) %copy-start.7) | copy-done | bytes 1835032
  8.7 2.8 %collective-permute-start.1 = (bf16[2,2,32,896]{3,2,1,0:T(8,128)(2,1)S(1)}, bf16[2,2,32,896]{3,2,1,0:T(8,128)(2,1)S(1)}, u32[]{:S(2)}, u32[]{:S(2)}) collective-permute-start(bf16[2,2,32,896]{3,2,1,0:T(8,128)(2,1)S(1)} %get-tuple-element.55), channel_id=1, source_target_pairs={{0,2},{1,3},{2,0},{3,1},{4,6},{5,7},{6,4},{7,5},{8,10},{9,11},{10,... | collective-permute-start | bytes 688136 | tf_op jit(solution)/shard_map/ppermute | solution.py:273
  11.5 5.9 %collective-permute-done.1.refs_2_.near_ref = bf16[2,2,32,896]{3,2,1,0:T(8,128)(2,1)S(1)} collective-permute-done((bf16[2,2,32,896]{3,2,1,0:T(8,128)(2,1)S(1)}, bf16[2,2,32,896]{3,2,1,0:T(8,128)(2,1)S(1)}, u32[]{:S(2)}, u32[]{:S(2)}) %collective-permute-start.1) | collective-permute-done | bytes 229408 | tf_op jit(solution)/shard_map/ppermute | solution.py:273
  19.6 3.9 %all-to-all-start = ((bf16[4,2,32,1024]{3,2,1,0:T(8,128)(2,1)}), bf16[4,2,32,1024]{3,2,1,0:T(8,128)(2,1)S(1)}, u32[]{:S(2)}, u32[]{:S(2)}) async-start(bf16[4,2,32,1024]{3,2,1,0:T(8,128)(2,1)} %copy-done.22), calls=%async_computation | async-start | bytes 1048576 | tf_op jit(solution)/shard_map/all_to_all | solution.py:277
  23.5 2.6 %collective-permute-start.2 = (bf16[2,32,896]{2,1,0:T(8,128)(2,1)}, bf16[2,32,896]{2,1,0:T(8,128)(2,1)S(1)}, u32[]{:S(2)}, u32[]{:S(2)}) collective-permute-start(bf16[2,32,896]{2,1,0:T(8,128)(2,1)} %copy-done.43), channel_id=1, source_target_pairs={{0,4},{1,5},{2,6},{3,7},{4,0},{5,1},{6,2},{7,3},{8,12},{9,13},{10,... | collective-permute-start | bytes 344072 | tf_op jit(solution)/shard_map/ppermute | solution.py:273
  27.4 1.7 %collective-permute-start.7 = (bf16[2,32,896]{2,1,0:T(8,128)(2,1)}, bf16[2,32,896]{2,1,0:T(8,128)(2,1)S(1)}, u32[]{:S(2)}, u32[]{:S(2)}) collective-permute-start(bf16[2,32,896]{2,1,0:T(8,128)(2,1)} %copy-done.41), channel_id=1, source_target_pairs={{0,4},{1,5},{2,6},{3,7},{4,0},{5,1},{6,2},{7,3},{8,12},{9,13},{10,... | collective-permute-start | bytes 344072 | tf_op jit(solution)/shard_map/ppermute | solution.py:273
  30.0 9.8 %collective-permute-done.2.refs_1_ = bf16[2,32,896]{2,1,0:T(8,128)(2,1)S(1)} collective-permute-done((bf16[2,32,896]{2,1,0:T(8,128)(2,1)}, bf16[2,32,896]{2,1,0:T(8,128)(2,1)S(1)}, u32[]{:S(2)}, u32[]{:S(2)}) %collective-permute-start.2) | collective-permute-done | bytes 114720 | tf_op jit(solution)/shard_map/ppermute | solution.py:273
  39.8 1.5 %copy-done.1 = bf16[1,896,1024]{2,1,0:T(8,128)(2,1)S(1)} copy-done((bf16[1,896,1024]{2,1,0:T(8,128)(2,1)S(1)}, bf16[1,896,1024]{2,1,0:T(8,128)(2,1)}, u32[]{:S(2)}) %copy-start.1) | copy-done | bytes 1835032
  43.6 1.6 %collective-permute-start.4 = (bf16[2,32,1024]{2,1,0:T(8,128)(2,1)S(1)}, bf16[2,32,1024]{2,1,0:T(8,128)(2,1)S(1)}, u32[]{:S(2)}, u32[]{:S(2)}) collective-permute-start(bf16[2,32,1024]{2,1,0:T(8,128)(2,1)S(1)} %get-tuple-element.62), channel_id=1, source_target_pairs={{0,8},{8,0},{16,24},{24,16},{1,9},{9,1},{17,25},{25,17},{2,10},{10... | collective-permute-start | bytes 393224 | tf_op jit(solution)/shard_map/ppermute | solution.py:273
  47.1 1.5 %shard_map.115 = (bf16[256,896]{1,0:T(8,128)(2,1)S(1)}, bf16[2,32,1024]{2,1,0:T(8,128)(2,1)S(1)}, bf16[2,32,1024]{2,1,0:T(8,128)(2,1)}, bf16[2,32,1024]{2,1,0:T(8,128)(2,1)}, bf16[2,32,1024]{2,1,0:T(8,128)(2,1)}) custom-call(bf16[2,4,32,896]{3,2,1,0:T(8,128)(2,1)S(1)} %copy-done.6, bf16[2,4,32,896]{3,2,1,0:T(8,128)(2,1)S(1)} %collective-permute-done.swap_ref.refs_1_, ...), custom_call_target="tpu_custom_call" | custom-call | flops 469762048 | bytes 1835008 | tf_op jit(solution)/shard_map/pallas_call | solution.py:349
  50.1 1.6 %collective-permute-start.12 = (bf16[2,32,1024]{2,1,0:T(8,128)(2,1)}, bf16[2,32,1024]{2,1,0:T(8,128)(2,1)S(1)}, u32[]{:S(2)}, u32[]{:S(2)}) collective-permute-start(bf16[2,32,1024]{2,1,0:T(8,128)(2,1)} %get-tuple-element.68), channel_id=1, source_target_pairs={{0,8},{8,0},{16,24},{24,16},{1,9},{9,1},{17,25},{25,17},{2,10},{10... | collective-permute-start | bytes 393224 | tf_op jit(solution)/shard_map/ppermute | solution.py:273
  60.4 1.7 %collective-permute-start.9 = (bf16[2,32,1024]{2,1,0:T(8,128)(2,1)S(1)}, bf16[2,32,1024]{2,1,0:T(8,128)(2,1)}, u32[]{:S(2)}, u32[]{:S(2)}) collective-permute-start(bf16[2,32,1024]{2,1,0:T(8,128)(2,1)S(1)} %shard_map.116.refs_0_), channel_id=1, source_target_pairs={{0,8},{8,0},{16,24},{24,16},{1,9},{9,1},{17,25},{25,17},{2,10},{10... | collective-permute-start | bytes 393224 | tf_op jit(solution)/shard_map/ppermute | solution.py:273
  67.8 3.8 %all-to-all-start.1 = ((bf16[4,2,32,1024]{3,2,1,0:T(8,128)(2,1)}), bf16[4,2,32,1024]{3,2,1,0:T(8,128)(2,1)S(1)}, u32[]{:S(2)}, u32[]{:S(2)}) async-start(bf16[4,2,32,1024]{3,2,1,0:T(8,128)(2,1)} %shard_map.121), calls=%async_computation.1 | async-start | bytes 1048576 | tf_op jit(solution)/shard_map/all_to_all | solution.py:277
  71.6 1.6 %copy-done.5 = bf16[1,1024,896]{2,1,0:T(8,128)(2,1)S(1)} copy-done((bf16[1,1024,896]{2,1,0:T(8,128)(2,1)S(1)}, bf16[1,1024,896]{2,1,0:T(8,128)(2,1)}, u32[]{:S(2)}) %copy-start.5) | copy-done | bytes 1835032
  73.2 1.8 %shard_map.117 = (bf16[256,1024]{1,0:T(8,128)(2,1)S(1)}, bf16[4,32,896]{2,1,0:T(8,128)(2,1)S(1)}, bf16[4,32,896]{2,1,0:T(8,128)(2,1)S(1)}) custom-call(bf16[2,32,1024]{2,1,0:T(8,128)(2,1)S(1)} %shard_map.116.refs_0_, bf16[2,32,1024]{2,1,0:T(8,128)(2,1)} %collective-permute-done.9.refs_1_, bf16[2,32,1024]{2,1,0:T(8,128)(2,1)} %collective-permute-done.10.refs_2_, ...), custom_call_target="tpu_custom_call" | custom-call | flops 469762048 | bytes 1835008 | tf_op jit(solution)/shard_map/pallas_call | solution.py:362
  75.1 2.1 %collective-permute-start.21 = (bf16[2,32,1024]{2,1,0:T(8,128)(2,1)S(1)}, bf16[2,32,1024]{2,1,0:T(8,128)(2,1)S(1)}, u32[]{:S(2)}, u32[]{:S(2)}) collective-permute-start(bf16[2,32,1024]{2,1,0:T(8,128)(2,1)S(1)} %shard_map.120.refs_5_.refs_0_), channel_id=1, source_target_pairs={{0,8},{8,0},{16,24},{24,16},{1,9},{9,1},{17,25},{25,17},{2,10},{10... | collective-permute-start | bytes 393224 | tf_op jit(solution)/shard_map/ppermute | solution.py:273
  78.8 4.0 %collective-permute-start.17 = (bf16[2,32,896]{2,1,0:T(8,128)(2,1)S(1)}, bf16[2,32,896]{2,1,0:T(8,128)(2,1)S(1)}, u32[]{:S(2)}, u32[]{:S(2)}) collective-permute-start(bf16[2,32,896]{2,1,0:T(8,128)(2,1)S(1)} %get-tuple-element.74), channel_id=1, source_target_pairs={{0,4},{1,5},{2,6},{3,7},{4,0},{5,1},{6,2},{7,3},{8,12},{9,13},{10,... | collective-permute-start | bytes 344072 | tf_op jit(solution)/shard_map/ppermute | solution.py:273
  85.6 1.9 %shard_map.124 = (bf16[128,1024]{1,0:T(8,128)(2,1)S(1)}, bf16[128,1024]{1,0:T(8,128)(2,1)S(1)}, bf16[2,32,896]{2,1,0:T(8,128)(2,1)S(1)}, bf16[2,32,896]{2,1,0:T(8,128)(2,1)}) custom-call(bf16[2,32,1024]{2,1,0:T(8,128)(2,1)S(1)} %shard_map.120.refs_5_.refs_0_, bf16[2,32,1024]{2,1,0:T(8,128)(2,1)S(1)} %collective-permute-done.21.refs_1_, ...), custom_call_target="tpu_custom_call" | custom-call | flops 469762048 | bytes 1835008 | tf_op jit(solution)/shard_map/pallas_call | solution.py:383
  92.9 3.0 %collective-permute-start.16 = (bf16[2,32,896]{2,1,0:T(8,128)(2,1)S(1)}, bf16[2,32,896]{2,1,0:T(8,128)(2,1)S(1)}, u32[]{:S(2)}, u32[]{:S(2)}) collective-permute-start(bf16[2,32,896]{2,1,0:T(8,128)(2,1)S(1)} %get-tuple-element.73.refs_6_), channel_id=1, source_target_pairs={{0,2},{1,3},{2,0},{3,1},{4,6},{5,7},{6,4},{7,5},{8,10},{9,11},{10,... | collective-permute-start | bytes 344072 | tf_op jit(solution)/shard_map/ppermute | solution.py:273
  98.0 1.5 %collective-permute-start.26 = (bf16[2,32,896]{2,1,0:T(8,128)(2,1)S(1)}, bf16[2,32,896]{2,1,0:T(8,128)(2,1)S(1)}, u32[]{:S(2)}, u32[]{:S(2)}) collective-permute-start(bf16[2,32,896]{2,1,0:T(8,128)(2,1)S(1)} %get-tuple-element.82), channel_id=1, source_target_pairs={{0,6},{1,7},{2,4},{3,5},{4,2},{5,3},{6,0},{7,1},{8,14},{9,15},{10,... | collective-permute-start | bytes 344072 | tf_op jit(solution)/shard_map/ppermute | solution.py:273
  100.7 2.0 %shard_map.128 = bf16[1024,896]{1,0:T(8,128)(2,1)} custom-call(bf16[256,1024]{1,0:T(8,128)(2,1)S(1)} %copy-done.24, bf16[256,896]{1,0:T(8,128)(2,1)S(1)} %copy-done.10), custom_call_target="tpu_custom_call" | custom-call | flops 469762048 | bytes 1835008 | tf_op jit(solution)/shard_map/pallas_call | solution.py:412
  102.7 2.5 %shard_map.127 = (bf16[896,1024]{1,0:T(8,128)(2,1)}, bf16[896,1024]{1,0:T(8,128)(2,1)}) custom-call(bf16[128,896]{1,0:T(8,128)(2,1)S(1)} %copy-done.30, bf16[128,896]{1,0:T(8,128)(2,1)S(1)} %copy-done.39, bf16[128,1024]{1,0:T(8,128)(2,1)S(1)} %get-tuple-element.84.refs_2_, bf16[128,1024]{1,0:T(8,128)(2,1)S(1)} %copy-done.35, ...), custom_call_target="tpu_custom_call" | custom-call | flops 939524096 | bytes 3670016 | tf_op jit(solution)/shard_map/pallas_call | solution.py:415
  106.7 1.8 %collective-permute-done.25.refs_1_ = bf16[2,32,896]{2,1,0:T(8,128)(2,1)S(1)} collective-permute-done((bf16[2,32,896]{2,1,0:T(8,128)(2,1)S(1)}, bf16[2,32,896]{2,1,0:T(8,128)(2,1)S(1)}, u32[]{:S(2)}, u32[]{:S(2)}) %collective-permute-start.25) | collective-permute-done | bytes 114720 | tf_op jit(solution)/shard_map/ppermute | solution.py:273
  (141 shorter events, 43.5 us)
Async XLA Ops:
  8.7 8.7 %collective-permute-start.1 = (bf16[2,2,32,896]{3,2,1,0:T(8,128)(2,1)S(1)}, bf16[2,2,32,896]{3,2,1,0:T(8,128)(2,1)S(1)}, u32[]{:S(2)}, u32[]{:S(2)}) collective-permute-start(bf16[2,2,32,896]{3,2,1,0:T(8,128)(2,1)S(1)} %get-tuple-element.55), channel_id=1, source_target_pairs={{0,2},{1,3},{2,0},{3,1},{4,6},{5,7},{6,4},{7,5},{8,10},{9,11},{10,... | collective-permute-start | bytes 688136 | tf_op jit(solution)/shard_map/ppermute | solution.py:273
  19.6 35.9 %all-to-all-start = ((bf16[4,2,32,1024]{3,2,1,0:T(8,128)(2,1)}), bf16[4,2,32,1024]{3,2,1,0:T(8,128)(2,1)S(1)}, u32[]{:S(2)}, u32[]{:S(2)}) async-start(bf16[4,2,32,1024]{3,2,1,0:T(8,128)(2,1)} %copy-done.22), calls=%async_computation | async-start | bytes 1048576 | tf_op jit(solution)/shard_map/all_to_all | solution.py:277
  23.5 16.3 %collective-permute-start.2 = (bf16[2,32,896]{2,1,0:T(8,128)(2,1)}, bf16[2,32,896]{2,1,0:T(8,128)(2,1)S(1)}, u32[]{:S(2)}, u32[]{:S(2)}) collective-permute-start(bf16[2,32,896]{2,1,0:T(8,128)(2,1)} %copy-done.43), channel_id=1, source_target_pairs={{0,4},{1,5},{2,6},{3,7},{4,0},{5,1},{6,2},{7,3},{8,12},{9,13},{10,... | collective-permute-start | bytes 344072 | tf_op jit(solution)/shard_map/ppermute | solution.py:273
  26.1 13.7 %collective-permute-start.3 = (bf16[2,32,896]{2,1,0:T(8,128)(2,1)}, bf16[2,32,896]{2,1,0:T(8,128)(2,1)S(1)}, u32[]{:S(2)}, u32[]{:S(2)}) collective-permute-start(bf16[2,32,896]{2,1,0:T(8,128)(2,1)} %copy-done.42), channel_id=1, source_target_pairs={{0,6},{1,7},{2,4},{3,5},{4,2},{5,3},{6,0},{7,1},{8,14},{9,15},{10,... | collective-permute-start | bytes 344072 | tf_op jit(solution)/shard_map/ppermute | solution.py:273
  27.4 19.7 %collective-permute-start.7 = (bf16[2,32,896]{2,1,0:T(8,128)(2,1)}, bf16[2,32,896]{2,1,0:T(8,128)(2,1)S(1)}, u32[]{:S(2)}, u32[]{:S(2)}) collective-permute-start(bf16[2,32,896]{2,1,0:T(8,128)(2,1)} %copy-done.41), channel_id=1, source_target_pairs={{0,4},{1,5},{2,6},{3,7},{4,0},{5,1},{6,2},{7,3},{8,12},{9,13},{10,... | collective-permute-start | bytes 344072 | tf_op jit(solution)/shard_map/ppermute | solution.py:273
  29.1 18.0 %collective-permute-start.8 = (bf16[2,32,896]{2,1,0:T(8,128)(2,1)}, bf16[2,32,896]{2,1,0:T(8,128)(2,1)S(1)}, u32[]{:S(2)}, u32[]{:S(2)}) collective-permute-start(bf16[2,32,896]{2,1,0:T(8,128)(2,1)} %copy-done.40), channel_id=1, source_target_pairs={{0,6},{1,7},{2,4},{3,5},{4,2},{5,3},{6,0},{7,1},{8,14},{9,15},{10,... | collective-permute-start | bytes 344072 | tf_op jit(solution)/shard_map/ppermute | solution.py:273
  43.6 9.5 %collective-permute-start.4 = (bf16[2,32,1024]{2,1,0:T(8,128)(2,1)S(1)}, bf16[2,32,1024]{2,1,0:T(8,128)(2,1)S(1)}, u32[]{:S(2)}, u32[]{:S(2)}) collective-permute-start(bf16[2,32,1024]{2,1,0:T(8,128)(2,1)S(1)} %get-tuple-element.62), channel_id=1, source_target_pairs={{0,8},{8,0},{16,24},{24,16},{1,9},{9,1},{17,25},{25,17},{2,10},{10... | collective-permute-start | bytes 393224 | tf_op jit(solution)/shard_map/ppermute | solution.py:273
  45.3 8.9 %collective-permute-start.5 = (bf16[2,32,1024]{2,1,0:T(8,128)(2,1)S(1)}, bf16[2,32,1024]{2,1,0:T(8,128)(2,1)S(1)}, u32[]{:S(2)}, u32[]{:S(2)}) collective-permute-start(bf16[2,32,1024]{2,1,0:T(8,128)(2,1)S(1)} %get-tuple-element.63), channel_id=1, source_target_pairs={{0,16},{8,24},{16,0},{24,8},{1,17},{9,25},{17,1},{25,9},{2,18},{10... | collective-permute-start | bytes 393224 | tf_op jit(solution)/shard_map/ppermute | solution.py:273
  46.8 8.1 %collective-permute-start.6 = (bf16[2,32,1024]{2,1,0:T(8,128)(2,1)S(1)}, bf16[2,32,1024]{2,1,0:T(8,128)(2,1)S(1)}, u32[]{:S(2)}, u32[]{:S(2)}) collective-permute-start(bf16[2,32,1024]{2,1,0:T(8,128)(2,1)S(1)} %get-tuple-element.64), channel_id=1, source_target_pairs={{0,24},{8,16},{16,8},{24,0},{1,25},{9,17},{17,9},{25,1},{2,26},{10... | collective-permute-start | bytes 393224 | tf_op jit(solution)/shard_map/ppermute | solution.py:273
  50.1 13.5 %collective-permute-start.12 = (bf16[2,32,1024]{2,1,0:T(8,128)(2,1)}, bf16[2,32,1024]{2,1,0:T(8,128)(2,1)S(1)}, u32[]{:S(2)}, u32[]{:S(2)}) collective-permute-start(bf16[2,32,1024]{2,1,0:T(8,128)(2,1)} %get-tuple-element.68), channel_id=1, source_target_pairs={{0,8},{8,0},{16,24},{24,16},{1,9},{9,1},{17,25},{25,17},{2,10},{10... | collective-permute-start | bytes 393224 | tf_op jit(solution)/shard_map/ppermute | solution.py:273
  51.7 12.2 %collective-permute-start.13 = (bf16[2,32,1024]{2,1,0:T(8,128)(2,1)}, bf16[2,32,1024]{2,1,0:T(8,128)(2,1)S(1)}, u32[]{:S(2)}, u32[]{:S(2)}) collective-permute-start(bf16[2,32,1024]{2,1,0:T(8,128)(2,1)} %get-tuple-element.69), channel_id=1, source_target_pairs={{0,16},{8,24},{16,0},{24,8},{1,17},{9,25},{17,1},{25,9},{2,18},{10... | collective-permute-start | bytes 393224 | tf_op jit(solution)/shard_map/ppermute | solution.py:273
  53.8 10.1 %collective-permute-start.14 = (bf16[2,32,1024]{2,1,0:T(8,128)(2,1)}, bf16[2,32,1024]{2,1,0:T(8,128)(2,1)S(1)}, u32[]{:S(2)}, u32[]{:S(2)}) collective-permute-start(bf16[2,32,1024]{2,1,0:T(8,128)(2,1)} %get-tuple-element.70), channel_id=1, source_target_pairs={{0,24},{8,16},{16,8},{24,0},{1,25},{9,17},{17,9},{25,1},{2,26},{10... | collective-permute-start | bytes 393224 | tf_op jit(solution)/shard_map/ppermute | solution.py:273
  60.4 11.2 %collective-permute-start.9 = (bf16[2,32,1024]{2,1,0:T(8,128)(2,1)S(1)}, bf16[2,32,1024]{2,1,0:T(8,128)(2,1)}, u32[]{:S(2)}, u32[]{:S(2)}) collective-permute-start(bf16[2,32,1024]{2,1,0:T(8,128)(2,1)S(1)} %shard_map.116.refs_0_), channel_id=1, source_target_pairs={{0,8},{8,0},{16,24},{24,16},{1,9},{9,1},{17,25},{25,17},{2,10},{10... | collective-permute-start | bytes 393224 | tf_op jit(solution)/shard_map/ppermute | solution.py:273
  62.1 9.5 %collective-permute-start.10 = (bf16[2,32,1024]{2,1,0:T(8,128)(2,1)S(1)}, bf16[2,32,1024]{2,1,0:T(8,128)(2,1)}, u32[]{:S(2)}, u32[]{:S(2)}) collective-permute-start(bf16[2,32,1024]{2,1,0:T(8,128)(2,1)S(1)} %shard_map.116.refs_0_), channel_id=1, source_target_pairs={{0,16},{8,24},{16,0},{24,8},{1,17},{9,25},{17,1},{25,9},{2,18},{10... | collective-permute-start | bytes 393224 | tf_op jit(solution)/shard_map/ppermute | solution.py:273
  63.6 8.0 %collective-permute-start.11 = (bf16[2,32,1024]{2,1,0:T(8,128)(2,1)S(1)}, bf16[2,32,1024]{2,1,0:T(8,128)(2,1)}, u32[]{:S(2)}, u32[]{:S(2)}) collective-permute-start(bf16[2,32,1024]{2,1,0:T(8,128)(2,1)S(1)} %shard_map.116.refs_0_), channel_id=1, source_target_pairs={{0,24},{8,16},{16,8},{24,0},{1,25},{9,17},{17,9},{25,1},{2,26},{10... | collective-permute-start | bytes 393224 | tf_op jit(solution)/shard_map/ppermute | solution.py:273
  67.8 21.8 %all-to-all-start.1 = ((bf16[4,2,32,1024]{3,2,1,0:T(8,128)(2,1)}), bf16[4,2,32,1024]{3,2,1,0:T(8,128)(2,1)S(1)}, u32[]{:S(2)}, u32[]{:S(2)}) async-start(bf16[4,2,32,1024]{3,2,1,0:T(8,128)(2,1)} %shard_map.121), calls=%async_computation.1 | async-start | bytes 1048576 | tf_op jit(solution)/shard_map/all_to_all | solution.py:277
  75.1 9.1 %collective-permute-start.21 = (bf16[2,32,1024]{2,1,0:T(8,128)(2,1)S(1)}, bf16[2,32,1024]{2,1,0:T(8,128)(2,1)S(1)}, u32[]{:S(2)}, u32[]{:S(2)}) collective-permute-start(bf16[2,32,1024]{2,1,0:T(8,128)(2,1)S(1)} %shard_map.120.refs_5_.refs_0_), channel_id=1, source_target_pairs={{0,8},{8,0},{16,24},{24,16},{1,9},{9,1},{17,25},{25,17},{2,10},{10... | collective-permute-start | bytes 393224 | tf_op jit(solution)/shard_map/ppermute | solution.py:273
  77.2 8.4 %collective-permute-start.22 = (bf16[2,32,1024]{2,1,0:T(8,128)(2,1)S(1)}, bf16[2,32,1024]{2,1,0:T(8,128)(2,1)S(1)}, u32[]{:S(2)}, u32[]{:S(2)}) collective-permute-start(bf16[2,32,1024]{2,1,0:T(8,128)(2,1)S(1)} %shard_map.120.refs_5_.refs_0_), channel_id=1, source_target_pairs={{0,16},{8,24},{16,0},{24,8},{1,17},{9,25},{17,1},{25,9},{2,18},{10... | collective-permute-start | bytes 393224 | tf_op jit(solution)/shard_map/ppermute | solution.py:273
  78.8 17.2 %collective-permute-start.17 = (bf16[2,32,896]{2,1,0:T(8,128)(2,1)S(1)}, bf16[2,32,896]{2,1,0:T(8,128)(2,1)S(1)}, u32[]{:S(2)}, u32[]{:S(2)}) collective-permute-start(bf16[2,32,896]{2,1,0:T(8,128)(2,1)S(1)} %get-tuple-element.74), channel_id=1, source_target_pairs={{0,4},{1,5},{2,6},{3,7},{4,0},{5,1},{6,2},{7,3},{8,12},{9,13},{10,... | collective-permute-start | bytes 344072 | tf_op jit(solution)/shard_map/ppermute | solution.py:273
  82.8 13.1 %collective-permute-start.18 = (bf16[2,32,896]{2,1,0:T(8,128)(2,1)S(1)}, bf16[2,32,896]{2,1,0:T(8,128)(2,1)S(1)}, u32[]{:S(2)}, u32[]{:S(2)}) collective-permute-start(bf16[2,32,896]{2,1,0:T(8,128)(2,1)S(1)} %get-tuple-element.75), channel_id=1, source_target_pairs={{0,6},{1,7},{2,4},{3,5},{4,2},{5,3},{6,0},{7,1},{8,14},{9,15},{10,... | collective-permute-start | bytes 344072 | tf_op jit(solution)/shard_map/ppermute | solution.py:273
  92.9 12.3 %collective-permute-start.16 = (bf16[2,32,896]{2,1,0:T(8,128)(2,1)S(1)}, bf16[2,32,896]{2,1,0:T(8,128)(2,1)S(1)}, u32[]{:S(2)}, u32[]{:S(2)}) collective-permute-start(bf16[2,32,896]{2,1,0:T(8,128)(2,1)S(1)} %get-tuple-element.73.refs_6_), channel_id=1, source_target_pairs={{0,2},{1,3},{2,0},{3,1},{4,6},{5,7},{6,4},{7,5},{8,10},{9,11},{10,... | collective-permute-start | bytes 344072 | tf_op jit(solution)/shard_map/ppermute | solution.py:273
  97.0 11.5 %collective-permute-start.25 = (bf16[2,32,896]{2,1,0:T(8,128)(2,1)S(1)}, bf16[2,32,896]{2,1,0:T(8,128)(2,1)S(1)}, u32[]{:S(2)}, u32[]{:S(2)}) collective-permute-start(bf16[2,32,896]{2,1,0:T(8,128)(2,1)S(1)} %get-tuple-element.81), channel_id=1, source_target_pairs={{0,4},{1,5},{2,6},{3,7},{4,0},{5,1},{6,2},{7,3},{8,12},{9,13},{10,... | collective-permute-start | bytes 344072 | tf_op jit(solution)/shard_map/ppermute | solution.py:273
  98.0 10.5 %collective-permute-start.26 = (bf16[2,32,896]{2,1,0:T(8,128)(2,1)S(1)}, bf16[2,32,896]{2,1,0:T(8,128)(2,1)S(1)}, u32[]{:S(2)}, u32[]{:S(2)}) collective-permute-start(bf16[2,32,896]{2,1,0:T(8,128)(2,1)S(1)} %get-tuple-element.82), channel_id=1, source_target_pairs={{0,6},{1,7},{2,4},{3,5},{4,2},{5,3},{6,0},{7,1},{8,14},{9,15},{10,... | collective-permute-start | bytes 344072 | tf_op jit(solution)/shard_map/ppermute | solution.py:273
  99.6 8.9 %collective-permute-start.20 = (bf16[2,32,896]{2,1,0:T(8,128)(2,1)S(1)}, bf16[2,32,896]{2,1,0:T(8,128)(2,1)S(1)}, u32[]{:S(2)}, u32[]{:S(2)}) collective-permute-start(bf16[2,32,896]{2,1,0:T(8,128)(2,1)S(1)} %shard_map.123), channel_id=1, source_target_pairs={{0,2},{1,3},{2,0},{3,1},{4,6},{5,7},{6,4},{7,5},{8,10},{9,11},{10,... | collective-permute-start | bytes 344072 | tf_op jit(solution)/shard_map/ppermute | solution.py:273
  (49 other events, 171.7 us)

commit v8 on v6

--- a/solution.py
+++ b/solution.py
@@ -10,6 +10,8 @@
 F32 = jnp.float32
 BF16 = jnp.bfloat16
 MIB = 1024 * 1024
+ANY = pl.BlockSpec(memory_space=pl.ANY)
+HERE = pl.BlockSpec()
 VMEM_LIMIT = 24 * MIB
 ROUTE_LIMIT = 59 * MIB
 
@@ -102,10 +104,10 @@
         out_ref[1] = swap_ref[k + 1]
 
 
-def pieces(at, keep_ref, swap_ref, near_ref, far_refs):
-    found = [keep_ref[at + (0,)], swap_ref[at + (0,)]]
-    found += [near_ref[at + (0,)], near_ref[at + (1,)]]
-    for ref in far_refs:
+def pieces(at, keep_ref, swap_ref, *refs):
+    far_refs, near_ref = refs[:-1], refs[-1]
+    found = [keep_ref[at, 0], swap_ref[at, 0], near_ref[at, 0], near_ref[at, 1]]
+    for ref in far_refs[::-1]:
         found += [ref[0], ref[1]]
     return found
 
@@ -122,11 +124,10 @@
     return jnp.concatenate([scratch[chunk_rows(rows, dp, k), :] for k in range(dp)], axis=0)
 
 
-def gate_up_kernel(half, keep_ref, swap_ref, near_ref, *refs):
-    far_refs, refs = refs[: half - 2], refs[half - 2 :]
-    gate_ref, up_ref, local_ref, *out_refs, scratch = refs
+def gate_up_kernel(half, *refs):
+    gate_ref, up_ref, local_ref, *out_refs, scratch = refs[half + 1 :]
     dp = len(out_refs)
-    rows = local_order(pieces((0,), keep_ref, swap_ref, near_ref, far_refs), scratch, dp)
+    rows = local_order(pieces(0, *refs[: half + 1]), scratch, dp)
     local_ref[...] = rows
     chunk = rows.shape[0] // dp
     for at, mat in enumerate((gate_ref, up_ref)):
@@ -135,11 +136,10 @@
             out_ref[at] = part[k * chunk : (k + 1) * chunk]
 
 
-def grad_act_kernel(half, keep_ref, swap_ref, near_ref, *refs):
-    far_refs, refs = refs[: half - 2], refs[half - 2 :]
-    down_ref, local_ref, *out_refs, scratch = refs
+def grad_act_kernel(half, *refs):
+    down_ref, local_ref, *out_refs, scratch = refs[half + 1 :]
     dp = len(out_refs)
-    rows = local_order(pieces((1,), keep_ref, swap_ref, near_ref, far_refs), scratch, dp)
+    rows = local_order(pieces(1, *refs[: half + 1]), scratch, dp)
     local_ref[...] = rows
     split_rows(out_refs, mm(rows, down_ref[...], ((1,), (1,))).astype(BF16))
 
@@ -198,20 +198,26 @@
 
 def returned(keep_ref, swap_ref, refs):
     found = [keep_ref[0], swap_ref[0]]
-    for ref in refs:
+    for ref in refs[::-1]:
         found += [ref[0], ref[1]]
     return jnp.concatenate(found, axis=0)
 
 
-def scatter_scaled_kernel(pick_ref, weight_ref, keep_ref, swap_ref, *refs):
-    back = returned(keep_ref, swap_ref, refs[:-1]).astype(F32)
+def scatter_scaled_kernel(half, pick_ref, weight_ref, *refs):
+    back = returned(*refs[:2], refs[2 : half + 1]).astype(F32)
     scaled = (weight_ref[...] * back).astype(BF16)
     refs[-1][...] = mm(pick_ref[...], scaled, ((0,), (0,))).astype(BF16)
 
 
-def scatter_kernel(pick_ref, keep_ref, swap_ref, *refs):
-    back = returned(keep_ref, swap_ref, refs[:-1])
+def scatter_kernel(half, pick_ref, *refs):
+    back = returned(*refs[:2], refs[2 : half + 1])
     refs[-1][...] = mm(pick_ref[...], back, ((0,), (0,))).astype(BF16)
+
+
+def grads_kernel(count, left_ref, *refs):
+    left = left_ref[...].T
+    for right_ref, out_ref in zip(refs[:count], refs[-count:]):
+        out_ref[...] = mm(left, right_ref[...], ((1,), (0,))).astype(BF16)
 
 
 def partner(value, axis, k):
@@ -254,7 +260,7 @@
         4 * slots * tok_rows * features,
         8 * tok_rows * features,
         limit=ROUTE_LIMIT,
-        in_specs=[pl.BlockSpec(memory_space=pl.ANY)] * 4,
+        in_specs=[ANY] * 4,
         scratch_shapes=[
             *[pltpu.VMEM(array.shape, array.dtype) for array in ins],
             pltpu.SemaphoreType.DMA((4,)),
@@ -276,8 +282,8 @@
         2 * product,
         2 * weights,
         scratch_shapes=in_order,
-    )(keep, swap, near_in, *far_rows, gate_mat, up_mat)
-    sums = trade(part_pre)[::-1]
+    )(keep, swap, *far_rows[::-1], near_in, gate_mat, up_mat)
+    sums = trade(part_pre)
     act_mine = call(
         functools.partial(act_kernel, dp),
         shape((chunk, hidden), BF16),
@@ -292,8 +298,8 @@
         product,
         weights,
         scratch_shapes=in_order,
-    )(keep, swap, near_in, *far_grads, down_mat)
-    grad_sums = trade(part_grad)[::-1]
+    )(keep, swap, *far_grads[::-1], near_in, down_mat)
+    grad_sums = trade(part_grad)
     pre_mine = call(
         functools.partial(grad_pre_kernel, dp),
         shape((2, chunk, hidden), BF16),
@@ -322,23 +328,37 @@
     )(*pre, gate_mat, up_mat)
     grad_swap = partner(grad_swap, "expert", 1)
     out_near = partner(out_near, "expert", 2)
-    grad_swap, gate_pre, up_pre = lax.optimization_barrier((grad_swap, gate_pre, up_pre))
-    grad_back = call(pack_back_kernel, back, 0, 8 * slots)(grad_keep, grad_swap)
-    grad_back = [
-        partner(grad_back[k], "expert", 2 * (1 + k)) for k in reversed(range(half - 1))
-    ][::-1]
-
-    grad_down = mm(act, grads, ((0,), (0,))).astype(BF16)
-    grad_gate = mm(rows, gate_pre, ((0,), (0,))).astype(BF16)
-    grad_up = mm(rows, up_pre, ((0,), (0,))).astype(BF16)
+    grad_to = call(pack_back_kernel, back, 0, 8 * slots)(grad_keep, grad_swap)
+    grad_back = [partner(value, "expert", 2 * (1 + k)) for k, value in enumerate(grad_to)]
+
+    (grad_down,) = call(
+        functools.partial(grads_kernel, 1),
+        [shape((hidden, features), BF16)],
+        product,
+        weights,
+    )(act, grads)
+    grad_gate, grad_up = call(
+        functools.partial(grads_kernel, 2),
+        [shape((features, hidden), BF16)] * 2,
+        2 * product,
+        2 * weights,
+        in_specs=[HERE] * 3 + [ANY],
+    )(rows, gate_pre, up_pre, grad_to[0])
 
     full = shape((tok_rows, features), BF16)
     mixed = call(
-        scatter_scaled_kernel, full, 2 * slots * tok_rows * features, 4 * tok_rows * features
-    )(pick, weight, out_keep, out_swap, out_near, *out_far)
+        functools.partial(scatter_scaled_kernel, half),
+        full,
+        2 * slots * tok_rows * features,
+        4 * tok_rows * features,
+        in_specs=[HERE] * (half + 3) + [ANY],
+    )(pick, weight, out_keep, out_swap, *out_far[::-1], out_near, grad_to[0])
     grad_tokens = call(
-        scatter_kernel, full, 2 * slots * tok_rows * features, 4 * tok_rows * features
-    )(pick, grad_keep, grad_swap, *grad_back)
+        functools.partial(scatter_kernel, half),
+        full,
+        2 * slots * tok_rows * features,
+        4 * tok_rows * features,
+    )(pick, grad_keep, grad_swap, *grad_back[::-1])
     return (mixed, grad_tokens, grad_gate[None], grad_up[None], grad_down[None])
 
 

time: 89.9 us -> 82 us (0.912)
  waiting for transfers between devices: 41.3 us -> 31 us
  matrix products: 5.77 us -> 0 us
  Pallas kernels: 10.9 us -> 15.4 us
  starting transfers between devices: 31.1 us -> 34.7 us
    ppermute x26, waiting for transfers between devices: 41.3 us -> 31 us  [partner(): return lax.ppermute(value, axis, [(i, i ^ k) for i in range(size)])]
    dot_general x3 -> x0, matrix products: 5.77 us -> none  [mm(): lax.dot_general(left, right, (dims, ((), ())), preferred_element_type=F32)]
    pallas_call x3 -> x5, Pallas kernels: 2.88 us -> 7.4 us  [the longest x1 2.54 us: body(): call(functools.partial(grads_kernel, 2), [shape((features, hidden), BF16)...]
    ppermute x26, starting transfers between devices: 31.1 us -> 34.7 us  [partner(): return lax.ppermute(value, axis, [(i, i ^ k) for i in range(size)])]
  transfers between devices with their start and end apart: 26 -> 26, of which waited for: 15 -> 13; matrix products, arithmetic and copies ran while one was open for 6% -> 0% of each run, Pallas kernels for 4% -> 10%
where the time goes in v8:
time: 82 us; the launch traced here: 81.9 us
  starting transfers between devices  34.7 us (42%)
  waiting for transfers between devices  31 us (38%)
  Pallas kernels  15.4 us (19%)
    ppermute x26, starting transfers between devices, partner(): return lax.ppermute(value, axis, [(i, i ^ k) for i in range(size)])  34.7 us
    ppermute x26, waiting for transfers between devices, partner(): return lax.ppermute(value, axis, [(i, i ^ k) for i in range(size)])  31 us
    pallas_call x1, Pallas kernels, body(): call(functools.partial(route_kernel, experts), outs, 4 * slots * tok_rows...  3.2 us
    pallas_call x1, Pallas kernels, body(): call(functools.partial(grads_kernel, 2), [shape((features, hidden), BF16)...  2.54 us
    pallas_call x1, Pallas kernels, body(): call(functools.partial(grads_kernel, 1), [shape((hidden, features), BF16)...  1.97 us
  transfers between devices with their start and end apart: 26, of which 13 were waited for; matrix products, arithmetic and copies ran while one was open for 0% of the time, Pallas kernels for 10%

profile of v8, /device:TPU:0, one launch (start us, length us, event | category | flops | bytes accessed | tf_op | source)
XLA Modules:
  0.0 81.9 jit_solution(557930454998445252)
XLA Ops:
  0.6 3.2 %shard_map.110 = (bf16[256,512]{1,0:T(8,128)(2,1)}, f32[256,1]{1,0:T(8,128)}, bf16[2,4,32,896]{3,2,1,0:T(8,128)(2,1)}, bf16[2,4,32,896]{3,2,1,0:T(8,128)(2,1)}) custom-call(s32[8,512]{1,0:T(8,128)} %bitcast.14, f32[8,512]{1,0:T(8,128)} %bitcast.15, bf16[512,896]{1,0:T(8,128)(2,1)} %refs_2_.1, bf16[512,896]{1,0:T(8,128)(2,1)} %refs_3_.1), custom_call_target="tpu_custom_call" | custom-call | flops 469762048 | bytes 3670016 | tf_op jit(solution)/shard_map/pallas_call | solution.py:257
  4.5 1.5 %collective-permute-done.swap_ref.refs_1_ = bf16[2,4,32,896]{3,2,1,0:T(8,128)(2,1)S(1)} collective-permute-done((bf16[2,4,32,896]{3,2,1,0:T(8,128)(2,1)}, bf16[2,4,32,896]{3,2,1,0:T(8,128)(2,1)S(1)}, u32[]{:S(2)}, u32[]{:S(2)}) %collective-permute-start) | collective-permute-done | bytes 458784 | tf_op jit(solution)/shard_map/ppermute | solution.py:225
  6.1 3.0 %collective-permute-start.3 = (bf16[2,2,32,896]{3,2,1,0:T(8,128)(2,1)S(1)}, bf16[2,2,32,896]{3,2,1,0:T(8,128)(2,1)S(1)}, u32[]{:S(2)}, u32[]{:S(2)}) collective-permute-start(bf16[2,2,32,896]{3,2,1,0:T(8,128)(2,1)S(1)} %get-tuple-element.60), channel_id=1, source_target_pairs={{0,2},{1,3},{2,0},{3,1},{4,6},{5,7},{6,4},{7,5},{8,10},{9,11},{10,... | collective-permute-start | bytes 688136 | tf_op jit(solution)/shard_map/ppermute | solution.py:225
  9.1 2.5 %collective-permute-start.1 = (bf16[2,32,896]{2,1,0:T(8,128)(2,1)S(1)}, bf16[2,32,896]{2,1,0:T(8,128)(2,1)S(1)}, u32[]{:S(2)}, u32[]{:S(2)}) collective-permute-start(bf16[2,32,896]{2,1,0:T(8,128)(2,1)S(1)} %get-tuple-element.58), channel_id=1, source_target_pairs={{0,6},{1,7},{2,4},{3,5},{4,2},{5,3},{6,0},{7,1},{8,14},{9,15},{10,... | collective-permute-start | bytes 344072 | tf_op jit(solution)/shard_map/ppermute | solution.py:225
  11.7 8.9 %collective-permute-done.1.refs_2_ = bf16[2,32,896]{2,1,0:T(8,128)(2,1)S(1)} collective-permute-done((bf16[2,32,896]{2,1,0:T(8,128)(2,1)S(1)}, bf16[2,32,896]{2,1,0:T(8,128)(2,1)S(1)}, u32[]{:S(2)}, u32[]{:S(2)}) %collective-permute-start.1) | collective-permute-done | bytes 114720 | tf_op jit(solution)/shard_map/ppermute | solution.py:225
  20.6 1.7 %collective-permute-done.2.refs_3_ = bf16[2,32,896]{2,1,0:T(8,128)(2,1)S(1)} collective-permute-done((bf16[2,32,896]{2,1,0:T(8,128)(2,1)S(1)}, bf16[2,32,896]{2,1,0:T(8,128)(2,1)S(1)}, u32[]{:S(2)}, u32[]{:S(2)}) %collective-permute-start.2) | collective-permute-done | bytes 114720 | tf_op jit(solution)/shard_map/ppermute | solution.py:225
  23.6 1.6 %collective-permute-start.4 = (bf16[2,64,1024]{2,1,0:T(8,128)(2,1)S(1)}, bf16[2,64,1024]{2,1,0:T(8,128)(2,1)S(1)}, u32[]{:S(2)}, u32[]{:S(2)}) collective-permute-start(bf16[2,64,1024]{2,1,0:T(8,128)(2,1)S(1)} %get-tuple-element.63), channel_id=1, source_target_pairs={{0,8},{8,0},{16,24},{24,16},{1,9},{9,1},{17,25},{25,17},{2,10},{10... | collective-permute-start | bytes 786440 | tf_op jit(solution)/shard_map/ppermute | solution.py:225
  25.1 1.5 %collective-permute-start.5 = (bf16[2,64,1024]{2,1,0:T(8,128)(2,1)S(1)}, bf16[2,64,1024]{2,1,0:T(8,128)(2,1)S(1)}, u32[]{:S(2)}, u32[]{:S(2)}) collective-permute-start(bf16[2,64,1024]{2,1,0:T(8,128)(2,1)S(1)} %get-tuple-element.64), channel_id=1, source_target_pairs={{0,16},{8,24},{16,0},{24,8},{1,17},{9,25},{17,1},{25,9},{2,18},{10... | collective-permute-start | bytes 786440 | tf_op jit(solution)/shard_map/ppermute | solution.py:225
  27.5 2.5 %collective-permute-start.12 = (bf16[2,32,896]{2,1,0:T(8,128)(2,1)S(1)}, bf16[2,32,896]{2,1,0:T(8,128)(2,1)S(1)}, u32[]{:S(2)}, u32[]{:S(2)}) collective-permute-start(bf16[2,32,896]{2,1,0:T(8,128)(2,1)S(1)} %get-tuple-element.69), channel_id=1, source_target_pairs={{0,6},{1,7},{2,4},{3,5},{4,2},{5,3},{6,0},{7,1},{8,14},{9,15},{10,... | collective-permute-start | bytes 344072 | tf_op jit(solution)/shard_map/ppermute | solution.py:225
  30.0 1.4 %collective-permute-done.4.refs_1_ = bf16[2,64,1024]{2,1,0:T(8,128)(2,1)S(1)} collective-permute-done((bf16[2,64,1024]{2,1,0:T(8,128)(2,1)S(1)}, bf16[2,64,1024]{2,1,0:T(8,128)(2,1)S(1)}, u32[]{:S(2)}, u32[]{:S(2)}) %collective-permute-start.4) | collective-permute-done | bytes 262176 | tf_op jit(solution)/shard_map/ppermute | solution.py:225
  31.4 5.3 %collective-permute-done.5.refs_2_ = bf16[2,64,1024]{2,1,0:T(8,128)(2,1)S(1)} collective-permute-done((bf16[2,64,1024]{2,1,0:T(8,128)(2,1)S(1)}, bf16[2,64,1024]{2,1,0:T(8,128)(2,1)S(1)}, u32[]{:S(2)}, u32[]{:S(2)}) %collective-permute-start.5) | collective-permute-done | bytes 262176 | tf_op jit(solution)/shard_map/ppermute | solution.py:225
  36.9 1.6 %collective-permute-start.7 = (bf16[64,1024]{1,0:T(8,128)(2,1)S(1)}, bf16[64,1024]{1,0:T(8,128)(2,1)S(1)}, u32[]{:S(2)}, u32[]{:S(2)}) collective-permute-start(bf16[64,1024]{1,0:T(8,128)(2,1)S(1)} %shard_map.114.refs_0_), channel_id=1, source_target_pairs={{0,8},{8,0},{16,24},{24,16},{1,9},{9,1},{17,25},{25,17},{2,10},{10... | collective-permute-start | bytes 393224 | tf_op jit(solution)/shard_map/ppermute | solution.py:225
  47.8 2.0 %collective-permute-done.15.refs_7_ = bf16[64,1024]{1,0:T(8,128)(2,1)S(1)} collective-permute-done((bf16[64,1024]{1,0:T(8,128)(2,1)S(1)}, bf16[64,1024]{1,0:T(8,128)(2,1)S(1)}, u32[]{:S(2)}, u32[]{:S(2)}) %collective-permute-start.15) | collective-permute-done | bytes 131104 | tf_op jit(solution)/shard_map/ppermute | solution.py:225
  50.2 2.0 %collective-permute-start.16 = (bf16[2,64,1024]{2,1,0:T(8,128)(2,1)S(1)}, bf16[2,64,1024]{2,1,0:T(8,128)(2,1)S(1)}, u32[]{:S(2)}, u32[]{:S(2)}) collective-permute-start(bf16[2,64,1024]{2,1,0:T(8,128)(2,1)S(1)} %shard_map.117.refs_0_), channel_id=1, source_target_pairs={{0,8},{8,0},{16,24},{24,16},{1,9},{9,1},{17,25},{25,17},{2,10},{10... | collective-permute-start | bytes 786440 | tf_op jit(solution)/shard_map/ppermute | solution.py:225
  53.8 2.0 %collective-permute-start.19 = (bf16[2,32,896]{2,1,0:T(8,128)(2,1)S(1)}, bf16[2,32,896]{2,1,0:T(8,128)(2,1)S(1)}, u32[]{:S(2)}, u32[]{:S(2)}) collective-permute-start(bf16[2,32,896]{2,1,0:T(8,128)(2,1)S(1)} %get-tuple-element.76), channel_id=1, source_target_pairs={{0,4},{1,5},{2,6},{3,7},{4,0},{5,1},{6,2},{7,3},{8,12},{9,13},{10,... | collective-permute-start | bytes 344072 | tf_op jit(solution)/shard_map/ppermute | solution.py:225
  55.8 2.5 %collective-permute-start.20 = (bf16[2,32,896]{2,1,0:T(8,128)(2,1)S(1)}, bf16[2,32,896]{2,1,0:T(8,128)(2,1)S(1)}, u32[]{:S(2)}, u32[]{:S(2)}) collective-permute-start(bf16[2,32,896]{2,1,0:T(8,128)(2,1)S(1)} %get-tuple-element.77), channel_id=1, source_target_pairs={{0,6},{1,7},{2,4},{3,5},{4,2},{5,3},{6,0},{7,1},{8,14},{9,15},{10,... | collective-permute-start | bytes 344072 | tf_op jit(solution)/shard_map/ppermute | solution.py:225
  58.5 4.6 %collective-permute-done.17.refs_2_ = bf16[2,64,1024]{2,1,0:T(8,128)(2,1)S(1)} collective-permute-done((bf16[2,64,1024]{2,1,0:T(8,128)(2,1)S(1)}, bf16[2,64,1024]{2,1,0:T(8,128)(2,1)S(1)}, u32[]{:S(2)}, u32[]{:S(2)}) %collective-permute-start.17) | collective-permute-done | bytes 262176 | tf_op jit(solution)/shard_map/ppermute | solution.py:225
  65.1 1.9 %collective-permute-start.21 = (bf16[2,32,896]{2,1,0:T(8,128)(2,1)S(1)}, bf16[2,32,896]{2,1,0:T(8,128)(2,1)S(1)}, u32[]{:S(2)}, u32[]{:S(2)}) collective-permute-start(bf16[2,32,896]{2,1,0:T(8,128)(2,1)S(1)} %get-tuple-element.80), channel_id=1, source_target_pairs={{0,2},{1,3},{2,0},{3,1},{4,6},{5,7},{6,4},{7,5},{8,10},{9,11},{10,... | collective-permute-start | bytes 344072 | tf_op jit(solution)/shard_map/ppermute | solution.py:225
  67.0 2.9 %collective-permute-start.23 = (bf16[2,32,896]{2,1,0:T(8,128)(2,1)S(1)}, bf16[2,32,896]{2,1,0:T(8,128)(2,1)S(1)}, u32[]{:S(2)}, u32[]{:S(2)}) collective-permute-start(bf16[2,32,896]{2,1,0:T(8,128)(2,1)S(1)} %get-tuple-element.88), channel_id=1, source_target_pairs={{0,6},{1,7},{2,4},{3,5},{4,2},{5,3},{6,0},{7,1},{8,14},{9,15},{10,... | collective-permute-start | bytes 344072 | tf_op jit(solution)/shard_map/ppermute | solution.py:225
  70.0 1.5 %collective-permute-start.25 = (bf16[2,32,896]{2,1,0:T(8,128)(2,1)S(1)}, bf16[2,32,896]{2,1,0:T(8,128)(2,1)S(1)}, u32[]{:S(2)}, u32[]{:S(2)}) collective-permute-start(bf16[2,32,896]{2,1,0:T(8,128)(2,1)S(1)} %get-tuple-element.87.refs_5_.refs_2_), channel_id=1, source_target_pairs={{0,2},{1,3},{2,0},{3,1},{4,6},{5,7},{6,4},{7,5},{8,10},{9,11},{10,... | collective-permute-start | bytes 344072 | tf_op jit(solution)/shard_map/ppermute | solution.py:225
  71.5 2.0 %shard_map.124 = bf16[1024,896]{1,0:T(8,128)(2,1)} custom-call(bf16[256,1024]{1,0:T(8,128)(2,1)S(1)} %get-tuple-element.95.left_ref, bf16[256,896]{1,0:T(8,128)(2,1)S(1)} %get-tuple-element.96.refs_0_), custom_call_target="tpu_custom_call" | custom-call | flops 469762048 | bytes 1835008 | tf_op jit(solution)/shard_map/pallas_call | solution.py:334
  73.5 1.5 %shard_map.121 = bf16[512,896]{1,0:T(8,128)(2,1)} custom-call(bf16[256,512]{1,0:T(8,128)(2,1)S(1)} %copy-done.4, f32[256,1]{1,0:T(8,128)S(1)} %copy-done.5, bf16[4,32,896]{2,1,0:T(8,128)(2,1)S(1)} %get-tuple-element.66.keep_ref.refs_0_, bf16[4,32,896]{2,1,0:T(8,128)(2,1)S(1)} %collective-permute-done.10.swap_ref.refs_1_, ...), custom_call_target="tpu_custom_call" | custom-call | flops 234881024 | bytes 1835008 | tf_op jit(solution)/shard_map/pallas_call | solution.py:349
  74.9 2.5 %shard_map.123 = (bf16[896,1024]{1,0:T(8,128)(2,1)}, bf16[896,1024]{1,0:T(8,128)(2,1)}) custom-call(bf16[256,896]{1,0:T(8,128)(2,1)S(1)} %get-tuple-element.90.left_ref, bf16[256,1024]{1,0:T(8,128)(2,1)S(1)} %get-tuple-element.91.refs_0_, bf16[256,1024]{1,0:T(8,128)(2,1)S(1)} %get-tuple-element.92.refs_1_, ...), custom_call_target="tpu_custom_call" | custom-call | flops 939524096 | bytes 3670016 | tf_op jit(solution)/shard_map/pallas_call | solution.py:340
  77.5 3.0 %collective-permute-done.24.refs_3_ = bf16[2,32,896]{2,1,0:T(8,128)(2,1)S(1)} collective-permute-done((bf16[2,32,896]{2,1,0:T(8,128)(2,1)S(1)}, bf16[2,32,896]{2,1,0:T(8,128)(2,1)S(1)}, u32[]{:S(2)}, u32[]{:S(2)}) %collective-permute-start.24) | collective-permute-done | bytes 114720 | tf_op jit(solution)/shard_map/ppermute | solution.py:225
  (55 shorter events, 17.9 us)
Async XLA Ops:
  6.1 16.2 %collective-permute-start.3 = (bf16[2,2,32,896]{3,2,1,0:T(8,128)(2,1)S(1)}, bf16[2,2,32,896]{3,2,1,0:T(8,128)(2,1)S(1)}, u32[]{:S(2)}, u32[]{:S(2)}) collective-permute-start(bf16[2,2,32,896]{3,2,1,0:T(8,128)(2,1)S(1)} %get-tuple-element.60), channel_id=1, source_target_pairs={{0,2},{1,3},{2,0},{3,1},{4,6},{5,7},{6,4},{7,5},{8,10},{9,11},{10,... | collective-permute-start | bytes 688136 | tf_op jit(solution)/shard_map/ppermute | solution.py:225
  9.1 11.5 %collective-permute-start.1 = (bf16[2,32,896]{2,1,0:T(8,128)(2,1)S(1)}, bf16[2,32,896]{2,1,0:T(8,128)(2,1)S(1)}, u32[]{:S(2)}, u32[]{:S(2)}) collective-permute-start(bf16[2,32,896]{2,1,0:T(8,128)(2,1)S(1)} %get-tuple-element.58), channel_id=1, source_target_pairs={{0,6},{1,7},{2,4},{3,5},{4,2},{5,3},{6,0},{7,1},{8,14},{9,15},{10,... | collective-permute-start | bytes 344072 | tf_op jit(solution)/shard_map/ppermute | solution.py:225
  11.6 10.7 %collective-permute-start.2 = (bf16[2,32,896]{2,1,0:T(8,128)(2,1)S(1)}, bf16[2,32,896]{2,1,0:T(8,128)(2,1)S(1)}, u32[]{:S(2)}, u32[]{:S(2)}) collective-permute-start(bf16[2,32,896]{2,1,0:T(8,128)(2,1)S(1)} %get-tuple-element.59), channel_id=1, source_target_pairs={{0,4},{1,5},{2,6},{3,7},{4,0},{5,1},{6,2},{7,3},{8,12},{9,13},{10,... | collective-permute-start | bytes 344072 | tf_op jit(solution)/shard_map/ppermute | solution.py:225
  23.6 7.8 %collective-permute-start.4 = (bf16[2,64,1024]{2,1,0:T(8,128)(2,1)S(1)}, bf16[2,64,1024]{2,1,0:T(8,128)(2,1)S(1)}, u32[]{:S(2)}, u32[]{:S(2)}) collective-permute-start(bf16[2,64,1024]{2,1,0:T(8,128)(2,1)S(1)} %get-tuple-element.63), channel_id=1, source_target_pairs={{0,8},{8,0},{16,24},{24,16},{1,9},{9,1},{17,25},{25,17},{2,10},{10... | collective-permute-start | bytes 786440 | tf_op jit(solution)/shard_map/ppermute | solution.py:225
  25.1 11.6 %collective-permute-start.5 = (bf16[2,64,1024]{2,1,0:T(8,128)(2,1)S(1)}, bf16[2,64,1024]{2,1,0:T(8,128)(2,1)S(1)}, u32[]{:S(2)}, u32[]{:S(2)}) collective-permute-start(bf16[2,64,1024]{2,1,0:T(8,128)(2,1)S(1)} %get-tuple-element.64), channel_id=1, source_target_pairs={{0,16},{8,24},{16,0},{24,8},{1,17},{9,25},{17,1},{25,9},{2,18},{10... | collective-permute-start | bytes 786440 | tf_op jit(solution)/shard_map/ppermute | solution.py:225
  26.7 10.1 %collective-permute-start.6 = (bf16[2,64,1024]{2,1,0:T(8,128)(2,1)S(1)}, bf16[2,64,1024]{2,1,0:T(8,128)(2,1)S(1)}, u32[]{:S(2)}, u32[]{:S(2)}) collective-permute-start(bf16[2,64,1024]{2,1,0:T(8,128)(2,1)S(1)} %get-tuple-element.65), channel_id=1, source_target_pairs={{0,24},{8,16},{16,8},{24,0},{1,25},{9,17},{17,9},{25,1},{2,26},{10... | collective-permute-start | bytes 786440 | tf_op jit(solution)/shard_map/ppermute | solution.py:225
  27.1 13.9 %collective-permute-start.11 = (bf16[2,32,896]{2,1,0:T(8,128)(2,1)S(1)}, bf16[2,32,896]{2,1,0:T(8,128)(2,1)S(1)}, u32[]{:S(2)}, u32[]{:S(2)}) collective-permute-start(bf16[2,32,896]{2,1,0:T(8,128)(2,1)S(1)} %get-tuple-element.68), channel_id=1, source_target_pairs={{0,4},{1,5},{2,6},{3,7},{4,0},{5,1},{6,2},{7,3},{8,12},{9,13},{10,... | collective-permute-start | bytes 344072 | tf_op jit(solution)/shard_map/ppermute | solution.py:225
  27.5 13.6 %collective-permute-start.12 = (bf16[2,32,896]{2,1,0:T(8,128)(2,1)S(1)}, bf16[2,32,896]{2,1,0:T(8,128)(2,1)S(1)}, u32[]{:S(2)}, u32[]{:S(2)}) collective-permute-start(bf16[2,32,896]{2,1,0:T(8,128)(2,1)S(1)} %get-tuple-element.69), channel_id=1, source_target_pairs={{0,6},{1,7},{2,4},{3,5},{4,2},{5,3},{6,0},{7,1},{8,14},{9,15},{10,... | collective-permute-start | bytes 344072 | tf_op jit(solution)/shard_map/ppermute | solution.py:225
  36.9 7.1 %collective-permute-start.7 = (bf16[64,1024]{1,0:T(8,128)(2,1)S(1)}, bf16[64,1024]{1,0:T(8,128)(2,1)S(1)}, u32[]{:S(2)}, u32[]{:S(2)}) collective-permute-start(bf16[64,1024]{1,0:T(8,128)(2,1)S(1)} %shard_map.114.refs_0_), channel_id=1, source_target_pairs={{0,8},{8,0},{16,24},{24,16},{1,9},{9,1},{17,25},{25,17},{2,10},{10... | collective-permute-start | bytes 393224 | tf_op jit(solution)/shard_map/ppermute | solution.py:225
  38.6 6.8 %collective-permute-start.8 = (bf16[64,1024]{1,0:T(8,128)(2,1)S(1)}, bf16[64,1024]{1,0:T(8,128)(2,1)S(1)}, u32[]{:S(2)}, u32[]{:S(2)}) collective-permute-start(bf16[64,1024]{1,0:T(8,128)(2,1)S(1)} %shard_map.114.refs_0_), channel_id=1, source_target_pairs={{0,16},{8,24},{16,0},{24,8},{1,17},{9,25},{17,1},{25,9},{2,18},{10... | collective-permute-start | bytes 393224 | tf_op jit(solution)/shard_map/ppermute | solution.py:225
  39.7 5.9 %collective-permute-start.9 = (bf16[64,1024]{1,0:T(8,128)(2,1)S(1)}, bf16[64,1024]{1,0:T(8,128)(2,1)S(1)}, u32[]{:S(2)}, u32[]{:S(2)}) collective-permute-start(bf16[64,1024]{1,0:T(8,128)(2,1)S(1)} %shard_map.114.refs_0_), channel_id=1, source_target_pairs={{0,24},{8,16},{16,8},{24,0},{1,25},{9,17},{17,9},{25,1},{2,26},{10... | collective-permute-start | bytes 393224 | tf_op jit(solution)/shard_map/ppermute | solution.py:225
  41.8 5.0 %collective-permute-start.13 = (bf16[64,1024]{1,0:T(8,128)(2,1)S(1)}, bf16[64,1024]{1,0:T(8,128)(2,1)S(1)}, u32[]{:S(2)}, u32[]{:S(2)}) collective-permute-start(bf16[64,1024]{1,0:T(8,128)(2,1)S(1)} %get-tuple-element.73), channel_id=1, source_target_pairs={{0,8},{8,0},{16,24},{24,16},{1,9},{9,1},{17,25},{25,17},{2,10},{10... | collective-permute-start | bytes 393224 | tf_op jit(solution)/shard_map/ppermute | solution.py:225
  42.9 5.0 %collective-permute-start.14 = (bf16[64,1024]{1,0:T(8,128)(2,1)S(1)}, bf16[64,1024]{1,0:T(8,128)(2,1)S(1)}, u32[]{:S(2)}, u32[]{:S(2)}) collective-permute-start(bf16[64,1024]{1,0:T(8,128)(2,1)S(1)} %get-tuple-element.74), channel_id=1, source_target_pairs={{0,16},{8,24},{16,0},{24,8},{1,17},{9,25},{17,1},{25,9},{2,18},{10... | collective-permute-start | bytes 393224 | tf_op jit(solution)/shard_map/ppermute | solution.py:225
  44.0 5.9 %collective-permute-start.15 = (bf16[64,1024]{1,0:T(8,128)(2,1)S(1)}, bf16[64,1024]{1,0:T(8,128)(2,1)S(1)}, u32[]{:S(2)}, u32[]{:S(2)}) collective-permute-start(bf16[64,1024]{1,0:T(8,128)(2,1)S(1)} %get-tuple-element.75), channel_id=1, source_target_pairs={{0,24},{8,16},{16,8},{24,0},{1,25},{9,17},{17,9},{25,1},{2,26},{10... | collective-permute-start | bytes 393224 | tf_op jit(solution)/shard_map/ppermute | solution.py:225
  46.3 7.4 %collective-permute-start.10 = (bf16[4,32,896]{2,1,0:T(8,128)(2,1)S(1)}, bf16[4,32,896]{2,1,0:T(8,128)(2,1)S(1)}, u32[]{:S(2)}, u32[]{:S(2)}) collective-permute-start(bf16[4,32,896]{2,1,0:T(8,128)(2,1)S(1)} %get-tuple-element.67), channel_id=1, source_target_pairs={{0,1},{1,0},{2,3},{3,2},{4,5},{5,4},{6,7},{7,6},{8,9},{9,8},{10,11... | collective-permute-start | bytes 688136 | tf_op jit(solution)/shard_map/ppermute | solution.py:225
  50.2 8.4 %collective-permute-start.16 = (bf16[2,64,1024]{2,1,0:T(8,128)(2,1)S(1)}, bf16[2,64,1024]{2,1,0:T(8,128)(2,1)S(1)}, u32[]{:S(2)}, u32[]{:S(2)}) collective-permute-start(bf16[2,64,1024]{2,1,0:T(8,128)(2,1)S(1)} %shard_map.117.refs_0_), channel_id=1, source_target_pairs={{0,8},{8,0},{16,24},{24,16},{1,9},{9,1},{17,25},{25,17},{2,10},{10... | collective-permute-start | bytes 786440 | tf_op jit(solution)/shard_map/ppermute | solution.py:225
  52.2 11.0 %collective-permute-start.17 = (bf16[2,64,1024]{2,1,0:T(8,128)(2,1)S(1)}, bf16[2,64,1024]{2,1,0:T(8,128)(2,1)S(1)}, u32[]{:S(2)}, u32[]{:S(2)}) collective-permute-start(bf16[2,64,1024]{2,1,0:T(8,128)(2,1)S(1)} %shard_map.117.refs_0_), channel_id=1, source_target_pairs={{0,16},{8,24},{16,0},{24,8},{1,17},{9,25},{17,1},{25,9},{2,18},{10... | collective-permute-start | bytes 786440 | tf_op jit(solution)/shard_map/ppermute | solution.py:225
  52.7 10.5 %collective-permute-start.18 = (bf16[2,64,1024]{2,1,0:T(8,128)(2,1)S(1)}, bf16[2,64,1024]{2,1,0:T(8,128)(2,1)S(1)}, u32[]{:S(2)}, u32[]{:S(2)}) collective-permute-start(bf16[2,64,1024]{2,1,0:T(8,128)(2,1)S(1)} %shard_map.117.refs_0_), channel_id=1, source_target_pairs={{0,24},{8,16},{16,8},{24,0},{1,25},{9,17},{17,9},{25,1},{2,26},{10... | collective-permute-start | bytes 786440 | tf_op jit(solution)/shard_map/ppermute | solution.py:225
  53.8 9.9 %collective-permute-start.19 = (bf16[2,32,896]{2,1,0:T(8,128)(2,1)S(1)}, bf16[2,32,896]{2,1,0:T(8,128)(2,1)S(1)}, u32[]{:S(2)}, u32[]{:S(2)}) collective-permute-start(bf16[2,32,896]{2,1,0:T(8,128)(2,1)S(1)} %get-tuple-element.76), channel_id=1, source_target_pairs={{0,4},{1,5},{2,6},{3,7},{4,0},{5,1},{6,2},{7,3},{8,12},{9,13},{10,... | collective-permute-start | bytes 344072 | tf_op jit(solution)/shard_map/ppermute | solution.py:225
  55.8 7.9 %collective-permute-start.20 = (bf16[2,32,896]{2,1,0:T(8,128)(2,1)S(1)}, bf16[2,32,896]{2,1,0:T(8,128)(2,1)S(1)}, u32[]{:S(2)}, u32[]{:S(2)}) collective-permute-start(bf16[2,32,896]{2,1,0:T(8,128)(2,1)S(1)} %get-tuple-element.77), channel_id=1, source_target_pairs={{0,6},{1,7},{2,4},{3,5},{4,2},{5,3},{6,0},{7,1},{8,14},{9,15},{10,... | collective-permute-start | bytes 344072 | tf_op jit(solution)/shard_map/ppermute | solution.py:225
  65.1 8.3 %collective-permute-start.21 = (bf16[2,32,896]{2,1,0:T(8,128)(2,1)S(1)}, bf16[2,32,896]{2,1,0:T(8,128)(2,1)S(1)}, u32[]{:S(2)}, u32[]{:S(2)}) collective-permute-start(bf16[2,32,896]{2,1,0:T(8,128)(2,1)S(1)} %get-tuple-element.80), channel_id=1, source_target_pairs={{0,2},{1,3},{2,0},{3,1},{4,6},{5,7},{6,4},{7,5},{8,10},{9,11},{10,... | collective-permute-start | bytes 344072 | tf_op jit(solution)/shard_map/ppermute | solution.py:225
  67.0 10.5 %collective-permute-start.23 = (bf16[2,32,896]{2,1,0:T(8,128)(2,1)S(1)}, bf16[2,32,896]{2,1,0:T(8,128)(2,1)S(1)}, u32[]{:S(2)}, u32[]{:S(2)}) collective-permute-start(bf16[2,32,896]{2,1,0:T(8,128)(2,1)S(1)} %get-tuple-element.88), channel_id=1, source_target_pairs={{0,6},{1,7},{2,4},{3,5},{4,2},{5,3},{6,0},{7,1},{8,14},{9,15},{10,... | collective-permute-start | bytes 344072 | tf_op jit(solution)/shard_map/ppermute | solution.py:225
  69.9 10.5 %collective-permute-start.24 = (bf16[2,32,896]{2,1,0:T(8,128)(2,1)S(1)}, bf16[2,32,896]{2,1,0:T(8,128)(2,1)S(1)}, u32[]{:S(2)}, u32[]{:S(2)}) collective-permute-start(bf16[2,32,896]{2,1,0:T(8,128)(2,1)S(1)} %get-tuple-element.89), channel_id=1, source_target_pairs={{0,4},{1,5},{2,6},{3,7},{4,0},{5,1},{6,2},{7,3},{8,12},{9,13},{10,... | collective-permute-start | bytes 344072 | tf_op jit(solution)/shard_map/ppermute | solution.py:225
  70.0 10.5 %collective-permute-start.25 = (bf16[2,32,896]{2,1,0:T(8,128)(2,1)S(1)}, bf16[2,32,896]{2,1,0:T(8,128)(2,1)S(1)}, u32[]{:S(2)}, u32[]{:S(2)}) collective-permute-start(bf16[2,32,896]{2,1,0:T(8,128)(2,1)S(1)} %get-tuple-element.87.refs_5_.refs_2_), channel_id=1, source_target_pairs={{0,2},{1,3},{2,0},{3,1},{4,6},{5,7},{6,4},{7,5},{8,10},{9,11},{10,... | collective-permute-start | bytes 344072 | tf_op jit(solution)/shard_map/ppermute | solution.py:225
  (8 other events, 64.1 us)

commit v9 on v8

--- a/solution.py
+++ b/solution.py
@@ -85,17 +85,17 @@
     split_cores(keep_ref, swap_ref, rows, 1)
 
 
-def load_kernel(from_ref, to_ref):
-    to_ref[...] = from_ref[...]
-
-
-def pack_kernel(half, keep_ref, swap_ref, near_ref, *far_refs):
-    for at in range(2):
-        near_ref[at, 0] = keep_ref[at, 1]
-        near_ref[at, 1] = swap_ref[at, 1]
-        for k in range(2, half):
-            far_refs[at * (half - 2) + k - 2][0] = keep_ref[at, k]
-            far_refs[at * (half - 2) + k - 2][1] = swap_ref[at, k]
+def load_kernel(*refs):
+    half = len(refs) // 2
+    for from_ref, to_ref in zip(refs[:half], refs[half:]):
+        to_ref[...] = from_ref[...]
+
+
+def pack_kernel(keep_ref, swap_ref, *out_refs):
+    for k, out_ref in enumerate(out_refs):
+        for at in range(2):
+            out_ref[at, 0] = keep_ref[at, k + 1]
+            out_ref[at, 1] = swap_ref[at, k + 1]
 
 
 def pack_back_kernel(keep_ref, swap_ref, *out_refs):
@@ -104,47 +104,47 @@
         out_ref[1] = swap_ref[k + 1]
 
 
-def pieces(at, keep_ref, swap_ref, *refs):
-    far_refs, near_ref = refs[:-1], refs[-1]
-    found = [keep_ref[at, 0], swap_ref[at, 0], near_ref[at, 0], near_ref[at, 1]]
-    for ref in far_refs[::-1]:
-        found += [ref[0], ref[1]]
-    return found
-
-
-def chunk_rows(rows, dp, k):
-    chunk = rows // dp
+def part_rows(rows, dp, k):
+    part = rows // dp
     mine = lax.axis_index("dp")
-    return pl.ds(pl.multiple_of((mine ^ k) * chunk, chunk), chunk)
+    return pl.ds(pl.multiple_of((mine ^ k) * part, part), part)
 
 
 def local_order(found, scratch, dp):
     scratch[...] = jnp.concatenate(found, axis=0)
     rows = scratch.shape[0]
-    return jnp.concatenate([scratch[chunk_rows(rows, dp, k), :] for k in range(dp)], axis=0)
-
-
-def gate_up_kernel(half, *refs):
-    gate_ref, up_ref, local_ref, *out_refs, scratch = refs[half + 1 :]
-    dp = len(out_refs)
-    rows = local_order(pieces(0, *refs[: half + 1]), scratch, dp)
-    local_ref[...] = rows
-    chunk = rows.shape[0] // dp
-    for at, mat in enumerate((gate_ref, up_ref)):
-        part = mm(rows, mat[...], ((1,), (0,))).astype(BF16)
+    return jnp.concatenate([scratch[part_rows(rows, dp, k), :] for k in range(dp)], axis=0)
+
+
+def natural_order(parts, scratch):
+    for k, part in enumerate(parts):
+        scratch[part_rows(scratch.shape[0], len(parts), k), :] = part
+    return scratch[...]
+
+
+def partial_kernel(dp, own, count, *refs):
+    gate_ref, up_ref, down_ref = refs[count : count + 3]
+    rows_ref, grads_ref, *out_refs, scratch = refs[-dp - 3 :]
+    local = []
+    for at in range(2):
+        found = [ref[at, 0] for ref in refs[:2]] if own else []
+        found += [ref[at, k] for ref in refs[2 * own : count] for k in range(2)]
+        local.append(local_order(found, scratch, dp))
+    rows_ref[...], grads_ref[...] = local
+    part = scratch.shape[0] // dp
+    for at, (left, mat, dims) in enumerate(
+        (
+            (local[0], gate_ref, ((1,), (0,))),
+            (local[0], up_ref, ((1,), (0,))),
+            (local[1], down_ref, ((1,), (1,))),
+        )
+    ):
+        sums = mm(left, mat[...], dims).astype(BF16)
         for k, out_ref in enumerate(out_refs):
-            out_ref[at] = part[k * chunk : (k + 1) * chunk]
-
-
-def grad_act_kernel(half, *refs):
-    down_ref, local_ref, *out_refs, scratch = refs[half + 1 :]
-    dp = len(out_refs)
-    rows = local_order(pieces(1, *refs[: half + 1]), scratch, dp)
-    local_ref[...] = rows
-    split_rows(out_refs, mm(rows, down_ref[...], ((1,), (1,))).astype(BF16))
-
-
-def group_sum(refs, *at):
+            out_ref[at] = sums[k * part : (k + 1) * part]
+
+
+def group_sum(refs, at):
     total = refs[0][at].astype(F32)
     for ref in refs[1:]:
         total = total + ref[at].astype(F32)
@@ -156,31 +156,36 @@
 
 
 def act_kernel(dp, *refs):
-    gate = group_sum(refs[:dp], 0)
-    up = group_sum(refs[:dp], 1)
-    refs[dp][...] = (gate * logistic(gate) * up).astype(BF16)
+    for at in range(2):
+        sums = refs[at * dp : (at + 1) * dp]
+        gate = group_sum(sums, 0)
+        refs[-1][at] = (gate * logistic(gate) * group_sum(sums, 1)).astype(BF16)
 
 
 def grad_pre_kernel(dp, *refs):
-    gate = group_sum(refs[:dp], 0)
-    up = group_sum(refs[:dp], 1)
-    grad = group_sum(refs[dp : 2 * dp], Ellipsis)
-    out_ref = refs[2 * dp]
-    soft = logistic(gate)
-    out_ref[0] = (grad * up * (soft * (1.0 + gate * (1.0 - soft)))).astype(BF16)
-    out_ref[1] = (grad * (gate * soft)).astype(BF16)
+    out_ref = refs[-1]
+    for at in range(2):
+        sums = refs[at * dp : (at + 1) * dp]
+        gate, up, grad = [group_sum(sums, k) for k in range(3)]
+        soft = logistic(gate)
+        out_ref[0, at] = (grad * up * (soft * (1.0 + gate * (1.0 - soft)))).astype(BF16)
+        out_ref[1, at] = (grad * (gate * soft)).astype(BF16)
 
 
 def send_back(keep_ref, swap_ref, scratch, rows, dp):
-    chunk = rows.shape[0] // dp
-    for k in range(dp):
-        scratch[chunk_rows(rows.shape[0], dp, k), :] = rows[k * chunk : (k + 1) * chunk]
-    split_cores(keep_ref, swap_ref, scratch[...])
+    part = rows.shape[0] // (2 * dp)
+    half, block = keep_ref.shape[:2]
+    parts = [rows[k * part : (k + 1) * part] for k in range(2 * dp)]
+    for at in range(2):
+        value = natural_order(parts[at * dp : (at + 1) * dp], scratch)
+        for k in range(half // 2):
+            keep_ref[at * half // 2 + k] = value[2 * k * block : (2 * k + 1) * block]
+            swap_ref[at * half // 2 + k] = value[(2 * k + 1) * block : (2 * k + 2) * block]
 
 
 def expert_out_kernel(dp, *refs):
     down_ref, act_ref, keep_ref, swap_ref, scratch = refs[dp:]
-    act = join_rows(refs[:dp])
+    act = jnp.concatenate([ref[at] for at in range(2) for ref in refs[:dp]], axis=0)
     act_ref[...] = act
     rows = mm(act, down_ref[...], ((1,), (0,))).astype(BF16)
     send_back(keep_ref, swap_ref, scratch, rows, dp)
@@ -188,8 +193,10 @@
 
 def row_grad_kernel(dp, *refs):
     gate_ref, up_ref, gate_pre_ref, up_pre_ref, keep_ref, swap_ref, scratch = refs[dp:]
-    gate_pre = jnp.concatenate([ref[0] for ref in refs[:dp]], axis=0)
-    up_pre = jnp.concatenate([ref[1] for ref in refs[:dp]], axis=0)
+    gate_pre, up_pre = [
+        jnp.concatenate([ref[k, at] for at in range(2) for ref in refs[:dp]], axis=0)
+        for k in range(2)
+    ]
     gate_pre_ref[...] = gate_pre
     up_pre_ref[...] = up_pre
     total = mm(gate_pre, gate_ref[...], ((1,), (1,))) + mm(up_pre, up_ref[...], ((1,), (1,)))
@@ -214,9 +221,14 @@
     refs[-1][...] = mm(pick_ref[...], back, ((0,), (0,))).astype(BF16)
 
 
-def grads_kernel(count, left_ref, *refs):
-    left = left_ref[...].T
-    for right_ref, out_ref in zip(refs[:count], refs[-count:]):
+def grad_down_kernel(act_ref, early_ref, late_ref, out_ref):
+    right = join_rows([early_ref, late_ref])
+    out_ref[...] = mm(act_ref[...].T, right, ((1,), (0,))).astype(BF16)
+
+
+def grad_gate_up_kernel(early_ref, late_ref, gate_pre_ref, up_pre_ref, _, gate_ref, up_ref):
+    left = join_rows([early_ref, late_ref]).T
+    for right_ref, out_ref in ((gate_pre_ref, gate_ref), (up_pre_ref, up_ref)):
         out_ref[...] = mm(left, right_ref[...], ((1,), (0,))).astype(BF16)
 
 
@@ -244,13 +256,16 @@
     weights = 2 * features * hidden
 
     half = experts // 2
+    early = half // 2
+    part = chunk // 2
     sized = shape((slots, features), BF16)
+    cut = shape((slots // 2, features), BF16)
     wide = shape((slots, hidden), BF16)
     both = shape((2, half, capacity, features), BF16)
     one = shape((half, capacity, features), BF16)
-    near = shape((2, 2, capacity, features), BF16)
-    far = [shape((2, capacity, features), BF16)] * (half - 2)
-    in_order = [pltpu.VMEM((slots, features), BF16)]
+    pair = shape((2, capacity, features), BF16)
+    pairs = shape((2, 2, capacity, features), BF16)
+    in_order = [pltpu.VMEM((slots // 2, features), BF16)]
 
     ins = (expert_ids.T, gates.T, tokens, grad_out)
     outs = (shape((slots, tok_rows), BF16), shape((slots, 1), F32), both, both)
@@ -266,46 +281,40 @@
             pltpu.SemaphoreType.DMA((4,)),
         ],
     )(*ins)
-    swap_to, up_mat = lax.optimization_barrier((swap, up_mat))
+    swap_to, up_mat, down_mat = lax.optimization_barrier((swap, up_mat, down_mat))
     swap = partner(swap_to, "expert", 1)
-    up_mat = call(load_kernel, shape(up_mat.shape, BF16), 0, 2 * weights)(up_mat)
-    swap, up_mat = lax.optimization_barrier((swap, up_mat))
-    near_to, *far_to = call(functools.partial(pack_kernel, half), (near, *far, *far), 0, 8 * slots)(
-        keep, swap
-    )
-    far_rows = [partner(far_to[k], "expert", 2 * (2 + k)) for k in reversed(range(half - 2))][::-1]
-    near_in = partner(near_to, "expert", 2)
-    far_grads = [partner(far_to[half - 2 + k], "expert", 2 * (2 + k)) for k in range(half - 2)]
-    rows, *part_pre = call(
-        functools.partial(gate_up_kernel, half),
-        (sized, *[shape((2, chunk, hidden), BF16)] * dp),
-        2 * product,
-        2 * weights,
-        scratch_shapes=in_order,
-    )(keep, swap, *far_rows[::-1], near_in, gate_mat, up_mat)
-    sums = trade(part_pre)
+    up_mat, down_mat = call(
+        load_kernel, (shape(up_mat.shape, BF16), shape(down_mat.shape, BF16)), 0, 4 * weights
+    )(up_mat, down_mat)
+    swap, up_mat, down_mat = lax.optimization_barrier((swap, up_mat, down_mat))
+    mats = (gate_mat, up_mat, down_mat)
+    sent = call(pack_kernel, [pairs] * (half - 1), 0, 8 * slots)(keep, swap)
+    arrived = [partner(value, "expert", 2 * (1 + k)) for k, value in enumerate(sent)]
+
+    def partial_sums(own, found, *after):
+        return call(
+            functools.partial(partial_kernel, dp, own, len(found)),
+            (cut, cut, *[shape((3, part, hidden), BF16)] * dp),
+            3 * product // 2,
+            3 * weights,
+            in_specs=[HERE] * (len(found) + 3) + [ANY] * len(after),
+            scratch_shapes=in_order,
+        )(*found, *mats, *after)
+
+    rows_early, grads_early, *sums = partial_sums(True, (keep, swap, *arrived[: early - 1]))
+    sums_early = trade(sums)
+    rows_late, grads_late, *sums = partial_sums(False, arrived[early - 1 :], rows_early)
+    sums_late = trade(sums)
     act_mine = call(
-        functools.partial(act_kernel, dp),
-        shape((chunk, hidden), BF16),
-        0,
-        4 * dp * chunk * hidden,
-    )(*sums)
+        functools.partial(act_kernel, dp), shape((2, part, hidden), BF16), 0, 4 * slots * hidden
+    )(*sums_early, *sums_late)
     acts = trade([act_mine] * dp)
-    far_grads, act_mine = lax.optimization_barrier((far_grads, act_mine))
-    grads, *part_grad = call(
-        functools.partial(grad_act_kernel, half),
-        (sized, *[shape((chunk, hidden), BF16)] * dp),
-        product,
-        weights,
-        scratch_shapes=in_order,
-    )(keep, swap, *far_grads[::-1], near_in, down_mat)
-    grad_sums = trade(part_grad)
     pre_mine = call(
         functools.partial(grad_pre_kernel, dp),
-        shape((2, chunk, hidden), BF16),
+        shape((2, 2, part, hidden), BF16),
         0,
-        6 * dp * chunk * hidden,
-    )(*sums, *grad_sums)
+        6 * slots * hidden,
+    )(*sums_early, *sums_late)
     pre = trade([pre_mine] * dp)
     act, out_keep, out_swap = call(
         functools.partial(expert_out_kernel, dp),
@@ -314,7 +323,7 @@
         weights,
         scratch_shapes=in_order,
     )(*acts, down_mat)
-    back = [far[0]] * (half - 1)
+    back = [pair] * (half - 1)
     out_swap = partner(out_swap, "expert", 1)
     out_near, *out_far = call(pack_back_kernel, back, 0, 8 * slots)(out_keep, out_swap)
     out_far = [partner(value, "expert", 2 * (2 + k)) for k, value in enumerate(out_far)]
@@ -331,19 +340,16 @@
     grad_to = call(pack_back_kernel, back, 0, 8 * slots)(grad_keep, grad_swap)
     grad_back = [partner(value, "expert", 2 * (1 + k)) for k, value in enumerate(grad_to)]
 
-    (grad_down,) = call(
-        functools.partial(grads_kernel, 1),
-        [shape((hidden, features), BF16)],
-        product,
-        weights,
-    )(act, grads)
+    grad_down = call(
+        grad_down_kernel, shape((hidden, features), BF16), product, weights
+    )(act, grads_early, grads_late)
     grad_gate, grad_up = call(
-        functools.partial(grads_kernel, 2),
+        grad_gate_up_kernel,
         [shape((features, hidden), BF16)] * 2,
         2 * product,
         2 * weights,
-        in_specs=[HERE] * 3 + [ANY],
-    )(rows, gate_pre, up_pre, grad_to[0])
+        in_specs=[HERE] * 4 + [ANY],
+    )(rows_early, rows_late, gate_pre, up_pre, grad_to[0])
 
     full = shape((tok_rows, features), BF16)
     mixed = call(

time: 82 us -> 87.1 us (1.062)
  waiting for transfers between devices: 31 us -> 34.8 us
  local copies, waits for them, and re-layouts: 0.03 us -> 1.68 us
  starting transfers between devices: 34.7 us -> 33.6 us
    ppermute x26 -> x24, waiting for transfers between devices: 31 us -> 34.8 us  [partner(): return lax.ppermute(value, axis, [(i, i ^ k) for i in range(size)])]
    unnamed x12, local copies, waits for them, and re-layouts: 0.03 us -> 1.68 us
    ppermute x26 -> x24, starting transfers between devices: 34.7 us -> 33.6 us  [partner(): return lax.ppermute(value, axis, [(i, i ^ k) for i in range(size)])]
  transfers between devices with their start and end apart: 26 -> 24, of which waited for: 13 -> 11; matrix products, arithmetic and copies ran while one was open for 0% -> 0% of each run, Pallas kernels for 10% -> 11%
where the time goes in v9:
time: 87.1 us; the launch traced here: 86.9 us
  waiting for transfers between devices  34.8 us (40%)
  starting transfers between devices  33.6 us (39%)
  Pallas kernels  16.1 us (18%)
  local copies, waits for them, and re-layouts  1.68 us (2%)
    ppermute x24, waiting for transfers between devices, partner(): return lax.ppermute(value, axis, [(i, i ^ k) for i in range(size)])  34.8 us
    ppermute x24, starting transfers between devices, partner(): return lax.ppermute(value, axis, [(i, i ^ k) for i in range(size)])  33.6 us
    pallas_call x1, Pallas kernels, body(): call(functools.partial(route_kernel, experts), outs, 4 * slots * tok_rows...  3.19 us
    pallas_call x2, Pallas kernels, partial_sums(): call(functools.partial(partial_kernel, dp, own, len(found)), (cut, cut, *...  2.63 us
    pallas_call x1, Pallas kernels, body(): call(grad_gate_up_kernel, [shape((features, hidden), BF16)] * 2, 2 * prod...  2.54 us
    pallas_call x1, Pallas kernels, body(): call(grad_down_kernel, shape((hidden, features), BF16), product, weights)  1.97 us
  transfers between devices with their start and end apart: 24, of which 11 were waited for; matrix products, arithmetic and copies ran while one was open for 0% of the time, Pallas kernels for 11%

profile of v9, /device:TPU:0, one launch (start us, length us, event | category | flops | bytes accessed | tf_op | source)
XLA Modules:
  0.0 86.9 jit_solution(13444162716653412824)
XLA Ops:
  0.6 3.2 %shard_map.110 = (bf16[256,512]{1,0:T(8,128)(2,1)}, f32[256,1]{1,0:T(8,128)}, bf16[2,4,32,896]{3,2,1,0:T(8,128)(2,1)}, bf16[2,4,32,896]{3,2,1,0:T(8,128)(2,1)}) custom-call(s32[8,512]{1,0:T(8,128)} %bitcast.14, f32[8,512]{1,0:T(8,128)} %bitcast.15, bf16[512,896]{1,0:T(8,128)(2,1)} %refs_2_.1, bf16[512,896]{1,0:T(8,128)(2,1)} %refs_3_.1), custom_call_target="tpu_custom_call" | custom-call | flops 469762048 | bytes 3670016 | tf_op jit(solution)/shard_map/pallas_call | solution.py:272
  4.4 1.6 %copy-done.3 = bf16[1,1024,896]{2,1,0:T(8,128)(2,1)S(1)} copy-done((bf16[1,1024,896]{2,1,0:T(8,128)(2,1)S(1)}, bf16[1,1024,896]{2,1,0:T(8,128)(2,1)}, u32[]{:S(2)}) %copy-start.3) | copy-done | bytes 1835032
  6.4 2.7 %collective-permute-start.1 = (bf16[2,2,32,896]{3,2,1,0:T(8,128)(2,1)S(1)}, bf16[2,2,32,896]{3,2,1,0:T(8,128)(2,1)S(1)}, u32[]{:S(2)}, u32[]{:S(2)}) collective-permute-start(bf16[2,2,32,896]{3,2,1,0:T(8,128)(2,1)S(1)} %get-tuple-element.63), channel_id=1, source_target_pairs={{0,2},{1,3},{2,0},{3,1},{4,6},{5,7},{6,4},{7,5},{8,10},{9,11},{10,... | collective-permute-start | bytes 688136 | tf_op jit(solution)/shard_map/ppermute | solution.py:237
  9.1 2.6 %collective-permute-start.5 = (bf16[2,2,32,896]{3,2,1,0:T(8,128)(2,1)S(1)}, bf16[2,2,32,896]{3,2,1,0:T(8,128)(2,1)S(1)}, u32[]{:S(2)}, u32[]{:S(2)}) collective-permute-start(bf16[2,2,32,896]{3,2,1,0:T(8,128)(2,1)S(1)} %get-tuple-element.70), channel_id=1, source_target_pairs={{0,4},{1,5},{2,6},{3,7},{4,0},{5,1},{6,2},{7,3},{8,12},{9,13},{10,... | collective-permute-start | bytes 688136 | tf_op jit(solution)/shard_map/ppermute | solution.py:237
  11.7 7.8 %collective-permute-done.1.refs_2_ = bf16[2,2,32,896]{3,2,1,0:T(8,128)(2,1)S(1)} collective-permute-done((bf16[2,2,32,896]{3,2,1,0:T(8,128)(2,1)S(1)}, bf16[2,2,32,896]{3,2,1,0:T(8,128)(2,1)S(1)}, u32[]{:S(2)}, u32[]{:S(2)}) %collective-permute-start.1) | collective-permute-done | bytes 229408 | tf_op jit(solution)/shard_map/ppermute | solution.py:237
  20.8 1.7 %collective-permute-start.2 = (bf16[3,32,1024]{2,1,0:T(8,128)(2,1)S(1)}, bf16[3,32,1024]{2,1,0:T(8,128)(2,1)S(1)}, u32[]{:S(2)}, u32[]{:S(2)}) collective-permute-start(bf16[3,32,1024]{2,1,0:T(8,128)(2,1)S(1)} %get-tuple-element.67), channel_id=1, source_target_pairs={{0,8},{8,0},{16,24},{24,16},{1,9},{9,1},{17,25},{25,17},{2,10},{10... | collective-permute-start | bytes 589832 | tf_op jit(solution)/shard_map/ppermute | solution.py:237
  22.6 1.5 %collective-permute-start.3 = (bf16[3,32,1024]{2,1,0:T(8,128)(2,1)S(1)}, bf16[3,32,1024]{2,1,0:T(8,128)(2,1)S(1)}, u32[]{:S(2)}, u32[]{:S(2)}) collective-permute-start(bf16[3,32,1024]{2,1,0:T(8,128)(2,1)S(1)} %get-tuple-element.68), channel_id=1, source_target_pairs={{0,16},{8,24},{16,0},{24,8},{1,17},{9,25},{17,1},{25,9},{2,18},{10... | collective-permute-start | bytes 589832 | tf_op jit(solution)/shard_map/ppermute | solution.py:237
  24.4 3.9 %collective-permute-done.5.refs_0_ = bf16[2,2,32,896]{3,2,1,0:T(8,128)(2,1)S(1)} collective-permute-done((bf16[2,2,32,896]{3,2,1,0:T(8,128)(2,1)S(1)}, bf16[2,2,32,896]{3,2,1,0:T(8,128)(2,1)S(1)}, u32[]{:S(2)}, u32[]{:S(2)}) %collective-permute-start.5) | collective-permute-done | bytes 229408 | tf_op jit(solution)/shard_map/ppermute | solution.py:237
  29.7 1.6 %collective-permute-start.7 = (bf16[3,32,1024]{2,1,0:T(8,128)(2,1)S(1)}, bf16[3,32,1024]{2,1,0:T(8,128)(2,1)S(1)}, u32[]{:S(2)}, u32[]{:S(2)}) collective-permute-start(bf16[3,32,1024]{2,1,0:T(8,128)(2,1)S(1)} %get-tuple-element.74), channel_id=1, source_target_pairs={{0,8},{8,0},{16,24},{24,16},{1,9},{9,1},{17,25},{25,17},{2,10},{10... | collective-permute-start | bytes 589832 | tf_op jit(solution)/shard_map/ppermute | solution.py:237
  31.2 1.5 %collective-permute-start.8 = (bf16[3,32,1024]{2,1,0:T(8,128)(2,1)S(1)}, bf16[3,32,1024]{2,1,0:T(8,128)(2,1)S(1)}, u32[]{:S(2)}, u32[]{:S(2)}) collective-permute-start(bf16[3,32,1024]{2,1,0:T(8,128)(2,1)S(1)} %get-tuple-element.75), channel_id=1, source_target_pairs={{0,16},{8,24},{16,0},{24,8},{1,17},{9,25},{17,1},{25,9},{2,18},{10... | collective-permute-start | bytes 589832 | tf_op jit(solution)/shard_map/ppermute | solution.py:237
  33.5 4.1 %collective-permute-done.7.refs_5_ = bf16[3,32,1024]{2,1,0:T(8,128)(2,1)S(1)} collective-permute-done((bf16[3,32,1024]{2,1,0:T(8,128)(2,1)S(1)}, bf16[3,32,1024]{2,1,0:T(8,128)(2,1)S(1)}, u32[]{:S(2)}, u32[]{:S(2)}) %collective-permute-start.7) | collective-permute-done | bytes 196640 | tf_op jit(solution)/shard_map/ppermute | solution.py:237
  37.6 3.6 %collective-permute-done.8.refs_6_ = bf16[3,32,1024]{2,1,0:T(8,128)(2,1)S(1)} collective-permute-done((bf16[3,32,1024]{2,1,0:T(8,128)(2,1)S(1)}, bf16[3,32,1024]{2,1,0:T(8,128)(2,1)S(1)}, u32[]{:S(2)}, u32[]{:S(2)}) %collective-permute-start.8) | collective-permute-done | bytes 196640 | tf_op jit(solution)/shard_map/ppermute | solution.py:237
  44.9 2.4 %collective-permute-done.10.refs_1_ = bf16[2,32,1024]{2,1,0:T(8,128)(2,1)S(1)} collective-permute-done((bf16[2,32,1024]{2,1,0:T(8,128)(2,1)S(1)}, bf16[2,32,1024]{2,1,0:T(8,128)(2,1)S(1)}, u32[]{:S(2)}, u32[]{:S(2)}) %collective-permute-start.10) | collective-permute-done | bytes 131104 | tf_op jit(solution)/shard_map/ppermute | solution.py:237
  47.7 1.7 %collective-permute-done.12.refs_3_ = bf16[2,32,1024]{2,1,0:T(8,128)(2,1)S(1)} collective-permute-done((bf16[2,32,1024]{2,1,0:T(8,128)(2,1)S(1)}, bf16[2,32,1024]{2,1,0:T(8,128)(2,1)S(1)}, u32[]{:S(2)}, u32[]{:S(2)}) %collective-permute-start.12) | collective-permute-done | bytes 131104 | tf_op jit(solution)/shard_map/ppermute | solution.py:237
  50.5 1.6 %collective-permute-start.14 = (bf16[2,2,32,1024]{3,2,1,0:T(8,128)(2,1)S(1)}, bf16[2,2,32,1024]{3,2,1,0:T(8,128)(2,1)S(1)}, u32[]{:S(2)}, u32[]{:S(2)}) collective-permute-start(bf16[2,2,32,1024]{3,2,1,0:T(8,128)(2,1)S(1)} %shard_map.117.refs_0_), channel_id=1, source_target_pairs={{0,8},{8,0},{16,24},{24,16},{1,9},{9,1},{17,25},{25,17},{2,10},{10... | collective-permute-start | bytes 786440 | tf_op jit(solution)/shard_map/ppermute | solution.py:237
  54.1 5.5 %collective-permute-start.17 = (bf16[2,32,896]{2,1,0:T(8,128)(2,1)S(1)}, bf16[2,32,896]{2,1,0:T(8,128)(2,1)S(1)}, u32[]{:S(2)}, u32[]{:S(2)}) collective-permute-start(bf16[2,32,896]{2,1,0:T(8,128)(2,1)S(1)} %get-tuple-element.79), channel_id=1, source_target_pairs={{0,4},{1,5},{2,6},{3,7},{4,0},{5,1},{6,2},{7,3},{8,12},{9,13},{10,... | collective-permute-start | bytes 344072 | tf_op jit(solution)/shard_map/ppermute | solution.py:237
  61.0 5.1 %collective-permute-done.15.refs_2_ = bf16[2,2,32,1024]{3,2,1,0:T(8,128)(2,1)S(1)} collective-permute-done((bf16[2,2,32,1024]{3,2,1,0:T(8,128)(2,1)S(1)}, bf16[2,2,32,1024]{3,2,1,0:T(8,128)(2,1)S(1)}, u32[]{:S(2)}, u32[]{:S(2)}) %collective-permute-start.15) | collective-permute-done | bytes 262176 | tf_op jit(solution)/shard_map/ppermute | solution.py:237
  66.1 2.4 %collective-permute-done.17.refs_3_ = bf16[2,32,896]{2,1,0:T(8,128)(2,1)S(1)} collective-permute-done((bf16[2,32,896]{2,1,0:T(8,128)(2,1)S(1)}, bf16[2,32,896]{2,1,0:T(8,128)(2,1)S(1)}, u32[]{:S(2)}, u32[]{:S(2)}) %collective-permute-start.17) | collective-permute-done | bytes 114720 | tf_op jit(solution)/shard_map/ppermute | solution.py:237
  70.0 2.1 %collective-permute-start.19 = (bf16[2,32,896]{2,1,0:T(8,128)(2,1)S(1)}, bf16[2,32,896]{2,1,0:T(8,128)(2,1)S(1)}, u32[]{:S(2)}, u32[]{:S(2)}) collective-permute-start(bf16[2,32,896]{2,1,0:T(8,128)(2,1)S(1)} %get-tuple-element.83), channel_id=1, source_target_pairs={{0,2},{1,3},{2,0},{3,1},{4,6},{5,7},{6,4},{7,5},{8,10},{9,11},{10,... | collective-permute-start | bytes 344072 | tf_op jit(solution)/shard_map/ppermute | solution.py:237
  72.1 2.5 %collective-permute-start.21 = (bf16[2,32,896]{2,1,0:T(8,128)(2,1)S(1)}, bf16[2,32,896]{2,1,0:T(8,128)(2,1)S(1)}, u32[]{:S(2)}, u32[]{:S(2)}) collective-permute-start(bf16[2,32,896]{2,1,0:T(8,128)(2,1)S(1)} %get-tuple-element.91), channel_id=1, source_target_pairs={{0,6},{1,7},{2,4},{3,5},{4,2},{5,3},{6,0},{7,1},{8,14},{9,15},{10,... | collective-permute-start | bytes 344072 | tf_op jit(solution)/shard_map/ppermute | solution.py:237
  75.0 1.5 %collective-permute-start.23 = (bf16[2,32,896]{2,1,0:T(8,128)(2,1)S(1)}, bf16[2,32,896]{2,1,0:T(8,128)(2,1)S(1)}, u32[]{:S(2)}, u32[]{:S(2)}) collective-permute-start(bf16[2,32,896]{2,1,0:T(8,128)(2,1)S(1)} %get-tuple-element.90.refs_5_._), channel_id=1, source_target_pairs={{0,2},{1,3},{2,0},{3,1},{4,6},{5,7},{6,4},{7,5},{8,10},{9,11},{10,... | collective-permute-start | bytes 344072 | tf_op jit(solution)/shard_map/ppermute | solution.py:237
  76.5 2.0 %shard_map.124 = bf16[1024,896]{1,0:T(8,128)(2,1)} custom-call(bf16[256,1024]{1,0:T(8,128)(2,1)S(1)} %get-tuple-element.98.act_ref, bf16[128,896]{1,0:T(8,128)(2,1)S(1)} %get-tuple-element.99.early_ref, bf16[128,896]{1,0:T(8,128)(2,1)S(1)} %get-tuple-element.100.late_ref), custom_call_target="tpu_custom_call" | custom-call | flops 469762048 | bytes 1835008 | tf_op jit(solution)/shard_map/pallas_call | solution.py:343
  80.0 2.5 %shard_map.123 = (bf16[896,1024]{1,0:T(8,128)(2,1)}, bf16[896,1024]{1,0:T(8,128)(2,1)}) custom-call(bf16[128,896]{1,0:T(8,128)(2,1)S(1)} %get-tuple-element.72.refs_5_.early_ref, bf16[128,896]{1,0:T(8,128)(2,1)S(1)} %get-tuple-element.93.late_ref, bf16[256,1024]{1,0:T(8,128)(2,1)S(1)} %get-tuple-element.94.gate_pre_ref, ...), custom_call_target="tpu_custom_call" | custom-call | flops 939524096 | bytes 3670016 | tf_op jit(solution)/shard_map/pallas_call | solution.py:346
  82.5 3.0 %collective-permute-done.22.refs_3_ = bf16[2,32,896]{2,1,0:T(8,128)(2,1)S(1)} collective-permute-done((bf16[2,32,896]{2,1,0:T(8,128)(2,1)S(1)}, bf16[2,32,896]{2,1,0:T(8,128)(2,1)S(1)}, u32[]{:S(2)}, u32[]{:S(2)}) %collective-permute-start.22) | collective-permute-done | bytes 114720 | tf_op jit(solution)/shard_map/ppermute | solution.py:237
  (51 shorter events, 17.8 us)
Async XLA Ops:
  3.9 2.4 %collective-permute-start = (bf16[2,4,32,896]{3,2,1,0:T(8,128)(2,1)}, bf16[2,4,32,896]{3,2,1,0:T(8,128)(2,1)S(1)}, u32[]{:S(2)}, u32[]{:S(2)}) collective-permute-start(bf16[2,4,32,896]{3,2,1,0:T(8,128)(2,1)} %get-tuple-element.57), channel_id=1, source_target_pairs={{0,1},{1,0},{2,3},{3,2},{4,5},{5,4},{6,7},{7,6},{8,9},{9,8},{10,11... | collective-permute-start | bytes 1376264 | tf_op jit(solution)/shard_map/ppermute | solution.py:237
  6.4 13.1 %collective-permute-start.1 = (bf16[2,2,32,896]{3,2,1,0:T(8,128)(2,1)S(1)}, bf16[2,2,32,896]{3,2,1,0:T(8,128)(2,1)S(1)}, u32[]{:S(2)}, u32[]{:S(2)}) collective-permute-start(bf16[2,2,32,896]{3,2,1,0:T(8,128)(2,1)S(1)} %get-tuple-element.63), channel_id=1, source_target_pairs={{0,2},{1,3},{2,0},{3,1},{4,6},{5,7},{6,4},{7,5},{8,10},{9,11},{10,... | collective-permute-start | bytes 688136 | tf_op jit(solution)/shard_map/ppermute | solution.py:237
  9.1 19.2 %collective-permute-start.5 = (bf16[2,2,32,896]{3,2,1,0:T(8,128)(2,1)S(1)}, bf16[2,2,32,896]{3,2,1,0:T(8,128)(2,1)S(1)}, u32[]{:S(2)}, u32[]{:S(2)}) collective-permute-start(bf16[2,2,32,896]{3,2,1,0:T(8,128)(2,1)S(1)} %get-tuple-element.70), channel_id=1, source_target_pairs={{0,4},{1,5},{2,6},{3,7},{4,0},{5,1},{6,2},{7,3},{8,12},{9,13},{10,... | collective-permute-start | bytes 688136 | tf_op jit(solution)/shard_map/ppermute | solution.py:237
  11.7 16.6 %collective-permute-start.6 = (bf16[2,2,32,896]{3,2,1,0:T(8,128)(2,1)S(1)}, bf16[2,2,32,896]{3,2,1,0:T(8,128)(2,1)S(1)}, u32[]{:S(2)}, u32[]{:S(2)}) collective-permute-start(bf16[2,2,32,896]{3,2,1,0:T(8,128)(2,1)S(1)} %get-tuple-element.71), channel_id=1, source_target_pairs={{0,6},{1,7},{2,4},{3,5},{4,2},{5,3},{6,0},{7,1},{8,14},{9,15},{10,... | collective-permute-start | bytes 688136 | tf_op jit(solution)/shard_map/ppermute | solution.py:237
  20.8 11.9 %collective-permute-start.2 = (bf16[3,32,1024]{2,1,0:T(8,128)(2,1)S(1)}, bf16[3,32,1024]{2,1,0:T(8,128)(2,1)S(1)}, u32[]{:S(2)}, u32[]{:S(2)}) collective-permute-start(bf16[3,32,1024]{2,1,0:T(8,128)(2,1)S(1)} %get-tuple-element.67), channel_id=1, source_target_pairs={{0,8},{8,0},{16,24},{24,16},{1,9},{9,1},{17,25},{25,17},{2,10},{10... | collective-permute-start | bytes 589832 | tf_op jit(solution)/shard_map/ppermute | solution.py:237
  22.6 10.7 %collective-permute-start.3 = (bf16[3,32,1024]{2,1,0:T(8,128)(2,1)S(1)}, bf16[3,32,1024]{2,1,0:T(8,128)(2,1)S(1)}, u32[]{:S(2)}, u32[]{:S(2)}) collective-permute-start(bf16[3,32,1024]{2,1,0:T(8,128)(2,1)S(1)} %get-tuple-element.68), channel_id=1, source_target_pairs={{0,16},{8,24},{16,0},{24,8},{1,17},{9,25},{17,1},{25,9},{2,18},{10... | collective-permute-start | bytes 589832 | tf_op jit(solution)/shard_map/ppermute | solution.py:237
  24.1 9.4 %collective-permute-start.4 = (bf16[3,32,1024]{2,1,0:T(8,128)(2,1)S(1)}, bf16[3,32,1024]{2,1,0:T(8,128)(2,1)S(1)}, u32[]{:S(2)}, u32[]{:S(2)}) collective-permute-start(bf16[3,32,1024]{2,1,0:T(8,128)(2,1)S(1)} %get-tuple-element.69), channel_id=1, source_target_pairs={{0,24},{8,16},{16,8},{24,0},{1,25},{9,17},{17,9},{25,1},{2,26},{10... | collective-permute-start | bytes 589832 | tf_op jit(solution)/shard_map/ppermute | solution.py:237
  29.7 7.9 %collective-permute-start.7 = (bf16[3,32,1024]{2,1,0:T(8,128)(2,1)S(1)}, bf16[3,32,1024]{2,1,0:T(8,128)(2,1)S(1)}, u32[]{:S(2)}, u32[]{:S(2)}) collective-permute-start(bf16[3,32,1024]{2,1,0:T(8,128)(2,1)S(1)} %get-tuple-element.74), channel_id=1, source_target_pairs={{0,8},{8,0},{16,24},{24,16},{1,9},{9,1},{17,25},{25,17},{2,10},{10... | collective-permute-start | bytes 589832 | tf_op jit(solution)/shard_map/ppermute | solution.py:237
  31.2 10.0 %collective-permute-start.8 = (bf16[3,32,1024]{2,1,0:T(8,128)(2,1)S(1)}, bf16[3,32,1024]{2,1,0:T(8,128)(2,1)S(1)}, u32[]{:S(2)}, u32[]{:S(2)}) collective-permute-start(bf16[3,32,1024]{2,1,0:T(8,128)(2,1)S(1)} %get-tuple-element.75), channel_id=1, source_target_pairs={{0,16},{8,24},{16,0},{24,8},{1,17},{9,25},{17,1},{25,9},{2,18},{10... | collective-permute-start | bytes 589832 | tf_op jit(solution)/shard_map/ppermute | solution.py:237
  32.7 8.4 %collective-permute-start.9 = (bf16[3,32,1024]{2,1,0:T(8,128)(2,1)S(1)}, bf16[3,32,1024]{2,1,0:T(8,128)(2,1)S(1)}, u32[]{:S(2)}, u32[]{:S(2)}) collective-permute-start(bf16[3,32,1024]{2,1,0:T(8,128)(2,1)S(1)} %get-tuple-element.76), channel_id=1, source_target_pairs={{0,24},{8,16},{16,8},{24,0},{1,25},{9,17},{17,9},{25,1},{2,26},{10... | collective-permute-start | bytes 589832 | tf_op jit(solution)/shard_map/ppermute | solution.py:237
  41.4 5.9 %collective-permute-start.10 = (bf16[2,32,1024]{2,1,0:T(8,128)(2,1)S(1)}, bf16[2,32,1024]{2,1,0:T(8,128)(2,1)S(1)}, u32[]{:S(2)}, u32[]{:S(2)}) collective-permute-start(bf16[2,32,1024]{2,1,0:T(8,128)(2,1)S(1)} %shard_map.115.refs_0_), channel_id=1, source_target_pairs={{0,8},{8,0},{16,24},{24,16},{1,9},{9,1},{17,25},{25,17},{2,10},{10... | collective-permute-start | bytes 393224 | tf_op jit(solution)/shard_map/ppermute | solution.py:237
  42.7 5.0 %collective-permute-start.11 = (bf16[2,32,1024]{2,1,0:T(8,128)(2,1)S(1)}, bf16[2,32,1024]{2,1,0:T(8,128)(2,1)S(1)}, u32[]{:S(2)}, u32[]{:S(2)}) collective-permute-start(bf16[2,32,1024]{2,1,0:T(8,128)(2,1)S(1)} %shard_map.115.refs_0_), channel_id=1, source_target_pairs={{0,16},{8,24},{16,0},{24,8},{1,17},{9,25},{17,1},{25,9},{2,18},{10... | collective-permute-start | bytes 393224 | tf_op jit(solution)/shard_map/ppermute | solution.py:237
  43.5 5.9 %collective-permute-start.12 = (bf16[2,32,1024]{2,1,0:T(8,128)(2,1)S(1)}, bf16[2,32,1024]{2,1,0:T(8,128)(2,1)S(1)}, u32[]{:S(2)}, u32[]{:S(2)}) collective-permute-start(bf16[2,32,1024]{2,1,0:T(8,128)(2,1)S(1)} %shard_map.115.refs_0_), channel_id=1, source_target_pairs={{0,24},{8,16},{16,8},{24,0},{1,25},{9,17},{17,9},{25,1},{2,26},{10... | collective-permute-start | bytes 393224 | tf_op jit(solution)/shard_map/ppermute | solution.py:237
  50.1 3.9 %collective-permute-start.13 = (bf16[4,32,896]{2,1,0:T(8,128)(2,1)S(1)}, bf16[4,32,896]{2,1,0:T(8,128)(2,1)S(1)}, u32[]{:S(2)}, u32[]{:S(2)}) collective-permute-start(bf16[4,32,896]{2,1,0:T(8,128)(2,1)S(1)} %get-tuple-element.78), channel_id=1, source_target_pairs={{0,1},{1,0},{2,3},{3,2},{4,5},{5,4},{6,7},{7,6},{8,9},{9,8},{10,11... | collective-permute-start | bytes 688136 | tf_op jit(solution)/shard_map/ppermute | solution.py:237
  50.5 10.5 %collective-permute-start.14 = (bf16[2,2,32,1024]{3,2,1,0:T(8,128)(2,1)S(1)}, bf16[2,2,32,1024]{3,2,1,0:T(8,128)(2,1)S(1)}, u32[]{:S(2)}, u32[]{:S(2)}) collective-permute-start(bf16[2,2,32,1024]{3,2,1,0:T(8,128)(2,1)S(1)} %shard_map.117.refs_0_), channel_id=1, source_target_pairs={{0,8},{8,0},{16,24},{24,16},{1,9},{9,1},{17,25},{25,17},{2,10},{10... | collective-permute-start | bytes 786440 | tf_op jit(solution)/shard_map/ppermute | solution.py:237
  52.1 14.0 %collective-permute-start.15 = (bf16[2,2,32,1024]{3,2,1,0:T(8,128)(2,1)S(1)}, bf16[2,2,32,1024]{3,2,1,0:T(8,128)(2,1)S(1)}, u32[]{:S(2)}, u32[]{:S(2)}) collective-permute-start(bf16[2,2,32,1024]{3,2,1,0:T(8,128)(2,1)S(1)} %shard_map.117.refs_0_), channel_id=1, source_target_pairs={{0,16},{8,24},{16,0},{24,8},{1,17},{9,25},{17,1},{25,9},{2,18},{10... | collective-permute-start | bytes 786440 | tf_op jit(solution)/shard_map/ppermute | solution.py:237
  52.6 13.5 %collective-permute-start.16 = (bf16[2,2,32,1024]{3,2,1,0:T(8,128)(2,1)S(1)}, bf16[2,2,32,1024]{3,2,1,0:T(8,128)(2,1)S(1)}, u32[]{:S(2)}, u32[]{:S(2)}) collective-permute-start(bf16[2,2,32,1024]{3,2,1,0:T(8,128)(2,1)S(1)} %shard_map.117.refs_0_), channel_id=1, source_target_pairs={{0,24},{8,16},{16,8},{24,0},{1,25},{9,17},{17,9},{25,1},{2,26},{10... | collective-permute-start | bytes 786440 | tf_op jit(solution)/shard_map/ppermute | solution.py:237
  54.1 14.4 %collective-permute-start.17 = (bf16[2,32,896]{2,1,0:T(8,128)(2,1)S(1)}, bf16[2,32,896]{2,1,0:T(8,128)(2,1)S(1)}, u32[]{:S(2)}, u32[]{:S(2)}) collective-permute-start(bf16[2,32,896]{2,1,0:T(8,128)(2,1)S(1)} %get-tuple-element.79), channel_id=1, source_target_pairs={{0,4},{1,5},{2,6},{3,7},{4,0},{5,1},{6,2},{7,3},{8,12},{9,13},{10,... | collective-permute-start | bytes 344072 | tf_op jit(solution)/shard_map/ppermute | solution.py:237
  59.6 8.9 %collective-permute-start.18 = (bf16[2,32,896]{2,1,0:T(8,128)(2,1)S(1)}, bf16[2,32,896]{2,1,0:T(8,128)(2,1)S(1)}, u32[]{:S(2)}, u32[]{:S(2)}) collective-permute-start(bf16[2,32,896]{2,1,0:T(8,128)(2,1)S(1)} %get-tuple-element.80), channel_id=1, source_target_pairs={{0,6},{1,7},{2,4},{3,5},{4,2},{5,3},{6,0},{7,1},{8,14},{9,15},{10,... | collective-permute-start | bytes 344072 | tf_op jit(solution)/shard_map/ppermute | solution.py:237
  69.9 2.2 %collective-permute-start.20 = (bf16[4,32,896]{2,1,0:T(8,128)(2,1)S(1)}, bf16[4,32,896]{2,1,0:T(8,128)(2,1)S(1)}, u32[]{:S(2)}, u32[]{:S(2)}) collective-permute-start(bf16[4,32,896]{2,1,0:T(8,128)(2,1)S(1)} %get-tuple-element.89), channel_id=1, source_target_pairs={{0,1},{1,0},{2,3},{3,2},{4,5},{5,4},{6,7},{7,6},{8,9},{9,8},{10,11... | collective-permute-start | bytes 688136 | tf_op jit(solution)/shard_map/ppermute | solution.py:237
  70.0 8.6 %collective-permute-start.19 = (bf16[2,32,896]{2,1,0:T(8,128)(2,1)S(1)}, bf16[2,32,896]{2,1,0:T(8,128)(2,1)S(1)}, u32[]{:S(2)}, u32[]{:S(2)}) collective-permute-start(bf16[2,32,896]{2,1,0:T(8,128)(2,1)S(1)} %get-tuple-element.83), channel_id=1, source_target_pairs={{0,2},{1,3},{2,0},{3,1},{4,6},{5,7},{6,4},{7,5},{8,10},{9,11},{10,... | collective-permute-start | bytes 344072 | tf_op jit(solution)/shard_map/ppermute | solution.py:237
  72.1 10.4 %collective-permute-start.21 = (bf16[2,32,896]{2,1,0:T(8,128)(2,1)S(1)}, bf16[2,32,896]{2,1,0:T(8,128)(2,1)S(1)}, u32[]{:S(2)}, u32[]{:S(2)}) collective-permute-start(bf16[2,32,896]{2,1,0:T(8,128)(2,1)S(1)} %get-tuple-element.91), channel_id=1, source_target_pairs={{0,6},{1,7},{2,4},{3,5},{4,2},{5,3},{6,0},{7,1},{8,14},{9,15},{10,... | collective-permute-start | bytes 344072 | tf_op jit(solution)/shard_map/ppermute | solution.py:237
  74.6 10.9 %collective-permute-start.22 = (bf16[2,32,896]{2,1,0:T(8,128)(2,1)S(1)}, bf16[2,32,896]{2,1,0:T(8,128)(2,1)S(1)}, u32[]{:S(2)}, u32[]{:S(2)}) collective-permute-start(bf16[2,32,896]{2,1,0:T(8,128)(2,1)S(1)} %get-tuple-element.92), channel_id=1, source_target_pairs={{0,4},{1,5},{2,6},{3,7},{4,0},{5,1},{6,2},{7,3},{8,12},{9,13},{10,... | collective-permute-start | bytes 344072 | tf_op jit(solution)/shard_map/ppermute | solution.py:237
  75.0 10.5 %collective-permute-start.23 = (bf16[2,32,896]{2,1,0:T(8,128)(2,1)S(1)}, bf16[2,32,896]{2,1,0:T(8,128)(2,1)S(1)}, u32[]{:S(2)}, u32[]{:S(2)}) collective-permute-start(bf16[2,32,896]{2,1,0:T(8,128)(2,1)S(1)} %get-tuple-element.90.refs_5_._), channel_id=1, source_target_pairs={{0,2},{1,3},{2,0},{3,1},{4,6},{5,7},{6,4},{7,5},{8,10},{9,11},{10,... | collective-permute-start | bytes 344072 | tf_op jit(solution)/shard_map/ppermute | solution.py:237
  (6 other events, 40.8 us)

commit v10 on v8

--- a/solution.py
+++ b/solution.py
@@ -13,6 +13,7 @@
 ANY = pl.BlockSpec(memory_space=pl.ANY)
 HERE = pl.BlockSpec()
 VMEM_LIMIT = 24 * MIB
+STAGE = 2 * 10**10
 ROUTE_LIMIT = 59 * MIB
 
 
@@ -47,11 +48,17 @@
         swap_ref[(*at, k)] = value[(2 * k + 1) * rows : (2 * k + 2) * rows]
 
 
+def own_blocks(own_refs, value):
+    for k, own_ref in enumerate(own_refs):
+        rows = own_ref.shape[0]
+        own_ref[...] = value[(2 * k + 4) * rows : (2 * k + 5) * rows]
+
+
 def route_kernel(experts, *refs):
-    pick_ref, weight_ref, keep_ref, swap_ref = refs[4:8]
-    ids_ref, gates_ref, tokens_ref, grad_ref, sems = refs[8:]
+    pick_ref, weight_ref, keep_ref, swap_ref, *own_refs = refs[4:-5]
+    ids_ref, gates_ref, tokens_ref, grad_ref, sems = refs[-5:]
     copies = [
-        pltpu.make_async_copy(refs[k], refs[8 + k], sems.at[k]) for k in range(4)
+        pltpu.make_async_copy(refs[k], refs[k - 5], sems.at[k]) for k in range(4)
     ]
     for copy in copies:
         copy.start()
@@ -80,6 +87,7 @@
     copies[2].wait()
     rows = mm(pick, tokens_ref[...], ((1,), (0,))).astype(BF16)
     split_cores(keep_ref, swap_ref, rows, 0)
+    own_blocks(own_refs, rows)
     copies[3].wait()
     rows = (slot_weight * mm(pick, grad_ref[...], ((1,), (0,)))).astype(BF16)
     split_cores(keep_ref, swap_ref, rows, 1)
@@ -87,26 +95,50 @@
 
 def load_kernel(from_ref, to_ref):
     to_ref[...] = from_ref[...]
+
+
+def stage_kernel(*refs):
+    rows = refs[0].shape[0]
+    refs[-1][...] = join_rows(refs[: refs[-1].shape[0] // rows])
 
 
 def pack_kernel(half, keep_ref, swap_ref, near_ref, *far_refs):
     for at in range(2):
         near_ref[at, 0] = keep_ref[at, 1]
         near_ref[at, 1] = swap_ref[at, 1]
-        for k in range(2, half):
-            far_refs[at * (half - 2) + k - 2][0] = keep_ref[at, k]
-            far_refs[at * (half - 2) + k - 2][1] = swap_ref[at, k]
+    for k in range(2, half):
+        far_refs[k - 2][...] = swap_ref[0, k]
+        far_refs[half + k - 4][0] = keep_ref[1, k]
+        far_refs[half + k - 4][1] = swap_ref[1, k]
 
 
 def pack_back_kernel(keep_ref, swap_ref, *out_refs):
     for k, out_ref in enumerate(out_refs):
-        out_ref[0] = keep_ref[k + 1]
-        out_ref[1] = swap_ref[k + 1]
-
-
-def pieces(at, keep_ref, swap_ref, *refs):
+        out_ref[0] = keep_ref[k + 2]
+        out_ref[1] = swap_ref[k + 2]
+
+
+def pack_last_kernel(out_keep_ref, out_swap_ref, keep_ref, swap_ref, near_ref, *far_refs):
+    near_ref[0, 0] = out_keep_ref[1]
+    near_ref[0, 1] = out_swap_ref[1]
+    near_ref[1, 0] = keep_ref[1]
+    near_ref[1, 1] = swap_ref[1]
+    for k, far_ref in enumerate(far_refs):
+        far_ref[...] = swap_ref[k + 2]
+
+
+def rows_in_order(half, keep_ref, swap_ref, own_ref, *refs):
     far_refs, near_ref = refs[:-1], refs[-1]
-    found = [keep_ref[at, 0], swap_ref[at, 0], near_ref[at, 0], near_ref[at, 1]]
+    found = [keep_ref[0, 0], swap_ref[0, 0], near_ref[0, 0], near_ref[0, 1]]
+    rows = far_refs[0].shape[0]
+    for k in range(half - 2):
+        found += [own_ref[k * rows : (k + 1) * rows], far_refs[k][...]]
+    return found
+
+
+def grads_in_order(keep_ref, swap_ref, *refs):
+    far_refs, near_ref = refs[:-1], refs[-1]
+    found = [keep_ref[1, 0], swap_ref[1, 0], near_ref[1, 0], near_ref[1, 1]]
     for ref in far_refs[::-1]:
         found += [ref[0], ref[1]]
     return found
@@ -125,9 +157,10 @@
 
 
 def gate_up_kernel(half, *refs):
-    gate_ref, up_ref, local_ref, *out_refs, scratch = refs[half + 1 :]
+    count = half + 2
+    gate_ref, up_ref, local_ref, *out_refs, scratch = refs[count:]
     dp = len(out_refs)
-    rows = local_order(pieces(0, *refs[: half + 1]), scratch, dp)
+    rows = local_order(rows_in_order(half, *refs[:count]), scratch, dp)
     local_ref[...] = rows
     chunk = rows.shape[0] // dp
     for at, mat in enumerate((gate_ref, up_ref)):
@@ -139,7 +172,7 @@
 def grad_act_kernel(half, *refs):
     down_ref, local_ref, *out_refs, scratch = refs[half + 1 :]
     dp = len(out_refs)
-    rows = local_order(pieces(1, *refs[: half + 1]), scratch, dp)
+    rows = local_order(grads_in_order(*refs[: half + 1]), scratch, dp)
     local_ref[...] = rows
     split_rows(out_refs, mm(rows, down_ref[...], ((1,), (1,))).astype(BF16))
 
@@ -175,7 +208,9 @@
     chunk = rows.shape[0] // dp
     for k in range(dp):
         scratch[chunk_rows(rows.shape[0], dp, k), :] = rows[k * chunk : (k + 1) * chunk]
-    split_cores(keep_ref, swap_ref, scratch[...])
+    rows = scratch[...]
+    split_cores(keep_ref, swap_ref, rows)
+    return rows
 
 
 def expert_out_kernel(dp, *refs):
@@ -187,37 +222,37 @@
 
 
 def row_grad_kernel(dp, *refs):
-    gate_ref, up_ref, gate_pre_ref, up_pre_ref, keep_ref, swap_ref, scratch = refs[dp:]
+    gate_ref, up_ref, gate_pre_ref, up_pre_ref, keep_ref, swap_ref, *own_refs, scratch = refs[dp:]
     gate_pre = jnp.concatenate([ref[0] for ref in refs[:dp]], axis=0)
     up_pre = jnp.concatenate([ref[1] for ref in refs[:dp]], axis=0)
     gate_pre_ref[...] = gate_pre
     up_pre_ref[...] = up_pre
     total = mm(gate_pre, gate_ref[...], ((1,), (1,))) + mm(up_pre, up_ref[...], ((1,), (1,)))
-    send_back(keep_ref, swap_ref, scratch, total.astype(BF16), dp)
-
-
-def returned(keep_ref, swap_ref, refs):
-    found = [keep_ref[0], swap_ref[0]]
-    for ref in refs[::-1]:
-        found += [ref[0], ref[1]]
-    return jnp.concatenate(found, axis=0)
-
-
-def scatter_scaled_kernel(half, pick_ref, weight_ref, *refs):
-    back = returned(*refs[:2], refs[2 : half + 1]).astype(F32)
-    scaled = (weight_ref[...] * back).astype(BF16)
-    refs[-1][...] = mm(pick_ref[...], scaled, ((0,), (0,))).astype(BF16)
-
-
-def scatter_kernel(half, pick_ref, *refs):
-    back = returned(*refs[:2], refs[2 : half + 1])
-    refs[-1][...] = mm(pick_ref[...], back, ((0,), (0,))).astype(BF16)
+    own_blocks(own_refs, send_back(keep_ref, swap_ref, scratch, total.astype(BF16), dp))
+
+
+def scatter_kernel(half, pick_ref, weight_ref, *refs):
+    near_ref, mixed_ref, tokens_ref = refs[-3:]
+    out_keep_ref, out_swap_ref, *out_refs = refs[:half]
+    keep_ref, swap_ref, own_ref, *far_refs = refs[half:-3]
+    outs = [out_keep_ref[0], out_swap_ref[0], near_ref[0, 0], near_ref[0, 1]]
+    outs += [ref[k] for ref in out_refs for k in range(2)]
+    found = [keep_ref[0], swap_ref[0], near_ref[1, 0], near_ref[1, 1]]
+    rows = keep_ref.shape[1]
+    for k in range(half - 2):
+        found += [own_ref[k * rows : (k + 1) * rows], far_refs[k][...]]
+    scaled = (weight_ref[...] * jnp.concatenate(outs, axis=0).astype(F32)).astype(BF16)
+    pick = pick_ref[...].T
+    mixed_ref[...] = mm(pick, scaled, ((1,), (0,))).astype(BF16)
+    tokens_ref[...] = mm(pick, jnp.concatenate(found, axis=0), ((1,), (0,))).astype(BF16)
 
 
 def grads_kernel(count, left_ref, *refs):
     left = left_ref[...].T
-    for right_ref, out_ref in zip(refs[:count], refs[-count:]):
+    *out_refs, token_ref = refs[-count - 1 :]
+    for right_ref, out_ref in zip(refs[:count], out_refs):
         out_ref[...] = mm(left, right_ref[...], ((1,), (0,))).astype(BF16)
+    token_ref[...] = jnp.zeros_like(token_ref)
 
 
 def partner(value, axis, k):
@@ -245,16 +280,20 @@
 
     half = experts // 2
     sized = shape((slots, features), BF16)
+    token = shape((8, 128), F32)
+    staged = shape(((half - 2) * capacity, features), BF16)
     wide = shape((slots, hidden), BF16)
     both = shape((2, half, capacity, features), BF16)
     one = shape((half, capacity, features), BF16)
     near = shape((2, 2, capacity, features), BF16)
-    far = [shape((2, capacity, features), BF16)] * (half - 2)
+    pair = shape((2, capacity, features), BF16)
+    far = [pair] * (half - 2)
     in_order = [pltpu.VMEM((slots, features), BF16)]
 
     ins = (expert_ids.T, gates.T, tokens, grad_out)
-    outs = (shape((slots, tok_rows), BF16), shape((slots, 1), F32), both, both)
-    pick, weight, keep, swap = call(
+    block = [shape((capacity, features), BF16)] * (half - 2)
+    outs = (shape((slots, tok_rows), BF16), shape((slots, 1), F32), both, both, *block)
+    pick, weight, keep, swap, *own_to = call(
         functools.partial(route_kernel, experts),
         outs,
         4 * slots * tok_rows * features,
@@ -270,19 +309,21 @@
     swap = partner(swap_to, "expert", 1)
     up_mat = call(load_kernel, shape(up_mat.shape, BF16), 0, 2 * weights)(up_mat)
     swap, up_mat = lax.optimization_barrier((swap, up_mat))
-    near_to, *far_to = call(functools.partial(pack_kernel, half), (near, *far, *far), 0, 8 * slots)(
-        keep, swap
-    )
-    far_rows = [partner(far_to[k], "expert", 2 * (2 + k)) for k in reversed(range(half - 2))][::-1]
+    far_own = [partner(value, "expert", 2 * (2 + k)) for k, value in enumerate(own_to)]
+    near_to, *far_to = call(
+        functools.partial(pack_kernel, half), (near, *block, *far), 0, 8 * slots
+    )(keep, swap)
+    far_other = [partner(value, "expert", 2 * (2 + k)) for k, value in enumerate(far_to[: half - 2])]
     near_in = partner(near_to, "expert", 2)
-    far_grads = [partner(far_to[half - 2 + k], "expert", 2 * (2 + k)) for k in range(half - 2)]
+    far_grads = [partner(value, "expert", 2 * (2 + k)) for k, value in enumerate(far_to[half - 2 :])]
+    far_own = call(stage_kernel, staged, STAGE, STAGE // 256)(*far_own)
     rows, *part_pre = call(
         functools.partial(gate_up_kernel, half),
         (sized, *[shape((2, chunk, hidden), BF16)] * dp),
         2 * product,
         2 * weights,
         scratch_shapes=in_order,
-    )(keep, swap, *far_rows[::-1], near_in, gate_mat, up_mat)
+    )(keep, swap, far_own, *far_other, near_in, gate_mat, up_mat)
     sums = trade(part_pre)
     act_mine = call(
         functools.partial(act_kernel, dp),
@@ -314,51 +355,59 @@
         weights,
         scratch_shapes=in_order,
     )(*acts, down_mat)
-    back = [far[0]] * (half - 1)
     out_swap = partner(out_swap, "expert", 1)
-    out_near, *out_far = call(pack_back_kernel, back, 0, 8 * slots)(out_keep, out_swap)
+    out_far = call(pack_back_kernel, far, 0, 8 * slots)(out_keep, out_swap)
     out_far = [partner(value, "expert", 2 * (2 + k)) for k, value in enumerate(out_far)]
     pre, out_far = lax.optimization_barrier((pre, out_far))
-    gate_pre, up_pre, grad_keep, grad_swap = call(
+    gate_pre, up_pre, grad_keep, grad_swap, *own_to = call(
         functools.partial(row_grad_kernel, dp),
-        (wide, wide, one, one),
+        (wide, wide, one, one, *block),
         2 * product,
         2 * weights,
         scratch_shapes=in_order,
     )(*pre, gate_mat, up_mat)
     grad_swap = partner(grad_swap, "expert", 1)
-    out_near = partner(out_near, "expert", 2)
-    grad_to = call(pack_back_kernel, back, 0, 8 * slots)(grad_keep, grad_swap)
-    grad_back = [partner(value, "expert", 2 * (1 + k)) for k, value in enumerate(grad_to)]
-
-    (grad_down,) = call(
+    back_own = [partner(value, "expert", 2 * (2 + k)) for k, value in enumerate(own_to)]
+    near_to, *far_to = call(pack_last_kernel, (near, *block), 0, 8 * slots)(
+        out_keep, out_swap, grad_keep, grad_swap
+    )
+    back_other = [partner(value, "expert", 2 * (2 + k)) for k, value in enumerate(far_to)]
+    back_near = partner(near_to, "expert", 2)
+
+    grad_down, _ = call(
         functools.partial(grads_kernel, 1),
-        [shape((hidden, features), BF16)],
-        product,
-        weights,
+        [shape((hidden, features), BF16), token],
+        0,
+        0,
     )(act, grads)
-    grad_gate, grad_up = call(
+    grad_gate, grad_up, grads_done = call(
         functools.partial(grads_kernel, 2),
-        [shape((features, hidden), BF16)] * 2,
-        2 * product,
-        2 * weights,
+        [shape((features, hidden), BF16)] * 2 + [token],
+        0,
+        0,
         in_specs=[HERE] * 3 + [ANY],
-    )(rows, gate_pre, up_pre, grad_to[0])
+    )(rows, gate_pre, up_pre, near_to)
 
     full = shape((tok_rows, features), BF16)
-    mixed = call(
-        functools.partial(scatter_scaled_kernel, half),
-        full,
-        2 * slots * tok_rows * features,
-        4 * tok_rows * features,
-        in_specs=[HERE] * (half + 3) + [ANY],
-    )(pick, weight, out_keep, out_swap, *out_far[::-1], out_near, grad_to[0])
-    grad_tokens = call(
-        functools.partial(scatter_kernel, half),
-        full,
-        2 * slots * tok_rows * features,
-        4 * tok_rows * features,
-    )(pick, grad_keep, grad_swap, *grad_back[::-1])
+    back_own = call(
+        stage_kernel,
+        staged,
+        STAGE,
+        STAGE // 256,
+        in_specs=[HERE] * (half - 2) + [ANY],
+    )(*back_own, grads_done)
+    mixed, grad_tokens = call(functools.partial(scatter_kernel, half), (full, full), 0, 0)(
+        pick,
+        weight,
+        out_keep,
+        out_swap,
+        *out_far,
+        grad_keep,
+        grad_swap,
+        back_own,
+        *back_other,
+        back_near,
+    )
     return (mixed, grad_tokens, grad_gate[None], grad_up[None], grad_down[None])
 
 

time: 82 us -> 86.4 us (1.054)
  waiting for transfers between devices: 31 us -> 34.9 us
  starting transfers between devices: 34.7 us -> 36.2 us
  Pallas kernels: 15.4 us -> 14.3 us
    ppermute x26 -> x29, waiting for transfers between devices: 31 us -> 34.9 us  [partner(): return lax.ppermute(value, axis, [(i, i ^ k) for i in range(size)])]
    ppermute x26 -> x29, starting transfers between devices: 34.7 us -> 36.2 us  [partner(): return lax.ppermute(value, axis, [(i, i ^ k) for i in range(size)])]
    pallas_call x6 -> x7, Pallas kernels: 4.28 us -> 3.21 us  [the longest x1 1.77 us: body(): call(functools.partial(scatter_kernel, half), (full, full), 0, 0)]
  transfers between devices with their start and end apart: 26 -> 29, of which waited for: 13 -> 13; matrix products, arithmetic and copies ran while one was open for 0% -> 0% of each run, Pallas kernels for 10% -> 8%
where the time goes in v10:
time: 86.4 us; the launch traced here: 86.2 us
  starting transfers between devices  36.2 us (42%)
  waiting for transfers between devices  34.9 us (40%)
  Pallas kernels  14.3 us (17%)
    ppermute x29, starting transfers between devices, partner(): return lax.ppermute(value, axis, [(i, i ^ k) for i in range(size)])  36.2 us
    ppermute x29, waiting for transfers between devices, partner(): return lax.ppermute(value, axis, [(i, i ^ k) for i in range(size)])  34.9 us
    pallas_call x1, Pallas kernels, body(): call(functools.partial(route_kernel, experts), outs, 4 * slots * tok_rows...  3.2 us
    pallas_call x1, Pallas kernels, body(): call(functools.partial(grads_kernel, 2), [shape((features, hidden), BF16)...  2.54 us
    pallas_call x1, Pallas kernels, body(): call(functools.partial(grads_kernel, 1), [shape((hidden, features), BF16)...  1.98 us
    pallas_call x1, Pallas kernels, body(): call(functools.partial(scatter_kernel, half), (full, full), 0, 0)  1.77 us
  transfers between devices with their start and end apart: 29, of which 13 were waited for; matrix products, arithmetic and copies ran while one was open for 0% of the time, Pallas kernels for 8%

profile of v10, /device:TPU:0, one launch (start us, length us, event | category | flops | bytes accessed | tf_op | source)
XLA Modules:
  0.0 86.2 jit_solution(1984363958365208882)
XLA Ops:
  0.6 3.2 %shard_map.110 = (bf16[256,512]{1,0:T(8,128)(2,1)}, f32[256,1]{1,0:T(8,128)}, bf16[2,4,32,896]{3,2,1,0:T(8,128)(2,1)}, bf16[2,4,32,896]{3,2,1,0:T(8,128)(2,1)}, ...) custom-call(s32[8,512]{1,0:T(8,128)} %bitcast.13, f32[8,512]{1,0:T(8,128)} %bitcast.14, bf16[512,896]{1,0:T(8,128)(2,1)} %refs_2_.1, ...), custom_call_target="tpu_custom_call" | custom-call | flops 469762048 | bytes 3670016 | tf_op jit(solution)/shard_map/pallas_call | solution.py:296
  4.4 3.7 %collective-permute-start.1 = (bf16[32,896]{1,0:T(8,128)(2,1)}, bf16[32,896]{1,0:T(8,128)(2,1)S(1)}, u32[]{:S(2)}, u32[]{:S(2)}) collective-permute-start(bf16[32,896]{1,0:T(8,128)(2,1)} %get-tuple-element.65), channel_id=1, source_target_pairs={{0,4},{1,5},{2,6},{3,7},{4,0},{5,1},{6,2},{7,3},{8,12},{9,13},{10,... | collective-permute-start | bytes 172040 | tf_op jit(solution)/shard_map/ppermute | solution.py:260
  9.6 1.8 %collective-permute-start.3 = (bf16[32,896]{1,0:T(8,128)(2,1)S(1)}, bf16[32,896]{1,0:T(8,128)(2,1)S(1)}, u32[]{:S(2)}, u32[]{:S(2)}) collective-permute-start(bf16[32,896]{1,0:T(8,128)(2,1)S(1)} %get-tuple-element.67), channel_id=1, source_target_pairs={{0,4},{1,5},{2,6},{3,7},{4,0},{5,1},{6,2},{7,3},{8,12},{9,13},{10,... | collective-permute-start | bytes 172040 | tf_op jit(solution)/shard_map/ppermute | solution.py:260
  11.3 1.8 %collective-permute-start.4 = (bf16[32,896]{1,0:T(8,128)(2,1)S(1)}, bf16[32,896]{1,0:T(8,128)(2,1)S(1)}, u32[]{:S(2)}, u32[]{:S(2)}) collective-permute-start(bf16[32,896]{1,0:T(8,128)(2,1)S(1)} %get-tuple-element.68), channel_id=1, source_target_pairs={{0,6},{1,7},{2,4},{3,5},{4,2},{5,3},{6,0},{7,1},{8,14},{9,15},{10,... | collective-permute-start | bytes 172040 | tf_op jit(solution)/shard_map/ppermute | solution.py:260
  14.6 4.3 %collective-permute-done.3.refs_3_ = bf16[32,896]{1,0:T(8,128)(2,1)S(1)} collective-permute-done((bf16[32,896]{1,0:T(8,128)(2,1)S(1)}, bf16[32,896]{1,0:T(8,128)(2,1)S(1)}, u32[]{:S(2)}, u32[]{:S(2)}) %collective-permute-start.3) | collective-permute-done | bytes 57376 | tf_op jit(solution)/shard_map/ppermute | solution.py:260
  18.9 3.6 %collective-permute-done.5.refs_5_.refs_4_ = bf16[2,2,32,896]{3,2,1,0:T(8,128)(2,1)S(1)} collective-permute-done((bf16[2,2,32,896]{3,2,1,0:T(8,128)(2,1)S(1)}, bf16[2,2,32,896]{3,2,1,0:T(8,128)(2,1)S(1)}, u32[]{:S(2)}, u32[]{:S(2)}) %collective-permute-start.5) | collective-permute-done | bytes 229408 | tf_op jit(solution)/shard_map/ppermute | solution.py:260
  23.9 1.6 %collective-permute-start.6 = (bf16[2,64,1024]{2,1,0:T(8,128)(2,1)S(1)}, bf16[2,64,1024]{2,1,0:T(8,128)(2,1)S(1)}, u32[]{:S(2)}, u32[]{:S(2)}) collective-permute-start(bf16[2,64,1024]{2,1,0:T(8,128)(2,1)S(1)} %get-tuple-element.72), channel_id=1, source_target_pairs={{0,8},{8,0},{16,24},{24,16},{1,9},{9,1},{17,25},{25,17},{2,10},{10... | collective-permute-start | bytes 786440 | tf_op jit(solution)/shard_map/ppermute | solution.py:260
  25.4 1.5 %collective-permute-start.7 = (bf16[2,64,1024]{2,1,0:T(8,128)(2,1)S(1)}, bf16[2,64,1024]{2,1,0:T(8,128)(2,1)S(1)}, u32[]{:S(2)}, u32[]{:S(2)}) collective-permute-start(bf16[2,64,1024]{2,1,0:T(8,128)(2,1)S(1)} %get-tuple-element.73), channel_id=1, source_target_pairs={{0,16},{8,24},{16,0},{24,8},{1,17},{9,25},{17,1},{25,9},{2,18},{10... | collective-permute-start | bytes 786440 | tf_op jit(solution)/shard_map/ppermute | solution.py:260
  28.0 1.9 %collective-permute-start.14 = (bf16[2,32,896]{2,1,0:T(8,128)(2,1)S(1)}, bf16[2,32,896]{2,1,0:T(8,128)(2,1)S(1)}, u32[]{:S(2)}, u32[]{:S(2)}) collective-permute-start(bf16[2,32,896]{2,1,0:T(8,128)(2,1)S(1)} %get-tuple-element.78), channel_id=1, source_target_pairs={{0,6},{1,7},{2,4},{3,5},{4,2},{5,3},{6,0},{7,1},{8,14},{9,15},{10,... | collective-permute-start | bytes 344072 | tf_op jit(solution)/shard_map/ppermute | solution.py:260
  29.9 3.3 %collective-permute-done.6.refs_1_ = bf16[2,64,1024]{2,1,0:T(8,128)(2,1)S(1)} collective-permute-done((bf16[2,64,1024]{2,1,0:T(8,128)(2,1)S(1)}, bf16[2,64,1024]{2,1,0:T(8,128)(2,1)S(1)}, u32[]{:S(2)}, u32[]{:S(2)}) %collective-permute-start.6) | collective-permute-done | bytes 262176 | tf_op jit(solution)/shard_map/ppermute | solution.py:260
  33.2 5.4 %collective-permute-done.7.refs_2_ = bf16[2,64,1024]{2,1,0:T(8,128)(2,1)S(1)} collective-permute-done((bf16[2,64,1024]{2,1,0:T(8,128)(2,1)S(1)}, bf16[2,64,1024]{2,1,0:T(8,128)(2,1)S(1)}, u32[]{:S(2)}, u32[]{:S(2)}) %collective-permute-start.7) | collective-permute-done | bytes 262176 | tf_op jit(solution)/shard_map/ppermute | solution.py:260
  46.7 2.4 %collective-permute-done.11.refs_3_ = bf16[64,1024]{1,0:T(8,128)(2,1)S(1)} collective-permute-done((bf16[64,1024]{1,0:T(8,128)(2,1)S(1)}, bf16[64,1024]{1,0:T(8,128)(2,1)S(1)}, u32[]{:S(2)}, u32[]{:S(2)}) %collective-permute-start.11) | collective-permute-done | bytes 131104 | tf_op jit(solution)/shard_map/ppermute | solution.py:260
  50.7 1.6 %collective-permute-done.16.refs_6_ = bf16[64,1024]{1,0:T(8,128)(2,1)S(1)} collective-permute-done((bf16[64,1024]{1,0:T(8,128)(2,1)S(1)}, bf16[64,1024]{1,0:T(8,128)(2,1)S(1)}, u32[]{:S(2)}, u32[]{:S(2)}) %collective-permute-start.16) | collective-permute-done | bytes 131104 | tf_op jit(solution)/shard_map/ppermute | solution.py:260
  53.3 1.5 %collective-permute-start.19 = (bf16[2,64,1024]{2,1,0:T(8,128)(2,1)S(1)}, bf16[2,64,1024]{2,1,0:T(8,128)(2,1)S(1)}, u32[]{:S(2)}, u32[]{:S(2)}) collective-permute-start(bf16[2,64,1024]{2,1,0:T(8,128)(2,1)S(1)} %shard_map.118.refs_0_), channel_id=1, source_target_pairs={{0,16},{8,24},{16,0},{24,8},{1,17},{9,25},{17,1},{25,9},{2,18},{10... | collective-permute-start | bytes 786440 | tf_op jit(solution)/shard_map/ppermute | solution.py:260
  56.8 2.0 %collective-permute-start.22 = (bf16[2,32,896]{2,1,0:T(8,128)(2,1)S(1)}, bf16[2,32,896]{2,1,0:T(8,128)(2,1)S(1)}, u32[]{:S(2)}, u32[]{:S(2)}) collective-permute-start(bf16[2,32,896]{2,1,0:T(8,128)(2,1)S(1)} %get-tuple-element.86), channel_id=1, source_target_pairs={{0,6},{1,7},{2,4},{3,5},{4,2},{5,3},{6,0},{7,1},{8,14},{9,15},{10,... | collective-permute-start | bytes 344072 | tf_op jit(solution)/shard_map/ppermute | solution.py:260
  58.8 3.0 %collective-permute-done.18.refs_1_ = bf16[2,64,1024]{2,1,0:T(8,128)(2,1)S(1)} collective-permute-done((bf16[2,64,1024]{2,1,0:T(8,128)(2,1)S(1)}, bf16[2,64,1024]{2,1,0:T(8,128)(2,1)S(1)}, u32[]{:S(2)}, u32[]{:S(2)}) %collective-permute-start.18) | collective-permute-done | bytes 262176 | tf_op jit(solution)/shard_map/ppermute | solution.py:260
  61.8 2.2 %collective-permute-done.19.refs_2_ = bf16[2,64,1024]{2,1,0:T(8,128)(2,1)S(1)} collective-permute-done((bf16[2,64,1024]{2,1,0:T(8,128)(2,1)S(1)}, bf16[2,64,1024]{2,1,0:T(8,128)(2,1)S(1)}, u32[]{:S(2)}, u32[]{:S(2)}) %collective-permute-start.19) | collective-permute-done | bytes 262176 | tf_op jit(solution)/shard_map/ppermute | solution.py:260
  66.9 2.0 %collective-permute-start.24 = (bf16[32,896]{1,0:T(8,128)(2,1)S(1)}, bf16[32,896]{1,0:T(8,128)(2,1)S(1)}, u32[]{:S(2)}, u32[]{:S(2)}) collective-permute-start(bf16[32,896]{1,0:T(8,128)(2,1)S(1)} %get-tuple-element.95), channel_id=1, source_target_pairs={{0,4},{1,5},{2,6},{3,7},{4,0},{5,1},{6,2},{7,3},{8,12},{9,13},{10,... | collective-permute-start | bytes 172040 | tf_op jit(solution)/shard_map/ppermute | solution.py:260
  68.9 2.2 %collective-permute-start.25 = (bf16[32,896]{1,0:T(8,128)(2,1)S(1)}, bf16[32,896]{1,0:T(8,128)(2,1)S(1)}, u32[]{:S(2)}, u32[]{:S(2)}) collective-permute-start(bf16[32,896]{1,0:T(8,128)(2,1)S(1)} %get-tuple-element.96), channel_id=1, source_target_pairs={{0,6},{1,7},{2,4},{3,5},{4,2},{5,3},{6,0},{7,1},{8,14},{9,15},{10,... | collective-permute-start | bytes 172040 | tf_op jit(solution)/shard_map/ppermute | solution.py:260
  71.1 2.0 %shard_map.125 = (bf16[1024,896]{1,0:T(8,128)(2,1)}, f32[8,128]{1,0:T(8,128)}) custom-call(bf16[256,1024]{1,0:T(8,128)(2,1)S(1)} %get-tuple-element.108.left_ref, bf16[256,896]{1,0:T(8,128)(2,1)S(1)} %get-tuple-element.109.refs_0_), custom_call_target="tpu_custom_call" | custom-call | tf_op jit(solution)/shard_map/pallas_call | solution.py:377
  74.9 1.8 %collective-permute-start.28 = (bf16[2,2,32,896]{3,2,1,0:T(8,128)(2,1)S(1)}, bf16[2,2,32,896]{3,2,1,0:T(8,128)(2,1)S(1)}, u32[]{:S(2)}, u32[]{:S(2)}) collective-permute-start(bf16[2,2,32,896]{3,2,1,0:T(8,128)(2,1)S(1)} %get-tuple-element.100.refs_2_), channel_id=1, source_target_pairs={{0,2},{1,3},{2,0},{3,1},{4,6},{5,7},{6,4},{7,5},{8,10},{9,11},{10,... | collective-permute-start | bytes 688136 | tf_op jit(solution)/shard_map/ppermute | solution.py:260
  76.7 2.5 %shard_map.122 = (bf16[896,1024]{1,0:T(8,128)(2,1)}, bf16[896,1024]{1,0:T(8,128)(2,1)}, f32[8,128]{1,0:T(8,128)S(1)}) custom-call(bf16[256,896]{1,0:T(8,128)(2,1)S(1)} %get-tuple-element.97.left_ref, bf16[256,1024]{1,0:T(8,128)(2,1)S(1)} %get-tuple-element.98.refs_0_, bf16[256,1024]{1,0:T(8,128)(2,1)S(1)} %get-tuple-element.99.refs_1_, ...), custom_call_target="tpu_custom_call" | custom-call | tf_op jit(solution)/shard_map/pallas_call | solution.py:383
  80.1 4.3 %collective-permute-done.28.refs_9_ = bf16[2,2,32,896]{3,2,1,0:T(8,128)(2,1)S(1)} collective-permute-done((bf16[2,2,32,896]{3,2,1,0:T(8,128)(2,1)S(1)}, bf16[2,2,32,896]{3,2,1,0:T(8,128)(2,1)S(1)}, u32[]{:S(2)}, u32[]{:S(2)}) %collective-permute-start.28) | collective-permute-done | bytes 229408 | tf_op jit(solution)/shard_map/ppermute | solution.py:260
  84.5 1.8 %shard_map.124 = (bf16[512,896]{1,0:T(8,128)(2,1)}, bf16[512,896]{1,0:T(8,128)(2,1)}) custom-call(bf16[256,512]{1,0:T(8,128)(2,1)S(1)} %copy-done.4, f32[256,1]{1,0:T(8,128)S(1)} %copy-done.5, bf16[4,32,896]{2,1,0:T(8,128)(2,1)S(1)} %get-tuple-element.75.keep_ref.out_keep_ref.refs_0_, ...), custom_call_target="tpu_custom_call" | custom-call | tf_op jit(solution)/shard_map/pallas_call | solution.py:399
  (62 shorter events, 24.0 us)
Async XLA Ops:
  4.4 8.8 %collective-permute-start.1 = (bf16[32,896]{1,0:T(8,128)(2,1)}, bf16[32,896]{1,0:T(8,128)(2,1)S(1)}, u32[]{:S(2)}, u32[]{:S(2)}) collective-permute-start(bf16[32,896]{1,0:T(8,128)(2,1)} %get-tuple-element.65), channel_id=1, source_target_pairs={{0,4},{1,5},{2,6},{3,7},{4,0},{5,1},{6,2},{7,3},{8,12},{9,13},{10,... | collective-permute-start | bytes 172040 | tf_op jit(solution)/shard_map/ppermute | solution.py:260
  8.0 6.6 %collective-permute-start.2 = (bf16[32,896]{1,0:T(8,128)(2,1)}, bf16[32,896]{1,0:T(8,128)(2,1)S(1)}, u32[]{:S(2)}, u32[]{:S(2)}) collective-permute-start(bf16[32,896]{1,0:T(8,128)(2,1)} %get-tuple-element.66), channel_id=1, source_target_pairs={{0,6},{1,7},{2,4},{3,5},{4,2},{5,3},{6,0},{7,1},{8,14},{9,15},{10,... | collective-permute-start | bytes 172040 | tf_op jit(solution)/shard_map/ppermute | solution.py:260
  9.6 9.4 %collective-permute-start.3 = (bf16[32,896]{1,0:T(8,128)(2,1)S(1)}, bf16[32,896]{1,0:T(8,128)(2,1)S(1)}, u32[]{:S(2)}, u32[]{:S(2)}) collective-permute-start(bf16[32,896]{1,0:T(8,128)(2,1)S(1)} %get-tuple-element.67), channel_id=1, source_target_pairs={{0,4},{1,5},{2,6},{3,7},{4,0},{5,1},{6,2},{7,3},{8,12},{9,13},{10,... | collective-permute-start | bytes 172040 | tf_op jit(solution)/shard_map/ppermute | solution.py:260
  11.3 7.6 %collective-permute-start.4 = (bf16[32,896]{1,0:T(8,128)(2,1)S(1)}, bf16[32,896]{1,0:T(8,128)(2,1)S(1)}, u32[]{:S(2)}, u32[]{:S(2)}) collective-permute-start(bf16[32,896]{1,0:T(8,128)(2,1)S(1)} %get-tuple-element.68), channel_id=1, source_target_pairs={{0,6},{1,7},{2,4},{3,5},{4,2},{5,3},{6,0},{7,1},{8,14},{9,15},{10,... | collective-permute-start | bytes 172040 | tf_op jit(solution)/shard_map/ppermute | solution.py:260
  13.1 9.5 %collective-permute-start.5 = (bf16[2,2,32,896]{3,2,1,0:T(8,128)(2,1)S(1)}, bf16[2,2,32,896]{3,2,1,0:T(8,128)(2,1)S(1)}, u32[]{:S(2)}, u32[]{:S(2)}) collective-permute-start(bf16[2,2,32,896]{3,2,1,0:T(8,128)(2,1)S(1)} %get-tuple-element.69), channel_id=1, source_target_pairs={{0,2},{1,3},{2,0},{3,1},{4,6},{5,7},{6,4},{7,5},{8,10},{9,11},{10,... | collective-permute-start | bytes 688136 | tf_op jit(solution)/shard_map/ppermute | solution.py:260
  23.9 9.3 %collective-permute-start.6 = (bf16[2,64,1024]{2,1,0:T(8,128)(2,1)S(1)}, bf16[2,64,1024]{2,1,0:T(8,128)(2,1)S(1)}, u32[]{:S(2)}, u32[]{:S(2)}) collective-permute-start(bf16[2,64,1024]{2,1,0:T(8,128)(2,1)S(1)} %get-tuple-element.72), channel_id=1, source_target_pairs={{0,8},{8,0},{16,24},{24,16},{1,9},{9,1},{17,25},{25,17},{2,10},{10... | collective-permute-start | bytes 786440 | tf_op jit(solution)/shard_map/ppermute | solution.py:260
  25.4 13.2 %collective-permute-start.7 = (bf16[2,64,1024]{2,1,0:T(8,128)(2,1)S(1)}, bf16[2,64,1024]{2,1,0:T(8,128)(2,1)S(1)}, u32[]{:S(2)}, u32[]{:S(2)}) collective-permute-start(bf16[2,64,1024]{2,1,0:T(8,128)(2,1)S(1)} %get-tuple-element.73), channel_id=1, source_target_pairs={{0,16},{8,24},{16,0},{24,8},{1,17},{9,25},{17,1},{25,9},{2,18},{10... | collective-permute-start | bytes 786440 | tf_op jit(solution)/shard_map/ppermute | solution.py:260
  27.0 11.6 %collective-permute-start.8 = (bf16[2,64,1024]{2,1,0:T(8,128)(2,1)S(1)}, bf16[2,64,1024]{2,1,0:T(8,128)(2,1)S(1)}, u32[]{:S(2)}, u32[]{:S(2)}) collective-permute-start(bf16[2,64,1024]{2,1,0:T(8,128)(2,1)S(1)} %get-tuple-element.74), channel_id=1, source_target_pairs={{0,24},{8,16},{16,8},{24,0},{1,25},{9,17},{17,9},{25,1},{2,26},{10... | collective-permute-start | bytes 786440 | tf_op jit(solution)/shard_map/ppermute | solution.py:260
  27.4 14.9 %collective-permute-start.13 = (bf16[2,32,896]{2,1,0:T(8,128)(2,1)S(1)}, bf16[2,32,896]{2,1,0:T(8,128)(2,1)S(1)}, u32[]{:S(2)}, u32[]{:S(2)}) collective-permute-start(bf16[2,32,896]{2,1,0:T(8,128)(2,1)S(1)} %get-tuple-element.77), channel_id=1, source_target_pairs={{0,4},{1,5},{2,6},{3,7},{4,0},{5,1},{6,2},{7,3},{8,12},{9,13},{10,... | collective-permute-start | bytes 344072 | tf_op jit(solution)/shard_map/ppermute | solution.py:260
  28.0 14.4 %collective-permute-start.14 = (bf16[2,32,896]{2,1,0:T(8,128)(2,1)S(1)}, bf16[2,32,896]{2,1,0:T(8,128)(2,1)S(1)}, u32[]{:S(2)}, u32[]{:S(2)}) collective-permute-start(bf16[2,32,896]{2,1,0:T(8,128)(2,1)S(1)} %get-tuple-element.78), channel_id=1, source_target_pairs={{0,6},{1,7},{2,4},{3,5},{4,2},{5,3},{6,0},{7,1},{8,14},{9,15},{10,... | collective-permute-start | bytes 344072 | tf_op jit(solution)/shard_map/ppermute | solution.py:260
  40.1 6.6 %collective-permute-start.10 = (bf16[64,1024]{1,0:T(8,128)(2,1)S(1)}, bf16[64,1024]{1,0:T(8,128)(2,1)S(1)}, u32[]{:S(2)}, u32[]{:S(2)}) collective-permute-start(bf16[64,1024]{1,0:T(8,128)(2,1)S(1)} %shard_map.115.refs_0_), channel_id=1, source_target_pairs={{0,16},{8,24},{16,0},{24,8},{1,17},{9,25},{17,1},{25,9},{2,18},{10... | collective-permute-start | bytes 393224 | tf_op jit(solution)/shard_map/ppermute | solution.py:260
  40.9 8.2 %collective-permute-start.11 = (bf16[64,1024]{1,0:T(8,128)(2,1)S(1)}, bf16[64,1024]{1,0:T(8,128)(2,1)S(1)}, u32[]{:S(2)}, u32[]{:S(2)}) collective-permute-start(bf16[64,1024]{1,0:T(8,128)(2,1)S(1)} %shard_map.115.refs_0_), channel_id=1, source_target_pairs={{0,24},{8,16},{16,8},{24,0},{1,25},{9,17},{17,9},{25,1},{2,26},{10... | collective-permute-start | bytes 393224 | tf_op jit(solution)/shard_map/ppermute | solution.py:260
  43.1 7.6 %collective-permute-start.15 = (bf16[64,1024]{1,0:T(8,128)(2,1)S(1)}, bf16[64,1024]{1,0:T(8,128)(2,1)S(1)}, u32[]{:S(2)}, u32[]{:S(2)}) collective-permute-start(bf16[64,1024]{1,0:T(8,128)(2,1)S(1)} %get-tuple-element.82), channel_id=1, source_target_pairs={{0,8},{8,0},{16,24},{24,16},{1,9},{9,1},{17,25},{25,17},{2,10},{10... | collective-permute-start | bytes 393224 | tf_op jit(solution)/shard_map/ppermute | solution.py:260
  44.4 7.9 %collective-permute-start.16 = (bf16[64,1024]{1,0:T(8,128)(2,1)S(1)}, bf16[64,1024]{1,0:T(8,128)(2,1)S(1)}, u32[]{:S(2)}, u32[]{:S(2)}) collective-permute-start(bf16[64,1024]{1,0:T(8,128)(2,1)S(1)} %get-tuple-element.83), channel_id=1, source_target_pairs={{0,16},{8,24},{16,0},{24,8},{1,17},{9,25},{17,1},{25,9},{2,18},{10... | collective-permute-start | bytes 393224 | tf_op jit(solution)/shard_map/ppermute | solution.py:260
  45.2 7.1 %collective-permute-start.17 = (bf16[64,1024]{1,0:T(8,128)(2,1)S(1)}, bf16[64,1024]{1,0:T(8,128)(2,1)S(1)}, u32[]{:S(2)}, u32[]{:S(2)}) collective-permute-start(bf16[64,1024]{1,0:T(8,128)(2,1)S(1)} %get-tuple-element.84), channel_id=1, source_target_pairs={{0,24},{8,16},{16,8},{24,0},{1,25},{9,17},{17,9},{25,1},{2,26},{10... | collective-permute-start | bytes 393224 | tf_op jit(solution)/shard_map/ppermute | solution.py:260
  52.7 9.2 %collective-permute-start.18 = (bf16[2,64,1024]{2,1,0:T(8,128)(2,1)S(1)}, bf16[2,64,1024]{2,1,0:T(8,128)(2,1)S(1)}, u32[]{:S(2)}, u32[]{:S(2)}) collective-permute-start(bf16[2,64,1024]{2,1,0:T(8,128)(2,1)S(1)} %shard_map.118.refs_0_), channel_id=1, source_target_pairs={{0,8},{8,0},{16,24},{24,16},{1,9},{9,1},{17,25},{25,17},{2,10},{10... | collective-permute-start | bytes 786440 | tf_op jit(solution)/shard_map/ppermute | solution.py:260
  53.3 10.7 %collective-permute-start.19 = (bf16[2,64,1024]{2,1,0:T(8,128)(2,1)S(1)}, bf16[2,64,1024]{2,1,0:T(8,128)(2,1)S(1)}, u32[]{:S(2)}, u32[]{:S(2)}) collective-permute-start(bf16[2,64,1024]{2,1,0:T(8,128)(2,1)S(1)} %shard_map.118.refs_0_), channel_id=1, source_target_pairs={{0,16},{8,24},{16,0},{24,8},{1,17},{9,25},{17,1},{25,9},{2,18},{10... | collective-permute-start | bytes 786440 | tf_op jit(solution)/shard_map/ppermute | solution.py:260
  54.9 10.7 %collective-permute-start.20 = (bf16[2,64,1024]{2,1,0:T(8,128)(2,1)S(1)}, bf16[2,64,1024]{2,1,0:T(8,128)(2,1)S(1)}, u32[]{:S(2)}, u32[]{:S(2)}) collective-permute-start(bf16[2,64,1024]{2,1,0:T(8,128)(2,1)S(1)} %shard_map.118.refs_0_), channel_id=1, source_target_pairs={{0,24},{8,16},{16,8},{24,0},{1,25},{9,17},{17,9},{25,1},{2,26},{10... | collective-permute-start | bytes 786440 | tf_op jit(solution)/shard_map/ppermute | solution.py:260
  56.2 9.3 %collective-permute-start.21 = (bf16[2,32,896]{2,1,0:T(8,128)(2,1)S(1)}, bf16[2,32,896]{2,1,0:T(8,128)(2,1)S(1)}, u32[]{:S(2)}, u32[]{:S(2)}) collective-permute-start(bf16[2,32,896]{2,1,0:T(8,128)(2,1)S(1)} %get-tuple-element.85), channel_id=1, source_target_pairs={{0,4},{1,5},{2,6},{3,7},{4,0},{5,1},{6,2},{7,3},{8,12},{9,13},{10,... | collective-permute-start | bytes 344072 | tf_op jit(solution)/shard_map/ppermute | solution.py:260
  56.8 8.7 %collective-permute-start.22 = (bf16[2,32,896]{2,1,0:T(8,128)(2,1)S(1)}, bf16[2,32,896]{2,1,0:T(8,128)(2,1)S(1)}, u32[]{:S(2)}, u32[]{:S(2)}) collective-permute-start(bf16[2,32,896]{2,1,0:T(8,128)(2,1)S(1)} %get-tuple-element.86), channel_id=1, source_target_pairs={{0,6},{1,7},{2,4},{3,5},{4,2},{5,3},{6,0},{7,1},{8,14},{9,15},{10,... | collective-permute-start | bytes 344072 | tf_op jit(solution)/shard_map/ppermute | solution.py:260
  66.9 12.3 %collective-permute-start.24 = (bf16[32,896]{1,0:T(8,128)(2,1)S(1)}, bf16[32,896]{1,0:T(8,128)(2,1)S(1)}, u32[]{:S(2)}, u32[]{:S(2)}) collective-permute-start(bf16[32,896]{1,0:T(8,128)(2,1)S(1)} %get-tuple-element.95), channel_id=1, source_target_pairs={{0,4},{1,5},{2,6},{3,7},{4,0},{5,1},{6,2},{7,3},{8,12},{9,13},{10,... | collective-permute-start | bytes 172040 | tf_op jit(solution)/shard_map/ppermute | solution.py:260
  68.9 10.3 %collective-permute-start.25 = (bf16[32,896]{1,0:T(8,128)(2,1)S(1)}, bf16[32,896]{1,0:T(8,128)(2,1)S(1)}, u32[]{:S(2)}, u32[]{:S(2)}) collective-permute-start(bf16[32,896]{1,0:T(8,128)(2,1)S(1)} %get-tuple-element.96), channel_id=1, source_target_pairs={{0,6},{1,7},{2,4},{3,5},{4,2},{5,3},{6,0},{7,1},{8,14},{9,15},{10,... | collective-permute-start | bytes 172040 | tf_op jit(solution)/shard_map/ppermute | solution.py:260
  73.1 7.0 %collective-permute-start.26 = (bf16[32,896]{1,0:T(8,128)(2,1)S(1)}, bf16[32,896]{1,0:T(8,128)(2,1)S(1)}, u32[]{:S(2)}, u32[]{:S(2)}) collective-permute-start(bf16[32,896]{1,0:T(8,128)(2,1)S(1)} %get-tuple-element.102), channel_id=1, source_target_pairs={{0,4},{1,5},{2,6},{3,7},{4,0},{5,1},{6,2},{7,3},{8,12},{9,13},{10,... | collective-permute-start | bytes 172040 | tf_op jit(solution)/shard_map/ppermute | solution.py:260
  74.9 9.5 %collective-permute-start.28 = (bf16[2,2,32,896]{3,2,1,0:T(8,128)(2,1)S(1)}, bf16[2,2,32,896]{3,2,1,0:T(8,128)(2,1)S(1)}, u32[]{:S(2)}, u32[]{:S(2)}) collective-permute-start(bf16[2,2,32,896]{3,2,1,0:T(8,128)(2,1)S(1)} %get-tuple-element.100.refs_2_), channel_id=1, source_target_pairs={{0,2},{1,3},{2,0},{3,1},{4,6},{5,7},{6,4},{7,5},{8,10},{9,11},{10,... | collective-permute-start | bytes 688136 | tf_op jit(solution)/shard_map/ppermute | solution.py:260
  (11 other events, 81.2 us)

commit v11 on v8

--- a/solution.py
+++ b/solution.py
@@ -89,13 +89,12 @@
     to_ref[...] = from_ref[...]
 
 
-def pack_kernel(half, keep_ref, swap_ref, near_ref, *far_refs):
+def pack_kernel(keep_ref, swap_ref, *out_refs):
+    half = keep_ref.shape[1]
     for at in range(2):
-        near_ref[at, 0] = keep_ref[at, 1]
-        near_ref[at, 1] = swap_ref[at, 1]
-        for k in range(2, half):
-            far_refs[at * (half - 2) + k - 2][0] = keep_ref[at, k]
-            far_refs[at * (half - 2) + k - 2][1] = swap_ref[at, k]
+        for k in range(1, half):
+            out_refs[at * (half - 1) + k - 1][0] = keep_ref[at, k]
+            out_refs[at * (half - 1) + k - 1][1] = swap_ref[at, k]
 
 
 def pack_back_kernel(keep_ref, swap_ref, *out_refs):
@@ -105,9 +104,8 @@
 
 
 def pieces(at, keep_ref, swap_ref, *refs):
-    far_refs, near_ref = refs[:-1], refs[-1]
-    found = [keep_ref[at, 0], swap_ref[at, 0], near_ref[at, 0], near_ref[at, 1]]
-    for ref in far_refs[::-1]:
+    found = [keep_ref[at, 0], swap_ref[at, 0]]
+    for ref in refs[::-1]:
         found += [ref[0], ref[1]]
     return found
 
@@ -203,15 +201,31 @@
     return jnp.concatenate(found, axis=0)
 
 
+def turn_kernel(pick_ref, out_ref):
+    out_ref[...] = pick_ref[...].T
+
+
+def scatter_out(pick_ref, rows, out_ref, scratch, sems):
+    parts = sems.shape[0]
+    size = pick_ref.shape[0] // parts
+    copies = []
+    for k in range(parts):
+        at = pl.ds(k * size, size)
+        scratch[at, :] = mm(pick_ref[at, :], rows, ((1,), (0,))).astype(BF16)
+        copies.append(pltpu.make_async_copy(scratch.at[at, :], out_ref.at[at, :], sems.at[k]))
+        copies[-1].start()
+    for copy in copies:
+        copy.wait()
+
+
 def scatter_scaled_kernel(half, pick_ref, weight_ref, *refs):
     back = returned(*refs[:2], refs[2 : half + 1]).astype(F32)
     scaled = (weight_ref[...] * back).astype(BF16)
-    refs[-1][...] = mm(pick_ref[...], scaled, ((0,), (0,))).astype(BF16)
+    scatter_out(pick_ref, scaled, *refs[-3:])
 
 
 def scatter_kernel(half, pick_ref, *refs):
-    back = returned(*refs[:2], refs[2 : half + 1])
-    refs[-1][...] = mm(pick_ref[...], back, ((0,), (0,))).astype(BF16)
+    scatter_out(pick_ref, returned(*refs[:2], refs[2 : half + 1]), *refs[-3:])
 
 
 def grads_kernel(count, left_ref, *refs):
@@ -248,8 +262,7 @@
     wide = shape((slots, hidden), BF16)
     both = shape((2, half, capacity, features), BF16)
     one = shape((half, capacity, features), BF16)
-    near = shape((2, 2, capacity, features), BF16)
-    far = [shape((2, capacity, features), BF16)] * (half - 2)
+    pair = shape((2, capacity, features), BF16)
     in_order = [pltpu.VMEM((slots, features), BF16)]
 
     ins = (expert_ids.T, gates.T, tokens, grad_out)
@@ -270,19 +283,18 @@
     swap = partner(swap_to, "expert", 1)
     up_mat = call(load_kernel, shape(up_mat.shape, BF16), 0, 2 * weights)(up_mat)
     swap, up_mat = lax.optimization_barrier((swap, up_mat))
-    near_to, *far_to = call(functools.partial(pack_kernel, half), (near, *far, *far), 0, 8 * slots)(
-        keep, swap
-    )
-    far_rows = [partner(far_to[k], "expert", 2 * (2 + k)) for k in reversed(range(half - 2))][::-1]
-    near_in = partner(near_to, "expert", 2)
-    far_grads = [partner(far_to[half - 2 + k], "expert", 2 * (2 + k)) for k in range(half - 2)]
+    sent = call(pack_kernel, [pair] * (2 * half - 2), 0, 8 * slots)(keep, swap)
+    arrived = [
+        partner(value, "expert", 2 * (1 + k % (half - 1))) for k, value in enumerate(sent)
+    ]
+    row_blocks, grad_blocks = arrived[: half - 1][::-1], arrived[half - 1 :][::-1]
     rows, *part_pre = call(
         functools.partial(gate_up_kernel, half),
         (sized, *[shape((2, chunk, hidden), BF16)] * dp),
         2 * product,
         2 * weights,
         scratch_shapes=in_order,
-    )(keep, swap, *far_rows[::-1], near_in, gate_mat, up_mat)
+    )(keep, swap, *row_blocks, gate_mat, up_mat)
     sums = trade(part_pre)
     act_mine = call(
         functools.partial(act_kernel, dp),
@@ -291,14 +303,14 @@
         4 * dp * chunk * hidden,
     )(*sums)
     acts = trade([act_mine] * dp)
-    far_grads, act_mine = lax.optimization_barrier((far_grads, act_mine))
+    grad_blocks, act_mine = lax.optimization_barrier((grad_blocks, act_mine))
     grads, *part_grad = call(
         functools.partial(grad_act_kernel, half),
         (sized, *[shape((chunk, hidden), BF16)] * dp),
         product,
         weights,
         scratch_shapes=in_order,
-    )(keep, swap, *far_grads[::-1], near_in, down_mat)
+    )(keep, swap, *grad_blocks, down_mat)
     grad_sums = trade(part_grad)
     pre_mine = call(
         functools.partial(grad_pre_kernel, dp),
@@ -314,7 +326,7 @@
         weights,
         scratch_shapes=in_order,
     )(*acts, down_mat)
-    back = [far[0]] * (half - 1)
+    back = [pair] * (half - 1)
     out_swap = partner(out_swap, "expert", 1)
     out_near, *out_far = call(pack_back_kernel, back, 0, 8 * slots)(out_keep, out_swap)
     out_far = [partner(value, "expert", 2 * (2 + k)) for k, value in enumerate(out_far)]
@@ -346,19 +358,26 @@
     )(rows, gate_pre, up_pre, grad_to[0])
 
     full = shape((tok_rows, features), BF16)
+    turned = call(turn_kernel, shape((tok_rows, slots), BF16))(pick)
+    flight = dict(
+        out_specs=ANY,
+        scratch_shapes=[pltpu.VMEM(full.shape, BF16), pltpu.SemaphoreType.DMA((4,))],
+    )
     mixed = call(
         functools.partial(scatter_scaled_kernel, half),
         full,
         2 * slots * tok_rows * features,
         4 * tok_rows * features,
         in_specs=[HERE] * (half + 3) + [ANY],
-    )(pick, weight, out_keep, out_swap, *out_far[::-1], out_near, grad_to[0])
+        **flight,
+    )(turned, weight, out_keep, out_swap, *out_far[::-1], out_near, grad_to[0])
     grad_tokens = call(
         functools.partial(scatter_kernel, half),
         full,
         2 * slots * tok_rows * features,
         4 * tok_rows * features,
-    )(pick, grad_keep, grad_swap, *grad_back[::-1])
+        **flight,
+    )(turned, grad_keep, grad_swap, *grad_back[::-1])
     return (mixed, grad_tokens, grad_gate[None], grad_up[None], grad_down[None])
 
 

time: 82 us -> 81.9 us (level)
  waiting for transfers between devices: 31 us -> 33.3 us
  starting transfers between devices: 34.7 us -> 32.5 us
    ppermute x26 -> x27, waiting for transfers between devices: 31 us -> 33.3 us  [partner(): return lax.ppermute(value, axis, [(i, i ^ k) for i in range(size)])]
    ppermute x26 -> x27, starting transfers between devices: 34.7 us -> 32.5 us  [partner(): return lax.ppermute(value, axis, [(i, i ^ k) for i in range(size)])]
  transfers between devices with their start and end apart: 26 -> 27, of which waited for: 13 -> 13; matrix products, arithmetic and copies ran while one was open for 0% -> 0% of each run, Pallas kernels for 10% -> 10%
where the time goes in v11:
time: 81.9 us; the launch traced here: 81.7 us
  waiting for transfers between devices  33.3 us (41%)
  starting transfers between devices  32.5 us (40%)
  Pallas kernels  15.1 us (18%)
    ppermute x27, waiting for transfers between devices, partner(): return lax.ppermute(value, axis, [(i, i ^ k) for i in range(size)])  33.3 us
    ppermute x27, starting transfers between devices, partner(): return lax.ppermute(value, axis, [(i, i ^ k) for i in range(size)])  32.5 us
    pallas_call x1, Pallas kernels, body(): call(functools.partial(route_kernel, experts), outs, 4 * slots * tok_rows...  3.19 us
    pallas_call x1, Pallas kernels, body(): call(functools.partial(grads_kernel, 2), [shape((features, hidden), BF16)...  2.54 us
    pallas_call x1, Pallas kernels, body(): call(functools.partial(grads_kernel, 1), [shape((hidden, features), BF16)...  1.97 us
  transfers between devices with their start and end apart: 27, of which 13 were waited for; matrix products, arithmetic and copies ran while one was open for 0% of the time, Pallas kernels for 10%

profile of v11, /device:TPU:0, one launch (start us, length us, event | category | flops | bytes accessed | tf_op | source)
XLA Modules:
  0.0 81.7 jit_solution(1878077356308575507)
XLA Ops:
  0.6 3.2 %shard_map.110 = (bf16[256,512]{1,0:T(8,128)(2,1)}, f32[256,1]{1,0:T(8,128)}, bf16[2,4,32,896]{3,2,1,0:T(8,128)(2,1)}, bf16[2,4,32,896]{3,2,1,0:T(8,128)(2,1)}) custom-call(s32[8,512]{1,0:T(8,128)} %bitcast.14, f32[8,512]{1,0:T(8,128)} %bitcast.15, bf16[512,896]{1,0:T(8,128)(2,1)} %refs_2_.1, bf16[512,896]{1,0:T(8,128)(2,1)} %refs_3_.1), custom_call_target="tpu_custom_call" | custom-call | flops 469762048 | bytes 3670016 | tf_op jit(solution)/shard_map/pallas_call | solution.py:270
  4.5 1.5 %collective-permute-done.swap_ref.refs_1_ = bf16[2,4,32,896]{3,2,1,0:T(8,128)(2,1)S(1)} collective-permute-done((bf16[2,4,32,896]{3,2,1,0:T(8,128)(2,1)}, bf16[2,4,32,896]{3,2,1,0:T(8,128)(2,1)S(1)}, u32[]{:S(2)}, u32[]{:S(2)}) %collective-permute-start) | collective-permute-done | bytes 458784 | tf_op jit(solution)/shard_map/ppermute | solution.py:239
  6.1 5.0 %collective-permute-start.1 = (bf16[2,32,896]{2,1,0:T(8,128)(2,1)S(1)}, bf16[2,32,896]{2,1,0:T(8,128)(2,1)S(1)}, u32[]{:S(2)}, u32[]{:S(2)}) collective-permute-start(bf16[2,32,896]{2,1,0:T(8,128)(2,1)S(1)} %get-tuple-element.60), channel_id=1, source_target_pairs={{0,6},{1,7},{2,4},{3,5},{4,2},{5,3},{6,0},{7,1},{8,14},{9,15},{10,... | collective-permute-start | bytes 344072 | tf_op jit(solution)/shard_map/ppermute | solution.py:239
  11.8 3.4 %collective-permute-done.1.refs_2_ = bf16[2,32,896]{2,1,0:T(8,128)(2,1)S(1)} collective-permute-done((bf16[2,32,896]{2,1,0:T(8,128)(2,1)S(1)}, bf16[2,32,896]{2,1,0:T(8,128)(2,1)S(1)}, u32[]{:S(2)}, u32[]{:S(2)}) %collective-permute-start.1) | collective-permute-done | bytes 114720 | tf_op jit(solution)/shard_map/ppermute | solution.py:239
  15.2 5.9 %collective-permute-done.2.refs_3_ = bf16[2,32,896]{2,1,0:T(8,128)(2,1)S(1)} collective-permute-done((bf16[2,32,896]{2,1,0:T(8,128)(2,1)S(1)}, bf16[2,32,896]{2,1,0:T(8,128)(2,1)S(1)}, u32[]{:S(2)}, u32[]{:S(2)}) %collective-permute-start.2) | collective-permute-done | bytes 114720 | tf_op jit(solution)/shard_map/ppermute | solution.py:239
  22.4 1.6 %collective-permute-start.4 = (bf16[2,64,1024]{2,1,0:T(8,128)(2,1)S(1)}, bf16[2,64,1024]{2,1,0:T(8,128)(2,1)S(1)}, u32[]{:S(2)}, u32[]{:S(2)}) collective-permute-start(bf16[2,64,1024]{2,1,0:T(8,128)(2,1)S(1)} %get-tuple-element.65), channel_id=1, source_target_pairs={{0,8},{8,0},{16,24},{24,16},{1,9},{9,1},{17,25},{25,17},{2,10},{10... | collective-permute-start | bytes 786440 | tf_op jit(solution)/shard_map/ppermute | solution.py:239
  24.0 1.5 %collective-permute-start.5 = (bf16[2,64,1024]{2,1,0:T(8,128)(2,1)S(1)}, bf16[2,64,1024]{2,1,0:T(8,128)(2,1)S(1)}, u32[]{:S(2)}, u32[]{:S(2)}) collective-permute-start(bf16[2,64,1024]{2,1,0:T(8,128)(2,1)S(1)} %get-tuple-element.66), channel_id=1, source_target_pairs={{0,16},{8,24},{16,0},{24,8},{1,17},{9,25},{17,1},{25,9},{2,18},{10... | collective-permute-start | bytes 786440 | tf_op jit(solution)/shard_map/ppermute | solution.py:239
  26.0 2.5 %collective-permute-start.11 = (bf16[2,32,896]{2,1,0:T(8,128)(2,1)S(1)}, bf16[2,32,896]{2,1,0:T(8,128)(2,1)S(1)}, u32[]{:S(2)}, u32[]{:S(2)}) collective-permute-start(bf16[2,32,896]{2,1,0:T(8,128)(2,1)S(1)} %get-tuple-element.70), channel_id=1, source_target_pairs={{0,6},{1,7},{2,4},{3,5},{4,2},{5,3},{6,0},{7,1},{8,14},{9,15},{10,... | collective-permute-start | bytes 344072 | tf_op jit(solution)/shard_map/ppermute | solution.py:239
  28.4 3.3 %collective-permute-done.4.refs_1_ = bf16[2,64,1024]{2,1,0:T(8,128)(2,1)S(1)} collective-permute-done((bf16[2,64,1024]{2,1,0:T(8,128)(2,1)S(1)}, bf16[2,64,1024]{2,1,0:T(8,128)(2,1)S(1)}, u32[]{:S(2)}, u32[]{:S(2)}) %collective-permute-start.4) | collective-permute-done | bytes 262176 | tf_op jit(solution)/shard_map/ppermute | solution.py:239
  31.9 4.9 %collective-permute-done.5.refs_2_ = bf16[2,64,1024]{2,1,0:T(8,128)(2,1)S(1)} collective-permute-done((bf16[2,64,1024]{2,1,0:T(8,128)(2,1)S(1)}, bf16[2,64,1024]{2,1,0:T(8,128)(2,1)S(1)}, u32[]{:S(2)}, u32[]{:S(2)}) %collective-permute-start.5) | collective-permute-done | bytes 262176 | tf_op jit(solution)/shard_map/ppermute | solution.py:239
  39.1 1.4 %collective-permute-start.9 = (bf16[64,1024]{1,0:T(8,128)(2,1)S(1)}, bf16[64,1024]{1,0:T(8,128)(2,1)S(1)}, u32[]{:S(2)}, u32[]{:S(2)}) collective-permute-start(bf16[64,1024]{1,0:T(8,128)(2,1)S(1)} %shard_map.115.refs_0_), channel_id=1, source_target_pairs={{0,24},{8,16},{16,8},{24,0},{1,25},{9,17},{17,9},{25,1},{2,26},{10... | collective-permute-start | bytes 393224 | tf_op jit(solution)/shard_map/ppermute | solution.py:239
  43.5 1.4 %collective-permute-start.16 = (bf16[64,1024]{1,0:T(8,128)(2,1)S(1)}, bf16[64,1024]{1,0:T(8,128)(2,1)S(1)}, u32[]{:S(2)}, u32[]{:S(2)}) collective-permute-start(bf16[64,1024]{1,0:T(8,128)(2,1)S(1)} %get-tuple-element.79), channel_id=1, source_target_pairs={{0,24},{8,16},{16,8},{24,0},{1,25},{9,17},{17,9},{25,1},{2,26},{10... | collective-permute-start | bytes 393224 | tf_op jit(solution)/shard_map/ppermute | solution.py:239
  44.9 2.5 %collective-permute-done.9.refs_3_ = bf16[64,1024]{1,0:T(8,128)(2,1)S(1)} collective-permute-done((bf16[64,1024]{1,0:T(8,128)(2,1)S(1)}, bf16[64,1024]{1,0:T(8,128)(2,1)S(1)}, u32[]{:S(2)}, u32[]{:S(2)}) %collective-permute-start.9) | collective-permute-done | bytes 131104 | tf_op jit(solution)/shard_map/ppermute | solution.py:239
  48.6 1.7 %collective-permute-done.15.refs_6_ = bf16[64,1024]{1,0:T(8,128)(2,1)S(1)} collective-permute-done((bf16[64,1024]{1,0:T(8,128)(2,1)S(1)}, bf16[64,1024]{1,0:T(8,128)(2,1)S(1)}, u32[]{:S(2)}, u32[]{:S(2)}) %collective-permute-start.15) | collective-permute-done | bytes 131104 | tf_op jit(solution)/shard_map/ppermute | solution.py:239
  52.6 1.6 %collective-permute-start.19 = (bf16[2,64,1024]{2,1,0:T(8,128)(2,1)S(1)}, bf16[2,64,1024]{2,1,0:T(8,128)(2,1)S(1)}, u32[]{:S(2)}, u32[]{:S(2)}) collective-permute-start(bf16[2,64,1024]{2,1,0:T(8,128)(2,1)S(1)} %shard_map.118.refs_0_), channel_id=1, source_target_pairs={{0,24},{8,16},{16,8},{24,0},{1,25},{9,17},{17,9},{25,1},{2,26},{10... | collective-permute-start | bytes 786440 | tf_op jit(solution)/shard_map/ppermute | solution.py:239
  54.3 2.5 %collective-permute-start.21 = (bf16[2,32,896]{2,1,0:T(8,128)(2,1)S(1)}, bf16[2,32,896]{2,1,0:T(8,128)(2,1)S(1)}, u32[]{:S(2)}, u32[]{:S(2)}) collective-permute-start(bf16[2,32,896]{2,1,0:T(8,128)(2,1)S(1)} %get-tuple-element.81), channel_id=1, source_target_pairs={{0,6},{1,7},{2,4},{3,5},{4,2},{5,3},{6,0},{7,1},{8,14},{9,15},{10,... | collective-permute-start | bytes 344072 | tf_op jit(solution)/shard_map/ppermute | solution.py:239
  56.8 3.1 %collective-permute-done.17.refs_1_ = bf16[2,64,1024]{2,1,0:T(8,128)(2,1)S(1)} collective-permute-done((bf16[2,64,1024]{2,1,0:T(8,128)(2,1)S(1)}, bf16[2,64,1024]{2,1,0:T(8,128)(2,1)S(1)}, u32[]{:S(2)}, u32[]{:S(2)}) %collective-permute-start.17) | collective-permute-done | bytes 262176 | tf_op jit(solution)/shard_map/ppermute | solution.py:239
  60.5 2.8 %collective-permute-done.19.refs_3_ = bf16[2,64,1024]{2,1,0:T(8,128)(2,1)S(1)} collective-permute-done((bf16[2,64,1024]{2,1,0:T(8,128)(2,1)S(1)}, bf16[2,64,1024]{2,1,0:T(8,128)(2,1)S(1)}, u32[]{:S(2)}, u32[]{:S(2)}) %collective-permute-start.19) | collective-permute-done | bytes 262176 | tf_op jit(solution)/shard_map/ppermute | solution.py:239
  64.8 2.2 %collective-permute-start.22 = (bf16[2,32,896]{2,1,0:T(8,128)(2,1)S(1)}, bf16[2,32,896]{2,1,0:T(8,128)(2,1)S(1)}, u32[]{:S(2)}, u32[]{:S(2)}) collective-permute-start(bf16[2,32,896]{2,1,0:T(8,128)(2,1)S(1)} %get-tuple-element.84), channel_id=1, source_target_pairs={{0,2},{1,3},{2,0},{3,1},{4,6},{5,7},{6,4},{7,5},{8,10},{9,11},{10,... | collective-permute-start | bytes 344072 | tf_op jit(solution)/shard_map/ppermute | solution.py:239
  67.2 1.5 %collective-permute-start.24 = (bf16[2,32,896]{2,1,0:T(8,128)(2,1)S(1)}, bf16[2,32,896]{2,1,0:T(8,128)(2,1)S(1)}, u32[]{:S(2)}, u32[]{:S(2)}) collective-permute-start(bf16[2,32,896]{2,1,0:T(8,128)(2,1)S(1)} %get-tuple-element.92), channel_id=1, source_target_pairs={{0,6},{1,7},{2,4},{3,5},{4,2},{5,3},{6,0},{7,1},{8,14},{9,15},{10,... | collective-permute-start | bytes 344072 | tf_op jit(solution)/shard_map/ppermute | solution.py:239
  70.0 1.7 %collective-permute-start.26 = (bf16[2,32,896]{2,1,0:T(8,128)(2,1)S(1)}, bf16[2,32,896]{2,1,0:T(8,128)(2,1)S(1)}, u32[]{:S(2)}, u32[]{:S(2)}) collective-permute-start(bf16[2,32,896]{2,1,0:T(8,128)(2,1)S(1)} %get-tuple-element.91.refs_5_.refs_2_), channel_id=1, source_target_pairs={{0,2},{1,3},{2,0},{3,1},{4,6},{5,7},{6,4},{7,5},{8,10},{9,11},{10,... | collective-permute-start | bytes 344072 | tf_op jit(solution)/shard_map/ppermute | solution.py:239
  71.6 2.0 %shard_map.125 = bf16[1024,896]{1,0:T(8,128)(2,1)} custom-call(bf16[256,1024]{1,0:T(8,128)(2,1)S(1)} %get-tuple-element.99.left_ref, bf16[256,896]{1,0:T(8,128)(2,1)S(1)} %get-tuple-element.100.refs_0_), custom_call_target="tpu_custom_call" | custom-call | flops 469762048 | bytes 1835008 | tf_op jit(solution)/shard_map/pallas_call | solution.py:346
  74.9 2.5 %shard_map.124 = (bf16[896,1024]{1,0:T(8,128)(2,1)}, bf16[896,1024]{1,0:T(8,128)(2,1)}) custom-call(bf16[256,896]{1,0:T(8,128)(2,1)S(1)} %get-tuple-element.94.left_ref, bf16[256,1024]{1,0:T(8,128)(2,1)S(1)} %get-tuple-element.95.refs_0_, bf16[256,1024]{1,0:T(8,128)(2,1)S(1)} %get-tuple-element.96.refs_1_, ...), custom_call_target="tpu_custom_call" | custom-call | flops 939524096 | bytes 3670016 | tf_op jit(solution)/shard_map/pallas_call | solution.py:352
  77.5 3.1 %collective-permute-done.25.refs_3_ = bf16[2,32,896]{2,1,0:T(8,128)(2,1)S(1)} collective-permute-done((bf16[2,32,896]{2,1,0:T(8,128)(2,1)S(1)}, bf16[2,32,896]{2,1,0:T(8,128)(2,1)S(1)}, u32[]{:S(2)}, u32[]{:S(2)}) %collective-permute-start.25) | collective-permute-done | bytes 114720 | tf_op jit(solution)/shard_map/ppermute | solution.py:239
  (58 shorter events, 18.1 us)
Async XLA Ops:
  6.1 9.1 %collective-permute-start.1 = (bf16[2,32,896]{2,1,0:T(8,128)(2,1)S(1)}, bf16[2,32,896]{2,1,0:T(8,128)(2,1)S(1)}, u32[]{:S(2)}, u32[]{:S(2)}) collective-permute-start(bf16[2,32,896]{2,1,0:T(8,128)(2,1)S(1)} %get-tuple-element.60), channel_id=1, source_target_pairs={{0,6},{1,7},{2,4},{3,5},{4,2},{5,3},{6,0},{7,1},{8,14},{9,15},{10,... | collective-permute-start | bytes 344072 | tf_op jit(solution)/shard_map/ppermute | solution.py:239
  11.1 10.0 %collective-permute-start.2 = (bf16[2,32,896]{2,1,0:T(8,128)(2,1)S(1)}, bf16[2,32,896]{2,1,0:T(8,128)(2,1)S(1)}, u32[]{:S(2)}, u32[]{:S(2)}) collective-permute-start(bf16[2,32,896]{2,1,0:T(8,128)(2,1)S(1)} %get-tuple-element.61), channel_id=1, source_target_pairs={{0,4},{1,5},{2,6},{3,7},{4,0},{5,1},{6,2},{7,3},{8,12},{9,13},{10,... | collective-permute-start | bytes 344072 | tf_op jit(solution)/shard_map/ppermute | solution.py:239
  11.1 10.0 %collective-permute-start.3 = (bf16[2,32,896]{2,1,0:T(8,128)(2,1)S(1)}, bf16[2,32,896]{2,1,0:T(8,128)(2,1)S(1)}, u32[]{:S(2)}, u32[]{:S(2)}) collective-permute-start(bf16[2,32,896]{2,1,0:T(8,128)(2,1)S(1)} %get-tuple-element.62), channel_id=1, source_target_pairs={{0,2},{1,3},{2,0},{3,1},{4,6},{5,7},{6,4},{7,5},{8,10},{9,11},{10,... | collective-permute-start | bytes 344072 | tf_op jit(solution)/shard_map/ppermute | solution.py:239
  22.4 9.3 %collective-permute-start.4 = (bf16[2,64,1024]{2,1,0:T(8,128)(2,1)S(1)}, bf16[2,64,1024]{2,1,0:T(8,128)(2,1)S(1)}, u32[]{:S(2)}, u32[]{:S(2)}) collective-permute-start(bf16[2,64,1024]{2,1,0:T(8,128)(2,1)S(1)} %get-tuple-element.65), channel_id=1, source_target_pairs={{0,8},{8,0},{16,24},{24,16},{1,9},{9,1},{17,25},{25,17},{2,10},{10... | collective-permute-start | bytes 786440 | tf_op jit(solution)/shard_map/ppermute | solution.py:239
  24.0 12.9 %collective-permute-start.5 = (bf16[2,64,1024]{2,1,0:T(8,128)(2,1)S(1)}, bf16[2,64,1024]{2,1,0:T(8,128)(2,1)S(1)}, u32[]{:S(2)}, u32[]{:S(2)}) collective-permute-start(bf16[2,64,1024]{2,1,0:T(8,128)(2,1)S(1)} %get-tuple-element.66), channel_id=1, source_target_pairs={{0,16},{8,24},{16,0},{24,8},{1,17},{9,25},{17,1},{25,9},{2,18},{10... | collective-permute-start | bytes 786440 | tf_op jit(solution)/shard_map/ppermute | solution.py:239
  25.5 11.3 %collective-permute-start.6 = (bf16[2,64,1024]{2,1,0:T(8,128)(2,1)S(1)}, bf16[2,64,1024]{2,1,0:T(8,128)(2,1)S(1)}, u32[]{:S(2)}, u32[]{:S(2)}) collective-permute-start(bf16[2,64,1024]{2,1,0:T(8,128)(2,1)S(1)} %get-tuple-element.67), channel_id=1, source_target_pairs={{0,24},{8,16},{16,8},{24,0},{1,25},{9,17},{17,9},{25,1},{2,26},{10... | collective-permute-start | bytes 786440 | tf_op jit(solution)/shard_map/ppermute | solution.py:239
  26.0 13.2 %collective-permute-start.11 = (bf16[2,32,896]{2,1,0:T(8,128)(2,1)S(1)}, bf16[2,32,896]{2,1,0:T(8,128)(2,1)S(1)}, u32[]{:S(2)}, u32[]{:S(2)}) collective-permute-start(bf16[2,32,896]{2,1,0:T(8,128)(2,1)S(1)} %get-tuple-element.70), channel_id=1, source_target_pairs={{0,6},{1,7},{2,4},{3,5},{4,2},{5,3},{6,0},{7,1},{8,14},{9,15},{10,... | collective-permute-start | bytes 344072 | tf_op jit(solution)/shard_map/ppermute | solution.py:239
  28.4 12.1 %collective-permute-start.12 = (bf16[2,32,896]{2,1,0:T(8,128)(2,1)S(1)}, bf16[2,32,896]{2,1,0:T(8,128)(2,1)S(1)}, u32[]{:S(2)}, u32[]{:S(2)}) collective-permute-start(bf16[2,32,896]{2,1,0:T(8,128)(2,1)S(1)} %get-tuple-element.71), channel_id=1, source_target_pairs={{0,4},{1,5},{2,6},{3,7},{4,0},{5,1},{6,2},{7,3},{8,12},{9,13},{10,... | collective-permute-start | bytes 344072 | tf_op jit(solution)/shard_map/ppermute | solution.py:239
  31.7 8.9 %collective-permute-start.13 = (bf16[2,32,896]{2,1,0:T(8,128)(2,1)S(1)}, bf16[2,32,896]{2,1,0:T(8,128)(2,1)S(1)}, u32[]{:S(2)}, u32[]{:S(2)}) collective-permute-start(bf16[2,32,896]{2,1,0:T(8,128)(2,1)S(1)} %get-tuple-element.72), channel_id=1, source_target_pairs={{0,2},{1,3},{2,0},{3,1},{4,6},{5,7},{6,4},{7,5},{8,10},{9,11},{10,... | collective-permute-start | bytes 344072 | tf_op jit(solution)/shard_map/ppermute | solution.py:239
  37.0 6.4 %collective-permute-start.7 = (bf16[64,1024]{1,0:T(8,128)(2,1)S(1)}, bf16[64,1024]{1,0:T(8,128)(2,1)S(1)}, u32[]{:S(2)}, u32[]{:S(2)}) collective-permute-start(bf16[64,1024]{1,0:T(8,128)(2,1)S(1)} %shard_map.115.refs_0_), channel_id=1, source_target_pairs={{0,8},{8,0},{16,24},{24,16},{1,9},{9,1},{17,25},{25,17},{2,10},{10... | collective-permute-start | bytes 393224 | tf_op jit(solution)/shard_map/ppermute | solution.py:239
  38.3 6.6 %collective-permute-start.8 = (bf16[64,1024]{1,0:T(8,128)(2,1)S(1)}, bf16[64,1024]{1,0:T(8,128)(2,1)S(1)}, u32[]{:S(2)}, u32[]{:S(2)}) collective-permute-start(bf16[64,1024]{1,0:T(8,128)(2,1)S(1)} %shard_map.115.refs_0_), channel_id=1, source_target_pairs={{0,16},{8,24},{16,0},{24,8},{1,17},{9,25},{17,1},{25,9},{2,18},{10... | collective-permute-start | bytes 393224 | tf_op jit(solution)/shard_map/ppermute | solution.py:239
  39.1 8.2 %collective-permute-start.9 = (bf16[64,1024]{1,0:T(8,128)(2,1)S(1)}, bf16[64,1024]{1,0:T(8,128)(2,1)S(1)}, u32[]{:S(2)}, u32[]{:S(2)}) collective-permute-start(bf16[64,1024]{1,0:T(8,128)(2,1)S(1)} %shard_map.115.refs_0_), channel_id=1, source_target_pairs={{0,24},{8,16},{16,8},{24,0},{1,25},{9,17},{17,9},{25,1},{2,26},{10... | collective-permute-start | bytes 393224 | tf_op jit(solution)/shard_map/ppermute | solution.py:239
  41.3 7.3 %collective-permute-start.14 = (bf16[64,1024]{1,0:T(8,128)(2,1)S(1)}, bf16[64,1024]{1,0:T(8,128)(2,1)S(1)}, u32[]{:S(2)}, u32[]{:S(2)}) collective-permute-start(bf16[64,1024]{1,0:T(8,128)(2,1)S(1)} %get-tuple-element.77), channel_id=1, source_target_pairs={{0,8},{8,0},{16,24},{24,16},{1,9},{9,1},{17,25},{25,17},{2,10},{10... | collective-permute-start | bytes 393224 | tf_op jit(solution)/shard_map/ppermute | solution.py:239
  42.6 7.7 %collective-permute-start.15 = (bf16[64,1024]{1,0:T(8,128)(2,1)S(1)}, bf16[64,1024]{1,0:T(8,128)(2,1)S(1)}, u32[]{:S(2)}, u32[]{:S(2)}) collective-permute-start(bf16[64,1024]{1,0:T(8,128)(2,1)S(1)} %get-tuple-element.78), channel_id=1, source_target_pairs={{0,16},{8,24},{16,0},{24,8},{1,17},{9,25},{17,1},{25,9},{2,18},{10... | collective-permute-start | bytes 393224 | tf_op jit(solution)/shard_map/ppermute | solution.py:239
  43.5 6.8 %collective-permute-start.16 = (bf16[64,1024]{1,0:T(8,128)(2,1)S(1)}, bf16[64,1024]{1,0:T(8,128)(2,1)S(1)}, u32[]{:S(2)}, u32[]{:S(2)}) collective-permute-start(bf16[64,1024]{1,0:T(8,128)(2,1)S(1)} %get-tuple-element.79), channel_id=1, source_target_pairs={{0,24},{8,16},{16,8},{24,0},{1,25},{9,17},{17,9},{25,1},{2,26},{10... | collective-permute-start | bytes 393224 | tf_op jit(solution)/shard_map/ppermute | solution.py:239
  50.6 9.3 %collective-permute-start.17 = (bf16[2,64,1024]{2,1,0:T(8,128)(2,1)S(1)}, bf16[2,64,1024]{2,1,0:T(8,128)(2,1)S(1)}, u32[]{:S(2)}, u32[]{:S(2)}) collective-permute-start(bf16[2,64,1024]{2,1,0:T(8,128)(2,1)S(1)} %shard_map.118.refs_0_), channel_id=1, source_target_pairs={{0,8},{8,0},{16,24},{24,16},{1,9},{9,1},{17,25},{25,17},{2,10},{10... | collective-permute-start | bytes 786440 | tf_op jit(solution)/shard_map/ppermute | solution.py:239
  51.5 9.0 %collective-permute-start.18 = (bf16[2,64,1024]{2,1,0:T(8,128)(2,1)S(1)}, bf16[2,64,1024]{2,1,0:T(8,128)(2,1)S(1)}, u32[]{:S(2)}, u32[]{:S(2)}) collective-permute-start(bf16[2,64,1024]{2,1,0:T(8,128)(2,1)S(1)} %shard_map.118.refs_0_), channel_id=1, source_target_pairs={{0,16},{8,24},{16,0},{24,8},{1,17},{9,25},{17,1},{25,9},{2,18},{10... | collective-permute-start | bytes 786440 | tf_op jit(solution)/shard_map/ppermute | solution.py:239
  52.6 10.7 %collective-permute-start.19 = (bf16[2,64,1024]{2,1,0:T(8,128)(2,1)S(1)}, bf16[2,64,1024]{2,1,0:T(8,128)(2,1)S(1)}, u32[]{:S(2)}, u32[]{:S(2)}) collective-permute-start(bf16[2,64,1024]{2,1,0:T(8,128)(2,1)S(1)} %shard_map.118.refs_0_), channel_id=1, source_target_pairs={{0,24},{8,16},{16,8},{24,0},{1,25},{9,17},{17,9},{25,1},{2,26},{10... | collective-permute-start | bytes 786440 | tf_op jit(solution)/shard_map/ppermute | solution.py:239
  54.2 9.2 %collective-permute-start.20 = (bf16[2,32,896]{2,1,0:T(8,128)(2,1)S(1)}, bf16[2,32,896]{2,1,0:T(8,128)(2,1)S(1)}, u32[]{:S(2)}, u32[]{:S(2)}) collective-permute-start(bf16[2,32,896]{2,1,0:T(8,128)(2,1)S(1)} %get-tuple-element.80), channel_id=1, source_target_pairs={{0,4},{1,5},{2,6},{3,7},{4,0},{5,1},{6,2},{7,3},{8,12},{9,13},{10,... | collective-permute-start | bytes 344072 | tf_op jit(solution)/shard_map/ppermute | solution.py:239
  54.3 9.1 %collective-permute-start.21 = (bf16[2,32,896]{2,1,0:T(8,128)(2,1)S(1)}, bf16[2,32,896]{2,1,0:T(8,128)(2,1)S(1)}, u32[]{:S(2)}, u32[]{:S(2)}) collective-permute-start(bf16[2,32,896]{2,1,0:T(8,128)(2,1)S(1)} %get-tuple-element.81), channel_id=1, source_target_pairs={{0,6},{1,7},{2,4},{3,5},{4,2},{5,3},{6,0},{7,1},{8,14},{9,15},{10,... | collective-permute-start | bytes 344072 | tf_op jit(solution)/shard_map/ppermute | solution.py:239
  64.8 8.8 %collective-permute-start.22 = (bf16[2,32,896]{2,1,0:T(8,128)(2,1)S(1)}, bf16[2,32,896]{2,1,0:T(8,128)(2,1)S(1)}, u32[]{:S(2)}, u32[]{:S(2)}) collective-permute-start(bf16[2,32,896]{2,1,0:T(8,128)(2,1)S(1)} %get-tuple-element.84), channel_id=1, source_target_pairs={{0,2},{1,3},{2,0},{3,1},{4,6},{5,7},{6,4},{7,5},{8,10},{9,11},{10,... | collective-permute-start | bytes 344072 | tf_op jit(solution)/shard_map/ppermute | solution.py:239
  67.2 10.3 %collective-permute-start.24 = (bf16[2,32,896]{2,1,0:T(8,128)(2,1)S(1)}, bf16[2,32,896]{2,1,0:T(8,128)(2,1)S(1)}, u32[]{:S(2)}, u32[]{:S(2)}) collective-permute-start(bf16[2,32,896]{2,1,0:T(8,128)(2,1)S(1)} %get-tuple-element.92), channel_id=1, source_target_pairs={{0,6},{1,7},{2,4},{3,5},{4,2},{5,3},{6,0},{7,1},{8,14},{9,15},{10,... | collective-permute-start | bytes 344072 | tf_op jit(solution)/shard_map/ppermute | solution.py:239
  68.7 11.8 %collective-permute-start.25 = (bf16[2,32,896]{2,1,0:T(8,128)(2,1)S(1)}, bf16[2,32,896]{2,1,0:T(8,128)(2,1)S(1)}, u32[]{:S(2)}, u32[]{:S(2)}) collective-permute-start(bf16[2,32,896]{2,1,0:T(8,128)(2,1)S(1)} %get-tuple-element.93), channel_id=1, source_target_pairs={{0,4},{1,5},{2,6},{3,7},{4,0},{5,1},{6,2},{7,3},{8,12},{9,13},{10,... | collective-permute-start | bytes 344072 | tf_op jit(solution)/shard_map/ppermute | solution.py:239
  70.0 10.5 %collective-permute-start.26 = (bf16[2,32,896]{2,1,0:T(8,128)(2,1)S(1)}, bf16[2,32,896]{2,1,0:T(8,128)(2,1)S(1)}, u32[]{:S(2)}, u32[]{:S(2)}) collective-permute-start(bf16[2,32,896]{2,1,0:T(8,128)(2,1)S(1)} %get-tuple-element.91.refs_5_.refs_2_), channel_id=1, source_target_pairs={{0,2},{1,3},{2,0},{3,1},{4,6},{5,7},{6,4},{7,5},{8,10},{9,11},{10,... | collective-permute-start | bytes 344072 | tf_op jit(solution)/shard_map/ppermute | solution.py:239
  (9 other events, 72.7 us)

commit v12 on v11

--- a/solution.py
+++ b/solution.py
@@ -48,41 +48,54 @@
 
 
 def route_kernel(experts, *refs):
-    pick_ref, weight_ref, keep_ref, swap_ref = refs[4:8]
-    ids_ref, gates_ref, tokens_ref, grad_ref, sems = refs[8:]
-    copies = [
-        pltpu.make_async_copy(refs[k], refs[8 + k], sems.at[k]) for k in range(4)
-    ]
+    outs, scratch, (earlier_ref, in_sems, out_sems) = refs[4:8], refs[8:16], refs[16:]
+    ids_ref, gates_ref, tokens_ref, grad_ref, pick_ref, weight_ref, keep_ref, swap_ref = scratch
+    copies = [pltpu.make_async_copy(refs[k], scratch[k], in_sems.at[k]) for k in range(4)]
     for copy in copies:
         copy.start()
+    sent = []
+
+    def send(from_ref, to_ref):
+        sent.append(pltpu.make_async_copy(from_ref, to_ref, out_sems.at[len(sent)]))
+        sent[-1].start()
+
+    tok_rows = ids_ref.shape[1]
+    slots = pick_ref.shape[0]
+    earlier = lax.broadcasted_iota(jnp.int32, (tok_rows, tok_rows), 0) < lax.broadcasted_iota(
+        jnp.int32, (tok_rows, tok_rows), 1
+    )
+    earlier_ref[...] = earlier.astype(F32).astype(BF16)
     copies[0].wait()
     copies[1].wait()
     ids = ids_ref[...]
-    tok_rows = ids.shape[1]
-    slots = pick_ref.shape[0]
     inside = ids < experts
     routed = jnp.max(inside.astype(jnp.int32), axis=0, keepdims=True)
     chosen = jnp.sum(jnp.where(inside, ids, 0), axis=0, keepdims=True)
     weight = jnp.sum(jnp.where(inside, gates_ref[...], 0.0), axis=0, keepdims=True)
     key = jnp.where(routed > 0, chosen ^ lax.axis_index("expert"), experts)
     hot = lax.broadcasted_iota(jnp.int32, (experts, tok_rows), 0) == key
-    earlier = lax.broadcasted_iota(jnp.int32, (tok_rows, tok_rows), 0) < lax.broadcasted_iota(
-        jnp.int32, (tok_rows, tok_rows), 1
-    )
-    before = mm(hot.astype(F32).astype(BF16), earlier.astype(F32).astype(BF16), ((1,), (0,)))
+    before = mm(hot.astype(F32).astype(BF16), earlier_ref[...], ((1,), (0,)))
     position = jnp.sum(jnp.where(hot, before, 0.0), axis=0, keepdims=True).astype(jnp.int32)
     slot = jnp.where(routed > 0, key * (slots // experts) + position, slots)
-    pick = lax.broadcasted_iota(jnp.int32, (slots, tok_rows), 0) == slot
-    slot_weight = jnp.sum(jnp.where(pick, weight, 0.0), axis=1, keepdims=True)
-    weight_ref[...] = slot_weight
-    pick = pick.astype(F32).astype(BF16)
+    match = lax.broadcasted_iota(jnp.int32, (slots, tok_rows), 0) == slot
+    pick = match.astype(F32).astype(BF16)
     pick_ref[...] = pick
     copies[2].wait()
     rows = mm(pick, tokens_ref[...], ((1,), (0,))).astype(BF16)
     split_cores(keep_ref, swap_ref, rows, 0)
+    send(swap_ref.at[0], outs[3].at[0])
+    send(keep_ref.at[0], outs[2].at[0])
+    send(pick_ref, outs[0])
+    slot_weight = jnp.sum(jnp.where(match, weight, 0.0), axis=1, keepdims=True)
+    weight_ref[...] = slot_weight
+    send(weight_ref, outs[1])
     copies[3].wait()
     rows = (slot_weight * mm(pick, grad_ref[...], ((1,), (0,)))).astype(BF16)
     split_cores(keep_ref, swap_ref, rows, 1)
+    send(swap_ref.at[1], outs[3].at[1])
+    send(keep_ref.at[1], outs[2].at[1])
+    for copy in sent:
+        copy.wait()
 
 
 def load_kernel(from_ref, to_ref):
@@ -274,9 +287,12 @@
         8 * tok_rows * features,
         limit=ROUTE_LIMIT,
         in_specs=[ANY] * 4,
+        out_specs=(ANY,) * 4,
         scratch_shapes=[
-            *[pltpu.VMEM(array.shape, array.dtype) for array in ins],
+            *[pltpu.VMEM(array.shape, array.dtype) for array in (*ins, *outs)],
+            pltpu.VMEM((tok_rows, tok_rows), BF16),
             pltpu.SemaphoreType.DMA((4,)),
+            pltpu.SemaphoreType.DMA((6,)),
         ],
     )(*ins)
     swap_to, up_mat = lax.optimization_barrier((swap, up_mat))
@@ -330,7 +346,8 @@
     out_swap = partner(out_swap, "expert", 1)
     out_near, *out_far = call(pack_back_kernel, back, 0, 8 * slots)(out_keep, out_swap)
     out_far = [partner(value, "expert", 2 * (2 + k)) for k, value in enumerate(out_far)]
-    pre, out_far = lax.optimization_barrier((pre, out_far))
+    out_near = partner(out_near, "expert", 2)
+    pre, out_far, out_near = lax.optimization_barrier((pre, out_far, out_near))
     gate_pre, up_pre, grad_keep, grad_swap = call(
         functools.partial(row_grad_kernel, dp),
         (wide, wide, one, one),
@@ -339,7 +356,6 @@
         scratch_shapes=in_order,
     )(*pre, gate_mat, up_mat)
     grad_swap = partner(grad_swap, "expert", 1)
-    out_near = partner(out_near, "expert", 2)
     grad_to = call(pack_back_kernel, back, 0, 8 * slots)(grad_keep, grad_swap)
     grad_back = [partner(value, "expert", 2 * (1 + k)) for k, value in enumerate(grad_to)]
 

time: 81.9 us -> 88.1 us (1.076)
  waiting for transfers between devices: 33.3 us -> 38.4 us
  starting transfers between devices: 32.5 us -> 33.7 us
    ppermute x27, waiting for transfers between devices: 33.3 us -> 38.4 us  [partner(): return lax.ppermute(value, axis, [(i, i ^ k) for i in range(size)])]
    ppermute x27, starting transfers between devices: 32.5 us -> 33.7 us  [partner(): return lax.ppermute(value, axis, [(i, i ^ k) for i in range(size)])]
  transfers between devices with their start and end apart: 27 -> 27, of which waited for: 13 -> 16; matrix products, arithmetic and copies ran while one was open for 0% -> 0% of each run, Pallas kernels for 10% -> 8%
where the time goes in v12:
time: 88.1 us; the launch traced here: 87.9 us
  waiting for transfers between devices  38.4 us (44%)
  starting transfers between devices  33.7 us (38%)
  Pallas kernels  15 us (17%)
    ppermute x27, waiting for transfers between devices, partner(): return lax.ppermute(value, axis, [(i, i ^ k) for i in range(size)])  38.4 us
    ppermute x27, starting transfers between devices, partner(): return lax.ppermute(value, axis, [(i, i ^ k) for i in range(size)])  33.7 us
    pallas_call x1, Pallas kernels, body(): call(functools.partial(route_kernel, experts), outs, 4 * slots * tok_rows...  3.12 us
    pallas_call x1, Pallas kernels, body(): call(functools.partial(grads_kernel, 2), [shape((features, hidden), BF16)...  2.54 us
    pallas_call x1, Pallas kernels, body(): call(functools.partial(grads_kernel, 1), [shape((hidden, features), BF16)...  1.97 us
  transfers between devices with their start and end apart: 27, of which 16 were waited for; matrix products, arithmetic and copies ran while one was open for 0% of the time, Pallas kernels for 8%

profile of v12, /device:TPU:0, one launch (start us, length us, event | category | flops | bytes accessed | tf_op | source)
XLA Modules:
  0.0 87.9 jit_solution(724116348097954208)
XLA Ops:
  0.6 3.1 %shard_map.110 = (bf16[256,512]{1,0:T(8,128)(2,1)}, f32[256,1]{1,0:T(8,128)}, bf16[2,4,32,896]{3,2,1,0:T(8,128)(2,1)}, bf16[2,4,32,896]{3,2,1,0:T(8,128)(2,1)}) custom-call(s32[8,512]{1,0:T(8,128)} %bitcast.14, f32[8,512]{1,0:T(8,128)} %bitcast.15, bf16[512,896]{1,0:T(8,128)(2,1)} %refs_2_.1, bf16[512,896]{1,0:T(8,128)(2,1)} %refs_3_.1), custom_call_target="tpu_custom_call" | custom-call | flops 469762048 | bytes 3670016 | tf_op jit(solution)/shard_map/pallas_call | solution.py:283
  4.4 1.5 %collective-permute-done.swap_ref.refs_1_ = bf16[2,4,32,896]{3,2,1,0:T(8,128)(2,1)S(1)} collective-permute-done((bf16[2,4,32,896]{3,2,1,0:T(8,128)(2,1)}, bf16[2,4,32,896]{3,2,1,0:T(8,128)(2,1)S(1)}, u32[]{:S(2)}, u32[]{:S(2)}) %collective-permute-start) | collective-permute-done | bytes 458784 | tf_op jit(solution)/shard_map/ppermute | solution.py:252
  6.0 5.0 %collective-permute-start.1 = (bf16[2,32,896]{2,1,0:T(8,128)(2,1)S(1)}, bf16[2,32,896]{2,1,0:T(8,128)(2,1)S(1)}, u32[]{:S(2)}, u32[]{:S(2)}) collective-permute-start(bf16[2,32,896]{2,1,0:T(8,128)(2,1)S(1)} %get-tuple-element.61), channel_id=1, source_target_pairs={{0,6},{1,7},{2,4},{3,5},{4,2},{5,3},{6,0},{7,1},{8,14},{9,15},{10,... | collective-permute-start | bytes 344072 | tf_op jit(solution)/shard_map/ppermute | solution.py:252
  11.7 3.4 %collective-permute-done.1.refs_2_ = bf16[2,32,896]{2,1,0:T(8,128)(2,1)S(1)} collective-permute-done((bf16[2,32,896]{2,1,0:T(8,128)(2,1)S(1)}, bf16[2,32,896]{2,1,0:T(8,128)(2,1)S(1)}, u32[]{:S(2)}, u32[]{:S(2)}) %collective-permute-start.1) | collective-permute-done | bytes 114720 | tf_op jit(solution)/shard_map/ppermute | solution.py:252
  15.1 5.9 %collective-permute-done.2.refs_3_ = bf16[2,32,896]{2,1,0:T(8,128)(2,1)S(1)} collective-permute-done((bf16[2,32,896]{2,1,0:T(8,128)(2,1)S(1)}, bf16[2,32,896]{2,1,0:T(8,128)(2,1)S(1)}, u32[]{:S(2)}, u32[]{:S(2)}) %collective-permute-start.2) | collective-permute-done | bytes 114720 | tf_op jit(solution)/shard_map/ppermute | solution.py:252
  22.3 1.6 %collective-permute-start.4 = (bf16[2,64,1024]{2,1,0:T(8,128)(2,1)S(1)}, bf16[2,64,1024]{2,1,0:T(8,128)(2,1)S(1)}, u32[]{:S(2)}, u32[]{:S(2)}) collective-permute-start(bf16[2,64,1024]{2,1,0:T(8,128)(2,1)S(1)} %get-tuple-element.66), channel_id=1, source_target_pairs={{0,8},{8,0},{16,24},{24,16},{1,9},{9,1},{17,25},{25,17},{2,10},{10... | collective-permute-start | bytes 786440 | tf_op jit(solution)/shard_map/ppermute | solution.py:252
  23.9 1.5 %collective-permute-start.5 = (bf16[2,64,1024]{2,1,0:T(8,128)(2,1)S(1)}, bf16[2,64,1024]{2,1,0:T(8,128)(2,1)S(1)}, u32[]{:S(2)}, u32[]{:S(2)}) collective-permute-start(bf16[2,64,1024]{2,1,0:T(8,128)(2,1)S(1)} %get-tuple-element.67), channel_id=1, source_target_pairs={{0,16},{8,24},{16,0},{24,8},{1,17},{9,25},{17,1},{25,9},{2,18},{10... | collective-permute-start | bytes 786440 | tf_op jit(solution)/shard_map/ppermute | solution.py:252
  25.9 2.5 %collective-permute-start.11 = (bf16[2,32,896]{2,1,0:T(8,128)(2,1)S(1)}, bf16[2,32,896]{2,1,0:T(8,128)(2,1)S(1)}, u32[]{:S(2)}, u32[]{:S(2)}) collective-permute-start(bf16[2,32,896]{2,1,0:T(8,128)(2,1)S(1)} %get-tuple-element.71), channel_id=1, source_target_pairs={{0,6},{1,7},{2,4},{3,5},{4,2},{5,3},{6,0},{7,1},{8,14},{9,15},{10,... | collective-permute-start | bytes 344072 | tf_op jit(solution)/shard_map/ppermute | solution.py:252
  28.4 3.3 %collective-permute-done.4.refs_1_ = bf16[2,64,1024]{2,1,0:T(8,128)(2,1)S(1)} collective-permute-done((bf16[2,64,1024]{2,1,0:T(8,128)(2,1)S(1)}, bf16[2,64,1024]{2,1,0:T(8,128)(2,1)S(1)}, u32[]{:S(2)}, u32[]{:S(2)}) %collective-permute-start.4) | collective-permute-done | bytes 262176 | tf_op jit(solution)/shard_map/ppermute | solution.py:252
  31.8 4.9 %collective-permute-done.5.refs_2_ = bf16[2,64,1024]{2,1,0:T(8,128)(2,1)S(1)} collective-permute-done((bf16[2,64,1024]{2,1,0:T(8,128)(2,1)S(1)}, bf16[2,64,1024]{2,1,0:T(8,128)(2,1)S(1)}, u32[]{:S(2)}, u32[]{:S(2)}) %collective-permute-start.5) | collective-permute-done | bytes 262176 | tf_op jit(solution)/shard_map/ppermute | solution.py:252
  38.9 1.6 %collective-permute-start.14 = (bf16[64,1024]{1,0:T(8,128)(2,1)S(1)}, bf16[64,1024]{1,0:T(8,128)(2,1)S(1)}, u32[]{:S(2)}, u32[]{:S(2)}) collective-permute-start(bf16[64,1024]{1,0:T(8,128)(2,1)S(1)} %get-tuple-element.78), channel_id=1, source_target_pairs={{0,8},{8,0},{16,24},{24,16},{1,9},{9,1},{17,25},{25,17},{2,10},{10... | collective-permute-start | bytes 393224 | tf_op jit(solution)/shard_map/ppermute | solution.py:252
  40.5 1.5 %collective-permute-start.15 = (bf16[64,1024]{1,0:T(8,128)(2,1)S(1)}, bf16[64,1024]{1,0:T(8,128)(2,1)S(1)}, u32[]{:S(2)}, u32[]{:S(2)}) collective-permute-start(bf16[64,1024]{1,0:T(8,128)(2,1)S(1)} %get-tuple-element.79), channel_id=1, source_target_pairs={{0,16},{8,24},{16,0},{24,8},{1,17},{9,25},{17,1},{25,9},{2,18},{10... | collective-permute-start | bytes 393224 | tf_op jit(solution)/shard_map/ppermute | solution.py:252
  42.5 1.5 %collective-permute-start.7 = (bf16[64,1024]{1,0:T(8,128)(2,1)S(1)}, bf16[64,1024]{1,0:T(8,128)(2,1)S(1)}, u32[]{:S(2)}, u32[]{:S(2)}) collective-permute-start(bf16[64,1024]{1,0:T(8,128)(2,1)S(1)} %shard_map.115.refs_0_), channel_id=1, source_target_pairs={{0,8},{8,0},{16,24},{24,16},{1,9},{9,1},{17,25},{25,17},{2,10},{10... | collective-permute-start | bytes 393224 | tf_op jit(solution)/shard_map/ppermute | solution.py:252
  44.0 1.5 %collective-permute-start.8 = (bf16[64,1024]{1,0:T(8,128)(2,1)S(1)}, bf16[64,1024]{1,0:T(8,128)(2,1)S(1)}, u32[]{:S(2)}, u32[]{:S(2)}) collective-permute-start(bf16[64,1024]{1,0:T(8,128)(2,1)S(1)} %shard_map.115.refs_0_), channel_id=1, source_target_pairs={{0,16},{8,24},{16,0},{24,8},{1,17},{9,25},{17,1},{25,9},{2,18},{10... | collective-permute-start | bytes 393224 | tf_op jit(solution)/shard_map/ppermute | solution.py:252
  45.5 2.4 %collective-permute-start.9 = (bf16[64,1024]{1,0:T(8,128)(2,1)S(1)}, bf16[64,1024]{1,0:T(8,128)(2,1)S(1)}, u32[]{:S(2)}, u32[]{:S(2)}) collective-permute-start(bf16[64,1024]{1,0:T(8,128)(2,1)S(1)} %shard_map.115.refs_0_), channel_id=1, source_target_pairs={{0,24},{8,16},{16,8},{24,0},{1,25},{9,17},{17,9},{25,1},{2,26},{10... | collective-permute-start | bytes 393224 | tf_op jit(solution)/shard_map/ppermute | solution.py:252
  51.6 3.4 %collective-permute-done.9.refs_3_ = bf16[64,1024]{1,0:T(8,128)(2,1)S(1)} collective-permute-done((bf16[64,1024]{1,0:T(8,128)(2,1)S(1)}, bf16[64,1024]{1,0:T(8,128)(2,1)S(1)}, u32[]{:S(2)}, u32[]{:S(2)}) %collective-permute-start.9) | collective-permute-done | bytes 131104 | tf_op jit(solution)/shard_map/ppermute | solution.py:252
  56.4 2.3 %collective-permute-start.19 = (bf16[2,64,1024]{2,1,0:T(8,128)(2,1)S(1)}, bf16[2,64,1024]{2,1,0:T(8,128)(2,1)S(1)}, u32[]{:S(2)}, u32[]{:S(2)}) collective-permute-start(bf16[2,64,1024]{2,1,0:T(8,128)(2,1)S(1)} %shard_map.118.refs_0_), channel_id=1, source_target_pairs={{0,24},{8,16},{16,8},{24,0},{1,25},{9,17},{17,9},{25,1},{2,26},{10... | collective-permute-start | bytes 786440 | tf_op jit(solution)/shard_map/ppermute | solution.py:252
  58.8 1.9 %collective-permute-start.21 = (bf16[2,32,896]{2,1,0:T(8,128)(2,1)S(1)}, bf16[2,32,896]{2,1,0:T(8,128)(2,1)S(1)}, u32[]{:S(2)}, u32[]{:S(2)}) collective-permute-start(bf16[2,32,896]{2,1,0:T(8,128)(2,1)S(1)} %get-tuple-element.82), channel_id=1, source_target_pairs={{0,6},{1,7},{2,4},{3,5},{4,2},{5,3},{6,0},{7,1},{8,14},{9,15},{10,... | collective-permute-start | bytes 344072 | tf_op jit(solution)/shard_map/ppermute | solution.py:252
  60.7 1.5 %collective-permute-start.22 = (bf16[2,32,896]{2,1,0:T(8,128)(2,1)S(1)}, bf16[2,32,896]{2,1,0:T(8,128)(2,1)S(1)}, u32[]{:S(2)}, u32[]{:S(2)}) collective-permute-start(bf16[2,32,896]{2,1,0:T(8,128)(2,1)S(1)} %get-tuple-element.83), channel_id=1, source_target_pairs={{0,2},{1,3},{2,0},{3,1},{4,6},{5,7},{6,4},{7,5},{8,10},{9,11},{10,... | collective-permute-start | bytes 344072 | tf_op jit(solution)/shard_map/ppermute | solution.py:252
  62.3 7.9 %collective-permute-done.18.refs_2_ = bf16[2,64,1024]{2,1,0:T(8,128)(2,1)S(1)} collective-permute-done((bf16[2,64,1024]{2,1,0:T(8,128)(2,1)S(1)}, bf16[2,64,1024]{2,1,0:T(8,128)(2,1)S(1)}, u32[]{:S(2)}, u32[]{:S(2)}) %collective-permute-start.18) | collective-permute-done | bytes 262176 | tf_op jit(solution)/shard_map/ppermute | solution.py:252
  73.1 2.0 %collective-permute-start.24 = (bf16[2,32,896]{2,1,0:T(8,128)(2,1)S(1)}, bf16[2,32,896]{2,1,0:T(8,128)(2,1)S(1)}, u32[]{:S(2)}, u32[]{:S(2)}) collective-permute-start(bf16[2,32,896]{2,1,0:T(8,128)(2,1)S(1)} %get-tuple-element.94), channel_id=1, source_target_pairs={{0,6},{1,7},{2,4},{3,5},{4,2},{5,3},{6,0},{7,1},{8,14},{9,15},{10,... | collective-permute-start | bytes 344072 | tf_op jit(solution)/shard_map/ppermute | solution.py:252
  77.6 2.0 %shard_map.125 = bf16[1024,896]{1,0:T(8,128)(2,1)} custom-call(bf16[256,1024]{1,0:T(8,128)(2,1)S(1)} %get-tuple-element.101.left_ref, bf16[256,896]{1,0:T(8,128)(2,1)S(1)} %get-tuple-element.102.refs_0_), custom_call_target="tpu_custom_call" | custom-call | flops 469762048 | bytes 1835008 | tf_op jit(solution)/shard_map/pallas_call | solution.py:362
  80.9 2.5 %shard_map.124 = (bf16[896,1024]{1,0:T(8,128)(2,1)}, bf16[896,1024]{1,0:T(8,128)(2,1)}) custom-call(bf16[256,896]{1,0:T(8,128)(2,1)S(1)} %get-tuple-element.96.left_ref, bf16[256,1024]{1,0:T(8,128)(2,1)S(1)} %get-tuple-element.97.refs_0_, bf16[256,1024]{1,0:T(8,128)(2,1)S(1)} %get-tuple-element.98.refs_1_, ...), custom_call_target="tpu_custom_call" | custom-call | flops 939524096 | bytes 3670016 | tf_op jit(solution)/shard_map/pallas_call | solution.py:368
  83.4 3.3 %collective-permute-done.25.refs_3_ = bf16[2,32,896]{2,1,0:T(8,128)(2,1)S(1)} collective-permute-done((bf16[2,32,896]{2,1,0:T(8,128)(2,1)S(1)}, bf16[2,32,896]{2,1,0:T(8,128)(2,1)S(1)}, u32[]{:S(2)}, u32[]{:S(2)}) %collective-permute-start.25) | collective-permute-done | bytes 114720 | tf_op jit(solution)/shard_map/ppermute | solution.py:252
  (58 shorter events, 19.0 us)
Async XLA Ops:
  6.0 9.1 %collective-permute-start.1 = (bf16[2,32,896]{2,1,0:T(8,128)(2,1)S(1)}, bf16[2,32,896]{2,1,0:T(8,128)(2,1)S(1)}, u32[]{:S(2)}, u32[]{:S(2)}) collective-permute-start(bf16[2,32,896]{2,1,0:T(8,128)(2,1)S(1)} %get-tuple-element.61), channel_id=1, source_target_pairs={{0,6},{1,7},{2,4},{3,5},{4,2},{5,3},{6,0},{7,1},{8,14},{9,15},{10,... | collective-permute-start | bytes 344072 | tf_op jit(solution)/shard_map/ppermute | solution.py:252
  11.1 10.0 %collective-permute-start.2 = (bf16[2,32,896]{2,1,0:T(8,128)(2,1)S(1)}, bf16[2,32,896]{2,1,0:T(8,128)(2,1)S(1)}, u32[]{:S(2)}, u32[]{:S(2)}) collective-permute-start(bf16[2,32,896]{2,1,0:T(8,128)(2,1)S(1)} %get-tuple-element.62), channel_id=1, source_target_pairs={{0,4},{1,5},{2,6},{3,7},{4,0},{5,1},{6,2},{7,3},{8,12},{9,13},{10,... | collective-permute-start | bytes 344072 | tf_op jit(solution)/shard_map/ppermute | solution.py:252
  11.1 10.0 %collective-permute-start.3 = (bf16[2,32,896]{2,1,0:T(8,128)(2,1)S(1)}, bf16[2,32,896]{2,1,0:T(8,128)(2,1)S(1)}, u32[]{:S(2)}, u32[]{:S(2)}) collective-permute-start(bf16[2,32,896]{2,1,0:T(8,128)(2,1)S(1)} %get-tuple-element.63), channel_id=1, source_target_pairs={{0,2},{1,3},{2,0},{3,1},{4,6},{5,7},{6,4},{7,5},{8,10},{9,11},{10,... | collective-permute-start | bytes 344072 | tf_op jit(solution)/shard_map/ppermute | solution.py:252
  22.3 9.3 %collective-permute-start.4 = (bf16[2,64,1024]{2,1,0:T(8,128)(2,1)S(1)}, bf16[2,64,1024]{2,1,0:T(8,128)(2,1)S(1)}, u32[]{:S(2)}, u32[]{:S(2)}) collective-permute-start(bf16[2,64,1024]{2,1,0:T(8,128)(2,1)S(1)} %get-tuple-element.66), channel_id=1, source_target_pairs={{0,8},{8,0},{16,24},{24,16},{1,9},{9,1},{17,25},{25,17},{2,10},{10... | collective-permute-start | bytes 786440 | tf_op jit(solution)/shard_map/ppermute | solution.py:252
  23.9 12.9 %collective-permute-start.5 = (bf16[2,64,1024]{2,1,0:T(8,128)(2,1)S(1)}, bf16[2,64,1024]{2,1,0:T(8,128)(2,1)S(1)}, u32[]{:S(2)}, u32[]{:S(2)}) collective-permute-start(bf16[2,64,1024]{2,1,0:T(8,128)(2,1)S(1)} %get-tuple-element.67), channel_id=1, source_target_pairs={{0,16},{8,24},{16,0},{24,8},{1,17},{9,25},{17,1},{25,9},{2,18},{10... | collective-permute-start | bytes 786440 | tf_op jit(solution)/shard_map/ppermute | solution.py:252
  25.4 11.3 %collective-permute-start.6 = (bf16[2,64,1024]{2,1,0:T(8,128)(2,1)S(1)}, bf16[2,64,1024]{2,1,0:T(8,128)(2,1)S(1)}, u32[]{:S(2)}, u32[]{:S(2)}) collective-permute-start(bf16[2,64,1024]{2,1,0:T(8,128)(2,1)S(1)} %get-tuple-element.68), channel_id=1, source_target_pairs={{0,24},{8,16},{16,8},{24,0},{1,25},{9,17},{17,9},{25,1},{2,26},{10... | collective-permute-start | bytes 786440 | tf_op jit(solution)/shard_map/ppermute | solution.py:252
  25.9 11.1 %collective-permute-start.11 = (bf16[2,32,896]{2,1,0:T(8,128)(2,1)S(1)}, bf16[2,32,896]{2,1,0:T(8,128)(2,1)S(1)}, u32[]{:S(2)}, u32[]{:S(2)}) collective-permute-start(bf16[2,32,896]{2,1,0:T(8,128)(2,1)S(1)} %get-tuple-element.71), channel_id=1, source_target_pairs={{0,6},{1,7},{2,4},{3,5},{4,2},{5,3},{6,0},{7,1},{8,14},{9,15},{10,... | collective-permute-start | bytes 344072 | tf_op jit(solution)/shard_map/ppermute | solution.py:252
  28.4 9.1 %collective-permute-start.12 = (bf16[2,32,896]{2,1,0:T(8,128)(2,1)S(1)}, bf16[2,32,896]{2,1,0:T(8,128)(2,1)S(1)}, u32[]{:S(2)}, u32[]{:S(2)}) collective-permute-start(bf16[2,32,896]{2,1,0:T(8,128)(2,1)S(1)} %get-tuple-element.72), channel_id=1, source_target_pairs={{0,4},{1,5},{2,6},{3,7},{4,0},{5,1},{6,2},{7,3},{8,12},{9,13},{10,... | collective-permute-start | bytes 344072 | tf_op jit(solution)/shard_map/ppermute | solution.py:252
  31.6 6.5 %collective-permute-start.13 = (bf16[2,32,896]{2,1,0:T(8,128)(2,1)S(1)}, bf16[2,32,896]{2,1,0:T(8,128)(2,1)S(1)}, u32[]{:S(2)}, u32[]{:S(2)}) collective-permute-start(bf16[2,32,896]{2,1,0:T(8,128)(2,1)S(1)} %get-tuple-element.73), channel_id=1, source_target_pairs={{0,2},{1,3},{2,0},{3,1},{4,6},{5,7},{6,4},{7,5},{8,10},{9,11},{10,... | collective-permute-start | bytes 344072 | tf_op jit(solution)/shard_map/ppermute | solution.py:252
  38.9 6.6 %collective-permute-start.14 = (bf16[64,1024]{1,0:T(8,128)(2,1)S(1)}, bf16[64,1024]{1,0:T(8,128)(2,1)S(1)}, u32[]{:S(2)}, u32[]{:S(2)}) collective-permute-start(bf16[64,1024]{1,0:T(8,128)(2,1)S(1)} %get-tuple-element.78), channel_id=1, source_target_pairs={{0,8},{8,0},{16,24},{24,16},{1,9},{9,1},{17,25},{25,17},{2,10},{10... | collective-permute-start | bytes 393224 | tf_op jit(solution)/shard_map/ppermute | solution.py:252
  40.5 7.9 %collective-permute-start.15 = (bf16[64,1024]{1,0:T(8,128)(2,1)S(1)}, bf16[64,1024]{1,0:T(8,128)(2,1)S(1)}, u32[]{:S(2)}, u32[]{:S(2)}) collective-permute-start(bf16[64,1024]{1,0:T(8,128)(2,1)S(1)} %get-tuple-element.79), channel_id=1, source_target_pairs={{0,16},{8,24},{16,0},{24,8},{1,17},{9,25},{17,1},{25,9},{2,18},{10... | collective-permute-start | bytes 393224 | tf_op jit(solution)/shard_map/ppermute | solution.py:252
  42.0 7.4 %collective-permute-start.16 = (bf16[64,1024]{1,0:T(8,128)(2,1)S(1)}, bf16[64,1024]{1,0:T(8,128)(2,1)S(1)}, u32[]{:S(2)}, u32[]{:S(2)}) collective-permute-start(bf16[64,1024]{1,0:T(8,128)(2,1)S(1)} %get-tuple-element.80), channel_id=1, source_target_pairs={{0,24},{8,16},{16,8},{24,0},{1,25},{9,17},{17,9},{25,1},{2,26},{10... | collective-permute-start | bytes 393224 | tf_op jit(solution)/shard_map/ppermute | solution.py:252
  42.5 8.8 %collective-permute-start.7 = (bf16[64,1024]{1,0:T(8,128)(2,1)S(1)}, bf16[64,1024]{1,0:T(8,128)(2,1)S(1)}, u32[]{:S(2)}, u32[]{:S(2)}) collective-permute-start(bf16[64,1024]{1,0:T(8,128)(2,1)S(1)} %shard_map.115.refs_0_), channel_id=1, source_target_pairs={{0,8},{8,0},{16,24},{24,16},{1,9},{9,1},{17,25},{25,17},{2,10},{10... | collective-permute-start | bytes 393224 | tf_op jit(solution)/shard_map/ppermute | solution.py:252
  44.0 7.6 %collective-permute-start.8 = (bf16[64,1024]{1,0:T(8,128)(2,1)S(1)}, bf16[64,1024]{1,0:T(8,128)(2,1)S(1)}, u32[]{:S(2)}, u32[]{:S(2)}) collective-permute-start(bf16[64,1024]{1,0:T(8,128)(2,1)S(1)} %shard_map.115.refs_0_), channel_id=1, source_target_pairs={{0,16},{8,24},{16,0},{24,8},{1,17},{9,25},{17,1},{25,9},{2,18},{10... | collective-permute-start | bytes 393224 | tf_op jit(solution)/shard_map/ppermute | solution.py:252
  45.5 9.5 %collective-permute-start.9 = (bf16[64,1024]{1,0:T(8,128)(2,1)S(1)}, bf16[64,1024]{1,0:T(8,128)(2,1)S(1)}, u32[]{:S(2)}, u32[]{:S(2)}) collective-permute-start(bf16[64,1024]{1,0:T(8,128)(2,1)S(1)} %shard_map.115.refs_0_), channel_id=1, source_target_pairs={{0,24},{8,16},{16,8},{24,0},{1,25},{9,17},{17,9},{25,1},{2,26},{10... | collective-permute-start | bytes 393224 | tf_op jit(solution)/shard_map/ppermute | solution.py:252
  49.7 11.0 %collective-permute-start.17 = (bf16[2,64,1024]{2,1,0:T(8,128)(2,1)S(1)}, bf16[2,64,1024]{2,1,0:T(8,128)(2,1)S(1)}, u32[]{:S(2)}, u32[]{:S(2)}) collective-permute-start(bf16[2,64,1024]{2,1,0:T(8,128)(2,1)S(1)} %shard_map.118.refs_0_), channel_id=1, source_target_pairs={{0,8},{8,0},{16,24},{24,16},{1,9},{9,1},{17,25},{25,17},{2,10},{10... | collective-permute-start | bytes 786440 | tf_op jit(solution)/shard_map/ppermute | solution.py:252
  55.8 14.3 %collective-permute-start.18 = (bf16[2,64,1024]{2,1,0:T(8,128)(2,1)S(1)}, bf16[2,64,1024]{2,1,0:T(8,128)(2,1)S(1)}, u32[]{:S(2)}, u32[]{:S(2)}) collective-permute-start(bf16[2,64,1024]{2,1,0:T(8,128)(2,1)S(1)} %shard_map.118.refs_0_), channel_id=1, source_target_pairs={{0,16},{8,24},{16,0},{24,8},{1,17},{9,25},{17,1},{25,9},{2,18},{10... | collective-permute-start | bytes 786440 | tf_op jit(solution)/shard_map/ppermute | solution.py:252
  56.4 13.8 %collective-permute-start.19 = (bf16[2,64,1024]{2,1,0:T(8,128)(2,1)S(1)}, bf16[2,64,1024]{2,1,0:T(8,128)(2,1)S(1)}, u32[]{:S(2)}, u32[]{:S(2)}) collective-permute-start(bf16[2,64,1024]{2,1,0:T(8,128)(2,1)S(1)} %shard_map.118.refs_0_), channel_id=1, source_target_pairs={{0,24},{8,16},{16,8},{24,0},{1,25},{9,17},{17,9},{25,1},{2,26},{10... | collective-permute-start | bytes 786440 | tf_op jit(solution)/shard_map/ppermute | solution.py:252
  58.7 11.5 %collective-permute-start.20 = (bf16[2,32,896]{2,1,0:T(8,128)(2,1)S(1)}, bf16[2,32,896]{2,1,0:T(8,128)(2,1)S(1)}, u32[]{:S(2)}, u32[]{:S(2)}) collective-permute-start(bf16[2,32,896]{2,1,0:T(8,128)(2,1)S(1)} %get-tuple-element.81), channel_id=1, source_target_pairs={{0,4},{1,5},{2,6},{3,7},{4,0},{5,1},{6,2},{7,3},{8,12},{9,13},{10,... | collective-permute-start | bytes 344072 | tf_op jit(solution)/shard_map/ppermute | solution.py:252
  58.8 11.4 %collective-permute-start.21 = (bf16[2,32,896]{2,1,0:T(8,128)(2,1)S(1)}, bf16[2,32,896]{2,1,0:T(8,128)(2,1)S(1)}, u32[]{:S(2)}, u32[]{:S(2)}) collective-permute-start(bf16[2,32,896]{2,1,0:T(8,128)(2,1)S(1)} %get-tuple-element.82), channel_id=1, source_target_pairs={{0,6},{1,7},{2,4},{3,5},{4,2},{5,3},{6,0},{7,1},{8,14},{9,15},{10,... | collective-permute-start | bytes 344072 | tf_op jit(solution)/shard_map/ppermute | solution.py:252
  60.7 9.5 %collective-permute-start.22 = (bf16[2,32,896]{2,1,0:T(8,128)(2,1)S(1)}, bf16[2,32,896]{2,1,0:T(8,128)(2,1)S(1)}, u32[]{:S(2)}, u32[]{:S(2)}) collective-permute-start(bf16[2,32,896]{2,1,0:T(8,128)(2,1)S(1)} %get-tuple-element.83), channel_id=1, source_target_pairs={{0,2},{1,3},{2,0},{3,1},{4,6},{5,7},{6,4},{7,5},{8,10},{9,11},{10,... | collective-permute-start | bytes 344072 | tf_op jit(solution)/shard_map/ppermute | solution.py:252
  73.1 10.3 %collective-permute-start.24 = (bf16[2,32,896]{2,1,0:T(8,128)(2,1)S(1)}, bf16[2,32,896]{2,1,0:T(8,128)(2,1)S(1)}, u32[]{:S(2)}, u32[]{:S(2)}) collective-permute-start(bf16[2,32,896]{2,1,0:T(8,128)(2,1)S(1)} %get-tuple-element.94), channel_id=1, source_target_pairs={{0,6},{1,7},{2,4},{3,5},{4,2},{5,3},{6,0},{7,1},{8,14},{9,15},{10,... | collective-permute-start | bytes 344072 | tf_op jit(solution)/shard_map/ppermute | solution.py:252
  75.2 11.6 %collective-permute-start.25 = (bf16[2,32,896]{2,1,0:T(8,128)(2,1)S(1)}, bf16[2,32,896]{2,1,0:T(8,128)(2,1)S(1)}, u32[]{:S(2)}, u32[]{:S(2)}) collective-permute-start(bf16[2,32,896]{2,1,0:T(8,128)(2,1)S(1)} %get-tuple-element.95), channel_id=1, source_target_pairs={{0,4},{1,5},{2,6},{3,7},{4,0},{5,1},{6,2},{7,3},{8,12},{9,13},{10,... | collective-permute-start | bytes 344072 | tf_op jit(solution)/shard_map/ppermute | solution.py:252
  76.2 10.5 %collective-permute-start.26 = (bf16[2,32,896]{2,1,0:T(8,128)(2,1)S(1)}, bf16[2,32,896]{2,1,0:T(8,128)(2,1)S(1)}, u32[]{:S(2)}, u32[]{:S(2)}) collective-permute-start(bf16[2,32,896]{2,1,0:T(8,128)(2,1)S(1)} %get-tuple-element.93.refs_5_.refs_2_), channel_id=1, source_target_pairs={{0,2},{1,3},{2,0},{3,1},{4,6},{5,7},{6,4},{7,5},{8,10},{9,11},{10,... | collective-permute-start | bytes 344072 | tf_op jit(solution)/shard_map/ppermute | solution.py:252
  (9 other events, 65.8 us)

commit v13 on v11

--- a/solution.py
+++ b/solution.py
@@ -163,7 +163,7 @@
     gate = group_sum(refs[:dp], 0)
     up = group_sum(refs[:dp], 1)
     grad = group_sum(refs[dp : 2 * dp], Ellipsis)
-    out_ref = refs[2 * dp]
+    out_ref = refs[-1]
     soft = logistic(gate)
     out_ref[0] = (grad * up * (soft * (1.0 + gate * (1.0 - soft)))).astype(BF16)
     out_ref[1] = (grad * (gate * soft)).astype(BF16)
@@ -312,13 +312,6 @@
         scratch_shapes=in_order,
     )(keep, swap, *grad_blocks, down_mat)
     grad_sums = trade(part_grad)
-    pre_mine = call(
-        functools.partial(grad_pre_kernel, dp),
-        shape((2, chunk, hidden), BF16),
-        0,
-        6 * dp * chunk * hidden,
-    )(*sums, *grad_sums)
-    pre = trade([pre_mine] * dp)
     act, out_keep, out_swap = call(
         functools.partial(expert_out_kernel, dp),
         (wide, one, one),
@@ -326,11 +319,20 @@
         weights,
         scratch_shapes=in_order,
     )(*acts, down_mat)
+    pre_mine = call(
+        functools.partial(grad_pre_kernel, dp),
+        shape((2, chunk, hidden), BF16),
+        0,
+        6 * dp * chunk * hidden,
+        in_specs=[HERE] * (2 * dp) + [ANY],
+    )(*sums, *grad_sums, out_keep)
+    pre = trade([pre_mine] * dp)
     back = [pair] * (half - 1)
     out_swap = partner(out_swap, "expert", 1)
     out_near, *out_far = call(pack_back_kernel, back, 0, 8 * slots)(out_keep, out_swap)
     out_far = [partner(value, "expert", 2 * (2 + k)) for k, value in enumerate(out_far)]
-    pre, out_far = lax.optimization_barrier((pre, out_far))
+    out_near = partner(out_near, "expert", 2)
+    pre, out_far, out_near = lax.optimization_barrier((pre, out_far, out_near))
     gate_pre, up_pre, grad_keep, grad_swap = call(
         functools.partial(row_grad_kernel, dp),
         (wide, wide, one, one),
@@ -339,7 +341,6 @@
         scratch_shapes=in_order,
     )(*pre, gate_mat, up_mat)
     grad_swap = partner(grad_swap, "expert", 1)
-    out_near = partner(out_near, "expert", 2)
     grad_to = call(pack_back_kernel, back, 0, 8 * slots)(grad_keep, grad_swap)
     grad_back = [partner(value, "expert", 2 * (1 + k)) for k, value in enumerate(grad_to)]
 

time: 81.9 us -> 84.3 us (1.029)
  waiting for transfers between devices: 33.3 us -> 37.9 us
  starting transfers between devices: 32.5 us -> 30.4 us
    ppermute x27, waiting for transfers between devices: 33.3 us -> 37.9 us  [partner(): return lax.ppermute(value, axis, [(i, i ^ k) for i in range(size)])]
    ppermute x27, starting transfers between devices: 32.5 us -> 30.4 us  [partner(): return lax.ppermute(value, axis, [(i, i ^ k) for i in range(size)])]
  transfers between devices with their start and end apart: 27 -> 27, of which waited for: 13 -> 13; matrix products, arithmetic and copies ran while one was open for 0% -> 0% of each run, Pallas kernels for 10% -> 9%
where the time goes in v13:
time: 84.3 us; the launch traced here: 84.2 us
  waiting for transfers between devices  37.9 us (45%)
  starting transfers between devices  30.4 us (36%)
  Pallas kernels  15.1 us (18%)
    ppermute x27, waiting for transfers between devices, partner(): return lax.ppermute(value, axis, [(i, i ^ k) for i in range(size)])  37.9 us
    ppermute x27, starting transfers between devices, partner(): return lax.ppermute(value, axis, [(i, i ^ k) for i in range(size)])  30.4 us
    pallas_call x1, Pallas kernels, body(): call(functools.partial(route_kernel, experts), outs, 4 * slots * tok_rows...  3.19 us
    pallas_call x1, Pallas kernels, body(): call(functools.partial(grads_kernel, 2), [shape((features, hidden), BF16)...  2.54 us
    pallas_call x1, Pallas kernels, body(): call(functools.partial(grads_kernel, 1), [shape((hidden, features), BF16)...  1.97 us
  transfers between devices with their start and end apart: 27, of which 13 were waited for; matrix products, arithmetic and copies ran while one was open for 0% of the time, Pallas kernels for 9%

profile of v13, /device:TPU:0, one launch (start us, length us, event | category | flops | bytes accessed | tf_op | source)
XLA Modules:
  0.0 84.2 jit_solution(12474067852401932539)
XLA Ops:
  0.6 3.2 %shard_map.110 = (bf16[256,512]{1,0:T(8,128)(2,1)}, f32[256,1]{1,0:T(8,128)}, bf16[2,4,32,896]{3,2,1,0:T(8,128)(2,1)}, bf16[2,4,32,896]{3,2,1,0:T(8,128)(2,1)}) custom-call(s32[8,512]{1,0:T(8,128)} %bitcast.14, f32[8,512]{1,0:T(8,128)} %bitcast.15, bf16[512,896]{1,0:T(8,128)(2,1)} %refs_2_.1, bf16[512,896]{1,0:T(8,128)(2,1)} %refs_3_.1), custom_call_target="tpu_custom_call" | custom-call | flops 469762048 | bytes 3670016 | tf_op jit(solution)/shard_map/pallas_call | solution.py:270
  4.5 1.5 %collective-permute-done.swap_ref.refs_1_ = bf16[2,4,32,896]{3,2,1,0:T(8,128)(2,1)S(1)} collective-permute-done((bf16[2,4,32,896]{3,2,1,0:T(8,128)(2,1)}, bf16[2,4,32,896]{3,2,1,0:T(8,128)(2,1)S(1)}, u32[]{:S(2)}, u32[]{:S(2)}) %collective-permute-start) | collective-permute-done | bytes 458784 | tf_op jit(solution)/shard_map/ppermute | solution.py:239
  6.1 5.0 %collective-permute-start.1 = (bf16[2,32,896]{2,1,0:T(8,128)(2,1)S(1)}, bf16[2,32,896]{2,1,0:T(8,128)(2,1)S(1)}, u32[]{:S(2)}, u32[]{:S(2)}) collective-permute-start(bf16[2,32,896]{2,1,0:T(8,128)(2,1)S(1)} %get-tuple-element.61), channel_id=1, source_target_pairs={{0,6},{1,7},{2,4},{3,5},{4,2},{5,3},{6,0},{7,1},{8,14},{9,15},{10,... | collective-permute-start | bytes 344072 | tf_op jit(solution)/shard_map/ppermute | solution.py:239
  11.8 3.4 %collective-permute-done.1.refs_2_ = bf16[2,32,896]{2,1,0:T(8,128)(2,1)S(1)} collective-permute-done((bf16[2,32,896]{2,1,0:T(8,128)(2,1)S(1)}, bf16[2,32,896]{2,1,0:T(8,128)(2,1)S(1)}, u32[]{:S(2)}, u32[]{:S(2)}) %collective-permute-start.1) | collective-permute-done | bytes 114720 | tf_op jit(solution)/shard_map/ppermute | solution.py:239
  15.2 5.9 %collective-permute-done.2.refs_3_ = bf16[2,32,896]{2,1,0:T(8,128)(2,1)S(1)} collective-permute-done((bf16[2,32,896]{2,1,0:T(8,128)(2,1)S(1)}, bf16[2,32,896]{2,1,0:T(8,128)(2,1)S(1)}, u32[]{:S(2)}, u32[]{:S(2)}) %collective-permute-start.2) | collective-permute-done | bytes 114720 | tf_op jit(solution)/shard_map/ppermute | solution.py:239
  22.4 1.6 %collective-permute-start.4 = (bf16[2,64,1024]{2,1,0:T(8,128)(2,1)S(1)}, bf16[2,64,1024]{2,1,0:T(8,128)(2,1)S(1)}, u32[]{:S(2)}, u32[]{:S(2)}) collective-permute-start(bf16[2,64,1024]{2,1,0:T(8,128)(2,1)S(1)} %get-tuple-element.66), channel_id=1, source_target_pairs={{0,8},{8,0},{16,24},{24,16},{1,9},{9,1},{17,25},{25,17},{2,10},{10... | collective-permute-start | bytes 786440 | tf_op jit(solution)/shard_map/ppermute | solution.py:239
  24.0 1.5 %collective-permute-start.5 = (bf16[2,64,1024]{2,1,0:T(8,128)(2,1)S(1)}, bf16[2,64,1024]{2,1,0:T(8,128)(2,1)S(1)}, u32[]{:S(2)}, u32[]{:S(2)}) collective-permute-start(bf16[2,64,1024]{2,1,0:T(8,128)(2,1)S(1)} %get-tuple-element.67), channel_id=1, source_target_pairs={{0,16},{8,24},{16,0},{24,8},{1,17},{9,25},{17,1},{25,9},{2,18},{10... | collective-permute-start | bytes 786440 | tf_op jit(solution)/shard_map/ppermute | solution.py:239
  26.0 2.5 %collective-permute-start.11 = (bf16[2,32,896]{2,1,0:T(8,128)(2,1)S(1)}, bf16[2,32,896]{2,1,0:T(8,128)(2,1)S(1)}, u32[]{:S(2)}, u32[]{:S(2)}) collective-permute-start(bf16[2,32,896]{2,1,0:T(8,128)(2,1)S(1)} %get-tuple-element.71), channel_id=1, source_target_pairs={{0,6},{1,7},{2,4},{3,5},{4,2},{5,3},{6,0},{7,1},{8,14},{9,15},{10,... | collective-permute-start | bytes 344072 | tf_op jit(solution)/shard_map/ppermute | solution.py:239
  28.4 3.3 %collective-permute-done.4.refs_1_ = bf16[2,64,1024]{2,1,0:T(8,128)(2,1)S(1)} collective-permute-done((bf16[2,64,1024]{2,1,0:T(8,128)(2,1)S(1)}, bf16[2,64,1024]{2,1,0:T(8,128)(2,1)S(1)}, u32[]{:S(2)}, u32[]{:S(2)}) %collective-permute-start.4) | collective-permute-done | bytes 262176 | tf_op jit(solution)/shard_map/ppermute | solution.py:239
  31.9 4.9 %collective-permute-done.5.refs_2_ = bf16[2,64,1024]{2,1,0:T(8,128)(2,1)S(1)} collective-permute-done((bf16[2,64,1024]{2,1,0:T(8,128)(2,1)S(1)}, bf16[2,64,1024]{2,1,0:T(8,128)(2,1)S(1)}, u32[]{:S(2)}, u32[]{:S(2)}) %collective-permute-start.5) | collective-permute-done | bytes 262176 | tf_op jit(solution)/shard_map/ppermute | solution.py:239
  39.1 1.4 %collective-permute-start.9 = (bf16[64,1024]{1,0:T(8,128)(2,1)S(1)}, bf16[64,1024]{1,0:T(8,128)(2,1)S(1)}, u32[]{:S(2)}, u32[]{:S(2)}) collective-permute-start(bf16[64,1024]{1,0:T(8,128)(2,1)S(1)} %shard_map.115.refs_0_), channel_id=1, source_target_pairs={{0,24},{8,16},{16,8},{24,0},{1,25},{9,17},{17,9},{25,1},{2,26},{10... | collective-permute-start | bytes 393224 | tf_op jit(solution)/shard_map/ppermute | solution.py:239
  43.5 1.4 %collective-permute-start.16 = (bf16[64,1024]{1,0:T(8,128)(2,1)S(1)}, bf16[64,1024]{1,0:T(8,128)(2,1)S(1)}, u32[]{:S(2)}, u32[]{:S(2)}) collective-permute-start(bf16[64,1024]{1,0:T(8,128)(2,1)S(1)} %get-tuple-element.80), channel_id=1, source_target_pairs={{0,24},{8,16},{16,8},{24,0},{1,25},{9,17},{17,9},{25,1},{2,26},{10... | collective-permute-start | bytes 393224 | tf_op jit(solution)/shard_map/ppermute | solution.py:239
  44.9 2.5 %collective-permute-done.9.refs_3_ = bf16[64,1024]{1,0:T(8,128)(2,1)S(1)} collective-permute-done((bf16[64,1024]{1,0:T(8,128)(2,1)S(1)}, bf16[64,1024]{1,0:T(8,128)(2,1)S(1)}, u32[]{:S(2)}, u32[]{:S(2)}) %collective-permute-start.9) | collective-permute-done | bytes 131104 | tf_op jit(solution)/shard_map/ppermute | solution.py:239
  48.6 1.7 %collective-permute-done.15.refs_6_ = bf16[64,1024]{1,0:T(8,128)(2,1)S(1)} collective-permute-done((bf16[64,1024]{1,0:T(8,128)(2,1)S(1)}, bf16[64,1024]{1,0:T(8,128)(2,1)S(1)}, u32[]{:S(2)}, u32[]{:S(2)}) %collective-permute-start.15) | collective-permute-done | bytes 131104 | tf_op jit(solution)/shard_map/ppermute | solution.py:239
  52.6 1.6 %collective-permute-start.19 = (bf16[2,64,1024]{2,1,0:T(8,128)(2,1)S(1)}, bf16[2,64,1024]{2,1,0:T(8,128)(2,1)S(1)}, u32[]{:S(2)}, u32[]{:S(2)}) collective-permute-start(bf16[2,64,1024]{2,1,0:T(8,128)(2,1)S(1)} %shard_map.118.refs_0_), channel_id=1, source_target_pairs={{0,24},{8,16},{16,8},{24,0},{1,25},{9,17},{17,9},{25,1},{2,26},{10... | collective-permute-start | bytes 786440 | tf_op jit(solution)/shard_map/ppermute | solution.py:239
  54.3 2.5 %collective-permute-start.21 = (bf16[2,32,896]{2,1,0:T(8,128)(2,1)S(1)}, bf16[2,32,896]{2,1,0:T(8,128)(2,1)S(1)}, u32[]{:S(2)}, u32[]{:S(2)}) collective-permute-start(bf16[2,32,896]{2,1,0:T(8,128)(2,1)S(1)} %get-tuple-element.82), channel_id=1, source_target_pairs={{0,6},{1,7},{2,4},{3,5},{4,2},{5,3},{6,0},{7,1},{8,14},{9,15},{10,... | collective-permute-start | bytes 344072 | tf_op jit(solution)/shard_map/ppermute | solution.py:239
  56.8 1.4 %collective-permute-done.17.refs_1_ = bf16[2,64,1024]{2,1,0:T(8,128)(2,1)S(1)} collective-permute-done((bf16[2,64,1024]{2,1,0:T(8,128)(2,1)S(1)}, bf16[2,64,1024]{2,1,0:T(8,128)(2,1)S(1)}, u32[]{:S(2)}, u32[]{:S(2)}) %collective-permute-start.17) | collective-permute-done | bytes 262176 | tf_op jit(solution)/shard_map/ppermute | solution.py:239
  58.4 7.4 %collective-permute-done.18.refs_2_ = bf16[2,64,1024]{2,1,0:T(8,128)(2,1)S(1)} collective-permute-done((bf16[2,64,1024]{2,1,0:T(8,128)(2,1)S(1)}, bf16[2,64,1024]{2,1,0:T(8,128)(2,1)S(1)}, u32[]{:S(2)}, u32[]{:S(2)}) %collective-permute-start.18) | collective-permute-done | bytes 262176 | tf_op jit(solution)/shard_map/ppermute | solution.py:239
  66.4 1.3 %shard_map.120 = (bf16[256,1024]{1,0:T(8,128)(2,1)S(1)}, bf16[256,1024]{1,0:T(8,128)(2,1)S(1)}, bf16[4,32,896]{2,1,0:T(8,128)(2,1)S(1)}, bf16[4,32,896]{2,1,0:T(8,128)(2,1)S(1)}) custom-call(bf16[2,64,1024]{2,1,0:T(8,128)(2,1)S(1)} %shard_map.118.refs_0_, bf16[2,64,1024]{2,1,0:T(8,128)(2,1)S(1)} %collective-permute-done.17.refs_1_, ...), custom_call_target="tpu_custom_call" | custom-call | flops 939524096 | bytes 3670016 | tf_op jit(solution)/shard_map/pallas_call | solution.py:336
  67.9 1.3 %collective-permute-done.23.swap_ref.refs_1_ = bf16[4,32,896]{2,1,0:T(8,128)(2,1)S(1)} collective-permute-done((bf16[4,32,896]{2,1,0:T(8,128)(2,1)S(1)}, bf16[4,32,896]{2,1,0:T(8,128)(2,1)S(1)}, u32[]{:S(2)}, u32[]{:S(2)}) %collective-permute-start.23) | collective-permute-done | bytes 229408 | tf_op jit(solution)/shard_map/ppermute | solution.py:239
  69.3 2.0 %collective-permute-start.24 = (bf16[2,32,896]{2,1,0:T(8,128)(2,1)S(1)}, bf16[2,32,896]{2,1,0:T(8,128)(2,1)S(1)}, u32[]{:S(2)}, u32[]{:S(2)}) collective-permute-start(bf16[2,32,896]{2,1,0:T(8,128)(2,1)S(1)} %get-tuple-element.94), channel_id=1, source_target_pairs={{0,6},{1,7},{2,4},{3,5},{4,2},{5,3},{6,0},{7,1},{8,14},{9,15},{10,... | collective-permute-start | bytes 344072 | tf_op jit(solution)/shard_map/ppermute | solution.py:239
  73.7 2.0 %shard_map.125 = bf16[1024,896]{1,0:T(8,128)(2,1)} custom-call(bf16[256,1024]{1,0:T(8,128)(2,1)S(1)} %get-tuple-element.101.left_ref, bf16[256,896]{1,0:T(8,128)(2,1)S(1)} %get-tuple-element.102.refs_0_), custom_call_target="tpu_custom_call" | custom-call | flops 469762048 | bytes 1835008 | tf_op jit(solution)/shard_map/pallas_call | solution.py:347
  77.0 2.5 %shard_map.124 = (bf16[896,1024]{1,0:T(8,128)(2,1)}, bf16[896,1024]{1,0:T(8,128)(2,1)}) custom-call(bf16[256,896]{1,0:T(8,128)(2,1)S(1)} %get-tuple-element.96.left_ref, bf16[256,1024]{1,0:T(8,128)(2,1)S(1)} %get-tuple-element.97.refs_0_, bf16[256,1024]{1,0:T(8,128)(2,1)S(1)} %get-tuple-element.98.refs_1_, ...), custom_call_target="tpu_custom_call" | custom-call | flops 939524096 | bytes 3670016 | tf_op jit(solution)/shard_map/pallas_call | solution.py:353
  79.5 3.4 %collective-permute-done.25.refs_3_ = bf16[2,32,896]{2,1,0:T(8,128)(2,1)S(1)} collective-permute-done((bf16[2,32,896]{2,1,0:T(8,128)(2,1)S(1)}, bf16[2,32,896]{2,1,0:T(8,128)(2,1)S(1)}, u32[]{:S(2)}, u32[]{:S(2)}) %collective-permute-start.25) | collective-permute-done | bytes 114720 | tf_op jit(solution)/shard_map/ppermute | solution.py:239
  (58 shorter events, 17.9 us)
Async XLA Ops:
  6.1 9.1 %collective-permute-start.1 = (bf16[2,32,896]{2,1,0:T(8,128)(2,1)S(1)}, bf16[2,32,896]{2,1,0:T(8,128)(2,1)S(1)}, u32[]{:S(2)}, u32[]{:S(2)}) collective-permute-start(bf16[2,32,896]{2,1,0:T(8,128)(2,1)S(1)} %get-tuple-element.61), channel_id=1, source_target_pairs={{0,6},{1,7},{2,4},{3,5},{4,2},{5,3},{6,0},{7,1},{8,14},{9,15},{10,... | collective-permute-start | bytes 344072 | tf_op jit(solution)/shard_map/ppermute | solution.py:239
  11.1 10.0 %collective-permute-start.2 = (bf16[2,32,896]{2,1,0:T(8,128)(2,1)S(1)}, bf16[2,32,896]{2,1,0:T(8,128)(2,1)S(1)}, u32[]{:S(2)}, u32[]{:S(2)}) collective-permute-start(bf16[2,32,896]{2,1,0:T(8,128)(2,1)S(1)} %get-tuple-element.62), channel_id=1, source_target_pairs={{0,4},{1,5},{2,6},{3,7},{4,0},{5,1},{6,2},{7,3},{8,12},{9,13},{10,... | collective-permute-start | bytes 344072 | tf_op jit(solution)/shard_map/ppermute | solution.py:239
  11.1 10.0 %collective-permute-start.3 = (bf16[2,32,896]{2,1,0:T(8,128)(2,1)S(1)}, bf16[2,32,896]{2,1,0:T(8,128)(2,1)S(1)}, u32[]{:S(2)}, u32[]{:S(2)}) collective-permute-start(bf16[2,32,896]{2,1,0:T(8,128)(2,1)S(1)} %get-tuple-element.63), channel_id=1, source_target_pairs={{0,2},{1,3},{2,0},{3,1},{4,6},{5,7},{6,4},{7,5},{8,10},{9,11},{10,... | collective-permute-start | bytes 344072 | tf_op jit(solution)/shard_map/ppermute | solution.py:239
  22.4 9.3 %collective-permute-start.4 = (bf16[2,64,1024]{2,1,0:T(8,128)(2,1)S(1)}, bf16[2,64,1024]{2,1,0:T(8,128)(2,1)S(1)}, u32[]{:S(2)}, u32[]{:S(2)}) collective-permute-start(bf16[2,64,1024]{2,1,0:T(8,128)(2,1)S(1)} %get-tuple-element.66), channel_id=1, source_target_pairs={{0,8},{8,0},{16,24},{24,16},{1,9},{9,1},{17,25},{25,17},{2,10},{10... | collective-permute-start | bytes 786440 | tf_op jit(solution)/shard_map/ppermute | solution.py:239
  24.0 12.9 %collective-permute-start.5 = (bf16[2,64,1024]{2,1,0:T(8,128)(2,1)S(1)}, bf16[2,64,1024]{2,1,0:T(8,128)(2,1)S(1)}, u32[]{:S(2)}, u32[]{:S(2)}) collective-permute-start(bf16[2,64,1024]{2,1,0:T(8,128)(2,1)S(1)} %get-tuple-element.67), channel_id=1, source_target_pairs={{0,16},{8,24},{16,0},{24,8},{1,17},{9,25},{17,1},{25,9},{2,18},{10... | collective-permute-start | bytes 786440 | tf_op jit(solution)/shard_map/ppermute | solution.py:239
  25.5 11.3 %collective-permute-start.6 = (bf16[2,64,1024]{2,1,0:T(8,128)(2,1)S(1)}, bf16[2,64,1024]{2,1,0:T(8,128)(2,1)S(1)}, u32[]{:S(2)}, u32[]{:S(2)}) collective-permute-start(bf16[2,64,1024]{2,1,0:T(8,128)(2,1)S(1)} %get-tuple-element.68), channel_id=1, source_target_pairs={{0,24},{8,16},{16,8},{24,0},{1,25},{9,17},{17,9},{25,1},{2,26},{10... | collective-permute-start | bytes 786440 | tf_op jit(solution)/shard_map/ppermute | solution.py:239
  26.0 13.2 %collective-permute-start.11 = (bf16[2,32,896]{2,1,0:T(8,128)(2,1)S(1)}, bf16[2,32,896]{2,1,0:T(8,128)(2,1)S(1)}, u32[]{:S(2)}, u32[]{:S(2)}) collective-permute-start(bf16[2,32,896]{2,1,0:T(8,128)(2,1)S(1)} %get-tuple-element.71), channel_id=1, source_target_pairs={{0,6},{1,7},{2,4},{3,5},{4,2},{5,3},{6,0},{7,1},{8,14},{9,15},{10,... | collective-permute-start | bytes 344072 | tf_op jit(solution)/shard_map/ppermute | solution.py:239
  28.4 12.1 %collective-permute-start.12 = (bf16[2,32,896]{2,1,0:T(8,128)(2,1)S(1)}, bf16[2,32,896]{2,1,0:T(8,128)(2,1)S(1)}, u32[]{:S(2)}, u32[]{:S(2)}) collective-permute-start(bf16[2,32,896]{2,1,0:T(8,128)(2,1)S(1)} %get-tuple-element.72), channel_id=1, source_target_pairs={{0,4},{1,5},{2,6},{3,7},{4,0},{5,1},{6,2},{7,3},{8,12},{9,13},{10,... | collective-permute-start | bytes 344072 | tf_op jit(solution)/shard_map/ppermute | solution.py:239
  31.7 8.9 %collective-permute-start.13 = (bf16[2,32,896]{2,1,0:T(8,128)(2,1)S(1)}, bf16[2,32,896]{2,1,0:T(8,128)(2,1)S(1)}, u32[]{:S(2)}, u32[]{:S(2)}) collective-permute-start(bf16[2,32,896]{2,1,0:T(8,128)(2,1)S(1)} %get-tuple-element.73), channel_id=1, source_target_pairs={{0,2},{1,3},{2,0},{3,1},{4,6},{5,7},{6,4},{7,5},{8,10},{9,11},{10,... | collective-permute-start | bytes 344072 | tf_op jit(solution)/shard_map/ppermute | solution.py:239
  37.0 6.4 %collective-permute-start.7 = (bf16[64,1024]{1,0:T(8,128)(2,1)S(1)}, bf16[64,1024]{1,0:T(8,128)(2,1)S(1)}, u32[]{:S(2)}, u32[]{:S(2)}) collective-permute-start(bf16[64,1024]{1,0:T(8,128)(2,1)S(1)} %shard_map.115.refs_0_), channel_id=1, source_target_pairs={{0,8},{8,0},{16,24},{24,16},{1,9},{9,1},{17,25},{25,17},{2,10},{10... | collective-permute-start | bytes 393224 | tf_op jit(solution)/shard_map/ppermute | solution.py:239
  38.3 6.6 %collective-permute-start.8 = (bf16[64,1024]{1,0:T(8,128)(2,1)S(1)}, bf16[64,1024]{1,0:T(8,128)(2,1)S(1)}, u32[]{:S(2)}, u32[]{:S(2)}) collective-permute-start(bf16[64,1024]{1,0:T(8,128)(2,1)S(1)} %shard_map.115.refs_0_), channel_id=1, source_target_pairs={{0,16},{8,24},{16,0},{24,8},{1,17},{9,25},{17,1},{25,9},{2,18},{10... | collective-permute-start | bytes 393224 | tf_op jit(solution)/shard_map/ppermute | solution.py:239
  39.1 8.2 %collective-permute-start.9 = (bf16[64,1024]{1,0:T(8,128)(2,1)S(1)}, bf16[64,1024]{1,0:T(8,128)(2,1)S(1)}, u32[]{:S(2)}, u32[]{:S(2)}) collective-permute-start(bf16[64,1024]{1,0:T(8,128)(2,1)S(1)} %shard_map.115.refs_0_), channel_id=1, source_target_pairs={{0,24},{8,16},{16,8},{24,0},{1,25},{9,17},{17,9},{25,1},{2,26},{10... | collective-permute-start | bytes 393224 | tf_op jit(solution)/shard_map/ppermute | solution.py:239
  41.3 7.3 %collective-permute-start.14 = (bf16[64,1024]{1,0:T(8,128)(2,1)S(1)}, bf16[64,1024]{1,0:T(8,128)(2,1)S(1)}, u32[]{:S(2)}, u32[]{:S(2)}) collective-permute-start(bf16[64,1024]{1,0:T(8,128)(2,1)S(1)} %get-tuple-element.78), channel_id=1, source_target_pairs={{0,8},{8,0},{16,24},{24,16},{1,9},{9,1},{17,25},{25,17},{2,10},{10... | collective-permute-start | bytes 393224 | tf_op jit(solution)/shard_map/ppermute | solution.py:239
  42.6 7.7 %collective-permute-start.15 = (bf16[64,1024]{1,0:T(8,128)(2,1)S(1)}, bf16[64,1024]{1,0:T(8,128)(2,1)S(1)}, u32[]{:S(2)}, u32[]{:S(2)}) collective-permute-start(bf16[64,1024]{1,0:T(8,128)(2,1)S(1)} %get-tuple-element.79), channel_id=1, source_target_pairs={{0,16},{8,24},{16,0},{24,8},{1,17},{9,25},{17,1},{25,9},{2,18},{10... | collective-permute-start | bytes 393224 | tf_op jit(solution)/shard_map/ppermute | solution.py:239
  43.5 6.8 %collective-permute-start.16 = (bf16[64,1024]{1,0:T(8,128)(2,1)S(1)}, bf16[64,1024]{1,0:T(8,128)(2,1)S(1)}, u32[]{:S(2)}, u32[]{:S(2)}) collective-permute-start(bf16[64,1024]{1,0:T(8,128)(2,1)S(1)} %get-tuple-element.80), channel_id=1, source_target_pairs={{0,24},{8,16},{16,8},{24,0},{1,25},{9,17},{17,9},{25,1},{2,26},{10... | collective-permute-start | bytes 393224 | tf_op jit(solution)/shard_map/ppermute | solution.py:239
  50.6 7.7 %collective-permute-start.17 = (bf16[2,64,1024]{2,1,0:T(8,128)(2,1)S(1)}, bf16[2,64,1024]{2,1,0:T(8,128)(2,1)S(1)}, u32[]{:S(2)}, u32[]{:S(2)}) collective-permute-start(bf16[2,64,1024]{2,1,0:T(8,128)(2,1)S(1)} %shard_map.118.refs_0_), channel_id=1, source_target_pairs={{0,8},{8,0},{16,24},{24,16},{1,9},{9,1},{17,25},{25,17},{2,10},{10... | collective-permute-start | bytes 786440 | tf_op jit(solution)/shard_map/ppermute | solution.py:239
  51.5 14.3 %collective-permute-start.18 = (bf16[2,64,1024]{2,1,0:T(8,128)(2,1)S(1)}, bf16[2,64,1024]{2,1,0:T(8,128)(2,1)S(1)}, u32[]{:S(2)}, u32[]{:S(2)}) collective-permute-start(bf16[2,64,1024]{2,1,0:T(8,128)(2,1)S(1)} %shard_map.118.refs_0_), channel_id=1, source_target_pairs={{0,16},{8,24},{16,0},{24,8},{1,17},{9,25},{17,1},{25,9},{2,18},{10... | collective-permute-start | bytes 786440 | tf_op jit(solution)/shard_map/ppermute | solution.py:239
  52.6 13.3 %collective-permute-start.19 = (bf16[2,64,1024]{2,1,0:T(8,128)(2,1)S(1)}, bf16[2,64,1024]{2,1,0:T(8,128)(2,1)S(1)}, u32[]{:S(2)}, u32[]{:S(2)}) collective-permute-start(bf16[2,64,1024]{2,1,0:T(8,128)(2,1)S(1)} %shard_map.118.refs_0_), channel_id=1, source_target_pairs={{0,24},{8,16},{16,8},{24,0},{1,25},{9,17},{17,9},{25,1},{2,26},{10... | collective-permute-start | bytes 786440 | tf_op jit(solution)/shard_map/ppermute | solution.py:239
  54.2 11.6 %collective-permute-start.20 = (bf16[2,32,896]{2,1,0:T(8,128)(2,1)S(1)}, bf16[2,32,896]{2,1,0:T(8,128)(2,1)S(1)}, u32[]{:S(2)}, u32[]{:S(2)}) collective-permute-start(bf16[2,32,896]{2,1,0:T(8,128)(2,1)S(1)} %get-tuple-element.81), channel_id=1, source_target_pairs={{0,4},{1,5},{2,6},{3,7},{4,0},{5,1},{6,2},{7,3},{8,12},{9,13},{10,... | collective-permute-start | bytes 344072 | tf_op jit(solution)/shard_map/ppermute | solution.py:239
  54.3 11.5 %collective-permute-start.21 = (bf16[2,32,896]{2,1,0:T(8,128)(2,1)S(1)}, bf16[2,32,896]{2,1,0:T(8,128)(2,1)S(1)}, u32[]{:S(2)}, u32[]{:S(2)}) collective-permute-start(bf16[2,32,896]{2,1,0:T(8,128)(2,1)S(1)} %get-tuple-element.82), channel_id=1, source_target_pairs={{0,6},{1,7},{2,4},{3,5},{4,2},{5,3},{6,0},{7,1},{8,14},{9,15},{10,... | collective-permute-start | bytes 344072 | tf_op jit(solution)/shard_map/ppermute | solution.py:239
  58.3 8.1 %collective-permute-start.22 = (bf16[2,32,896]{2,1,0:T(8,128)(2,1)S(1)}, bf16[2,32,896]{2,1,0:T(8,128)(2,1)S(1)}, u32[]{:S(2)}, u32[]{:S(2)}) collective-permute-start(bf16[2,32,896]{2,1,0:T(8,128)(2,1)S(1)} %get-tuple-element.83), channel_id=1, source_target_pairs={{0,2},{1,3},{2,0},{3,1},{4,6},{5,7},{6,4},{7,5},{8,10},{9,11},{10,... | collective-permute-start | bytes 344072 | tf_op jit(solution)/shard_map/ppermute | solution.py:239
  69.3 10.3 %collective-permute-start.24 = (bf16[2,32,896]{2,1,0:T(8,128)(2,1)S(1)}, bf16[2,32,896]{2,1,0:T(8,128)(2,1)S(1)}, u32[]{:S(2)}, u32[]{:S(2)}) collective-permute-start(bf16[2,32,896]{2,1,0:T(8,128)(2,1)S(1)} %get-tuple-element.94), channel_id=1, source_target_pairs={{0,6},{1,7},{2,4},{3,5},{4,2},{5,3},{6,0},{7,1},{8,14},{9,15},{10,... | collective-permute-start | bytes 344072 | tf_op jit(solution)/shard_map/ppermute | solution.py:239
  71.3 11.7 %collective-permute-start.25 = (bf16[2,32,896]{2,1,0:T(8,128)(2,1)S(1)}, bf16[2,32,896]{2,1,0:T(8,128)(2,1)S(1)}, u32[]{:S(2)}, u32[]{:S(2)}) collective-permute-start(bf16[2,32,896]{2,1,0:T(8,128)(2,1)S(1)} %get-tuple-element.95), channel_id=1, source_target_pairs={{0,4},{1,5},{2,6},{3,7},{4,0},{5,1},{6,2},{7,3},{8,12},{9,13},{10,... | collective-permute-start | bytes 344072 | tf_op jit(solution)/shard_map/ppermute | solution.py:239
  72.4 10.5 %collective-permute-start.26 = (bf16[2,32,896]{2,1,0:T(8,128)(2,1)S(1)}, bf16[2,32,896]{2,1,0:T(8,128)(2,1)S(1)}, u32[]{:S(2)}, u32[]{:S(2)}) collective-permute-start(bf16[2,32,896]{2,1,0:T(8,128)(2,1)S(1)} %get-tuple-element.93.refs_5_.refs_2_), channel_id=1, source_target_pairs={{0,2},{1,3},{2,0},{3,1},{4,6},{5,7},{6,4},{7,5},{8,10},{9,11},{10,... | collective-permute-start | bytes 344072 | tf_op jit(solution)/shard_map/ppermute | solution.py:239
  (9 other events, 66.5 us)

commit v14 on v11

--- a/solution.py
+++ b/solution.py
@@ -48,10 +48,10 @@
 
 
 def route_kernel(experts, *refs):
-    pick_ref, weight_ref, keep_ref, swap_ref = refs[4:8]
-    ids_ref, gates_ref, tokens_ref, grad_ref, sems = refs[8:]
+    pick_ref, weight_ref, keep_ref, swap_ref = refs[3:7]
+    ids_ref, gates_ref, tokens_ref, sems = refs[7:]
     copies = [
-        pltpu.make_async_copy(refs[k], refs[8 + k], sems.at[k]) for k in range(4)
+        pltpu.make_async_copy(refs[k], refs[7 + k], sems.at[k]) for k in range(3)
     ]
     for copy in copies:
         copy.start()
@@ -79,22 +79,16 @@
     pick_ref[...] = pick
     copies[2].wait()
     rows = mm(pick, tokens_ref[...], ((1,), (0,))).astype(BF16)
-    split_cores(keep_ref, swap_ref, rows, 0)
-    copies[3].wait()
-    rows = (slot_weight * mm(pick, grad_ref[...], ((1,), (0,)))).astype(BF16)
-    split_cores(keep_ref, swap_ref, rows, 1)
+    split_cores(keep_ref, swap_ref, rows)
+
+
+def gather_scaled_kernel(pick_ref, weight_ref, grad_ref, keep_ref, swap_ref):
+    rows = mm(pick_ref[...], grad_ref[...], ((1,), (0,)))
+    split_cores(keep_ref, swap_ref, (weight_ref[...] * rows).astype(BF16))
 
 
 def load_kernel(from_ref, to_ref):
     to_ref[...] = from_ref[...]
-
-
-def pack_kernel(keep_ref, swap_ref, *out_refs):
-    half = keep_ref.shape[1]
-    for at in range(2):
-        for k in range(1, half):
-            out_refs[at * (half - 1) + k - 1][0] = keep_ref[at, k]
-            out_refs[at * (half - 1) + k - 1][1] = swap_ref[at, k]
 
 
 def pack_back_kernel(keep_ref, swap_ref, *out_refs):
@@ -103,8 +97,8 @@
         out_ref[1] = swap_ref[k + 1]
 
 
-def pieces(at, keep_ref, swap_ref, *refs):
-    found = [keep_ref[at, 0], swap_ref[at, 0]]
+def pieces(keep_ref, swap_ref, *refs):
+    found = [keep_ref[0], swap_ref[0]]
     for ref in refs[::-1]:
         found += [ref[0], ref[1]]
     return found
@@ -125,7 +119,7 @@
 def gate_up_kernel(half, *refs):
     gate_ref, up_ref, local_ref, *out_refs, scratch = refs[half + 1 :]
     dp = len(out_refs)
-    rows = local_order(pieces(0, *refs[: half + 1]), scratch, dp)
+    rows = local_order(pieces(*refs[: half + 1]), scratch, dp)
     local_ref[...] = rows
     chunk = rows.shape[0] // dp
     for at, mat in enumerate((gate_ref, up_ref)):
@@ -137,7 +131,7 @@
 def grad_act_kernel(half, *refs):
     down_ref, local_ref, *out_refs, scratch = refs[half + 1 :]
     dp = len(out_refs)
-    rows = local_order(pieces(1, *refs[: half + 1]), scratch, dp)
+    rows = local_order(pieces(*refs[: half + 1]), scratch, dp)
     local_ref[...] = rows
     split_rows(out_refs, mm(rows, down_ref[...], ((1,), (1,))).astype(BF16))
 
@@ -260,34 +254,34 @@
     half = experts // 2
     sized = shape((slots, features), BF16)
     wide = shape((slots, hidden), BF16)
-    both = shape((2, half, capacity, features), BF16)
     one = shape((half, capacity, features), BF16)
     pair = shape((2, capacity, features), BF16)
     in_order = [pltpu.VMEM((slots, features), BF16)]
 
-    ins = (expert_ids.T, gates.T, tokens, grad_out)
-    outs = (shape((slots, tok_rows), BF16), shape((slots, 1), F32), both, both)
+    ins = (expert_ids.T, gates.T, tokens)
+    outs = (shape((slots, tok_rows), BF16), shape((slots, 1), F32), one, one)
     pick, weight, keep, swap = call(
         functools.partial(route_kernel, experts),
         outs,
         4 * slots * tok_rows * features,
         8 * tok_rows * features,
         limit=ROUTE_LIMIT,
-        in_specs=[ANY] * 4,
+        in_specs=[ANY] * 3,
         scratch_shapes=[
             *[pltpu.VMEM(array.shape, array.dtype) for array in ins],
-            pltpu.SemaphoreType.DMA((4,)),
+            pltpu.SemaphoreType.DMA((3,)),
         ],
     )(*ins)
     swap_to, up_mat = lax.optimization_barrier((swap, up_mat))
     swap = partner(swap_to, "expert", 1)
     up_mat = call(load_kernel, shape(up_mat.shape, BF16), 0, 2 * weights)(up_mat)
     swap, up_mat = lax.optimization_barrier((swap, up_mat))
-    sent = call(pack_kernel, [pair] * (2 * half - 2), 0, 8 * slots)(keep, swap)
-    arrived = [
-        partner(value, "expert", 2 * (1 + k % (half - 1))) for k, value in enumerate(sent)
-    ]
-    row_blocks, grad_blocks = arrived[: half - 1][::-1], arrived[half - 1 :][::-1]
+    sent = call(pack_back_kernel, [pair] * (half - 1), 0, 8 * slots)(keep, swap)
+    row_blocks = [partner(value, "expert", 2 * (1 + k)) for k, value in enumerate(sent)][::-1]
+    grad_keep, grad_swap = call(gather_scaled_kernel, (one, one), 0, 0)(pick, weight, grad_out)
+    grad_swap = partner(grad_swap, "expert", 1)
+    sent = call(pack_back_kernel, [pair] * (half - 1), 0, 8 * slots)(grad_keep, grad_swap)
+    grad_blocks = [partner(value, "expert", 2 * (1 + k)) for k, value in enumerate(sent)][::-1]
     rows, *part_pre = call(
         functools.partial(gate_up_kernel, half),
         (sized, *[shape((2, chunk, hidden), BF16)] * dp),
@@ -310,7 +304,7 @@
         product,
         weights,
         scratch_shapes=in_order,
-    )(keep, swap, *grad_blocks, down_mat)
+    )(grad_keep, grad_swap, *grad_blocks, down_mat)
     grad_sums = trade(part_grad)
     pre_mine = call(
         functools.partial(grad_pre_kernel, dp),

time: 81.9 us -> 82.2 us (level)
  local copies, waits for them, and re-layouts: 0.03 us -> 2.34 us
  waiting for transfers between devices: 33.3 us -> 31.8 us
    unnamed x12 -> x14, local copies, waits for them, and re-layouts: 0.03 us -> 2.34 us
    ppermute x27 -> x28, waiting for transfers between devices: 33.3 us -> 31.8 us  [partner(): return lax.ppermute(value, axis, [(i, i ^ k) for i in range(size)])]
    ppermute x27 -> x28, starting transfers between devices: 32.5 us -> 32.2 us  [partner(): return lax.ppermute(value, axis, [(i, i ^ k) for i in range(size)])]
  transfers between devices with their start and end apart: 27 -> 28, of which waited for: 13 -> 11; matrix products, arithmetic and copies ran while one was open for 0% -> 0% of each run, Pallas kernels for 10% -> 12%
where the time goes in v14:
time: 82.2 us; the launch traced here: 82 us
  starting transfers between devices  32.2 us (39%)
  waiting for transfers between devices  31.8 us (39%)
  Pallas kernels  14.8 us (18%)
  local copies, waits for them, and re-layouts  2.34 us (3%)
  between operations  0.83 us (1%)
    ppermute x28, starting transfers between devices, partner(): return lax.ppermute(value, axis, [(i, i ^ k) for i in range(size)])  32.2 us
    ppermute x28, waiting for transfers between devices, partner(): return lax.ppermute(value, axis, [(i, i ^ k) for i in range(size)])  31.8 us
    pallas_call x1, Pallas kernels, body(): call(functools.partial(grads_kernel, 2), [shape((features, hidden), BF16)...  2.54 us
    pallas_call x1, Pallas kernels, body(): call(functools.partial(route_kernel, experts), outs, 4 * slots * tok_rows...  2.45 us
    unnamed x14, local copies, waits for them, and re-layouts  2.34 us
    pallas_call x1, Pallas kernels, body(): call(functools.partial(grads_kernel, 1), [shape((hidden, features), BF16)...  1.97 us
  transfers between devices with their start and end apart: 28, of which 11 were waited for; matrix products, arithmetic and copies ran while one was open for 0% of the time, Pallas kernels for 12%

profile of v14, /device:TPU:0, one launch (start us, length us, event | category | flops | bytes accessed | tf_op | source)
XLA Modules:
  0.0 82.0 jit_solution(16399374647534244374)
XLA Ops:
  0.6 2.5 %shard_map.110 = (bf16[256,512]{1,0:T(8,128)(2,1)}, f32[256,1]{1,0:T(8,128)}, bf16[4,32,896]{2,1,0:T(8,128)(2,1)}, bf16[4,32,896]{2,1,0:T(8,128)(2,1)}) custom-call(s32[8,512]{1,0:T(8,128)} %bitcast.14, f32[8,512]{1,0:T(8,128)} %bitcast.15, bf16[512,896]{1,0:T(8,128)(2,1)} %refs_2_.1), custom_call_target="tpu_custom_call" | custom-call | flops 469762048 | bytes 3670016 | tf_op jit(solution)/shard_map/pallas_call | solution.py:263
  3.6 1.5 %copy-done.2 = bf16[1,896,1024]{2,1,0:T(8,128)(2,1)S(1)} copy-done((bf16[1,896,1024]{2,1,0:T(8,128)(2,1)S(1)}, bf16[1,896,1024]{2,1,0:T(8,128)(2,1)}, u32[]{:S(2)}) %copy-start.2) | copy-done | bytes 1835032
  6.1 4.8 %collective-permute-start.1 = (bf16[2,32,896]{2,1,0:T(8,128)(2,1)S(1)}, bf16[2,32,896]{2,1,0:T(8,128)(2,1)S(1)}, u32[]{:S(2)}, u32[]{:S(2)}) collective-permute-start(bf16[2,32,896]{2,1,0:T(8,128)(2,1)S(1)} %get-tuple-element.62), channel_id=1, source_target_pairs={{0,6},{1,7},{2,4},{3,5},{4,2},{5,3},{6,0},{7,1},{8,14},{9,15},{10,... | collective-permute-start | bytes 344072 | tf_op jit(solution)/shard_map/ppermute | solution.py:233
  12.1 2.9 %collective-permute-done.1.refs_2_ = bf16[2,32,896]{2,1,0:T(8,128)(2,1)S(1)} collective-permute-done((bf16[2,32,896]{2,1,0:T(8,128)(2,1)S(1)}, bf16[2,32,896]{2,1,0:T(8,128)(2,1)S(1)}, u32[]{:S(2)}, u32[]{:S(2)}) %collective-permute-start.1) | collective-permute-done | bytes 114720 | tf_op jit(solution)/shard_map/ppermute | solution.py:233
  15.0 6.1 %collective-permute-done.2.refs_3_ = bf16[2,32,896]{2,1,0:T(8,128)(2,1)S(1)} collective-permute-done((bf16[2,32,896]{2,1,0:T(8,128)(2,1)S(1)}, bf16[2,32,896]{2,1,0:T(8,128)(2,1)S(1)}, u32[]{:S(2)}, u32[]{:S(2)}) %collective-permute-start.2) | collective-permute-done | bytes 114720 | tf_op jit(solution)/shard_map/ppermute | solution.py:233
  22.4 1.6 %collective-permute-start.4 = (bf16[2,64,1024]{2,1,0:T(8,128)(2,1)S(1)}, bf16[2,64,1024]{2,1,0:T(8,128)(2,1)S(1)}, u32[]{:S(2)}, u32[]{:S(2)}) collective-permute-start(bf16[2,64,1024]{2,1,0:T(8,128)(2,1)S(1)} %get-tuple-element.67), channel_id=1, source_target_pairs={{0,8},{8,0},{16,24},{24,16},{1,9},{9,1},{17,25},{25,17},{2,10},{10... | collective-permute-start | bytes 786440 | tf_op jit(solution)/shard_map/ppermute | solution.py:233
  24.0 1.5 %collective-permute-start.5 = (bf16[2,64,1024]{2,1,0:T(8,128)(2,1)S(1)}, bf16[2,64,1024]{2,1,0:T(8,128)(2,1)S(1)}, u32[]{:S(2)}, u32[]{:S(2)}) collective-permute-start(bf16[2,64,1024]{2,1,0:T(8,128)(2,1)S(1)} %get-tuple-element.68), channel_id=1, source_target_pairs={{0,16},{8,24},{16,0},{24,8},{1,17},{9,25},{17,1},{25,9},{2,18},{10... | collective-permute-start | bytes 786440 | tf_op jit(solution)/shard_map/ppermute | solution.py:233
  26.0 2.6 %collective-permute-start.12 = (bf16[2,32,896]{2,1,0:T(8,128)(2,1)S(1)}, bf16[2,32,896]{2,1,0:T(8,128)(2,1)S(1)}, u32[]{:S(2)}, u32[]{:S(2)}) collective-permute-start(bf16[2,32,896]{2,1,0:T(8,128)(2,1)S(1)} %get-tuple-element.74), channel_id=1, source_target_pairs={{0,6},{1,7},{2,4},{3,5},{4,2},{5,3},{6,0},{7,1},{8,14},{9,15},{10,... | collective-permute-start | bytes 344072 | tf_op jit(solution)/shard_map/ppermute | solution.py:233
  28.5 3.1 %collective-permute-done.4.refs_1_ = bf16[2,64,1024]{2,1,0:T(8,128)(2,1)S(1)} collective-permute-done((bf16[2,64,1024]{2,1,0:T(8,128)(2,1)S(1)}, bf16[2,64,1024]{2,1,0:T(8,128)(2,1)S(1)}, u32[]{:S(2)}, u32[]{:S(2)}) %collective-permute-start.4) | collective-permute-done | bytes 262176 | tf_op jit(solution)/shard_map/ppermute | solution.py:233
  31.9 5.2 %collective-permute-done.5.refs_2_ = bf16[2,64,1024]{2,1,0:T(8,128)(2,1)S(1)} collective-permute-done((bf16[2,64,1024]{2,1,0:T(8,128)(2,1)S(1)}, bf16[2,64,1024]{2,1,0:T(8,128)(2,1)S(1)}, u32[]{:S(2)}, u32[]{:S(2)}) %collective-permute-start.5) | collective-permute-done | bytes 262176 | tf_op jit(solution)/shard_map/ppermute | solution.py:233
  39.4 1.4 %collective-permute-start.9 = (bf16[64,1024]{1,0:T(8,128)(2,1)S(1)}, bf16[64,1024]{1,0:T(8,128)(2,1)S(1)}, u32[]{:S(2)}, u32[]{:S(2)}) collective-permute-start(bf16[64,1024]{1,0:T(8,128)(2,1)S(1)} %shard_map.115.refs_0_), channel_id=1, source_target_pairs={{0,24},{8,16},{16,8},{24,0},{1,25},{9,17},{17,9},{25,1},{2,26},{10... | collective-permute-start | bytes 393224 | tf_op jit(solution)/shard_map/ppermute | solution.py:233
  43.7 1.4 %collective-permute-start.17 = (bf16[64,1024]{1,0:T(8,128)(2,1)S(1)}, bf16[64,1024]{1,0:T(8,128)(2,1)S(1)}, u32[]{:S(2)}, u32[]{:S(2)}) collective-permute-start(bf16[64,1024]{1,0:T(8,128)(2,1)S(1)} %get-tuple-element.83), channel_id=1, source_target_pairs={{0,24},{8,16},{16,8},{24,0},{1,25},{9,17},{17,9},{25,1},{2,26},{10... | collective-permute-start | bytes 393224 | tf_op jit(solution)/shard_map/ppermute | solution.py:233
  45.2 2.4 %collective-permute-done.9.refs_3_ = bf16[64,1024]{1,0:T(8,128)(2,1)S(1)} collective-permute-done((bf16[64,1024]{1,0:T(8,128)(2,1)S(1)}, bf16[64,1024]{1,0:T(8,128)(2,1)S(1)}, u32[]{:S(2)}, u32[]{:S(2)}) %collective-permute-start.9) | collective-permute-done | bytes 131104 | tf_op jit(solution)/shard_map/ppermute | solution.py:233
  49.1 1.6 %collective-permute-done.16.refs_6_ = bf16[64,1024]{1,0:T(8,128)(2,1)S(1)} collective-permute-done((bf16[64,1024]{1,0:T(8,128)(2,1)S(1)}, bf16[64,1024]{1,0:T(8,128)(2,1)S(1)}, u32[]{:S(2)}, u32[]{:S(2)}) %collective-permute-start.16) | collective-permute-done | bytes 131104 | tf_op jit(solution)/shard_map/ppermute | solution.py:233
  51.8 1.5 %collective-permute-start.19 = (bf16[2,64,1024]{2,1,0:T(8,128)(2,1)S(1)}, bf16[2,64,1024]{2,1,0:T(8,128)(2,1)S(1)}, u32[]{:S(2)}, u32[]{:S(2)}) collective-permute-start(bf16[2,64,1024]{2,1,0:T(8,128)(2,1)S(1)} %shard_map.120.refs_0_), channel_id=1, source_target_pairs={{0,16},{8,24},{16,0},{24,8},{1,17},{9,25},{17,1},{25,9},{2,18},{10... | collective-permute-start | bytes 786440 | tf_op jit(solution)/shard_map/ppermute | solution.py:233
  54.7 2.6 %collective-permute-start.22 = (bf16[2,32,896]{2,1,0:T(8,128)(2,1)S(1)}, bf16[2,32,896]{2,1,0:T(8,128)(2,1)S(1)}, u32[]{:S(2)}, u32[]{:S(2)}) collective-permute-start(bf16[2,32,896]{2,1,0:T(8,128)(2,1)S(1)} %get-tuple-element.85), channel_id=1, source_target_pairs={{0,6},{1,7},{2,4},{3,5},{4,2},{5,3},{6,0},{7,1},{8,14},{9,15},{10,... | collective-permute-start | bytes 344072 | tf_op jit(solution)/shard_map/ppermute | solution.py:233
  57.3 3.0 %collective-permute-done.18.refs_1_ = bf16[2,64,1024]{2,1,0:T(8,128)(2,1)S(1)} collective-permute-done((bf16[2,64,1024]{2,1,0:T(8,128)(2,1)S(1)}, bf16[2,64,1024]{2,1,0:T(8,128)(2,1)S(1)}, u32[]{:S(2)}, u32[]{:S(2)}) %collective-permute-start.18) | collective-permute-done | bytes 262176 | tf_op jit(solution)/shard_map/ppermute | solution.py:233
  60.3 2.1 %collective-permute-done.19.refs_2_ = bf16[2,64,1024]{2,1,0:T(8,128)(2,1)S(1)} collective-permute-done((bf16[2,64,1024]{2,1,0:T(8,128)(2,1)S(1)}, bf16[2,64,1024]{2,1,0:T(8,128)(2,1)S(1)}, u32[]{:S(2)}, u32[]{:S(2)}) %collective-permute-start.19) | collective-permute-done | bytes 262176 | tf_op jit(solution)/shard_map/ppermute | solution.py:233
  65.3 2.0 %collective-permute-start.23 = (bf16[2,32,896]{2,1,0:T(8,128)(2,1)S(1)}, bf16[2,32,896]{2,1,0:T(8,128)(2,1)S(1)}, u32[]{:S(2)}, u32[]{:S(2)}) collective-permute-start(bf16[2,32,896]{2,1,0:T(8,128)(2,1)S(1)} %get-tuple-element.88), channel_id=1, source_target_pairs={{0,2},{1,3},{2,0},{3,1},{4,6},{5,7},{6,4},{7,5},{8,10},{9,11},{10,... | collective-permute-start | bytes 344072 | tf_op jit(solution)/shard_map/ppermute | solution.py:233
  67.4 1.9 %collective-permute-start.25 = (bf16[2,32,896]{2,1,0:T(8,128)(2,1)S(1)}, bf16[2,32,896]{2,1,0:T(8,128)(2,1)S(1)}, u32[]{:S(2)}, u32[]{:S(2)}) collective-permute-start(bf16[2,32,896]{2,1,0:T(8,128)(2,1)S(1)} %get-tuple-element.96), channel_id=1, source_target_pairs={{0,6},{1,7},{2,4},{3,5},{4,2},{5,3},{6,0},{7,1},{8,14},{9,15},{10,... | collective-permute-start | bytes 344072 | tf_op jit(solution)/shard_map/ppermute | solution.py:233
  70.2 1.7 %collective-permute-start.27 = (bf16[2,32,896]{2,1,0:T(8,128)(2,1)S(1)}, bf16[2,32,896]{2,1,0:T(8,128)(2,1)S(1)}, u32[]{:S(2)}, u32[]{:S(2)}) collective-permute-start(bf16[2,32,896]{2,1,0:T(8,128)(2,1)S(1)} %get-tuple-element.95.refs_5_.refs_2_), channel_id=1, source_target_pairs={{0,2},{1,3},{2,0},{3,1},{4,6},{5,7},{6,4},{7,5},{8,10},{9,11},{10,... | collective-permute-start | bytes 344072 | tf_op jit(solution)/shard_map/ppermute | solution.py:233
  71.9 2.0 %shard_map.127 = bf16[1024,896]{1,0:T(8,128)(2,1)} custom-call(bf16[256,1024]{1,0:T(8,128)(2,1)S(1)} %get-tuple-element.103.left_ref, bf16[256,896]{1,0:T(8,128)(2,1)S(1)} %get-tuple-element.104.refs_0_), custom_call_target="tpu_custom_call" | custom-call | flops 469762048 | bytes 1835008 | tf_op jit(solution)/shard_map/pallas_call | solution.py:340
  75.1 2.5 %shard_map.126 = (bf16[896,1024]{1,0:T(8,128)(2,1)}, bf16[896,1024]{1,0:T(8,128)(2,1)}) custom-call(bf16[256,896]{1,0:T(8,128)(2,1)S(1)} %get-tuple-element.98.left_ref, bf16[256,1024]{1,0:T(8,128)(2,1)S(1)} %get-tuple-element.99.refs_0_, bf16[256,1024]{1,0:T(8,128)(2,1)S(1)} %get-tuple-element.100.refs_1_, ...), custom_call_target="tpu_custom_call" | custom-call | flops 939524096 | bytes 3670016 | tf_op jit(solution)/shard_map/pallas_call | solution.py:346
  77.7 3.1 %collective-permute-done.26.refs_3_ = bf16[2,32,896]{2,1,0:T(8,128)(2,1)S(1)} collective-permute-done((bf16[2,32,896]{2,1,0:T(8,128)(2,1)S(1)}, bf16[2,32,896]{2,1,0:T(8,128)(2,1)S(1)}, u32[]{:S(2)}, u32[]{:S(2)}) %collective-permute-start.26) | collective-permute-done | bytes 114720 | tf_op jit(solution)/shard_map/ppermute | solution.py:233
  (64 shorter events, 20.1 us)
Async XLA Ops:
  6.1 8.9 %collective-permute-start.1 = (bf16[2,32,896]{2,1,0:T(8,128)(2,1)S(1)}, bf16[2,32,896]{2,1,0:T(8,128)(2,1)S(1)}, u32[]{:S(2)}, u32[]{:S(2)}) collective-permute-start(bf16[2,32,896]{2,1,0:T(8,128)(2,1)S(1)} %get-tuple-element.62), channel_id=1, source_target_pairs={{0,6},{1,7},{2,4},{3,5},{4,2},{5,3},{6,0},{7,1},{8,14},{9,15},{10,... | collective-permute-start | bytes 344072 | tf_op jit(solution)/shard_map/ppermute | solution.py:233
  10.9 10.2 %collective-permute-start.2 = (bf16[2,32,896]{2,1,0:T(8,128)(2,1)S(1)}, bf16[2,32,896]{2,1,0:T(8,128)(2,1)S(1)}, u32[]{:S(2)}, u32[]{:S(2)}) collective-permute-start(bf16[2,32,896]{2,1,0:T(8,128)(2,1)S(1)} %get-tuple-element.63), channel_id=1, source_target_pairs={{0,4},{1,5},{2,6},{3,7},{4,0},{5,1},{6,2},{7,3},{8,12},{9,13},{10,... | collective-permute-start | bytes 344072 | tf_op jit(solution)/shard_map/ppermute | solution.py:233
  10.9 10.2 %collective-permute-start.3 = (bf16[2,32,896]{2,1,0:T(8,128)(2,1)S(1)}, bf16[2,32,896]{2,1,0:T(8,128)(2,1)S(1)}, u32[]{:S(2)}, u32[]{:S(2)}) collective-permute-start(bf16[2,32,896]{2,1,0:T(8,128)(2,1)S(1)} %get-tuple-element.64), channel_id=1, source_target_pairs={{0,2},{1,3},{2,0},{3,1},{4,6},{5,7},{6,4},{7,5},{8,10},{9,11},{10,... | collective-permute-start | bytes 344072 | tf_op jit(solution)/shard_map/ppermute | solution.py:233
  12.0 14.0 %collective-permute-start.11 = (bf16[4,32,896]{2,1,0:T(8,128)(2,1)S(1)}, bf16[4,32,896]{2,1,0:T(8,128)(2,1)S(1)}, u32[]{:S(2)}, u32[]{:S(2)}) collective-permute-start(bf16[4,32,896]{2,1,0:T(8,128)(2,1)S(1)} %get-tuple-element.73), channel_id=1, source_target_pairs={{0,1},{1,0},{2,3},{3,2},{4,5},{5,4},{6,7},{7,6},{8,9},{9,8},{10,11... | collective-permute-start | bytes 688136 | tf_op jit(solution)/shard_map/ppermute | solution.py:233
  22.4 9.3 %collective-permute-start.4 = (bf16[2,64,1024]{2,1,0:T(8,128)(2,1)S(1)}, bf16[2,64,1024]{2,1,0:T(8,128)(2,1)S(1)}, u32[]{:S(2)}, u32[]{:S(2)}) collective-permute-start(bf16[2,64,1024]{2,1,0:T(8,128)(2,1)S(1)} %get-tuple-element.67), channel_id=1, source_target_pairs={{0,8},{8,0},{16,24},{24,16},{1,9},{9,1},{17,25},{25,17},{2,10},{10... | collective-permute-start | bytes 786440 | tf_op jit(solution)/shard_map/ppermute | solution.py:233
  24.0 13.1 %collective-permute-start.5 = (bf16[2,64,1024]{2,1,0:T(8,128)(2,1)S(1)}, bf16[2,64,1024]{2,1,0:T(8,128)(2,1)S(1)}, u32[]{:S(2)}, u32[]{:S(2)}) collective-permute-start(bf16[2,64,1024]{2,1,0:T(8,128)(2,1)S(1)} %get-tuple-element.68), channel_id=1, source_target_pairs={{0,16},{8,24},{16,0},{24,8},{1,17},{9,25},{17,1},{25,9},{2,18},{10... | collective-permute-start | bytes 786440 | tf_op jit(solution)/shard_map/ppermute | solution.py:233
  25.5 11.6 %collective-permute-start.6 = (bf16[2,64,1024]{2,1,0:T(8,128)(2,1)S(1)}, bf16[2,64,1024]{2,1,0:T(8,128)(2,1)S(1)}, u32[]{:S(2)}, u32[]{:S(2)}) collective-permute-start(bf16[2,64,1024]{2,1,0:T(8,128)(2,1)S(1)} %get-tuple-element.69), channel_id=1, source_target_pairs={{0,24},{8,16},{16,8},{24,0},{1,25},{9,17},{17,9},{25,1},{2,26},{10... | collective-permute-start | bytes 786440 | tf_op jit(solution)/shard_map/ppermute | solution.py:233
  26.0 13.4 %collective-permute-start.12 = (bf16[2,32,896]{2,1,0:T(8,128)(2,1)S(1)}, bf16[2,32,896]{2,1,0:T(8,128)(2,1)S(1)}, u32[]{:S(2)}, u32[]{:S(2)}) collective-permute-start(bf16[2,32,896]{2,1,0:T(8,128)(2,1)S(1)} %get-tuple-element.74), channel_id=1, source_target_pairs={{0,6},{1,7},{2,4},{3,5},{4,2},{5,3},{6,0},{7,1},{8,14},{9,15},{10,... | collective-permute-start | bytes 344072 | tf_op jit(solution)/shard_map/ppermute | solution.py:233
  28.5 12.3 %collective-permute-start.13 = (bf16[2,32,896]{2,1,0:T(8,128)(2,1)S(1)}, bf16[2,32,896]{2,1,0:T(8,128)(2,1)S(1)}, u32[]{:S(2)}, u32[]{:S(2)}) collective-permute-start(bf16[2,32,896]{2,1,0:T(8,128)(2,1)S(1)} %get-tuple-element.75), channel_id=1, source_target_pairs={{0,4},{1,5},{2,6},{3,7},{4,0},{5,1},{6,2},{7,3},{8,12},{9,13},{10,... | collective-permute-start | bytes 344072 | tf_op jit(solution)/shard_map/ppermute | solution.py:233
  31.7 9.1 %collective-permute-start.14 = (bf16[2,32,896]{2,1,0:T(8,128)(2,1)S(1)}, bf16[2,32,896]{2,1,0:T(8,128)(2,1)S(1)}, u32[]{:S(2)}, u32[]{:S(2)}) collective-permute-start(bf16[2,32,896]{2,1,0:T(8,128)(2,1)S(1)} %get-tuple-element.76), channel_id=1, source_target_pairs={{0,2},{1,3},{2,0},{3,1},{4,6},{5,7},{6,4},{7,5},{8,10},{9,11},{10,... | collective-permute-start | bytes 344072 | tf_op jit(solution)/shard_map/ppermute | solution.py:233
  38.6 6.6 %collective-permute-start.8 = (bf16[64,1024]{1,0:T(8,128)(2,1)S(1)}, bf16[64,1024]{1,0:T(8,128)(2,1)S(1)}, u32[]{:S(2)}, u32[]{:S(2)}) collective-permute-start(bf16[64,1024]{1,0:T(8,128)(2,1)S(1)} %shard_map.115.refs_0_), channel_id=1, source_target_pairs={{0,16},{8,24},{16,0},{24,8},{1,17},{9,25},{17,1},{25,9},{2,18},{10... | collective-permute-start | bytes 393224 | tf_op jit(solution)/shard_map/ppermute | solution.py:233
  39.4 8.2 %collective-permute-start.9 = (bf16[64,1024]{1,0:T(8,128)(2,1)S(1)}, bf16[64,1024]{1,0:T(8,128)(2,1)S(1)}, u32[]{:S(2)}, u32[]{:S(2)}) collective-permute-start(bf16[64,1024]{1,0:T(8,128)(2,1)S(1)} %shard_map.115.refs_0_), channel_id=1, source_target_pairs={{0,24},{8,16},{16,8},{24,0},{1,25},{9,17},{17,9},{25,1},{2,26},{10... | collective-permute-start | bytes 393224 | tf_op jit(solution)/shard_map/ppermute | solution.py:233
  41.6 7.5 %collective-permute-start.15 = (bf16[64,1024]{1,0:T(8,128)(2,1)S(1)}, bf16[64,1024]{1,0:T(8,128)(2,1)S(1)}, u32[]{:S(2)}, u32[]{:S(2)}) collective-permute-start(bf16[64,1024]{1,0:T(8,128)(2,1)S(1)} %get-tuple-element.81), channel_id=1, source_target_pairs={{0,8},{8,0},{16,24},{24,16},{1,9},{9,1},{17,25},{25,17},{2,10},{10... | collective-permute-start | bytes 393224 | tf_op jit(solution)/shard_map/ppermute | solution.py:233
  42.9 7.9 %collective-permute-start.16 = (bf16[64,1024]{1,0:T(8,128)(2,1)S(1)}, bf16[64,1024]{1,0:T(8,128)(2,1)S(1)}, u32[]{:S(2)}, u32[]{:S(2)}) collective-permute-start(bf16[64,1024]{1,0:T(8,128)(2,1)S(1)} %get-tuple-element.82), channel_id=1, source_target_pairs={{0,16},{8,24},{16,0},{24,8},{1,17},{9,25},{17,1},{25,9},{2,18},{10... | collective-permute-start | bytes 393224 | tf_op jit(solution)/shard_map/ppermute | solution.py:233
  43.7 7.1 %collective-permute-start.17 = (bf16[64,1024]{1,0:T(8,128)(2,1)S(1)}, bf16[64,1024]{1,0:T(8,128)(2,1)S(1)}, u32[]{:S(2)}, u32[]{:S(2)}) collective-permute-start(bf16[64,1024]{1,0:T(8,128)(2,1)S(1)} %get-tuple-element.83), channel_id=1, source_target_pairs={{0,24},{8,16},{16,8},{24,0},{1,25},{9,17},{17,9},{25,1},{2,26},{10... | collective-permute-start | bytes 393224 | tf_op jit(solution)/shard_map/ppermute | solution.py:233
  51.1 9.3 %collective-permute-start.18 = (bf16[2,64,1024]{2,1,0:T(8,128)(2,1)S(1)}, bf16[2,64,1024]{2,1,0:T(8,128)(2,1)S(1)}, u32[]{:S(2)}, u32[]{:S(2)}) collective-permute-start(bf16[2,64,1024]{2,1,0:T(8,128)(2,1)S(1)} %shard_map.120.refs_0_), channel_id=1, source_target_pairs={{0,8},{8,0},{16,24},{24,16},{1,9},{9,1},{17,25},{25,17},{2,10},{10... | collective-permute-start | bytes 786440 | tf_op jit(solution)/shard_map/ppermute | solution.py:233
  51.8 10.7 %collective-permute-start.19 = (bf16[2,64,1024]{2,1,0:T(8,128)(2,1)S(1)}, bf16[2,64,1024]{2,1,0:T(8,128)(2,1)S(1)}, u32[]{:S(2)}, u32[]{:S(2)}) collective-permute-start(bf16[2,64,1024]{2,1,0:T(8,128)(2,1)S(1)} %shard_map.120.refs_0_), channel_id=1, source_target_pairs={{0,16},{8,24},{16,0},{24,8},{1,17},{9,25},{17,1},{25,9},{2,18},{10... | collective-permute-start | bytes 786440 | tf_op jit(solution)/shard_map/ppermute | solution.py:233
  53.2 10.7 %collective-permute-start.20 = (bf16[2,64,1024]{2,1,0:T(8,128)(2,1)S(1)}, bf16[2,64,1024]{2,1,0:T(8,128)(2,1)S(1)}, u32[]{:S(2)}, u32[]{:S(2)}) collective-permute-start(bf16[2,64,1024]{2,1,0:T(8,128)(2,1)S(1)} %shard_map.120.refs_0_), channel_id=1, source_target_pairs={{0,24},{8,16},{16,8},{24,0},{1,25},{9,17},{17,9},{25,1},{2,26},{10... | collective-permute-start | bytes 786440 | tf_op jit(solution)/shard_map/ppermute | solution.py:233
  54.7 9.2 %collective-permute-start.21 = (bf16[2,32,896]{2,1,0:T(8,128)(2,1)S(1)}, bf16[2,32,896]{2,1,0:T(8,128)(2,1)S(1)}, u32[]{:S(2)}, u32[]{:S(2)}) collective-permute-start(bf16[2,32,896]{2,1,0:T(8,128)(2,1)S(1)} %get-tuple-element.84), channel_id=1, source_target_pairs={{0,4},{1,5},{2,6},{3,7},{4,0},{5,1},{6,2},{7,3},{8,12},{9,13},{10,... | collective-permute-start | bytes 344072 | tf_op jit(solution)/shard_map/ppermute | solution.py:233
  54.7 9.2 %collective-permute-start.22 = (bf16[2,32,896]{2,1,0:T(8,128)(2,1)S(1)}, bf16[2,32,896]{2,1,0:T(8,128)(2,1)S(1)}, u32[]{:S(2)}, u32[]{:S(2)}) collective-permute-start(bf16[2,32,896]{2,1,0:T(8,128)(2,1)S(1)} %get-tuple-element.85), channel_id=1, source_target_pairs={{0,6},{1,7},{2,4},{3,5},{4,2},{5,3},{6,0},{7,1},{8,14},{9,15},{10,... | collective-permute-start | bytes 344072 | tf_op jit(solution)/shard_map/ppermute | solution.py:233
  65.3 8.6 %collective-permute-start.23 = (bf16[2,32,896]{2,1,0:T(8,128)(2,1)S(1)}, bf16[2,32,896]{2,1,0:T(8,128)(2,1)S(1)}, u32[]{:S(2)}, u32[]{:S(2)}) collective-permute-start(bf16[2,32,896]{2,1,0:T(8,128)(2,1)S(1)} %get-tuple-element.88), channel_id=1, source_target_pairs={{0,2},{1,3},{2,0},{3,1},{4,6},{5,7},{6,4},{7,5},{8,10},{9,11},{10,... | collective-permute-start | bytes 344072 | tf_op jit(solution)/shard_map/ppermute | solution.py:233
  67.4 10.3 %collective-permute-start.25 = (bf16[2,32,896]{2,1,0:T(8,128)(2,1)S(1)}, bf16[2,32,896]{2,1,0:T(8,128)(2,1)S(1)}, u32[]{:S(2)}, u32[]{:S(2)}) collective-permute-start(bf16[2,32,896]{2,1,0:T(8,128)(2,1)S(1)} %get-tuple-element.96), channel_id=1, source_target_pairs={{0,6},{1,7},{2,4},{3,5},{4,2},{5,3},{6,0},{7,1},{8,14},{9,15},{10,... | collective-permute-start | bytes 344072 | tf_op jit(solution)/shard_map/ppermute | solution.py:233
  69.4 11.4 %collective-permute-start.26 = (bf16[2,32,896]{2,1,0:T(8,128)(2,1)S(1)}, bf16[2,32,896]{2,1,0:T(8,128)(2,1)S(1)}, u32[]{:S(2)}, u32[]{:S(2)}) collective-permute-start(bf16[2,32,896]{2,1,0:T(8,128)(2,1)S(1)} %get-tuple-element.97), channel_id=1, source_target_pairs={{0,4},{1,5},{2,6},{3,7},{4,0},{5,1},{6,2},{7,3},{8,12},{9,13},{10,... | collective-permute-start | bytes 344072 | tf_op jit(solution)/shard_map/ppermute | solution.py:233
  70.2 10.5 %collective-permute-start.27 = (bf16[2,32,896]{2,1,0:T(8,128)(2,1)S(1)}, bf16[2,32,896]{2,1,0:T(8,128)(2,1)S(1)}, u32[]{:S(2)}, u32[]{:S(2)}) collective-permute-start(bf16[2,32,896]{2,1,0:T(8,128)(2,1)S(1)} %get-tuple-element.95.refs_5_.refs_2_), channel_id=1, source_target_pairs={{0,2},{1,3},{2,0},{3,1},{4,6},{5,7},{6,4},{7,5},{8,10},{9,11},{10,... | collective-permute-start | bytes 344072 | tf_op jit(solution)/shard_map/ppermute | solution.py:233
  (11 other events, 76.4 us)

commit v15 on v14

--- a/solution.py
+++ b/solution.py
@@ -82,12 +82,13 @@
     split_cores(keep_ref, swap_ref, rows)
 
 
-def gather_scaled_kernel(pick_ref, weight_ref, grad_ref, keep_ref, swap_ref):
+def gather_scaled_kernel(pick_ref, weight_ref, grad_ref, mat_ref, keep_ref, swap_ref, held_ref):
+    held_ref[...] = mat_ref[...]
     rows = mm(pick_ref[...], grad_ref[...], ((1,), (0,)))
     split_cores(keep_ref, swap_ref, (weight_ref[...] * rows).astype(BF16))
 
 
-def load_kernel(from_ref, to_ref):
+def hold_kernel(from_ref, to_ref):
     to_ref[...] = from_ref[...]
 
 
@@ -272,13 +273,14 @@
             pltpu.SemaphoreType.DMA((3,)),
         ],
     )(*ins)
-    swap_to, up_mat = lax.optimization_barrier((swap, up_mat))
-    swap = partner(swap_to, "expert", 1)
-    up_mat = call(load_kernel, shape(up_mat.shape, BF16), 0, 2 * weights)(up_mat)
-    swap, up_mat = lax.optimization_barrier((swap, up_mat))
+    swap = partner(swap, "expert", 1)
+    keep = call(hold_kernel, one)(keep)
+    swap, keep = lax.optimization_barrier((swap, keep))
     sent = call(pack_back_kernel, [pair] * (half - 1), 0, 8 * slots)(keep, swap)
     row_blocks = [partner(value, "expert", 2 * (1 + k)) for k, value in enumerate(sent)][::-1]
-    grad_keep, grad_swap = call(gather_scaled_kernel, (one, one), 0, 0)(pick, weight, grad_out)
+    grad_keep, grad_swap, up_mat = call(
+        gather_scaled_kernel, (one, one, shape(up_mat.shape, BF16)), 0, 0
+    )(pick, weight, grad_out, up_mat)
     grad_swap = partner(grad_swap, "expert", 1)
     sent = call(pack_back_kernel, [pair] * (half - 1), 0, 8 * slots)(grad_keep, grad_swap)
     grad_blocks = [partner(value, "expert", 2 * (1 + k)) for k, value in enumerate(sent)][::-1]

time: 82.2 us -> 81 us (0.985)
  waiting for transfers between devices: 31.8 us -> 28.4 us
  local copies, waits for them, and re-layouts: 2.34 us -> 4 us
    ppermute x28, waiting for transfers between devices: 31.8 us -> 28.4 us  [partner(): return lax.ppermute(value, axis, [(i, i ^ k) for i in range(size)])]
    unnamed x14 -> x18, local copies, waits for them, and re-layouts: 2.34 us -> 4 us
  transfers between devices with their start and end apart: 28 -> 28, of which waited for: 11 -> 12; matrix products, arithmetic and copies ran while one was open for 0% -> 0% of each run, Pallas kernels for 12% -> 12%
where the time goes in v15:
time: 81 us; the launch traced here: 80.7 us
  starting transfers between devices  32.6 us (40%)
  waiting for transfers between devices  28.4 us (35%)
  Pallas kernels  14.9 us (18%)
  local copies, waits for them, and re-layouts  4 us (5%)
  between operations  0.84 us (1%)
    ppermute x28, starting transfers between devices, partner(): return lax.ppermute(value, axis, [(i, i ^ k) for i in range(size)])  32.6 us
    ppermute x28, waiting for transfers between devices, partner(): return lax.ppermute(value, axis, [(i, i ^ k) for i in range(size)])  28.4 us
    unnamed x18, local copies, waits for them, and re-layouts  4 us
    pallas_call x1, Pallas kernels, body(): call(functools.partial(route_kernel, experts), outs, 4 * slots * tok_rows...  2.59 us
    pallas_call x1, Pallas kernels, body(): call(functools.partial(grads_kernel, 2), [shape((features, hidden), BF16)...  2.54 us
    pallas_call x1, Pallas kernels, body(): call(functools.partial(grads_kernel, 1), [shape((hidden, features), BF16)...  1.97 us
  transfers between devices with their start and end apart: 28, of which 12 were waited for; matrix products, arithmetic and copies ran while one was open for 0% of the time, Pallas kernels for 12%

profile of v15, /device:TPU:0, one launch (start us, length us, event | category | flops | bytes accessed | tf_op | source)
XLA Modules:
  0.0 80.7 jit_solution(7435136707919144839)
XLA Ops:
  0.6 2.6 %shard_map.110 = (bf16[256,512]{1,0:T(8,128)(2,1)}, f32[256,1]{1,0:T(8,128)}, bf16[4,32,896]{2,1,0:T(8,128)(2,1)}, bf16[4,32,896]{2,1,0:T(8,128)(2,1)}) custom-call(s32[8,512]{1,0:T(8,128)} %bitcast.14, f32[8,512]{1,0:T(8,128)} %bitcast.15, bf16[512,896]{1,0:T(8,128)(2,1)} %refs_2_.1), custom_call_target="tpu_custom_call" | custom-call | flops 469762048 | bytes 3670016 | tf_op jit(solution)/shard_map/pallas_call | solution.py:264
  5.1 5.0 %collective-permute-start.1 = (bf16[2,32,896]{2,1,0:T(8,128)(2,1)S(1)}, bf16[2,32,896]{2,1,0:T(8,128)(2,1)S(1)}, u32[]{:S(2)}, u32[]{:S(2)}) collective-permute-start(bf16[2,32,896]{2,1,0:T(8,128)(2,1)S(1)} %get-tuple-element.60), channel_id=1, source_target_pairs={{0,6},{1,7},{2,4},{3,5},{4,2},{5,3},{6,0},{7,1},{8,14},{9,15},{10,... | collective-permute-start | bytes 344072 | tf_op jit(solution)/shard_map/ppermute | solution.py:234
  14.5 5.6 %collective-permute-done.2.refs_3_ = bf16[2,32,896]{2,1,0:T(8,128)(2,1)S(1)} collective-permute-done((bf16[2,32,896]{2,1,0:T(8,128)(2,1)S(1)}, bf16[2,32,896]{2,1,0:T(8,128)(2,1)S(1)}, u32[]{:S(2)}, u32[]{:S(2)}) %collective-permute-start.2) | collective-permute-done | bytes 114720 | tf_op jit(solution)/shard_map/ppermute | solution.py:234
  21.4 1.6 %collective-permute-start.4 = (bf16[2,64,1024]{2,1,0:T(8,128)(2,1)S(1)}, bf16[2,64,1024]{2,1,0:T(8,128)(2,1)S(1)}, u32[]{:S(2)}, u32[]{:S(2)}) collective-permute-start(bf16[2,64,1024]{2,1,0:T(8,128)(2,1)S(1)} %get-tuple-element.65), channel_id=1, source_target_pairs={{0,8},{8,0},{16,24},{24,16},{1,9},{9,1},{17,25},{25,17},{2,10},{10... | collective-permute-start | bytes 786440 | tf_op jit(solution)/shard_map/ppermute | solution.py:234
  23.0 1.5 %collective-permute-start.5 = (bf16[2,64,1024]{2,1,0:T(8,128)(2,1)S(1)}, bf16[2,64,1024]{2,1,0:T(8,128)(2,1)S(1)}, u32[]{:S(2)}, u32[]{:S(2)}) collective-permute-start(bf16[2,64,1024]{2,1,0:T(8,128)(2,1)S(1)} %get-tuple-element.66), channel_id=1, source_target_pairs={{0,16},{8,24},{16,0},{24,8},{1,17},{9,25},{17,1},{25,9},{2,18},{10... | collective-permute-start | bytes 786440 | tf_op jit(solution)/shard_map/ppermute | solution.py:234
  25.0 2.5 %collective-permute-start.12 = (bf16[2,32,896]{2,1,0:T(8,128)(2,1)S(1)}, bf16[2,32,896]{2,1,0:T(8,128)(2,1)S(1)}, u32[]{:S(2)}, u32[]{:S(2)}) collective-permute-start(bf16[2,32,896]{2,1,0:T(8,128)(2,1)S(1)} %get-tuple-element.72), channel_id=1, source_target_pairs={{0,6},{1,7},{2,4},{3,5},{4,2},{5,3},{6,0},{7,1},{8,14},{9,15},{10,... | collective-permute-start | bytes 344072 | tf_op jit(solution)/shard_map/ppermute | solution.py:234
  27.5 3.2 %collective-permute-done.4.refs_1_ = bf16[2,64,1024]{2,1,0:T(8,128)(2,1)S(1)} collective-permute-done((bf16[2,64,1024]{2,1,0:T(8,128)(2,1)S(1)}, bf16[2,64,1024]{2,1,0:T(8,128)(2,1)S(1)}, u32[]{:S(2)}, u32[]{:S(2)}) %collective-permute-start.4) | collective-permute-done | bytes 262176 | tf_op jit(solution)/shard_map/ppermute | solution.py:234
  30.9 4.9 %collective-permute-done.5.refs_2_ = bf16[2,64,1024]{2,1,0:T(8,128)(2,1)S(1)} collective-permute-done((bf16[2,64,1024]{2,1,0:T(8,128)(2,1)S(1)}, bf16[2,64,1024]{2,1,0:T(8,128)(2,1)S(1)}, u32[]{:S(2)}, u32[]{:S(2)}) %collective-permute-start.5) | collective-permute-done | bytes 262176 | tf_op jit(solution)/shard_map/ppermute | solution.py:234
  36.0 1.3 %collective-permute-start.7 = (bf16[64,1024]{1,0:T(8,128)(2,1)S(1)}, bf16[64,1024]{1,0:T(8,128)(2,1)S(1)}, u32[]{:S(2)}, u32[]{:S(2)}) collective-permute-start(bf16[64,1024]{1,0:T(8,128)(2,1)S(1)} %shard_map.116.refs_0_), channel_id=1, source_target_pairs={{0,8},{8,0},{16,24},{24,16},{1,9},{9,1},{17,25},{25,17},{2,10},{10... | collective-permute-start | bytes 393224 | tf_op jit(solution)/shard_map/ppermute | solution.py:234
  38.1 1.4 %collective-permute-start.9 = (bf16[64,1024]{1,0:T(8,128)(2,1)S(1)}, bf16[64,1024]{1,0:T(8,128)(2,1)S(1)}, u32[]{:S(2)}, u32[]{:S(2)}) collective-permute-start(bf16[64,1024]{1,0:T(8,128)(2,1)S(1)} %shard_map.116.refs_0_), channel_id=1, source_target_pairs={{0,24},{8,16},{16,8},{24,0},{1,25},{9,17},{17,9},{25,1},{2,26},{10... | collective-permute-start | bytes 393224 | tf_op jit(solution)/shard_map/ppermute | solution.py:234
  42.5 1.4 %collective-permute-start.17 = (bf16[64,1024]{1,0:T(8,128)(2,1)S(1)}, bf16[64,1024]{1,0:T(8,128)(2,1)S(1)}, u32[]{:S(2)}, u32[]{:S(2)}) collective-permute-start(bf16[64,1024]{1,0:T(8,128)(2,1)S(1)} %get-tuple-element.81), channel_id=1, source_target_pairs={{0,24},{8,16},{16,8},{24,0},{1,25},{9,17},{17,9},{25,1},{2,26},{10... | collective-permute-start | bytes 393224 | tf_op jit(solution)/shard_map/ppermute | solution.py:234
  43.9 2.5 %collective-permute-done.9.refs_3_ = bf16[64,1024]{1,0:T(8,128)(2,1)S(1)} collective-permute-done((bf16[64,1024]{1,0:T(8,128)(2,1)S(1)}, bf16[64,1024]{1,0:T(8,128)(2,1)S(1)}, u32[]{:S(2)}, u32[]{:S(2)}) %collective-permute-start.9) | collective-permute-done | bytes 131104 | tf_op jit(solution)/shard_map/ppermute | solution.py:234
  47.6 1.7 %collective-permute-done.16.refs_6_ = bf16[64,1024]{1,0:T(8,128)(2,1)S(1)} collective-permute-done((bf16[64,1024]{1,0:T(8,128)(2,1)S(1)}, bf16[64,1024]{1,0:T(8,128)(2,1)S(1)}, u32[]{:S(2)}, u32[]{:S(2)}) %collective-permute-start.16) | collective-permute-done | bytes 131104 | tf_op jit(solution)/shard_map/ppermute | solution.py:234
  51.6 1.6 %collective-permute-start.20 = (bf16[2,64,1024]{2,1,0:T(8,128)(2,1)S(1)}, bf16[2,64,1024]{2,1,0:T(8,128)(2,1)S(1)}, u32[]{:S(2)}, u32[]{:S(2)}) collective-permute-start(bf16[2,64,1024]{2,1,0:T(8,128)(2,1)S(1)} %shard_map.120.refs_0_), channel_id=1, source_target_pairs={{0,24},{8,16},{16,8},{24,0},{1,25},{9,17},{17,9},{25,1},{2,26},{10... | collective-permute-start | bytes 786440 | tf_op jit(solution)/shard_map/ppermute | solution.py:234
  53.3 2.5 %collective-permute-start.22 = (bf16[2,32,896]{2,1,0:T(8,128)(2,1)S(1)}, bf16[2,32,896]{2,1,0:T(8,128)(2,1)S(1)}, u32[]{:S(2)}, u32[]{:S(2)}) collective-permute-start(bf16[2,32,896]{2,1,0:T(8,128)(2,1)S(1)} %get-tuple-element.83), channel_id=1, source_target_pairs={{0,6},{1,7},{2,4},{3,5},{4,2},{5,3},{6,0},{7,1},{8,14},{9,15},{10,... | collective-permute-start | bytes 344072 | tf_op jit(solution)/shard_map/ppermute | solution.py:234
  55.8 3.1 %collective-permute-done.18.refs_1_ = bf16[2,64,1024]{2,1,0:T(8,128)(2,1)S(1)} collective-permute-done((bf16[2,64,1024]{2,1,0:T(8,128)(2,1)S(1)}, bf16[2,64,1024]{2,1,0:T(8,128)(2,1)S(1)}, u32[]{:S(2)}, u32[]{:S(2)}) %collective-permute-start.18) | collective-permute-done | bytes 262176 | tf_op jit(solution)/shard_map/ppermute | solution.py:234
  59.5 2.8 %collective-permute-done.20.refs_3_ = bf16[2,64,1024]{2,1,0:T(8,128)(2,1)S(1)} collective-permute-done((bf16[2,64,1024]{2,1,0:T(8,128)(2,1)S(1)}, bf16[2,64,1024]{2,1,0:T(8,128)(2,1)S(1)}, u32[]{:S(2)}, u32[]{:S(2)}) %collective-permute-start.20) | collective-permute-done | bytes 262176 | tf_op jit(solution)/shard_map/ppermute | solution.py:234
  62.4 1.3 %shard_map.122 = (bf16[256,1024]{1,0:T(8,128)(2,1)S(1)}, bf16[256,1024]{1,0:T(8,128)(2,1)S(1)}, bf16[4,32,896]{2,1,0:T(8,128)(2,1)S(1)}, bf16[4,32,896]{2,1,0:T(8,128)(2,1)S(1)}) custom-call(bf16[2,64,1024]{2,1,0:T(8,128)(2,1)S(1)} %shard_map.120.refs_0_, bf16[2,64,1024]{2,1,0:T(8,128)(2,1)S(1)} %collective-permute-done.18.refs_1_, ...), custom_call_target="tpu_custom_call" | custom-call | flops 939524096 | bytes 3670016 | tf_op jit(solution)/shard_map/pallas_call | solution.py:330
  63.8 2.2 %collective-permute-start.23 = (bf16[2,32,896]{2,1,0:T(8,128)(2,1)S(1)}, bf16[2,32,896]{2,1,0:T(8,128)(2,1)S(1)}, u32[]{:S(2)}, u32[]{:S(2)}) collective-permute-start(bf16[2,32,896]{2,1,0:T(8,128)(2,1)S(1)} %get-tuple-element.86), channel_id=1, source_target_pairs={{0,2},{1,3},{2,0},{3,1},{4,6},{5,7},{6,4},{7,5},{8,10},{9,11},{10,... | collective-permute-start | bytes 344072 | tf_op jit(solution)/shard_map/ppermute | solution.py:234
  66.2 1.5 %collective-permute-start.25 = (bf16[2,32,896]{2,1,0:T(8,128)(2,1)S(1)}, bf16[2,32,896]{2,1,0:T(8,128)(2,1)S(1)}, u32[]{:S(2)}, u32[]{:S(2)}) collective-permute-start(bf16[2,32,896]{2,1,0:T(8,128)(2,1)S(1)} %get-tuple-element.94), channel_id=1, source_target_pairs={{0,6},{1,7},{2,4},{3,5},{4,2},{5,3},{6,0},{7,1},{8,14},{9,15},{10,... | collective-permute-start | bytes 344072 | tf_op jit(solution)/shard_map/ppermute | solution.py:234
  69.0 1.7 %collective-permute-start.27 = (bf16[2,32,896]{2,1,0:T(8,128)(2,1)S(1)}, bf16[2,32,896]{2,1,0:T(8,128)(2,1)S(1)}, u32[]{:S(2)}, u32[]{:S(2)}) collective-permute-start(bf16[2,32,896]{2,1,0:T(8,128)(2,1)S(1)} %get-tuple-element.93.refs_5_.refs_2_), channel_id=1, source_target_pairs={{0,2},{1,3},{2,0},{3,1},{4,6},{5,7},{6,4},{7,5},{8,10},{9,11},{10,... | collective-permute-start | bytes 344072 | tf_op jit(solution)/shard_map/ppermute | solution.py:234
  70.7 2.0 %shard_map.127 = bf16[1024,896]{1,0:T(8,128)(2,1)} custom-call(bf16[256,1024]{1,0:T(8,128)(2,1)S(1)} %get-tuple-element.101.left_ref, bf16[256,896]{1,0:T(8,128)(2,1)S(1)} %get-tuple-element.102.refs_0_), custom_call_target="tpu_custom_call" | custom-call | flops 469762048 | bytes 1835008 | tf_op jit(solution)/shard_map/pallas_call | solution.py:342
  73.9 2.5 %shard_map.126 = (bf16[896,1024]{1,0:T(8,128)(2,1)}, bf16[896,1024]{1,0:T(8,128)(2,1)}) custom-call(bf16[256,896]{1,0:T(8,128)(2,1)S(1)} %get-tuple-element.96.left_ref, bf16[256,1024]{1,0:T(8,128)(2,1)S(1)} %get-tuple-element.97.refs_0_, bf16[256,1024]{1,0:T(8,128)(2,1)S(1)} %get-tuple-element.98.refs_1_, ...), custom_call_target="tpu_custom_call" | custom-call | flops 939524096 | bytes 3670016 | tf_op jit(solution)/shard_map/pallas_call | solution.py:348
  76.5 3.1 %collective-permute-done.26.refs_3_ = bf16[2,32,896]{2,1,0:T(8,128)(2,1)S(1)} collective-permute-done((bf16[2,32,896]{2,1,0:T(8,128)(2,1)S(1)}, bf16[2,32,896]{2,1,0:T(8,128)(2,1)S(1)}, u32[]{:S(2)}, u32[]{:S(2)}) %collective-permute-start.26) | collective-permute-done | bytes 114720 | tf_op jit(solution)/shard_map/ppermute | solution.py:234
  (68 shorter events, 20.3 us)
Async XLA Ops:
  5.1 9.4 %collective-permute-start.1 = (bf16[2,32,896]{2,1,0:T(8,128)(2,1)S(1)}, bf16[2,32,896]{2,1,0:T(8,128)(2,1)S(1)}, u32[]{:S(2)}, u32[]{:S(2)}) collective-permute-start(bf16[2,32,896]{2,1,0:T(8,128)(2,1)S(1)} %get-tuple-element.60), channel_id=1, source_target_pairs={{0,6},{1,7},{2,4},{3,5},{4,2},{5,3},{6,0},{7,1},{8,14},{9,15},{10,... | collective-permute-start | bytes 344072 | tf_op jit(solution)/shard_map/ppermute | solution.py:234
  10.1 10.0 %collective-permute-start.2 = (bf16[2,32,896]{2,1,0:T(8,128)(2,1)S(1)}, bf16[2,32,896]{2,1,0:T(8,128)(2,1)S(1)}, u32[]{:S(2)}, u32[]{:S(2)}) collective-permute-start(bf16[2,32,896]{2,1,0:T(8,128)(2,1)S(1)} %get-tuple-element.61), channel_id=1, source_target_pairs={{0,4},{1,5},{2,6},{3,7},{4,0},{5,1},{6,2},{7,3},{8,12},{9,13},{10,... | collective-permute-start | bytes 344072 | tf_op jit(solution)/shard_map/ppermute | solution.py:234
  10.1 10.0 %collective-permute-start.3 = (bf16[2,32,896]{2,1,0:T(8,128)(2,1)S(1)}, bf16[2,32,896]{2,1,0:T(8,128)(2,1)S(1)}, u32[]{:S(2)}, u32[]{:S(2)}) collective-permute-start(bf16[2,32,896]{2,1,0:T(8,128)(2,1)S(1)} %get-tuple-element.62), channel_id=1, source_target_pairs={{0,2},{1,3},{2,0},{3,1},{4,6},{5,7},{6,4},{7,5},{8,10},{9,11},{10,... | collective-permute-start | bytes 344072 | tf_op jit(solution)/shard_map/ppermute | solution.py:234
  14.4 10.6 %collective-permute-start.11 = (bf16[4,32,896]{2,1,0:T(8,128)(2,1)S(1)}, bf16[4,32,896]{2,1,0:T(8,128)(2,1)S(1)}, u32[]{:S(2)}, u32[]{:S(2)}) collective-permute-start(bf16[4,32,896]{2,1,0:T(8,128)(2,1)S(1)} %get-tuple-element.71), channel_id=1, source_target_pairs={{0,1},{1,0},{2,3},{3,2},{4,5},{5,4},{6,7},{7,6},{8,9},{9,8},{10,11... | collective-permute-start | bytes 688136 | tf_op jit(solution)/shard_map/ppermute | solution.py:234
  21.4 9.3 %collective-permute-start.4 = (bf16[2,64,1024]{2,1,0:T(8,128)(2,1)S(1)}, bf16[2,64,1024]{2,1,0:T(8,128)(2,1)S(1)}, u32[]{:S(2)}, u32[]{:S(2)}) collective-permute-start(bf16[2,64,1024]{2,1,0:T(8,128)(2,1)S(1)} %get-tuple-element.65), channel_id=1, source_target_pairs={{0,8},{8,0},{16,24},{24,16},{1,9},{9,1},{17,25},{25,17},{2,10},{10... | collective-permute-start | bytes 786440 | tf_op jit(solution)/shard_map/ppermute | solution.py:234
  23.0 12.9 %collective-permute-start.5 = (bf16[2,64,1024]{2,1,0:T(8,128)(2,1)S(1)}, bf16[2,64,1024]{2,1,0:T(8,128)(2,1)S(1)}, u32[]{:S(2)}, u32[]{:S(2)}) collective-permute-start(bf16[2,64,1024]{2,1,0:T(8,128)(2,1)S(1)} %get-tuple-element.66), channel_id=1, source_target_pairs={{0,16},{8,24},{16,0},{24,8},{1,17},{9,25},{17,1},{25,9},{2,18},{10... | collective-permute-start | bytes 786440 | tf_op jit(solution)/shard_map/ppermute | solution.py:234
  24.5 11.3 %collective-permute-start.6 = (bf16[2,64,1024]{2,1,0:T(8,128)(2,1)S(1)}, bf16[2,64,1024]{2,1,0:T(8,128)(2,1)S(1)}, u32[]{:S(2)}, u32[]{:S(2)}) collective-permute-start(bf16[2,64,1024]{2,1,0:T(8,128)(2,1)S(1)} %get-tuple-element.67), channel_id=1, source_target_pairs={{0,24},{8,16},{16,8},{24,0},{1,25},{9,17},{17,9},{25,1},{2,26},{10... | collective-permute-start | bytes 786440 | tf_op jit(solution)/shard_map/ppermute | solution.py:234
  25.0 13.1 %collective-permute-start.12 = (bf16[2,32,896]{2,1,0:T(8,128)(2,1)S(1)}, bf16[2,32,896]{2,1,0:T(8,128)(2,1)S(1)}, u32[]{:S(2)}, u32[]{:S(2)}) collective-permute-start(bf16[2,32,896]{2,1,0:T(8,128)(2,1)S(1)} %get-tuple-element.72), channel_id=1, source_target_pairs={{0,6},{1,7},{2,4},{3,5},{4,2},{5,3},{6,0},{7,1},{8,14},{9,15},{10,... | collective-permute-start | bytes 344072 | tf_op jit(solution)/shard_map/ppermute | solution.py:234
  27.5 12.0 %collective-permute-start.13 = (bf16[2,32,896]{2,1,0:T(8,128)(2,1)S(1)}, bf16[2,32,896]{2,1,0:T(8,128)(2,1)S(1)}, u32[]{:S(2)}, u32[]{:S(2)}) collective-permute-start(bf16[2,32,896]{2,1,0:T(8,128)(2,1)S(1)} %get-tuple-element.73), channel_id=1, source_target_pairs={{0,4},{1,5},{2,6},{3,7},{4,0},{5,1},{6,2},{7,3},{8,12},{9,13},{10,... | collective-permute-start | bytes 344072 | tf_op jit(solution)/shard_map/ppermute | solution.py:234
  30.7 8.9 %collective-permute-start.14 = (bf16[2,32,896]{2,1,0:T(8,128)(2,1)S(1)}, bf16[2,32,896]{2,1,0:T(8,128)(2,1)S(1)}, u32[]{:S(2)}, u32[]{:S(2)}) collective-permute-start(bf16[2,32,896]{2,1,0:T(8,128)(2,1)S(1)} %get-tuple-element.74), channel_id=1, source_target_pairs={{0,2},{1,3},{2,0},{3,1},{4,6},{5,7},{6,4},{7,5},{8,10},{9,11},{10,... | collective-permute-start | bytes 344072 | tf_op jit(solution)/shard_map/ppermute | solution.py:234
  37.3 6.6 %collective-permute-start.8 = (bf16[64,1024]{1,0:T(8,128)(2,1)S(1)}, bf16[64,1024]{1,0:T(8,128)(2,1)S(1)}, u32[]{:S(2)}, u32[]{:S(2)}) collective-permute-start(bf16[64,1024]{1,0:T(8,128)(2,1)S(1)} %shard_map.116.refs_0_), channel_id=1, source_target_pairs={{0,16},{8,24},{16,0},{24,8},{1,17},{9,25},{17,1},{25,9},{2,18},{10... | collective-permute-start | bytes 393224 | tf_op jit(solution)/shard_map/ppermute | solution.py:234
  38.1 8.2 %collective-permute-start.9 = (bf16[64,1024]{1,0:T(8,128)(2,1)S(1)}, bf16[64,1024]{1,0:T(8,128)(2,1)S(1)}, u32[]{:S(2)}, u32[]{:S(2)}) collective-permute-start(bf16[64,1024]{1,0:T(8,128)(2,1)S(1)} %shard_map.116.refs_0_), channel_id=1, source_target_pairs={{0,24},{8,16},{16,8},{24,0},{1,25},{9,17},{17,9},{25,1},{2,26},{10... | collective-permute-start | bytes 393224 | tf_op jit(solution)/shard_map/ppermute | solution.py:234
  40.3 7.3 %collective-permute-start.15 = (bf16[64,1024]{1,0:T(8,128)(2,1)S(1)}, bf16[64,1024]{1,0:T(8,128)(2,1)S(1)}, u32[]{:S(2)}, u32[]{:S(2)}) collective-permute-start(bf16[64,1024]{1,0:T(8,128)(2,1)S(1)} %get-tuple-element.79), channel_id=1, source_target_pairs={{0,8},{8,0},{16,24},{24,16},{1,9},{9,1},{17,25},{25,17},{2,10},{10... | collective-permute-start | bytes 393224 | tf_op jit(solution)/shard_map/ppermute | solution.py:234
  41.6 7.7 %collective-permute-start.16 = (bf16[64,1024]{1,0:T(8,128)(2,1)S(1)}, bf16[64,1024]{1,0:T(8,128)(2,1)S(1)}, u32[]{:S(2)}, u32[]{:S(2)}) collective-permute-start(bf16[64,1024]{1,0:T(8,128)(2,1)S(1)} %get-tuple-element.80), channel_id=1, source_target_pairs={{0,16},{8,24},{16,0},{24,8},{1,17},{9,25},{17,1},{25,9},{2,18},{10... | collective-permute-start | bytes 393224 | tf_op jit(solution)/shard_map/ppermute | solution.py:234
  42.5 6.8 %collective-permute-start.17 = (bf16[64,1024]{1,0:T(8,128)(2,1)S(1)}, bf16[64,1024]{1,0:T(8,128)(2,1)S(1)}, u32[]{:S(2)}, u32[]{:S(2)}) collective-permute-start(bf16[64,1024]{1,0:T(8,128)(2,1)S(1)} %get-tuple-element.81), channel_id=1, source_target_pairs={{0,24},{8,16},{16,8},{24,0},{1,25},{9,17},{17,9},{25,1},{2,26},{10... | collective-permute-start | bytes 393224 | tf_op jit(solution)/shard_map/ppermute | solution.py:234
  49.6 9.3 %collective-permute-start.18 = (bf16[2,64,1024]{2,1,0:T(8,128)(2,1)S(1)}, bf16[2,64,1024]{2,1,0:T(8,128)(2,1)S(1)}, u32[]{:S(2)}, u32[]{:S(2)}) collective-permute-start(bf16[2,64,1024]{2,1,0:T(8,128)(2,1)S(1)} %shard_map.120.refs_0_), channel_id=1, source_target_pairs={{0,8},{8,0},{16,24},{24,16},{1,9},{9,1},{17,25},{25,17},{2,10},{10... | collective-permute-start | bytes 786440 | tf_op jit(solution)/shard_map/ppermute | solution.py:234
  50.5 9.0 %collective-permute-start.19 = (bf16[2,64,1024]{2,1,0:T(8,128)(2,1)S(1)}, bf16[2,64,1024]{2,1,0:T(8,128)(2,1)S(1)}, u32[]{:S(2)}, u32[]{:S(2)}) collective-permute-start(bf16[2,64,1024]{2,1,0:T(8,128)(2,1)S(1)} %shard_map.120.refs_0_), channel_id=1, source_target_pairs={{0,16},{8,24},{16,0},{24,8},{1,17},{9,25},{17,1},{25,9},{2,18},{10... | collective-permute-start | bytes 786440 | tf_op jit(solution)/shard_map/ppermute | solution.py:234
  51.6 10.7 %collective-permute-start.20 = (bf16[2,64,1024]{2,1,0:T(8,128)(2,1)S(1)}, bf16[2,64,1024]{2,1,0:T(8,128)(2,1)S(1)}, u32[]{:S(2)}, u32[]{:S(2)}) collective-permute-start(bf16[2,64,1024]{2,1,0:T(8,128)(2,1)S(1)} %shard_map.120.refs_0_), channel_id=1, source_target_pairs={{0,24},{8,16},{16,8},{24,0},{1,25},{9,17},{17,9},{25,1},{2,26},{10... | collective-permute-start | bytes 786440 | tf_op jit(solution)/shard_map/ppermute | solution.py:234
  53.2 9.2 %collective-permute-start.21 = (bf16[2,32,896]{2,1,0:T(8,128)(2,1)S(1)}, bf16[2,32,896]{2,1,0:T(8,128)(2,1)S(1)}, u32[]{:S(2)}, u32[]{:S(2)}) collective-permute-start(bf16[2,32,896]{2,1,0:T(8,128)(2,1)S(1)} %get-tuple-element.82), channel_id=1, source_target_pairs={{0,4},{1,5},{2,6},{3,7},{4,0},{5,1},{6,2},{7,3},{8,12},{9,13},{10,... | collective-permute-start | bytes 344072 | tf_op jit(solution)/shard_map/ppermute | solution.py:234
  53.3 9.1 %collective-permute-start.22 = (bf16[2,32,896]{2,1,0:T(8,128)(2,1)S(1)}, bf16[2,32,896]{2,1,0:T(8,128)(2,1)S(1)}, u32[]{:S(2)}, u32[]{:S(2)}) collective-permute-start(bf16[2,32,896]{2,1,0:T(8,128)(2,1)S(1)} %get-tuple-element.83), channel_id=1, source_target_pairs={{0,6},{1,7},{2,4},{3,5},{4,2},{5,3},{6,0},{7,1},{8,14},{9,15},{10,... | collective-permute-start | bytes 344072 | tf_op jit(solution)/shard_map/ppermute | solution.py:234
  63.8 8.8 %collective-permute-start.23 = (bf16[2,32,896]{2,1,0:T(8,128)(2,1)S(1)}, bf16[2,32,896]{2,1,0:T(8,128)(2,1)S(1)}, u32[]{:S(2)}, u32[]{:S(2)}) collective-permute-start(bf16[2,32,896]{2,1,0:T(8,128)(2,1)S(1)} %get-tuple-element.86), channel_id=1, source_target_pairs={{0,2},{1,3},{2,0},{3,1},{4,6},{5,7},{6,4},{7,5},{8,10},{9,11},{10,... | collective-permute-start | bytes 344072 | tf_op jit(solution)/shard_map/ppermute | solution.py:234
  66.2 10.3 %collective-permute-start.25 = (bf16[2,32,896]{2,1,0:T(8,128)(2,1)S(1)}, bf16[2,32,896]{2,1,0:T(8,128)(2,1)S(1)}, u32[]{:S(2)}, u32[]{:S(2)}) collective-permute-start(bf16[2,32,896]{2,1,0:T(8,128)(2,1)S(1)} %get-tuple-element.94), channel_id=1, source_target_pairs={{0,6},{1,7},{2,4},{3,5},{4,2},{5,3},{6,0},{7,1},{8,14},{9,15},{10,... | collective-permute-start | bytes 344072 | tf_op jit(solution)/shard_map/ppermute | solution.py:234
  67.7 11.8 %collective-permute-start.26 = (bf16[2,32,896]{2,1,0:T(8,128)(2,1)S(1)}, bf16[2,32,896]{2,1,0:T(8,128)(2,1)S(1)}, u32[]{:S(2)}, u32[]{:S(2)}) collective-permute-start(bf16[2,32,896]{2,1,0:T(8,128)(2,1)S(1)} %get-tuple-element.95), channel_id=1, source_target_pairs={{0,4},{1,5},{2,6},{3,7},{4,0},{5,1},{6,2},{7,3},{8,12},{9,13},{10,... | collective-permute-start | bytes 344072 | tf_op jit(solution)/shard_map/ppermute | solution.py:234
  69.0 10.5 %collective-permute-start.27 = (bf16[2,32,896]{2,1,0:T(8,128)(2,1)S(1)}, bf16[2,32,896]{2,1,0:T(8,128)(2,1)S(1)}, u32[]{:S(2)}, u32[]{:S(2)}) collective-permute-start(bf16[2,32,896]{2,1,0:T(8,128)(2,1)S(1)} %get-tuple-element.93.refs_5_.refs_2_), channel_id=1, source_target_pairs={{0,2},{1,3},{2,0},{3,1},{4,6},{5,7},{6,4},{7,5},{8,10},{9,11},{10,... | collective-permute-start | bytes 344072 | tf_op jit(solution)/shard_map/ppermute | solution.py:234
  (13 other events, 87.4 us)

commit v16 on v15

--- a/solution.py
+++ b/solution.py
@@ -82,9 +82,13 @@
     split_cores(keep_ref, swap_ref, rows)
 
 
-def gather_scaled_kernel(pick_ref, weight_ref, grad_ref, mat_ref, keep_ref, swap_ref, held_ref):
+def gather_scaled_kernel(
+    pick_ref, weight_ref, grad_ref, mat_ref, keep_ref, swap_ref, held_ref, turned_ref
+):
     held_ref[...] = mat_ref[...]
-    rows = mm(pick_ref[...], grad_ref[...], ((1,), (0,)))
+    pick = pick_ref[...]
+    turned_ref[...] = pick.T
+    rows = mm(pick, grad_ref[...], ((1,), (0,)))
     split_cores(keep_ref, swap_ref, (weight_ref[...] * rows).astype(BF16))
 
 
@@ -194,10 +198,6 @@
     for ref in refs[::-1]:
         found += [ref[0], ref[1]]
     return jnp.concatenate(found, axis=0)
-
-
-def turn_kernel(pick_ref, out_ref):
-    out_ref[...] = pick_ref[...].T
 
 
 def scatter_out(pick_ref, rows, out_ref, scratch, sems):
@@ -278,8 +278,11 @@
     swap, keep = lax.optimization_barrier((swap, keep))
     sent = call(pack_back_kernel, [pair] * (half - 1), 0, 8 * slots)(keep, swap)
     row_blocks = [partner(value, "expert", 2 * (1 + k)) for k, value in enumerate(sent)][::-1]
-    grad_keep, grad_swap, up_mat = call(
-        gather_scaled_kernel, (one, one, shape(up_mat.shape, BF16)), 0, 0
+    grad_keep, grad_swap, up_mat, turned = call(
+        gather_scaled_kernel,
+        (one, one, shape(up_mat.shape, BF16), shape((tok_rows, slots), BF16)),
+        0,
+        0,
     )(pick, weight, grad_out, up_mat)
     grad_swap = partner(grad_swap, "expert", 1)
     sent = call(pack_back_kernel, [pair] * (half - 1), 0, 8 * slots)(grad_keep, grad_swap)
@@ -354,7 +357,6 @@
     )(rows, gate_pre, up_pre, grad_to[0])
 
     full = shape((tok_rows, features), BF16)
-    turned = call(turn_kernel, shape((tok_rows, slots), BF16))(pick)
     flight = dict(
         out_specs=ANY,
         scratch_shapes=[pltpu.VMEM(full.shape, BF16), pltpu.SemaphoreType.DMA((4,))],

time: 81 us -> 81 us (level)
    unnamed x18 -> x16, local copies, waits for them, and re-layouts: 4 us -> 3.99 us
where the time goes in v16:
time: 81 us; the launch traced here: 80.8 us
  starting transfers between devices  32.6 us (40%)
  waiting for transfers between devices  28.5 us (35%)
  Pallas kernels  14.8 us (18%)
  local copies, waits for them, and re-layouts  3.99 us (5%)
  between operations  0.82 us (1%)
    ppermute x28, starting transfers between devices, partner(): return lax.ppermute(value, axis, [(i, i ^ k) for i in range(size)])  32.6 us
    ppermute x28, waiting for transfers between devices, partner(): return lax.ppermute(value, axis, [(i, i ^ k) for i in range(size)])  28.5 us
    unnamed x16, local copies, waits for them, and re-layouts  3.99 us
    pallas_call x1, Pallas kernels, body(): call(functools.partial(route_kernel, experts), outs, 4 * slots * tok_rows...  2.59 us
    pallas_call x1, Pallas kernels, body(): call(functools.partial(grads_kernel, 2), [shape((features, hidden), BF16)...  2.54 us
    pallas_call x1, Pallas kernels, body(): call(functools.partial(grads_kernel, 1), [shape((hidden, features), BF16)...  1.97 us
  transfers between devices with their start and end apart: 28, of which 12 were waited for; matrix products, arithmetic and copies ran while one was open for 0% of the time, Pallas kernels for 12%

profile of v16, /device:TPU:0, one launch (start us, length us, event | category | flops | bytes accessed | tf_op | source)
XLA Modules:
  0.0 80.8 jit_solution(6246480940824294137)
XLA Ops:
  0.6 2.6 %shard_map.110 = (bf16[256,512]{1,0:T(8,128)(2,1)}, f32[256,1]{1,0:T(8,128)}, bf16[4,32,896]{2,1,0:T(8,128)(2,1)}, bf16[4,32,896]{2,1,0:T(8,128)(2,1)}) custom-call(s32[8,512]{1,0:T(8,128)} %bitcast.14, f32[8,512]{1,0:T(8,128)} %bitcast.15, bf16[512,896]{1,0:T(8,128)(2,1)} %refs_2_.1), custom_call_target="tpu_custom_call" | custom-call | flops 469762048 | bytes 3670016 | tf_op jit(solution)/shard_map/pallas_call | solution.py:264
  5.1 5.0 %collective-permute-start.1 = (bf16[2,32,896]{2,1,0:T(8,128)(2,1)S(1)}, bf16[2,32,896]{2,1,0:T(8,128)(2,1)S(1)}, u32[]{:S(2)}, u32[]{:S(2)}) collective-permute-start(bf16[2,32,896]{2,1,0:T(8,128)(2,1)S(1)} %get-tuple-element.62), channel_id=1, source_target_pairs={{0,6},{1,7},{2,4},{3,5},{4,2},{5,3},{6,0},{7,1},{8,14},{9,15},{10,... | collective-permute-start | bytes 344072 | tf_op jit(solution)/shard_map/ppermute | solution.py:234
  14.5 5.6 %collective-permute-done.2.refs_3_ = bf16[2,32,896]{2,1,0:T(8,128)(2,1)S(1)} collective-permute-done((bf16[2,32,896]{2,1,0:T(8,128)(2,1)S(1)}, bf16[2,32,896]{2,1,0:T(8,128)(2,1)S(1)}, u32[]{:S(2)}, u32[]{:S(2)}) %collective-permute-start.2) | collective-permute-done | bytes 114720 | tf_op jit(solution)/shard_map/ppermute | solution.py:234
  21.4 1.6 %collective-permute-start.4 = (bf16[2,64,1024]{2,1,0:T(8,128)(2,1)S(1)}, bf16[2,64,1024]{2,1,0:T(8,128)(2,1)S(1)}, u32[]{:S(2)}, u32[]{:S(2)}) collective-permute-start(bf16[2,64,1024]{2,1,0:T(8,128)(2,1)S(1)} %get-tuple-element.67), channel_id=1, source_target_pairs={{0,8},{8,0},{16,24},{24,16},{1,9},{9,1},{17,25},{25,17},{2,10},{10... | collective-permute-start | bytes 786440 | tf_op jit(solution)/shard_map/ppermute | solution.py:234
  23.0 1.5 %collective-permute-start.5 = (bf16[2,64,1024]{2,1,0:T(8,128)(2,1)S(1)}, bf16[2,64,1024]{2,1,0:T(8,128)(2,1)S(1)}, u32[]{:S(2)}, u32[]{:S(2)}) collective-permute-start(bf16[2,64,1024]{2,1,0:T(8,128)(2,1)S(1)} %get-tuple-element.68), channel_id=1, source_target_pairs={{0,16},{8,24},{16,0},{24,8},{1,17},{9,25},{17,1},{25,9},{2,18},{10... | collective-permute-start | bytes 786440 | tf_op jit(solution)/shard_map/ppermute | solution.py:234
  25.0 2.5 %collective-permute-start.12 = (bf16[2,32,896]{2,1,0:T(8,128)(2,1)S(1)}, bf16[2,32,896]{2,1,0:T(8,128)(2,1)S(1)}, u32[]{:S(2)}, u32[]{:S(2)}) collective-permute-start(bf16[2,32,896]{2,1,0:T(8,128)(2,1)S(1)} %get-tuple-element.74), channel_id=1, source_target_pairs={{0,6},{1,7},{2,4},{3,5},{4,2},{5,3},{6,0},{7,1},{8,14},{9,15},{10,... | collective-permute-start | bytes 344072 | tf_op jit(solution)/shard_map/ppermute | solution.py:234
  27.5 3.2 %collective-permute-done.4.refs_1_ = bf16[2,64,1024]{2,1,0:T(8,128)(2,1)S(1)} collective-permute-done((bf16[2,64,1024]{2,1,0:T(8,128)(2,1)S(1)}, bf16[2,64,1024]{2,1,0:T(8,128)(2,1)S(1)}, u32[]{:S(2)}, u32[]{:S(2)}) %collective-permute-start.4) | collective-permute-done | bytes 262176 | tf_op jit(solution)/shard_map/ppermute | solution.py:234
  30.9 4.9 %collective-permute-done.5.refs_2_ = bf16[2,64,1024]{2,1,0:T(8,128)(2,1)S(1)} collective-permute-done((bf16[2,64,1024]{2,1,0:T(8,128)(2,1)S(1)}, bf16[2,64,1024]{2,1,0:T(8,128)(2,1)S(1)}, u32[]{:S(2)}, u32[]{:S(2)}) %collective-permute-start.5) | collective-permute-done | bytes 262176 | tf_op jit(solution)/shard_map/ppermute | solution.py:234
  36.0 1.3 %collective-permute-start.7 = (bf16[64,1024]{1,0:T(8,128)(2,1)S(1)}, bf16[64,1024]{1,0:T(8,128)(2,1)S(1)}, u32[]{:S(2)}, u32[]{:S(2)}) collective-permute-start(bf16[64,1024]{1,0:T(8,128)(2,1)S(1)} %shard_map.115.refs_0_), channel_id=1, source_target_pairs={{0,8},{8,0},{16,24},{24,16},{1,9},{9,1},{17,25},{25,17},{2,10},{10... | collective-permute-start | bytes 393224 | tf_op jit(solution)/shard_map/ppermute | solution.py:234
  38.1 1.4 %collective-permute-start.9 = (bf16[64,1024]{1,0:T(8,128)(2,1)S(1)}, bf16[64,1024]{1,0:T(8,128)(2,1)S(1)}, u32[]{:S(2)}, u32[]{:S(2)}) collective-permute-start(bf16[64,1024]{1,0:T(8,128)(2,1)S(1)} %shard_map.115.refs_0_), channel_id=1, source_target_pairs={{0,24},{8,16},{16,8},{24,0},{1,25},{9,17},{17,9},{25,1},{2,26},{10... | collective-permute-start | bytes 393224 | tf_op jit(solution)/shard_map/ppermute | solution.py:234
  42.5 1.4 %collective-permute-start.17 = (bf16[64,1024]{1,0:T(8,128)(2,1)S(1)}, bf16[64,1024]{1,0:T(8,128)(2,1)S(1)}, u32[]{:S(2)}, u32[]{:S(2)}) collective-permute-start(bf16[64,1024]{1,0:T(8,128)(2,1)S(1)} %get-tuple-element.83), channel_id=1, source_target_pairs={{0,24},{8,16},{16,8},{24,0},{1,25},{9,17},{17,9},{25,1},{2,26},{10... | collective-permute-start | bytes 393224 | tf_op jit(solution)/shard_map/ppermute | solution.py:234
  43.9 2.5 %collective-permute-done.9.refs_3_ = bf16[64,1024]{1,0:T(8,128)(2,1)S(1)} collective-permute-done((bf16[64,1024]{1,0:T(8,128)(2,1)S(1)}, bf16[64,1024]{1,0:T(8,128)(2,1)S(1)}, u32[]{:S(2)}, u32[]{:S(2)}) %collective-permute-start.9) | collective-permute-done | bytes 131104 | tf_op jit(solution)/shard_map/ppermute | solution.py:234
  47.6 1.7 %collective-permute-done.16.refs_6_ = bf16[64,1024]{1,0:T(8,128)(2,1)S(1)} collective-permute-done((bf16[64,1024]{1,0:T(8,128)(2,1)S(1)}, bf16[64,1024]{1,0:T(8,128)(2,1)S(1)}, u32[]{:S(2)}, u32[]{:S(2)}) %collective-permute-start.16) | collective-permute-done | bytes 131104 | tf_op jit(solution)/shard_map/ppermute | solution.py:234
  51.6 1.6 %collective-permute-start.20 = (bf16[2,64,1024]{2,1,0:T(8,128)(2,1)S(1)}, bf16[2,64,1024]{2,1,0:T(8,128)(2,1)S(1)}, u32[]{:S(2)}, u32[]{:S(2)}) collective-permute-start(bf16[2,64,1024]{2,1,0:T(8,128)(2,1)S(1)} %shard_map.119.refs_0_), channel_id=1, source_target_pairs={{0,24},{8,16},{16,8},{24,0},{1,25},{9,17},{17,9},{25,1},{2,26},{10... | collective-permute-start | bytes 786440 | tf_op jit(solution)/shard_map/ppermute | solution.py:234
  53.3 2.5 %collective-permute-start.22 = (bf16[2,32,896]{2,1,0:T(8,128)(2,1)S(1)}, bf16[2,32,896]{2,1,0:T(8,128)(2,1)S(1)}, u32[]{:S(2)}, u32[]{:S(2)}) collective-permute-start(bf16[2,32,896]{2,1,0:T(8,128)(2,1)S(1)} %get-tuple-element.85), channel_id=1, source_target_pairs={{0,6},{1,7},{2,4},{3,5},{4,2},{5,3},{6,0},{7,1},{8,14},{9,15},{10,... | collective-permute-start | bytes 344072 | tf_op jit(solution)/shard_map/ppermute | solution.py:234
  55.8 3.1 %collective-permute-done.18.refs_1_ = bf16[2,64,1024]{2,1,0:T(8,128)(2,1)S(1)} collective-permute-done((bf16[2,64,1024]{2,1,0:T(8,128)(2,1)S(1)}, bf16[2,64,1024]{2,1,0:T(8,128)(2,1)S(1)}, u32[]{:S(2)}, u32[]{:S(2)}) %collective-permute-start.18) | collective-permute-done | bytes 262176 | tf_op jit(solution)/shard_map/ppermute | solution.py:234
  59.5 2.8 %collective-permute-done.20.refs_3_ = bf16[2,64,1024]{2,1,0:T(8,128)(2,1)S(1)} collective-permute-done((bf16[2,64,1024]{2,1,0:T(8,128)(2,1)S(1)}, bf16[2,64,1024]{2,1,0:T(8,128)(2,1)S(1)}, u32[]{:S(2)}, u32[]{:S(2)}) %collective-permute-start.20) | collective-permute-done | bytes 262176 | tf_op jit(solution)/shard_map/ppermute | solution.py:234
  62.4 1.3 %shard_map.121 = (bf16[256,1024]{1,0:T(8,128)(2,1)S(1)}, bf16[256,1024]{1,0:T(8,128)(2,1)S(1)}, bf16[4,32,896]{2,1,0:T(8,128)(2,1)S(1)}, bf16[4,32,896]{2,1,0:T(8,128)(2,1)S(1)}) custom-call(bf16[2,64,1024]{2,1,0:T(8,128)(2,1)S(1)} %shard_map.119.refs_0_, bf16[2,64,1024]{2,1,0:T(8,128)(2,1)S(1)} %collective-permute-done.18.refs_1_, ...), custom_call_target="tpu_custom_call" | custom-call | flops 939524096 | bytes 3670016 | tf_op jit(solution)/shard_map/pallas_call | solution.py:333
  63.8 2.2 %collective-permute-start.23 = (bf16[2,32,896]{2,1,0:T(8,128)(2,1)S(1)}, bf16[2,32,896]{2,1,0:T(8,128)(2,1)S(1)}, u32[]{:S(2)}, u32[]{:S(2)}) collective-permute-start(bf16[2,32,896]{2,1,0:T(8,128)(2,1)S(1)} %get-tuple-element.88), channel_id=1, source_target_pairs={{0,2},{1,3},{2,0},{3,1},{4,6},{5,7},{6,4},{7,5},{8,10},{9,11},{10,... | collective-permute-start | bytes 344072 | tf_op jit(solution)/shard_map/ppermute | solution.py:234
  66.1 1.7 %collective-permute-start.25 = (bf16[2,32,896]{2,1,0:T(8,128)(2,1)S(1)}, bf16[2,32,896]{2,1,0:T(8,128)(2,1)S(1)}, u32[]{:S(2)}, u32[]{:S(2)}) collective-permute-start(bf16[2,32,896]{2,1,0:T(8,128)(2,1)S(1)} %get-tuple-element.96), channel_id=1, source_target_pairs={{0,6},{1,7},{2,4},{3,5},{4,2},{5,3},{6,0},{7,1},{8,14},{9,15},{10,... | collective-permute-start | bytes 344072 | tf_op jit(solution)/shard_map/ppermute | solution.py:234
  69.0 1.5 %collective-permute-start.27 = (bf16[2,32,896]{2,1,0:T(8,128)(2,1)S(1)}, bf16[2,32,896]{2,1,0:T(8,128)(2,1)S(1)}, u32[]{:S(2)}, u32[]{:S(2)}) collective-permute-start(bf16[2,32,896]{2,1,0:T(8,128)(2,1)S(1)} %get-tuple-element.95.refs_5_.refs_2_), channel_id=1, source_target_pairs={{0,2},{1,3},{2,0},{3,1},{4,6},{5,7},{6,4},{7,5},{8,10},{9,11},{10,... | collective-permute-start | bytes 344072 | tf_op jit(solution)/shard_map/ppermute | solution.py:234
  70.5 2.0 %shard_map.126 = bf16[1024,896]{1,0:T(8,128)(2,1)} custom-call(bf16[256,1024]{1,0:T(8,128)(2,1)S(1)} %get-tuple-element.103.left_ref, bf16[256,896]{1,0:T(8,128)(2,1)S(1)} %get-tuple-element.104.refs_0_), custom_call_target="tpu_custom_call" | custom-call | flops 469762048 | bytes 1835008 | tf_op jit(solution)/shard_map/pallas_call | solution.py:345
  73.8 2.5 %shard_map.125 = (bf16[896,1024]{1,0:T(8,128)(2,1)}, bf16[896,1024]{1,0:T(8,128)(2,1)}) custom-call(bf16[256,896]{1,0:T(8,128)(2,1)S(1)} %get-tuple-element.98.left_ref, bf16[256,1024]{1,0:T(8,128)(2,1)S(1)} %get-tuple-element.99.refs_0_, bf16[256,1024]{1,0:T(8,128)(2,1)S(1)} %get-tuple-element.100.refs_1_, ...), custom_call_target="tpu_custom_call" | custom-call | flops 939524096 | bytes 3670016 | tf_op jit(solution)/shard_map/pallas_call | solution.py:351
  76.3 3.2 %collective-permute-done.26.refs_3_ = bf16[2,32,896]{2,1,0:T(8,128)(2,1)S(1)} collective-permute-done((bf16[2,32,896]{2,1,0:T(8,128)(2,1)S(1)}, bf16[2,32,896]{2,1,0:T(8,128)(2,1)S(1)}, u32[]{:S(2)}, u32[]{:S(2)}) %collective-permute-start.26) | collective-permute-done | bytes 114720 | tf_op jit(solution)/shard_map/ppermute | solution.py:234
  (65 shorter events, 20.2 us)
Async XLA Ops:
  5.1 9.4 %collective-permute-start.1 = (bf16[2,32,896]{2,1,0:T(8,128)(2,1)S(1)}, bf16[2,32,896]{2,1,0:T(8,128)(2,1)S(1)}, u32[]{:S(2)}, u32[]{:S(2)}) collective-permute-start(bf16[2,32,896]{2,1,0:T(8,128)(2,1)S(1)} %get-tuple-element.62), channel_id=1, source_target_pairs={{0,6},{1,7},{2,4},{3,5},{4,2},{5,3},{6,0},{7,1},{8,14},{9,15},{10,... | collective-permute-start | bytes 344072 | tf_op jit(solution)/shard_map/ppermute | solution.py:234
  10.1 10.0 %collective-permute-start.2 = (bf16[2,32,896]{2,1,0:T(8,128)(2,1)S(1)}, bf16[2,32,896]{2,1,0:T(8,128)(2,1)S(1)}, u32[]{:S(2)}, u32[]{:S(2)}) collective-permute-start(bf16[2,32,896]{2,1,0:T(8,128)(2,1)S(1)} %get-tuple-element.63), channel_id=1, source_target_pairs={{0,4},{1,5},{2,6},{3,7},{4,0},{5,1},{6,2},{7,3},{8,12},{9,13},{10,... | collective-permute-start | bytes 344072 | tf_op jit(solution)/shard_map/ppermute | solution.py:234
  10.1 10.0 %collective-permute-start.3 = (bf16[2,32,896]{2,1,0:T(8,128)(2,1)S(1)}, bf16[2,32,896]{2,1,0:T(8,128)(2,1)S(1)}, u32[]{:S(2)}, u32[]{:S(2)}) collective-permute-start(bf16[2,32,896]{2,1,0:T(8,128)(2,1)S(1)} %get-tuple-element.64), channel_id=1, source_target_pairs={{0,2},{1,3},{2,0},{3,1},{4,6},{5,7},{6,4},{7,5},{8,10},{9,11},{10,... | collective-permute-start | bytes 344072 | tf_op jit(solution)/shard_map/ppermute | solution.py:234
  14.4 10.6 %collective-permute-start.11 = (bf16[4,32,896]{2,1,0:T(8,128)(2,1)S(1)}, bf16[4,32,896]{2,1,0:T(8,128)(2,1)S(1)}, u32[]{:S(2)}, u32[]{:S(2)}) collective-permute-start(bf16[4,32,896]{2,1,0:T(8,128)(2,1)S(1)} %get-tuple-element.73), channel_id=1, source_target_pairs={{0,1},{1,0},{2,3},{3,2},{4,5},{5,4},{6,7},{7,6},{8,9},{9,8},{10,11... | collective-permute-start | bytes 688136 | tf_op jit(solution)/shard_map/ppermute | solution.py:234
  21.4 9.3 %collective-permute-start.4 = (bf16[2,64,1024]{2,1,0:T(8,128)(2,1)S(1)}, bf16[2,64,1024]{2,1,0:T(8,128)(2,1)S(1)}, u32[]{:S(2)}, u32[]{:S(2)}) collective-permute-start(bf16[2,64,1024]{2,1,0:T(8,128)(2,1)S(1)} %get-tuple-element.67), channel_id=1, source_target_pairs={{0,8},{8,0},{16,24},{24,16},{1,9},{9,1},{17,25},{25,17},{2,10},{10... | collective-permute-start | bytes 786440 | tf_op jit(solution)/shard_map/ppermute | solution.py:234
  23.0 12.9 %collective-permute-start.5 = (bf16[2,64,1024]{2,1,0:T(8,128)(2,1)S(1)}, bf16[2,64,1024]{2,1,0:T(8,128)(2,1)S(1)}, u32[]{:S(2)}, u32[]{:S(2)}) collective-permute-start(bf16[2,64,1024]{2,1,0:T(8,128)(2,1)S(1)} %get-tuple-element.68), channel_id=1, source_target_pairs={{0,16},{8,24},{16,0},{24,8},{1,17},{9,25},{17,1},{25,9},{2,18},{10... | collective-permute-start | bytes 786440 | tf_op jit(solution)/shard_map/ppermute | solution.py:234
  24.5 11.3 %collective-permute-start.6 = (bf16[2,64,1024]{2,1,0:T(8,128)(2,1)S(1)}, bf16[2,64,1024]{2,1,0:T(8,128)(2,1)S(1)}, u32[]{:S(2)}, u32[]{:S(2)}) collective-permute-start(bf16[2,64,1024]{2,1,0:T(8,128)(2,1)S(1)} %get-tuple-element.69), channel_id=1, source_target_pairs={{0,24},{8,16},{16,8},{24,0},{1,25},{9,17},{17,9},{25,1},{2,26},{10... | collective-permute-start | bytes 786440 | tf_op jit(solution)/shard_map/ppermute | solution.py:234
  25.0 13.1 %collective-permute-start.12 = (bf16[2,32,896]{2,1,0:T(8,128)(2,1)S(1)}, bf16[2,32,896]{2,1,0:T(8,128)(2,1)S(1)}, u32[]{:S(2)}, u32[]{:S(2)}) collective-permute-start(bf16[2,32,896]{2,1,0:T(8,128)(2,1)S(1)} %get-tuple-element.74), channel_id=1, source_target_pairs={{0,6},{1,7},{2,4},{3,5},{4,2},{5,3},{6,0},{7,1},{8,14},{9,15},{10,... | collective-permute-start | bytes 344072 | tf_op jit(solution)/shard_map/ppermute | solution.py:234
  27.5 12.0 %collective-permute-start.13 = (bf16[2,32,896]{2,1,0:T(8,128)(2,1)S(1)}, bf16[2,32,896]{2,1,0:T(8,128)(2,1)S(1)}, u32[]{:S(2)}, u32[]{:S(2)}) collective-permute-start(bf16[2,32,896]{2,1,0:T(8,128)(2,1)S(1)} %get-tuple-element.75), channel_id=1, source_target_pairs={{0,4},{1,5},{2,6},{3,7},{4,0},{5,1},{6,2},{7,3},{8,12},{9,13},{10,... | collective-permute-start | bytes 344072 | tf_op jit(solution)/shard_map/ppermute | solution.py:234
  30.7 8.9 %collective-permute-start.14 = (bf16[2,32,896]{2,1,0:T(8,128)(2,1)S(1)}, bf16[2,32,896]{2,1,0:T(8,128)(2,1)S(1)}, u32[]{:S(2)}, u32[]{:S(2)}) collective-permute-start(bf16[2,32,896]{2,1,0:T(8,128)(2,1)S(1)} %get-tuple-element.76), channel_id=1, source_target_pairs={{0,2},{1,3},{2,0},{3,1},{4,6},{5,7},{6,4},{7,5},{8,10},{9,11},{10,... | collective-permute-start | bytes 344072 | tf_op jit(solution)/shard_map/ppermute | solution.py:234
  37.3 6.6 %collective-permute-start.8 = (bf16[64,1024]{1,0:T(8,128)(2,1)S(1)}, bf16[64,1024]{1,0:T(8,128)(2,1)S(1)}, u32[]{:S(2)}, u32[]{:S(2)}) collective-permute-start(bf16[64,1024]{1,0:T(8,128)(2,1)S(1)} %shard_map.115.refs_0_), channel_id=1, source_target_pairs={{0,16},{8,24},{16,0},{24,8},{1,17},{9,25},{17,1},{25,9},{2,18},{10... | collective-permute-start | bytes 393224 | tf_op jit(solution)/shard_map/ppermute | solution.py:234
  38.1 8.2 %collective-permute-start.9 = (bf16[64,1024]{1,0:T(8,128)(2,1)S(1)}, bf16[64,1024]{1,0:T(8,128)(2,1)S(1)}, u32[]{:S(2)}, u32[]{:S(2)}) collective-permute-start(bf16[64,1024]{1,0:T(8,128)(2,1)S(1)} %shard_map.115.refs_0_), channel_id=1, source_target_pairs={{0,24},{8,16},{16,8},{24,0},{1,25},{9,17},{17,9},{25,1},{2,26},{10... | collective-permute-start | bytes 393224 | tf_op jit(solution)/shard_map/ppermute | solution.py:234
  40.3 7.3 %collective-permute-start.15 = (bf16[64,1024]{1,0:T(8,128)(2,1)S(1)}, bf16[64,1024]{1,0:T(8,128)(2,1)S(1)}, u32[]{:S(2)}, u32[]{:S(2)}) collective-permute-start(bf16[64,1024]{1,0:T(8,128)(2,1)S(1)} %get-tuple-element.81), channel_id=1, source_target_pairs={{0,8},{8,0},{16,24},{24,16},{1,9},{9,1},{17,25},{25,17},{2,10},{10... | collective-permute-start | bytes 393224 | tf_op jit(solution)/shard_map/ppermute | solution.py:234
  41.6 7.7 %collective-permute-start.16 = (bf16[64,1024]{1,0:T(8,128)(2,1)S(1)}, bf16[64,1024]{1,0:T(8,128)(2,1)S(1)}, u32[]{:S(2)}, u32[]{:S(2)}) collective-permute-start(bf16[64,1024]{1,0:T(8,128)(2,1)S(1)} %get-tuple-element.82), channel_id=1, source_target_pairs={{0,16},{8,24},{16,0},{24,8},{1,17},{9,25},{17,1},{25,9},{2,18},{10... | collective-permute-start | bytes 393224 | tf_op jit(solution)/shard_map/ppermute | solution.py:234
  42.5 6.8 %collective-permute-start.17 = (bf16[64,1024]{1,0:T(8,128)(2,1)S(1)}, bf16[64,1024]{1,0:T(8,128)(2,1)S(1)}, u32[]{:S(2)}, u32[]{:S(2)}) collective-permute-start(bf16[64,1024]{1,0:T(8,128)(2,1)S(1)} %get-tuple-element.83), channel_id=1, source_target_pairs={{0,24},{8,16},{16,8},{24,0},{1,25},{9,17},{17,9},{25,1},{2,26},{10... | collective-permute-start | bytes 393224 | tf_op jit(solution)/shard_map/ppermute | solution.py:234
  49.6 9.3 %collective-permute-start.18 = (bf16[2,64,1024]{2,1,0:T(8,128)(2,1)S(1)}, bf16[2,64,1024]{2,1,0:T(8,128)(2,1)S(1)}, u32[]{:S(2)}, u32[]{:S(2)}) collective-permute-start(bf16[2,64,1024]{2,1,0:T(8,128)(2,1)S(1)} %shard_map.119.refs_0_), channel_id=1, source_target_pairs={{0,8},{8,0},{16,24},{24,16},{1,9},{9,1},{17,25},{25,17},{2,10},{10... | collective-permute-start | bytes 786440 | tf_op jit(solution)/shard_map/ppermute | solution.py:234
  50.5 9.0 %collective-permute-start.19 = (bf16[2,64,1024]{2,1,0:T(8,128)(2,1)S(1)}, bf16[2,64,1024]{2,1,0:T(8,128)(2,1)S(1)}, u32[]{:S(2)}, u32[]{:S(2)}) collective-permute-start(bf16[2,64,1024]{2,1,0:T(8,128)(2,1)S(1)} %shard_map.119.refs_0_), channel_id=1, source_target_pairs={{0,16},{8,24},{16,0},{24,8},{1,17},{9,25},{17,1},{25,9},{2,18},{10... | collective-permute-start | bytes 786440 | tf_op jit(solution)/shard_map/ppermute | solution.py:234
  51.6 10.7 %collective-permute-start.20 = (bf16[2,64,1024]{2,1,0:T(8,128)(2,1)S(1)}, bf16[2,64,1024]{2,1,0:T(8,128)(2,1)S(1)}, u32[]{:S(2)}, u32[]{:S(2)}) collective-permute-start(bf16[2,64,1024]{2,1,0:T(8,128)(2,1)S(1)} %shard_map.119.refs_0_), channel_id=1, source_target_pairs={{0,24},{8,16},{16,8},{24,0},{1,25},{9,17},{17,9},{25,1},{2,26},{10... | collective-permute-start | bytes 786440 | tf_op jit(solution)/shard_map/ppermute | solution.py:234
  53.2 9.2 %collective-permute-start.21 = (bf16[2,32,896]{2,1,0:T(8,128)(2,1)S(1)}, bf16[2,32,896]{2,1,0:T(8,128)(2,1)S(1)}, u32[]{:S(2)}, u32[]{:S(2)}) collective-permute-start(bf16[2,32,896]{2,1,0:T(8,128)(2,1)S(1)} %get-tuple-element.84), channel_id=1, source_target_pairs={{0,4},{1,5},{2,6},{3,7},{4,0},{5,1},{6,2},{7,3},{8,12},{9,13},{10,... | collective-permute-start | bytes 344072 | tf_op jit(solution)/shard_map/ppermute | solution.py:234
  53.3 9.1 %collective-permute-start.22 = (bf16[2,32,896]{2,1,0:T(8,128)(2,1)S(1)}, bf16[2,32,896]{2,1,0:T(8,128)(2,1)S(1)}, u32[]{:S(2)}, u32[]{:S(2)}) collective-permute-start(bf16[2,32,896]{2,1,0:T(8,128)(2,1)S(1)} %get-tuple-element.85), channel_id=1, source_target_pairs={{0,6},{1,7},{2,4},{3,5},{4,2},{5,3},{6,0},{7,1},{8,14},{9,15},{10,... | collective-permute-start | bytes 344072 | tf_op jit(solution)/shard_map/ppermute | solution.py:234
  63.8 8.7 %collective-permute-start.23 = (bf16[2,32,896]{2,1,0:T(8,128)(2,1)S(1)}, bf16[2,32,896]{2,1,0:T(8,128)(2,1)S(1)}, u32[]{:S(2)}, u32[]{:S(2)}) collective-permute-start(bf16[2,32,896]{2,1,0:T(8,128)(2,1)S(1)} %get-tuple-element.88), channel_id=1, source_target_pairs={{0,2},{1,3},{2,0},{3,1},{4,6},{5,7},{6,4},{7,5},{8,10},{9,11},{10,... | collective-permute-start | bytes 344072 | tf_op jit(solution)/shard_map/ppermute | solution.py:234
  66.1 10.3 %collective-permute-start.25 = (bf16[2,32,896]{2,1,0:T(8,128)(2,1)S(1)}, bf16[2,32,896]{2,1,0:T(8,128)(2,1)S(1)}, u32[]{:S(2)}, u32[]{:S(2)}) collective-permute-start(bf16[2,32,896]{2,1,0:T(8,128)(2,1)S(1)} %get-tuple-element.96), channel_id=1, source_target_pairs={{0,6},{1,7},{2,4},{3,5},{4,2},{5,3},{6,0},{7,1},{8,14},{9,15},{10,... | collective-permute-start | bytes 344072 | tf_op jit(solution)/shard_map/ppermute | solution.py:234
  67.7 11.8 %collective-permute-start.26 = (bf16[2,32,896]{2,1,0:T(8,128)(2,1)S(1)}, bf16[2,32,896]{2,1,0:T(8,128)(2,1)S(1)}, u32[]{:S(2)}, u32[]{:S(2)}) collective-permute-start(bf16[2,32,896]{2,1,0:T(8,128)(2,1)S(1)} %get-tuple-element.97), channel_id=1, source_target_pairs={{0,4},{1,5},{2,6},{3,7},{4,0},{5,1},{6,2},{7,3},{8,12},{9,13},{10,... | collective-permute-start | bytes 344072 | tf_op jit(solution)/shard_map/ppermute | solution.py:234
  69.0 10.5 %collective-permute-start.27 = (bf16[2,32,896]{2,1,0:T(8,128)(2,1)S(1)}, bf16[2,32,896]{2,1,0:T(8,128)(2,1)S(1)}, u32[]{:S(2)}, u32[]{:S(2)}) collective-permute-start(bf16[2,32,896]{2,1,0:T(8,128)(2,1)S(1)} %get-tuple-element.95.refs_5_.refs_2_), channel_id=1, source_target_pairs={{0,2},{1,3},{2,0},{3,1},{4,6},{5,7},{6,4},{7,5},{8,10},{9,11},{10,... | collective-permute-start | bytes 344072 | tf_op jit(solution)/shard_map/ppermute | solution.py:234
  (12 other events, 74.4 us)

commit v17 on v16

--- a/solution.py
+++ b/solution.py
@@ -109,10 +109,17 @@
     return found
 
 
+def turned_step(dp, k):
+    bits = dp.bit_length() - 1
+    low = bits // 2
+    return ((k << low) | (k >> (bits - low))) & (dp - 1)
+
+
 def chunk_rows(rows, dp, k):
     chunk = rows // dp
     mine = lax.axis_index("dp")
-    return pl.ds(pl.multiple_of((mine ^ k) * chunk, chunk), chunk)
+    step = jnp.where(lax.axis_index("expert") % 2 == 0, k, turned_step(dp, k))
+    return pl.ds(pl.multiple_of((mine ^ step) * chunk, chunk), chunk)
 
 
 def local_order(found, scratch, dp):
@@ -234,9 +241,20 @@
     return lax.ppermute(value, axis, [(i, i ^ k) for i in range(size)])
 
 
+def dp_partner(value, k):
+    size, experts = lax.axis_size("dp"), lax.axis_size("expert")
+    steps = (k, turned_step(size, k))
+    pairs = [
+        (i * experts + e, (i ^ steps[e % 2]) * experts + e)
+        for i in range(size)
+        for e in range(experts)
+    ]
+    return lax.ppermute(value, ("dp", "expert"), pairs)
+
+
 def trade(values):
     far_first = reversed(range(1, len(values)))
-    return [values[0]] + [partner(values[k], "dp", k) for k in far_first][::-1]
+    return [values[0]] + [dp_partner(values[k], k) for k in far_first][::-1]
 
 
 def body(tokens, grad_out, expert_ids, gates, w_gate, w_up, w_down):

time: 81 us -> 84 us (1.037)
  waiting for transfers between devices: 28.5 us -> 31.1 us
    ppermute x0 -> x12, waiting for transfers between devices: none -> 21.9 us  [dp_partner(): return lax.ppermute(value, ('dp', 'expert'), pairs)]
    ppermute x28 -> x16, waiting for transfers between devices: 28.5 us -> 9.23 us  [partner(): return lax.ppermute(value, axis, [(i, i ^ k) for i in range(size)])]
    ppermute x0 -> x12, starting transfers between devices: none -> 15.2 us  [dp_partner(): return lax.ppermute(value, ('dp', 'expert'), pairs)]
    ppermute x28 -> x16, starting transfers between devices: 32.6 us -> 17.8 us  [partner(): return lax.ppermute(value, axis, [(i, i ^ k) for i in range(size)])]
  transfers between devices with their start and end apart: 28 -> 28, of which waited for: 12 -> 11; matrix products, arithmetic and copies ran while one was open for 0% -> 0% of each run, Pallas kernels for 12% -> 12%
where the time goes in v17:
time: 84 us; the launch traced here: 83.7 us
  starting transfers between devices  33 us (39%)
  waiting for transfers between devices  31.1 us (37%)
  Pallas kernels  14.8 us (18%)
  local copies, waits for them, and re-layouts  3.99 us (5%)
    ppermute x12, waiting for transfers between devices, dp_partner(): return lax.ppermute(value, ('dp', 'expert'), pairs)  21.9 us
    ppermute x16, starting transfers between devices, partner(): return lax.ppermute(value, axis, [(i, i ^ k) for i in range(size)])  17.8 us
    ppermute x12, starting transfers between devices, dp_partner(): return lax.ppermute(value, ('dp', 'expert'), pairs)  15.2 us
    ppermute x16, waiting for transfers between devices, partner(): return lax.ppermute(value, axis, [(i, i ^ k) for i in range(size)])  9.23 us
    unnamed x16, local copies, waits for them, and re-layouts  3.99 us
    pallas_call x1, Pallas kernels, body(): call(functools.partial(route_kernel, experts), outs, 4 * slots * tok_rows...  2.59 us
    pallas_call x1, Pallas kernels, body(): call(functools.partial(grads_kernel, 2), [shape((features, hidden), BF16)...  2.54 us
    pallas_call x1, Pallas kernels, body(): call(functools.partial(grads_kernel, 1), [shape((hidden, features), BF16)...  1.97 us
  transfers between devices with their start and end apart: 28, of which 11 were waited for; matrix products, arithmetic and copies ran while one was open for 0% of the time, Pallas kernels for 12%

profile of v17, /device:TPU:0, one launch (start us, length us, event | category | flops | bytes accessed | tf_op | source)
XLA Modules:
  0.0 83.7 jit_solution(18378338112607461970)
XLA Ops:
  0.6 2.6 %shard_map.110 = (bf16[256,512]{1,0:T(8,128)(2,1)}, f32[256,1]{1,0:T(8,128)}, bf16[4,32,896]{2,1,0:T(8,128)(2,1)}, bf16[4,32,896]{2,1,0:T(8,128)(2,1)}) custom-call(s32[8,512]{1,0:T(8,128)} %bitcast.14, f32[8,512]{1,0:T(8,128)} %bitcast.15, bf16[512,896]{1,0:T(8,128)(2,1)} %refs_2_.1), custom_call_target="tpu_custom_call" | custom-call | flops 469762048 | bytes 3670016 | tf_op jit(solution)/shard_map/pallas_call | solution.py:282
  5.1 5.0 %collective-permute-start.1 = (bf16[2,32,896]{2,1,0:T(8,128)(2,1)S(1)}, bf16[2,32,896]{2,1,0:T(8,128)(2,1)S(1)}, u32[]{:S(2)}, u32[]{:S(2)}) collective-permute-start(bf16[2,32,896]{2,1,0:T(8,128)(2,1)S(1)} %get-tuple-element.62), channel_id=1, source_target_pairs={{0,6},{1,7},{2,4},{3,5},{4,2},{5,3},{6,0},{7,1},{8,14},{9,15},{10,... | collective-permute-start | bytes 344072 | tf_op jit(solution)/shard_map/ppermute | solution.py:241
  14.5 5.6 %collective-permute-done.2.refs_3_ = bf16[2,32,896]{2,1,0:T(8,128)(2,1)S(1)} collective-permute-done((bf16[2,32,896]{2,1,0:T(8,128)(2,1)S(1)}, bf16[2,32,896]{2,1,0:T(8,128)(2,1)S(1)}, u32[]{:S(2)}, u32[]{:S(2)}) %collective-permute-start.2) | collective-permute-done | bytes 114720 | tf_op jit(solution)/shard_map/ppermute | solution.py:241
  21.4 1.6 %collective-permute-start.4 = (bf16[2,64,1024]{2,1,0:T(8,128)(2,1)S(1)}, bf16[2,64,1024]{2,1,0:T(8,128)(2,1)S(1)}, u32[]{:S(2)}, u32[]{:S(2)}) collective-permute-start(bf16[2,64,1024]{2,1,0:T(8,128)(2,1)S(1)} %get-tuple-element.67), channel_id=1, source_target_pairs={{0,8},{1,17},{2,10},{3,19},{4,12},{5,21},{6,14},{7,23},{8,0},{9,25... | collective-permute-start | bytes 786440 | tf_op jit(solution)/shard_map/ppermute | solution.py:252
  23.0 1.5 %collective-permute-start.5 = (bf16[2,64,1024]{2,1,0:T(8,128)(2,1)S(1)}, bf16[2,64,1024]{2,1,0:T(8,128)(2,1)S(1)}, u32[]{:S(2)}, u32[]{:S(2)}) collective-permute-start(bf16[2,64,1024]{2,1,0:T(8,128)(2,1)S(1)} %get-tuple-element.68), channel_id=1, source_target_pairs={{0,16},{1,9},{2,18},{3,11},{4,20},{5,13},{6,22},{7,15},{8,24},{9,1... | collective-permute-start | bytes 786440 | tf_op jit(solution)/shard_map/ppermute | solution.py:252
  25.0 2.5 %collective-permute-start.12 = (bf16[2,32,896]{2,1,0:T(8,128)(2,1)S(1)}, bf16[2,32,896]{2,1,0:T(8,128)(2,1)S(1)}, u32[]{:S(2)}, u32[]{:S(2)}) collective-permute-start(bf16[2,32,896]{2,1,0:T(8,128)(2,1)S(1)} %get-tuple-element.74), channel_id=1, source_target_pairs={{0,6},{1,7},{2,4},{3,5},{4,2},{5,3},{6,0},{7,1},{8,14},{9,15},{10,... | collective-permute-start | bytes 344072 | tf_op jit(solution)/shard_map/ppermute | solution.py:241
  27.5 3.0 %collective-permute-done.4.refs_1_ = bf16[2,64,1024]{2,1,0:T(8,128)(2,1)S(1)} collective-permute-done((bf16[2,64,1024]{2,1,0:T(8,128)(2,1)S(1)}, bf16[2,64,1024]{2,1,0:T(8,128)(2,1)S(1)}, u32[]{:S(2)}, u32[]{:S(2)}) %collective-permute-start.4) | collective-permute-done | bytes 262176 | tf_op jit(solution)/shard_map/ppermute | solution.py:252
  30.7 5.1 %collective-permute-done.6.refs_3_ = bf16[2,64,1024]{2,1,0:T(8,128)(2,1)S(1)} collective-permute-done((bf16[2,64,1024]{2,1,0:T(8,128)(2,1)S(1)}, bf16[2,64,1024]{2,1,0:T(8,128)(2,1)S(1)}, u32[]{:S(2)}, u32[]{:S(2)}) %collective-permute-start.6) | collective-permute-done | bytes 262176 | tf_op jit(solution)/shard_map/ppermute | solution.py:252
  36.0 1.6 %collective-permute-start.7 = (bf16[64,1024]{1,0:T(8,128)(2,1)S(1)}, bf16[64,1024]{1,0:T(8,128)(2,1)S(1)}, u32[]{:S(2)}, u32[]{:S(2)}) collective-permute-start(bf16[64,1024]{1,0:T(8,128)(2,1)S(1)} %shard_map.115.refs_0_), channel_id=1, source_target_pairs={{0,8},{1,17},{2,10},{3,19},{4,12},{5,21},{6,14},{7,23},{8,0},{9,25... | collective-permute-start | bytes 393224 | tf_op jit(solution)/shard_map/ppermute | solution.py:252
  37.5 1.5 %collective-permute-start.8 = (bf16[64,1024]{1,0:T(8,128)(2,1)S(1)}, bf16[64,1024]{1,0:T(8,128)(2,1)S(1)}, u32[]{:S(2)}, u32[]{:S(2)}) collective-permute-start(bf16[64,1024]{1,0:T(8,128)(2,1)S(1)} %shard_map.115.refs_0_), channel_id=1, source_target_pairs={{0,16},{1,9},{2,18},{3,11},{4,20},{5,13},{6,22},{7,15},{8,24},{9,1... | collective-permute-start | bytes 393224 | tf_op jit(solution)/shard_map/ppermute | solution.py:252
  40.3 1.6 %collective-permute-start.15 = (bf16[64,1024]{1,0:T(8,128)(2,1)S(1)}, bf16[64,1024]{1,0:T(8,128)(2,1)S(1)}, u32[]{:S(2)}, u32[]{:S(2)}) collective-permute-start(bf16[64,1024]{1,0:T(8,128)(2,1)S(1)} %get-tuple-element.81), channel_id=1, source_target_pairs={{0,8},{1,17},{2,10},{3,19},{4,12},{5,21},{6,14},{7,23},{8,0},{9,25... | collective-permute-start | bytes 393224 | tf_op jit(solution)/shard_map/ppermute | solution.py:252
  41.9 1.5 %collective-permute-start.16 = (bf16[64,1024]{1,0:T(8,128)(2,1)S(1)}, bf16[64,1024]{1,0:T(8,128)(2,1)S(1)}, u32[]{:S(2)}, u32[]{:S(2)}) collective-permute-start(bf16[64,1024]{1,0:T(8,128)(2,1)S(1)} %get-tuple-element.82), channel_id=1, source_target_pairs={{0,16},{1,9},{2,18},{3,11},{4,20},{5,13},{6,22},{7,15},{8,24},{9,1... | collective-permute-start | bytes 393224 | tf_op jit(solution)/shard_map/ppermute | solution.py:252
  43.4 1.5 %collective-permute-start.17 = (bf16[64,1024]{1,0:T(8,128)(2,1)S(1)}, bf16[64,1024]{1,0:T(8,128)(2,1)S(1)}, u32[]{:S(2)}, u32[]{:S(2)}) collective-permute-start(bf16[64,1024]{1,0:T(8,128)(2,1)S(1)} %get-tuple-element.83), channel_id=1, source_target_pairs={{0,24},{1,25},{2,26},{3,27},{4,28},{5,29},{6,30},{7,31},{8,16},{9,... | collective-permute-start | bytes 393224 | tf_op jit(solution)/shard_map/ppermute | solution.py:252
  48.3 2.6 %collective-permute-done.16.refs_6_ = bf16[64,1024]{1,0:T(8,128)(2,1)S(1)} collective-permute-done((bf16[64,1024]{1,0:T(8,128)(2,1)S(1)}, bf16[64,1024]{1,0:T(8,128)(2,1)S(1)}, u32[]{:S(2)}, u32[]{:S(2)}) %collective-permute-start.16) | collective-permute-done | bytes 131104 | tf_op jit(solution)/shard_map/ppermute | solution.py:252
  52.6 1.6 %collective-permute-start.19 = (bf16[2,64,1024]{2,1,0:T(8,128)(2,1)S(1)}, bf16[2,64,1024]{2,1,0:T(8,128)(2,1)S(1)}, u32[]{:S(2)}, u32[]{:S(2)}) collective-permute-start(bf16[2,64,1024]{2,1,0:T(8,128)(2,1)S(1)} %shard_map.119.refs_0_), channel_id=1, source_target_pairs={{0,16},{1,9},{2,18},{3,11},{4,20},{5,13},{6,22},{7,15},{8,24},{9,1... | collective-permute-start | bytes 786440 | tf_op jit(solution)/shard_map/ppermute | solution.py:252
  54.9 2.5 %collective-permute-start.22 = (bf16[2,32,896]{2,1,0:T(8,128)(2,1)S(1)}, bf16[2,32,896]{2,1,0:T(8,128)(2,1)S(1)}, u32[]{:S(2)}, u32[]{:S(2)}) collective-permute-start(bf16[2,32,896]{2,1,0:T(8,128)(2,1)S(1)} %get-tuple-element.85), channel_id=1, source_target_pairs={{0,6},{1,7},{2,4},{3,5},{4,2},{5,3},{6,0},{7,1},{8,14},{9,15},{10,... | collective-permute-start | bytes 344072 | tf_op jit(solution)/shard_map/ppermute | solution.py:241
  57.5 2.9 %collective-permute-done.18.refs_1_ = bf16[2,64,1024]{2,1,0:T(8,128)(2,1)S(1)} collective-permute-done((bf16[2,64,1024]{2,1,0:T(8,128)(2,1)S(1)}, bf16[2,64,1024]{2,1,0:T(8,128)(2,1)S(1)}, u32[]{:S(2)}, u32[]{:S(2)}) %collective-permute-start.18) | collective-permute-done | bytes 262176 | tf_op jit(solution)/shard_map/ppermute | solution.py:252
  60.4 5.6 %collective-permute-done.20.refs_3_ = bf16[2,64,1024]{2,1,0:T(8,128)(2,1)S(1)} collective-permute-done((bf16[2,64,1024]{2,1,0:T(8,128)(2,1)S(1)}, bf16[2,64,1024]{2,1,0:T(8,128)(2,1)S(1)}, u32[]{:S(2)}, u32[]{:S(2)}) %collective-permute-start.20) | collective-permute-done | bytes 262176 | tf_op jit(solution)/shard_map/ppermute | solution.py:252
  67.4 1.6 %collective-permute-start.23 = (bf16[2,32,896]{2,1,0:T(8,128)(2,1)S(1)}, bf16[2,32,896]{2,1,0:T(8,128)(2,1)S(1)}, u32[]{:S(2)}, u32[]{:S(2)}) collective-permute-start(bf16[2,32,896]{2,1,0:T(8,128)(2,1)S(1)} %get-tuple-element.88), channel_id=1, source_target_pairs={{0,2},{1,3},{2,0},{3,1},{4,6},{5,7},{6,4},{7,5},{8,10},{9,11},{10,... | collective-permute-start | bytes 344072 | tf_op jit(solution)/shard_map/ppermute | solution.py:241
  69.1 2.4 %collective-permute-start.25 = (bf16[2,32,896]{2,1,0:T(8,128)(2,1)S(1)}, bf16[2,32,896]{2,1,0:T(8,128)(2,1)S(1)}, u32[]{:S(2)}, u32[]{:S(2)}) collective-permute-start(bf16[2,32,896]{2,1,0:T(8,128)(2,1)S(1)} %get-tuple-element.96), channel_id=1, source_target_pairs={{0,6},{1,7},{2,4},{3,5},{4,2},{5,3},{6,0},{7,1},{8,14},{9,15},{10,... | collective-permute-start | bytes 344072 | tf_op jit(solution)/shard_map/ppermute | solution.py:241
  72.0 1.5 %collective-permute-start.27 = (bf16[2,32,896]{2,1,0:T(8,128)(2,1)S(1)}, bf16[2,32,896]{2,1,0:T(8,128)(2,1)S(1)}, u32[]{:S(2)}, u32[]{:S(2)}) collective-permute-start(bf16[2,32,896]{2,1,0:T(8,128)(2,1)S(1)} %get-tuple-element.95.refs_5_.refs_2_), channel_id=1, source_target_pairs={{0,2},{1,3},{2,0},{3,1},{4,6},{5,7},{6,4},{7,5},{8,10},{9,11},{10,... | collective-permute-start | bytes 344072 | tf_op jit(solution)/shard_map/ppermute | solution.py:241
  73.5 2.0 %shard_map.126 = bf16[1024,896]{1,0:T(8,128)(2,1)} custom-call(bf16[256,1024]{1,0:T(8,128)(2,1)S(1)} %get-tuple-element.103.left_ref, bf16[256,896]{1,0:T(8,128)(2,1)S(1)} %get-tuple-element.104.refs_0_), custom_call_target="tpu_custom_call" | custom-call | flops 469762048 | bytes 1835008 | tf_op jit(solution)/shard_map/pallas_call | solution.py:363
  76.8 2.5 %shard_map.125 = (bf16[896,1024]{1,0:T(8,128)(2,1)}, bf16[896,1024]{1,0:T(8,128)(2,1)}) custom-call(bf16[256,896]{1,0:T(8,128)(2,1)S(1)} %get-tuple-element.98.left_ref, bf16[256,1024]{1,0:T(8,128)(2,1)S(1)} %get-tuple-element.99.refs_0_, bf16[256,1024]{1,0:T(8,128)(2,1)S(1)} %get-tuple-element.100.refs_1_, ...), custom_call_target="tpu_custom_call" | custom-call | flops 939524096 | bytes 3670016 | tf_op jit(solution)/shard_map/pallas_call | solution.py:369
  79.3 3.2 %collective-permute-done.26.refs_3_ = bf16[2,32,896]{2,1,0:T(8,128)(2,1)S(1)} collective-permute-done((bf16[2,32,896]{2,1,0:T(8,128)(2,1)S(1)}, bf16[2,32,896]{2,1,0:T(8,128)(2,1)S(1)}, u32[]{:S(2)}, u32[]{:S(2)}) %collective-permute-start.26) | collective-permute-done | bytes 114720 | tf_op jit(solution)/shard_map/ppermute | solution.py:241
  (65 shorter events, 19.7 us)
Async XLA Ops:
  5.1 9.4 %collective-permute-start.1 = (bf16[2,32,896]{2,1,0:T(8,128)(2,1)S(1)}, bf16[2,32,896]{2,1,0:T(8,128)(2,1)S(1)}, u32[]{:S(2)}, u32[]{:S(2)}) collective-permute-start(bf16[2,32,896]{2,1,0:T(8,128)(2,1)S(1)} %get-tuple-element.62), channel_id=1, source_target_pairs={{0,6},{1,7},{2,4},{3,5},{4,2},{5,3},{6,0},{7,1},{8,14},{9,15},{10,... | collective-permute-start | bytes 344072 | tf_op jit(solution)/shard_map/ppermute | solution.py:241
  10.1 10.0 %collective-permute-start.2 = (bf16[2,32,896]{2,1,0:T(8,128)(2,1)S(1)}, bf16[2,32,896]{2,1,0:T(8,128)(2,1)S(1)}, u32[]{:S(2)}, u32[]{:S(2)}) collective-permute-start(bf16[2,32,896]{2,1,0:T(8,128)(2,1)S(1)} %get-tuple-element.63), channel_id=1, source_target_pairs={{0,4},{1,5},{2,6},{3,7},{4,0},{5,1},{6,2},{7,3},{8,12},{9,13},{10,... | collective-permute-start | bytes 344072 | tf_op jit(solution)/shard_map/ppermute | solution.py:241
  10.1 10.0 %collective-permute-start.3 = (bf16[2,32,896]{2,1,0:T(8,128)(2,1)S(1)}, bf16[2,32,896]{2,1,0:T(8,128)(2,1)S(1)}, u32[]{:S(2)}, u32[]{:S(2)}) collective-permute-start(bf16[2,32,896]{2,1,0:T(8,128)(2,1)S(1)} %get-tuple-element.64), channel_id=1, source_target_pairs={{0,2},{1,3},{2,0},{3,1},{4,6},{5,7},{6,4},{7,5},{8,10},{9,11},{10,... | collective-permute-start | bytes 344072 | tf_op jit(solution)/shard_map/ppermute | solution.py:241
  14.4 10.6 %collective-permute-start.11 = (bf16[4,32,896]{2,1,0:T(8,128)(2,1)S(1)}, bf16[4,32,896]{2,1,0:T(8,128)(2,1)S(1)}, u32[]{:S(2)}, u32[]{:S(2)}) collective-permute-start(bf16[4,32,896]{2,1,0:T(8,128)(2,1)S(1)} %get-tuple-element.73), channel_id=1, source_target_pairs={{0,1},{1,0},{2,3},{3,2},{4,5},{5,4},{6,7},{7,6},{8,9},{9,8},{10,11... | collective-permute-start | bytes 688136 | tf_op jit(solution)/shard_map/ppermute | solution.py:241
  21.4 9.2 %collective-permute-start.4 = (bf16[2,64,1024]{2,1,0:T(8,128)(2,1)S(1)}, bf16[2,64,1024]{2,1,0:T(8,128)(2,1)S(1)}, u32[]{:S(2)}, u32[]{:S(2)}) collective-permute-start(bf16[2,64,1024]{2,1,0:T(8,128)(2,1)S(1)} %get-tuple-element.67), channel_id=1, source_target_pairs={{0,8},{1,17},{2,10},{3,19},{4,12},{5,21},{6,14},{7,23},{8,0},{9,25... | collective-permute-start | bytes 786440 | tf_op jit(solution)/shard_map/ppermute | solution.py:252
  23.0 7.8 %collective-permute-start.5 = (bf16[2,64,1024]{2,1,0:T(8,128)(2,1)S(1)}, bf16[2,64,1024]{2,1,0:T(8,128)(2,1)S(1)}, u32[]{:S(2)}, u32[]{:S(2)}) collective-permute-start(bf16[2,64,1024]{2,1,0:T(8,128)(2,1)S(1)} %get-tuple-element.68), channel_id=1, source_target_pairs={{0,16},{1,9},{2,18},{3,11},{4,20},{5,13},{6,22},{7,15},{8,24},{9,1... | collective-permute-start | bytes 786440 | tf_op jit(solution)/shard_map/ppermute | solution.py:252
  24.5 11.3 %collective-permute-start.6 = (bf16[2,64,1024]{2,1,0:T(8,128)(2,1)S(1)}, bf16[2,64,1024]{2,1,0:T(8,128)(2,1)S(1)}, u32[]{:S(2)}, u32[]{:S(2)}) collective-permute-start(bf16[2,64,1024]{2,1,0:T(8,128)(2,1)S(1)} %get-tuple-element.69), channel_id=1, source_target_pairs={{0,24},{1,25},{2,26},{3,27},{4,28},{5,29},{6,30},{7,31},{8,16},{9,... | collective-permute-start | bytes 786440 | tf_op jit(solution)/shard_map/ppermute | solution.py:252
  25.0 14.1 %collective-permute-start.12 = (bf16[2,32,896]{2,1,0:T(8,128)(2,1)S(1)}, bf16[2,32,896]{2,1,0:T(8,128)(2,1)S(1)}, u32[]{:S(2)}, u32[]{:S(2)}) collective-permute-start(bf16[2,32,896]{2,1,0:T(8,128)(2,1)S(1)} %get-tuple-element.74), channel_id=1, source_target_pairs={{0,6},{1,7},{2,4},{3,5},{4,2},{5,3},{6,0},{7,1},{8,14},{9,15},{10,... | collective-permute-start | bytes 344072 | tf_op jit(solution)/shard_map/ppermute | solution.py:241
  27.5 12.0 %collective-permute-start.13 = (bf16[2,32,896]{2,1,0:T(8,128)(2,1)S(1)}, bf16[2,32,896]{2,1,0:T(8,128)(2,1)S(1)}, u32[]{:S(2)}, u32[]{:S(2)}) collective-permute-start(bf16[2,32,896]{2,1,0:T(8,128)(2,1)S(1)} %get-tuple-element.75), channel_id=1, source_target_pairs={{0,4},{1,5},{2,6},{3,7},{4,0},{5,1},{6,2},{7,3},{8,12},{9,13},{10,... | collective-permute-start | bytes 344072 | tf_op jit(solution)/shard_map/ppermute | solution.py:241
  30.6 9.0 %collective-permute-start.14 = (bf16[2,32,896]{2,1,0:T(8,128)(2,1)S(1)}, bf16[2,32,896]{2,1,0:T(8,128)(2,1)S(1)}, u32[]{:S(2)}, u32[]{:S(2)}) collective-permute-start(bf16[2,32,896]{2,1,0:T(8,128)(2,1)S(1)} %get-tuple-element.76), channel_id=1, source_target_pairs={{0,2},{1,3},{2,0},{3,1},{4,6},{5,7},{6,4},{7,5},{8,10},{9,11},{10,... | collective-permute-start | bytes 344072 | tf_op jit(solution)/shard_map/ppermute | solution.py:241
  37.5 8.3 %collective-permute-start.8 = (bf16[64,1024]{1,0:T(8,128)(2,1)S(1)}, bf16[64,1024]{1,0:T(8,128)(2,1)S(1)}, u32[]{:S(2)}, u32[]{:S(2)}) collective-permute-start(bf16[64,1024]{1,0:T(8,128)(2,1)S(1)} %shard_map.115.refs_0_), channel_id=1, source_target_pairs={{0,16},{1,9},{2,18},{3,11},{4,20},{5,13},{6,22},{7,15},{8,24},{9,1... | collective-permute-start | bytes 393224 | tf_op jit(solution)/shard_map/ppermute | solution.py:252
  40.3 8.0 %collective-permute-start.15 = (bf16[64,1024]{1,0:T(8,128)(2,1)S(1)}, bf16[64,1024]{1,0:T(8,128)(2,1)S(1)}, u32[]{:S(2)}, u32[]{:S(2)}) collective-permute-start(bf16[64,1024]{1,0:T(8,128)(2,1)S(1)} %get-tuple-element.81), channel_id=1, source_target_pairs={{0,8},{1,17},{2,10},{3,19},{4,12},{5,21},{6,14},{7,23},{8,0},{9,25... | collective-permute-start | bytes 393224 | tf_op jit(solution)/shard_map/ppermute | solution.py:252
  41.9 9.1 %collective-permute-start.16 = (bf16[64,1024]{1,0:T(8,128)(2,1)S(1)}, bf16[64,1024]{1,0:T(8,128)(2,1)S(1)}, u32[]{:S(2)}, u32[]{:S(2)}) collective-permute-start(bf16[64,1024]{1,0:T(8,128)(2,1)S(1)} %get-tuple-element.82), channel_id=1, source_target_pairs={{0,16},{1,9},{2,18},{3,11},{4,20},{5,13},{6,22},{7,15},{8,24},{9,1... | collective-permute-start | bytes 393224 | tf_op jit(solution)/shard_map/ppermute | solution.py:252
  43.4 7.6 %collective-permute-start.17 = (bf16[64,1024]{1,0:T(8,128)(2,1)S(1)}, bf16[64,1024]{1,0:T(8,128)(2,1)S(1)}, u32[]{:S(2)}, u32[]{:S(2)}) collective-permute-start(bf16[64,1024]{1,0:T(8,128)(2,1)S(1)} %get-tuple-element.83), channel_id=1, source_target_pairs={{0,24},{1,25},{2,26},{3,27},{4,28},{5,29},{6,30},{7,31},{8,16},{9,... | collective-permute-start | bytes 393224 | tf_op jit(solution)/shard_map/ppermute | solution.py:252
  47.2 7.6 %collective-permute-start.10 = (bf16[4,32,896]{2,1,0:T(8,128)(2,1)S(1)}, bf16[4,32,896]{2,1,0:T(8,128)(2,1)S(1)}, u32[]{:S(2)}, u32[]{:S(2)}) collective-permute-start(bf16[4,32,896]{2,1,0:T(8,128)(2,1)S(1)} %get-tuple-element.71), channel_id=1, source_target_pairs={{0,1},{1,0},{2,3},{3,2},{4,5},{5,4},{6,7},{7,6},{8,9},{9,8},{10,11... | collective-permute-start | bytes 688136 | tf_op jit(solution)/shard_map/ppermute | solution.py:241
  51.3 9.1 %collective-permute-start.18 = (bf16[2,64,1024]{2,1,0:T(8,128)(2,1)S(1)}, bf16[2,64,1024]{2,1,0:T(8,128)(2,1)S(1)}, u32[]{:S(2)}, u32[]{:S(2)}) collective-permute-start(bf16[2,64,1024]{2,1,0:T(8,128)(2,1)S(1)} %shard_map.119.refs_0_), channel_id=1, source_target_pairs={{0,8},{1,17},{2,10},{3,19},{4,12},{5,21},{6,14},{7,23},{8,0},{9,25... | collective-permute-start | bytes 786440 | tf_op jit(solution)/shard_map/ppermute | solution.py:252
  52.6 7.8 %collective-permute-start.19 = (bf16[2,64,1024]{2,1,0:T(8,128)(2,1)S(1)}, bf16[2,64,1024]{2,1,0:T(8,128)(2,1)S(1)}, u32[]{:S(2)}, u32[]{:S(2)}) collective-permute-start(bf16[2,64,1024]{2,1,0:T(8,128)(2,1)S(1)} %shard_map.119.refs_0_), channel_id=1, source_target_pairs={{0,16},{1,9},{2,18},{3,11},{4,20},{5,13},{6,22},{7,15},{8,24},{9,1... | collective-permute-start | bytes 786440 | tf_op jit(solution)/shard_map/ppermute | solution.py:252
  54.2 11.8 %collective-permute-start.20 = (bf16[2,64,1024]{2,1,0:T(8,128)(2,1)S(1)}, bf16[2,64,1024]{2,1,0:T(8,128)(2,1)S(1)}, u32[]{:S(2)}, u32[]{:S(2)}) collective-permute-start(bf16[2,64,1024]{2,1,0:T(8,128)(2,1)S(1)} %shard_map.119.refs_0_), channel_id=1, source_target_pairs={{0,24},{1,25},{2,26},{3,27},{4,28},{5,29},{6,30},{7,31},{8,16},{9,... | collective-permute-start | bytes 786440 | tf_op jit(solution)/shard_map/ppermute | solution.py:252
  54.8 11.2 %collective-permute-start.21 = (bf16[2,32,896]{2,1,0:T(8,128)(2,1)S(1)}, bf16[2,32,896]{2,1,0:T(8,128)(2,1)S(1)}, u32[]{:S(2)}, u32[]{:S(2)}) collective-permute-start(bf16[2,32,896]{2,1,0:T(8,128)(2,1)S(1)} %get-tuple-element.84), channel_id=1, source_target_pairs={{0,4},{1,5},{2,6},{3,7},{4,0},{5,1},{6,2},{7,3},{8,12},{9,13},{10,... | collective-permute-start | bytes 344072 | tf_op jit(solution)/shard_map/ppermute | solution.py:241
  54.9 11.1 %collective-permute-start.22 = (bf16[2,32,896]{2,1,0:T(8,128)(2,1)S(1)}, bf16[2,32,896]{2,1,0:T(8,128)(2,1)S(1)}, u32[]{:S(2)}, u32[]{:S(2)}) collective-permute-start(bf16[2,32,896]{2,1,0:T(8,128)(2,1)S(1)} %get-tuple-element.85), channel_id=1, source_target_pairs={{0,6},{1,7},{2,4},{3,5},{4,2},{5,3},{6,0},{7,1},{8,14},{9,15},{10,... | collective-permute-start | bytes 344072 | tf_op jit(solution)/shard_map/ppermute | solution.py:241
  67.4 8.1 %collective-permute-start.23 = (bf16[2,32,896]{2,1,0:T(8,128)(2,1)S(1)}, bf16[2,32,896]{2,1,0:T(8,128)(2,1)S(1)}, u32[]{:S(2)}, u32[]{:S(2)}) collective-permute-start(bf16[2,32,896]{2,1,0:T(8,128)(2,1)S(1)} %get-tuple-element.88), channel_id=1, source_target_pairs={{0,2},{1,3},{2,0},{3,1},{4,6},{5,7},{6,4},{7,5},{8,10},{9,11},{10,... | collective-permute-start | bytes 344072 | tf_op jit(solution)/shard_map/ppermute | solution.py:241
  69.1 10.3 %collective-permute-start.25 = (bf16[2,32,896]{2,1,0:T(8,128)(2,1)S(1)}, bf16[2,32,896]{2,1,0:T(8,128)(2,1)S(1)}, u32[]{:S(2)}, u32[]{:S(2)}) collective-permute-start(bf16[2,32,896]{2,1,0:T(8,128)(2,1)S(1)} %get-tuple-element.96), channel_id=1, source_target_pairs={{0,6},{1,7},{2,4},{3,5},{4,2},{5,3},{6,0},{7,1},{8,14},{9,15},{10,... | collective-permute-start | bytes 344072 | tf_op jit(solution)/shard_map/ppermute | solution.py:241
  71.5 11.1 %collective-permute-start.26 = (bf16[2,32,896]{2,1,0:T(8,128)(2,1)S(1)}, bf16[2,32,896]{2,1,0:T(8,128)(2,1)S(1)}, u32[]{:S(2)}, u32[]{:S(2)}) collective-permute-start(bf16[2,32,896]{2,1,0:T(8,128)(2,1)S(1)} %get-tuple-element.97), channel_id=1, source_target_pairs={{0,4},{1,5},{2,6},{3,7},{4,0},{5,1},{6,2},{7,3},{8,12},{9,13},{10,... | collective-permute-start | bytes 344072 | tf_op jit(solution)/shard_map/ppermute | solution.py:241
  72.0 10.5 %collective-permute-start.27 = (bf16[2,32,896]{2,1,0:T(8,128)(2,1)S(1)}, bf16[2,32,896]{2,1,0:T(8,128)(2,1)S(1)}, u32[]{:S(2)}, u32[]{:S(2)}) collective-permute-start(bf16[2,32,896]{2,1,0:T(8,128)(2,1)S(1)} %get-tuple-element.95.refs_5_.refs_2_), channel_id=1, source_target_pairs={{0,2},{1,3},{2,0},{3,1},{4,6},{5,7},{6,4},{7,5},{8,10},{9,11},{10,... | collective-permute-start | bytes 344072 | tf_op jit(solution)/shard_map/ppermute | solution.py:241
  (12 other events, 75.5 us)

commit v18 on v16

--- a/solution.py
+++ b/solution.py
@@ -133,12 +133,18 @@
             out_ref[at] = part[k * chunk : (k + 1) * chunk]
 
 
-def grad_act_kernel(half, *refs):
+def grad_act_kernel(half, dp, *refs):
+    sums, refs = refs[:dp], refs[dp:]
     down_ref, local_ref, *out_refs, scratch = refs[half + 1 :]
-    dp = len(out_refs)
+    gate = group_sum(sums, 0)
+    act = (gate * logistic(gate) * group_sum(sums, 1)).astype(BF16)
     rows = local_order(pieces(*refs[: half + 1]), scratch, dp)
     local_ref[...] = rows
-    split_rows(out_refs, mm(rows, down_ref[...], ((1,), (1,))).astype(BF16))
+    part = mm(rows, down_ref[...], ((1,), (1,))).astype(BF16)
+    chunk = rows.shape[0] // dp
+    for k, out_ref in enumerate(out_refs):
+        out_ref[0] = act
+        out_ref[1] = part[k * chunk : (k + 1) * chunk]
 
 
 def group_sum(refs, *at):
@@ -152,16 +158,10 @@
     return 1.0 / (1.0 + jnp.exp(-value))
 
 
-def act_kernel(dp, *refs):
-    gate = group_sum(refs[:dp], 0)
-    up = group_sum(refs[:dp], 1)
-    refs[dp][...] = (gate * logistic(gate) * up).astype(BF16)
-
-
 def grad_pre_kernel(dp, *refs):
     gate = group_sum(refs[:dp], 0)
     up = group_sum(refs[:dp], 1)
-    grad = group_sum(refs[dp : 2 * dp], Ellipsis)
+    grad = group_sum(refs[dp : 2 * dp], 1)
     out_ref = refs[2 * dp]
     soft = logistic(gate)
     out_ref[0] = (grad * up * (soft * (1.0 + gate * (1.0 - soft)))).astype(BF16)
@@ -177,7 +177,7 @@
 
 def expert_out_kernel(dp, *refs):
     down_ref, act_ref, keep_ref, swap_ref, scratch = refs[dp:]
-    act = join_rows(refs[:dp])
+    act = jnp.concatenate([ref[0] for ref in refs[:dp]], axis=0)
     act_ref[...] = act
     rows = mm(act, down_ref[...], ((1,), (0,))).astype(BF16)
     send_back(keep_ref, swap_ref, scratch, rows, dp)
@@ -295,21 +295,13 @@
         scratch_shapes=in_order,
     )(keep, swap, *row_blocks, gate_mat, up_mat)
     sums = trade(part_pre)
-    act_mine = call(
-        functools.partial(act_kernel, dp),
-        shape((chunk, hidden), BF16),
-        0,
-        4 * dp * chunk * hidden,
-    )(*sums)
-    acts = trade([act_mine] * dp)
-    grad_blocks, act_mine = lax.optimization_barrier((grad_blocks, act_mine))
     grads, *part_grad = call(
-        functools.partial(grad_act_kernel, half),
-        (sized, *[shape((chunk, hidden), BF16)] * dp),
+        functools.partial(grad_act_kernel, half, dp),
+        (sized, *[shape((2, chunk, hidden), BF16)] * dp),
         product,
         weights,
         scratch_shapes=in_order,
-    )(grad_keep, grad_swap, *grad_blocks, down_mat)
+    )(*sums, grad_keep, grad_swap, *grad_blocks, down_mat)
     grad_sums = trade(part_grad)
     pre_mine = call(
         functools.partial(grad_pre_kernel, dp),
@@ -324,7 +316,7 @@
         product,
         weights,
         scratch_shapes=in_order,
-    )(*acts, down_mat)
+    )(*grad_sums, down_mat)
     back = [pair] * (half - 1)
     out_swap = partner(out_swap, "expert", 1)
     out_near, *out_far = call(pack_back_kernel, back, 0, 8 * slots)(out_keep, out_swap)

time: 81 us -> 86.4 us (1.067)
  waiting for transfers between devices: 28.5 us -> 33.4 us
    ppermute x28 -> x25, waiting for transfers between devices: 28.5 us -> 33.4 us  [partner(): return lax.ppermute(value, axis, [(i, i ^ k) for i in range(size)])]
    ppermute x28 -> x25, starting transfers between devices: 32.6 us -> 33.1 us  [partner(): return lax.ppermute(value, axis, [(i, i ^ k) for i in range(size)])]
  transfers between devices with their start and end apart: 28 -> 25, of which waited for: 12 -> 11; matrix products, arithmetic and copies ran while one was open for 0% -> 0% of each run, Pallas kernels for 12% -> 9%
where the time goes in v18:
time: 86.4 us; the launch traced here: 86.1 us
  waiting for transfers between devices  33.4 us (39%)
  starting transfers between devices  33.1 us (38%)
  Pallas kernels  14.8 us (17%)
  local copies, waits for them, and re-layouts  3.99 us (5%)
    ppermute x25, waiting for transfers between devices, partner(): return lax.ppermute(value, axis, [(i, i ^ k) for i in range(size)])  33.4 us
    ppermute x25, starting transfers between devices, partner(): return lax.ppermute(value, axis, [(i, i ^ k) for i in range(size)])  33.1 us
    unnamed x16, local copies, waits for them, and re-layouts  3.99 us
    pallas_call x1, Pallas kernels, body(): call(functools.partial(route_kernel, experts), outs, 4 * slots * tok_rows...  2.59 us
    pallas_call x1, Pallas kernels, body(): call(functools.partial(grads_kernel, 2), [shape((features, hidden), BF16)...  2.54 us
    pallas_call x1, Pallas kernels, body(): call(functools.partial(grads_kernel, 1), [shape((hidden, features), BF16)...  1.97 us
  transfers between devices with their start and end apart: 25, of which 11 were waited for; matrix products, arithmetic and copies ran while one was open for 0% of the time, Pallas kernels for 9%

profile of v18, /device:TPU:0, one launch (start us, length us, event | category | flops | bytes accessed | tf_op | source)
XLA Modules:
  0.0 86.1 jit_solution(17149249677778874760)
XLA Ops:
  0.6 2.6 %shard_map.110 = (bf16[256,512]{1,0:T(8,128)(2,1)}, f32[256,1]{1,0:T(8,128)}, bf16[4,32,896]{2,1,0:T(8,128)(2,1)}, bf16[4,32,896]{2,1,0:T(8,128)(2,1)}) custom-call(s32[8,512]{1,0:T(8,128)} %bitcast.14, f32[8,512]{1,0:T(8,128)} %bitcast.15, bf16[512,896]{1,0:T(8,128)(2,1)} %refs_2_.1), custom_call_target="tpu_custom_call" | custom-call | flops 469762048 | bytes 3670016 | tf_op jit(solution)/shard_map/pallas_call | solution.py:264
  5.1 5.0 %collective-permute-start.1 = (bf16[2,32,896]{2,1,0:T(8,128)(2,1)S(1)}, bf16[2,32,896]{2,1,0:T(8,128)(2,1)S(1)}, u32[]{:S(2)}, u32[]{:S(2)}) collective-permute-start(bf16[2,32,896]{2,1,0:T(8,128)(2,1)S(1)} %get-tuple-element.59), channel_id=1, source_target_pairs={{0,6},{1,7},{2,4},{3,5},{4,2},{5,3},{6,0},{7,1},{8,14},{9,15},{10,... | collective-permute-start | bytes 344072 | tf_op jit(solution)/shard_map/ppermute | solution.py:234
  14.5 5.6 %collective-permute-done.2.refs_3_ = bf16[2,32,896]{2,1,0:T(8,128)(2,1)S(1)} collective-permute-done((bf16[2,32,896]{2,1,0:T(8,128)(2,1)S(1)}, bf16[2,32,896]{2,1,0:T(8,128)(2,1)S(1)}, u32[]{:S(2)}, u32[]{:S(2)}) %collective-permute-start.2) | collective-permute-done | bytes 114720 | tf_op jit(solution)/shard_map/ppermute | solution.py:234
  21.4 1.5 %collective-permute-start.4 = (bf16[2,64,1024]{2,1,0:T(8,128)(2,1)S(1)}, bf16[2,64,1024]{2,1,0:T(8,128)(2,1)S(1)}, u32[]{:S(2)}, u32[]{:S(2)}) collective-permute-start(bf16[2,64,1024]{2,1,0:T(8,128)(2,1)S(1)} %get-tuple-element.64), channel_id=1, source_target_pairs={{0,8},{8,0},{16,24},{24,16},{1,9},{9,1},{17,25},{25,17},{2,10},{10... | collective-permute-start | bytes 786440 | tf_op jit(solution)/shard_map/ppermute | solution.py:234
  23.0 1.5 %collective-permute-start.5 = (bf16[2,64,1024]{2,1,0:T(8,128)(2,1)S(1)}, bf16[2,64,1024]{2,1,0:T(8,128)(2,1)S(1)}, u32[]{:S(2)}, u32[]{:S(2)}) collective-permute-start(bf16[2,64,1024]{2,1,0:T(8,128)(2,1)S(1)} %get-tuple-element.65), channel_id=1, source_target_pairs={{0,16},{8,24},{16,0},{24,8},{1,17},{9,25},{17,1},{25,9},{2,18},{10... | collective-permute-start | bytes 786440 | tf_op jit(solution)/shard_map/ppermute | solution.py:234
  25.0 2.5 %collective-permute-start.8 = (bf16[2,32,896]{2,1,0:T(8,128)(2,1)S(1)}, bf16[2,32,896]{2,1,0:T(8,128)(2,1)S(1)}, u32[]{:S(2)}, u32[]{:S(2)}) collective-permute-start(bf16[2,32,896]{2,1,0:T(8,128)(2,1)S(1)} %get-tuple-element.69), channel_id=1, source_target_pairs={{0,6},{1,7},{2,4},{3,5},{4,2},{5,3},{6,0},{7,1},{8,14},{9,15},{10,... | collective-permute-start | bytes 344072 | tf_op jit(solution)/shard_map/ppermute | solution.py:234
  27.5 4.2 %collective-permute-done.8.refs_6_ = bf16[2,32,896]{2,1,0:T(8,128)(2,1)S(1)} collective-permute-done((bf16[2,32,896]{2,1,0:T(8,128)(2,1)S(1)}, bf16[2,32,896]{2,1,0:T(8,128)(2,1)S(1)}, u32[]{:S(2)}, u32[]{:S(2)}) %collective-permute-start.8) | collective-permute-done | bytes 114720 | tf_op jit(solution)/shard_map/ppermute | solution.py:234
  31.7 4.1 %collective-permute-start.10 = (bf16[2,32,896]{2,1,0:T(8,128)(2,1)S(1)}, bf16[2,32,896]{2,1,0:T(8,128)(2,1)S(1)}, u32[]{:S(2)}, u32[]{:S(2)}) collective-permute-start(bf16[2,32,896]{2,1,0:T(8,128)(2,1)S(1)} %get-tuple-element.71), channel_id=1, source_target_pairs={{0,2},{1,3},{2,0},{3,1},{4,6},{5,7},{6,4},{7,5},{8,10},{9,11},{10,... | collective-permute-start | bytes 344072 | tf_op jit(solution)/shard_map/ppermute | solution.py:234
  36.5 2.0 %collective-permute-done.10.refs_8_ = bf16[2,32,896]{2,1,0:T(8,128)(2,1)S(1)} collective-permute-done((bf16[2,32,896]{2,1,0:T(8,128)(2,1)S(1)}, bf16[2,32,896]{2,1,0:T(8,128)(2,1)S(1)}, u32[]{:S(2)}, u32[]{:S(2)}) %collective-permute-start.10) | collective-permute-done | bytes 114720 | tf_op jit(solution)/shard_map/ppermute | solution.py:234
  39.5 1.6 %collective-permute-start.11 = (bf16[2,64,1024]{2,1,0:T(8,128)(2,1)S(1)}, bf16[2,64,1024]{2,1,0:T(8,128)(2,1)S(1)}, u32[]{:S(2)}, u32[]{:S(2)}) collective-permute-start(bf16[2,64,1024]{2,1,0:T(8,128)(2,1)S(1)} %get-tuple-element.73), channel_id=1, source_target_pairs={{0,8},{8,0},{16,24},{24,16},{1,9},{9,1},{17,25},{25,17},{2,10},{10... | collective-permute-start | bytes 786440 | tf_op jit(solution)/shard_map/ppermute | solution.py:234
  41.0 1.5 %collective-permute-start.12 = (bf16[2,64,1024]{2,1,0:T(8,128)(2,1)S(1)}, bf16[2,64,1024]{2,1,0:T(8,128)(2,1)S(1)}, u32[]{:S(2)}, u32[]{:S(2)}) collective-permute-start(bf16[2,64,1024]{2,1,0:T(8,128)(2,1)S(1)} %get-tuple-element.74), channel_id=1, source_target_pairs={{0,16},{8,24},{16,0},{24,8},{1,17},{9,25},{17,1},{25,9},{2,18},{10... | collective-permute-start | bytes 786440 | tf_op jit(solution)/shard_map/ppermute | solution.py:234
  43.0 4.6 %collective-permute-done.11.refs_1_.refs_5_ = bf16[2,64,1024]{2,1,0:T(8,128)(2,1)S(1)} collective-permute-done((bf16[2,64,1024]{2,1,0:T(8,128)(2,1)S(1)}, bf16[2,64,1024]{2,1,0:T(8,128)(2,1)S(1)}, u32[]{:S(2)}, u32[]{:S(2)}) %collective-permute-start.11) | collective-permute-done | bytes 262176 | tf_op jit(solution)/shard_map/ppermute | solution.py:234
  47.6 4.0 %collective-permute-done.12.refs_2_.refs_6_ = bf16[2,64,1024]{2,1,0:T(8,128)(2,1)S(1)} collective-permute-done((bf16[2,64,1024]{2,1,0:T(8,128)(2,1)S(1)}, bf16[2,64,1024]{2,1,0:T(8,128)(2,1)S(1)}, u32[]{:S(2)}, u32[]{:S(2)}) %collective-permute-start.12) | collective-permute-done | bytes 262176 | tf_op jit(solution)/shard_map/ppermute | solution.py:234
  54.8 1.5 %collective-permute-start.17 = (bf16[2,64,1024]{2,1,0:T(8,128)(2,1)S(1)}, bf16[2,64,1024]{2,1,0:T(8,128)(2,1)S(1)}, u32[]{:S(2)}, u32[]{:S(2)}) collective-permute-start(bf16[2,64,1024]{2,1,0:T(8,128)(2,1)S(1)} %shard_map.118.refs_0_), channel_id=1, source_target_pairs={{0,24},{8,16},{16,8},{24,0},{1,25},{9,17},{17,9},{25,1},{2,26},{10... | collective-permute-start | bytes 786440 | tf_op jit(solution)/shard_map/ppermute | solution.py:234
  56.4 3.0 %collective-permute-start.19 = (bf16[2,32,896]{2,1,0:T(8,128)(2,1)S(1)}, bf16[2,32,896]{2,1,0:T(8,128)(2,1)S(1)}, u32[]{:S(2)}, u32[]{:S(2)}) collective-permute-start(bf16[2,32,896]{2,1,0:T(8,128)(2,1)S(1)} %get-tuple-element.79), channel_id=1, source_target_pairs={{0,6},{1,7},{2,4},{3,5},{4,2},{5,3},{6,0},{7,1},{8,14},{9,15},{10,... | collective-permute-start | bytes 344072 | tf_op jit(solution)/shard_map/ppermute | solution.py:234
  59.4 2.5 %collective-permute-done.15.refs_1_ = bf16[2,64,1024]{2,1,0:T(8,128)(2,1)S(1)} collective-permute-done((bf16[2,64,1024]{2,1,0:T(8,128)(2,1)S(1)}, bf16[2,64,1024]{2,1,0:T(8,128)(2,1)S(1)}, u32[]{:S(2)}, u32[]{:S(2)}) %collective-permute-start.15) | collective-permute-done | bytes 262176 | tf_op jit(solution)/shard_map/ppermute | solution.py:234
  61.9 4.5 %collective-permute-done.16.refs_2_ = bf16[2,64,1024]{2,1,0:T(8,128)(2,1)S(1)} collective-permute-done((bf16[2,64,1024]{2,1,0:T(8,128)(2,1)S(1)}, bf16[2,64,1024]{2,1,0:T(8,128)(2,1)S(1)}, u32[]{:S(2)}, u32[]{:S(2)}) %collective-permute-start.16) | collective-permute-done | bytes 262176 | tf_op jit(solution)/shard_map/ppermute | solution.py:234
  66.4 1.6 %collective-permute-done.17.refs_3_ = bf16[2,64,1024]{2,1,0:T(8,128)(2,1)S(1)} collective-permute-done((bf16[2,64,1024]{2,1,0:T(8,128)(2,1)S(1)}, bf16[2,64,1024]{2,1,0:T(8,128)(2,1)S(1)}, u32[]{:S(2)}, u32[]{:S(2)}) %collective-permute-start.17) | collective-permute-done | bytes 262176 | tf_op jit(solution)/shard_map/ppermute | solution.py:234
  69.5 1.9 %collective-permute-start.20 = (bf16[2,32,896]{2,1,0:T(8,128)(2,1)S(1)}, bf16[2,32,896]{2,1,0:T(8,128)(2,1)S(1)}, u32[]{:S(2)}, u32[]{:S(2)}) collective-permute-start(bf16[2,32,896]{2,1,0:T(8,128)(2,1)S(1)} %get-tuple-element.82), channel_id=1, source_target_pairs={{0,2},{1,3},{2,0},{3,1},{4,6},{5,7},{6,4},{7,5},{8,10},{9,11},{10,... | collective-permute-start | bytes 344072 | tf_op jit(solution)/shard_map/ppermute | solution.py:234
  71.4 2.1 %collective-permute-start.22 = (bf16[2,32,896]{2,1,0:T(8,128)(2,1)S(1)}, bf16[2,32,896]{2,1,0:T(8,128)(2,1)S(1)}, u32[]{:S(2)}, u32[]{:S(2)}) collective-permute-start(bf16[2,32,896]{2,1,0:T(8,128)(2,1)S(1)} %get-tuple-element.90), channel_id=1, source_target_pairs={{0,6},{1,7},{2,4},{3,5},{4,2},{5,3},{6,0},{7,1},{8,14},{9,15},{10,... | collective-permute-start | bytes 344072 | tf_op jit(solution)/shard_map/ppermute | solution.py:234
  74.4 1.5 %collective-permute-start.24 = (bf16[2,32,896]{2,1,0:T(8,128)(2,1)S(1)}, bf16[2,32,896]{2,1,0:T(8,128)(2,1)S(1)}, u32[]{:S(2)}, u32[]{:S(2)}) collective-permute-start(bf16[2,32,896]{2,1,0:T(8,128)(2,1)S(1)} %get-tuple-element.89.refs_5_.refs_2_), channel_id=1, source_target_pairs={{0,2},{1,3},{2,0},{3,1},{4,6},{5,7},{6,4},{7,5},{8,10},{9,11},{10,... | collective-permute-start | bytes 344072 | tf_op jit(solution)/shard_map/ppermute | solution.py:234
  75.9 2.0 %shard_map.125 = bf16[1024,896]{1,0:T(8,128)(2,1)} custom-call(bf16[256,1024]{1,0:T(8,128)(2,1)S(1)} %get-tuple-element.97.left_ref, bf16[256,896]{1,0:T(8,128)(2,1)S(1)} %get-tuple-element.98.refs_0_), custom_call_target="tpu_custom_call" | custom-call | flops 469762048 | bytes 1835008 | tf_op jit(solution)/shard_map/pallas_call | solution.py:337
  79.2 2.5 %shard_map.124 = (bf16[896,1024]{1,0:T(8,128)(2,1)}, bf16[896,1024]{1,0:T(8,128)(2,1)}) custom-call(bf16[256,896]{1,0:T(8,128)(2,1)S(1)} %get-tuple-element.92.left_ref, bf16[256,1024]{1,0:T(8,128)(2,1)S(1)} %get-tuple-element.93.refs_0_, bf16[256,1024]{1,0:T(8,128)(2,1)S(1)} %get-tuple-element.94.refs_1_, ...), custom_call_target="tpu_custom_call" | custom-call | flops 939524096 | bytes 3670016 | tf_op jit(solution)/shard_map/pallas_call | solution.py:343
  81.7 3.2 %collective-permute-done.23.refs_3_ = bf16[2,32,896]{2,1,0:T(8,128)(2,1)S(1)} collective-permute-done((bf16[2,32,896]{2,1,0:T(8,128)(2,1)S(1)}, bf16[2,32,896]{2,1,0:T(8,128)(2,1)S(1)}, u32[]{:S(2)}, u32[]{:S(2)}) %collective-permute-start.23) | collective-permute-done | bytes 114720 | tf_op jit(solution)/shard_map/ppermute | solution.py:234
  (58 shorter events, 18.2 us)
Async XLA Ops:
  5.1 9.4 %collective-permute-start.1 = (bf16[2,32,896]{2,1,0:T(8,128)(2,1)S(1)}, bf16[2,32,896]{2,1,0:T(8,128)(2,1)S(1)}, u32[]{:S(2)}, u32[]{:S(2)}) collective-permute-start(bf16[2,32,896]{2,1,0:T(8,128)(2,1)S(1)} %get-tuple-element.59), channel_id=1, source_target_pairs={{0,6},{1,7},{2,4},{3,5},{4,2},{5,3},{6,0},{7,1},{8,14},{9,15},{10,... | collective-permute-start | bytes 344072 | tf_op jit(solution)/shard_map/ppermute | solution.py:234
  10.1 10.0 %collective-permute-start.2 = (bf16[2,32,896]{2,1,0:T(8,128)(2,1)S(1)}, bf16[2,32,896]{2,1,0:T(8,128)(2,1)S(1)}, u32[]{:S(2)}, u32[]{:S(2)}) collective-permute-start(bf16[2,32,896]{2,1,0:T(8,128)(2,1)S(1)} %get-tuple-element.60), channel_id=1, source_target_pairs={{0,4},{1,5},{2,6},{3,7},{4,0},{5,1},{6,2},{7,3},{8,12},{9,13},{10,... | collective-permute-start | bytes 344072 | tf_op jit(solution)/shard_map/ppermute | solution.py:234
  10.1 10.0 %collective-permute-start.3 = (bf16[2,32,896]{2,1,0:T(8,128)(2,1)S(1)}, bf16[2,32,896]{2,1,0:T(8,128)(2,1)S(1)}, u32[]{:S(2)}, u32[]{:S(2)}) collective-permute-start(bf16[2,32,896]{2,1,0:T(8,128)(2,1)S(1)} %get-tuple-element.61), channel_id=1, source_target_pairs={{0,2},{1,3},{2,0},{3,1},{4,6},{5,7},{6,4},{7,5},{8,10},{9,11},{10,... | collective-permute-start | bytes 344072 | tf_op jit(solution)/shard_map/ppermute | solution.py:234
  14.4 10.6 %collective-permute-start.7 = (bf16[4,32,896]{2,1,0:T(8,128)(2,1)S(1)}, bf16[4,32,896]{2,1,0:T(8,128)(2,1)S(1)}, u32[]{:S(2)}, u32[]{:S(2)}) collective-permute-start(bf16[4,32,896]{2,1,0:T(8,128)(2,1)S(1)} %get-tuple-element.68), channel_id=1, source_target_pairs={{0,1},{1,0},{2,3},{3,2},{4,5},{5,4},{6,7},{7,6},{8,9},{9,8},{10,11... | collective-permute-start | bytes 688136 | tf_op jit(solution)/shard_map/ppermute | solution.py:234
  21.4 17.1 %collective-permute-start.4 = (bf16[2,64,1024]{2,1,0:T(8,128)(2,1)S(1)}, bf16[2,64,1024]{2,1,0:T(8,128)(2,1)S(1)}, u32[]{:S(2)}, u32[]{:S(2)}) collective-permute-start(bf16[2,64,1024]{2,1,0:T(8,128)(2,1)S(1)} %get-tuple-element.64), channel_id=1, source_target_pairs={{0,8},{8,0},{16,24},{24,16},{1,9},{9,1},{17,25},{25,17},{2,10},{10... | collective-permute-start | bytes 786440 | tf_op jit(solution)/shard_map/ppermute | solution.py:234
  23.0 15.6 %collective-permute-start.5 = (bf16[2,64,1024]{2,1,0:T(8,128)(2,1)S(1)}, bf16[2,64,1024]{2,1,0:T(8,128)(2,1)S(1)}, u32[]{:S(2)}, u32[]{:S(2)}) collective-permute-start(bf16[2,64,1024]{2,1,0:T(8,128)(2,1)S(1)} %get-tuple-element.65), channel_id=1, source_target_pairs={{0,16},{8,24},{16,0},{24,8},{1,17},{9,25},{17,1},{25,9},{2,18},{10... | collective-permute-start | bytes 786440 | tf_op jit(solution)/shard_map/ppermute | solution.py:234
  24.5 14.1 %collective-permute-start.6 = (bf16[2,64,1024]{2,1,0:T(8,128)(2,1)S(1)}, bf16[2,64,1024]{2,1,0:T(8,128)(2,1)S(1)}, u32[]{:S(2)}, u32[]{:S(2)}) collective-permute-start(bf16[2,64,1024]{2,1,0:T(8,128)(2,1)S(1)} %get-tuple-element.66), channel_id=1, source_target_pairs={{0,24},{8,16},{16,8},{24,0},{1,25},{9,17},{17,9},{25,1},{2,26},{10... | collective-permute-start | bytes 786440 | tf_op jit(solution)/shard_map/ppermute | solution.py:234
  25.0 6.7 %collective-permute-start.8 = (bf16[2,32,896]{2,1,0:T(8,128)(2,1)S(1)}, bf16[2,32,896]{2,1,0:T(8,128)(2,1)S(1)}, u32[]{:S(2)}, u32[]{:S(2)}) collective-permute-start(bf16[2,32,896]{2,1,0:T(8,128)(2,1)S(1)} %get-tuple-element.69), channel_id=1, source_target_pairs={{0,6},{1,7},{2,4},{3,5},{4,2},{5,3},{6,0},{7,1},{8,14},{9,15},{10,... | collective-permute-start | bytes 344072 | tf_op jit(solution)/shard_map/ppermute | solution.py:234
  27.5 9.0 %collective-permute-start.9 = (bf16[2,32,896]{2,1,0:T(8,128)(2,1)S(1)}, bf16[2,32,896]{2,1,0:T(8,128)(2,1)S(1)}, u32[]{:S(2)}, u32[]{:S(2)}) collective-permute-start(bf16[2,32,896]{2,1,0:T(8,128)(2,1)S(1)} %get-tuple-element.70), channel_id=1, source_target_pairs={{0,4},{1,5},{2,6},{3,7},{4,0},{5,1},{6,2},{7,3},{8,12},{9,13},{10,... | collective-permute-start | bytes 344072 | tf_op jit(solution)/shard_map/ppermute | solution.py:234
  31.7 6.8 %collective-permute-start.10 = (bf16[2,32,896]{2,1,0:T(8,128)(2,1)S(1)}, bf16[2,32,896]{2,1,0:T(8,128)(2,1)S(1)}, u32[]{:S(2)}, u32[]{:S(2)}) collective-permute-start(bf16[2,32,896]{2,1,0:T(8,128)(2,1)S(1)} %get-tuple-element.71), channel_id=1, source_target_pairs={{0,2},{1,3},{2,0},{3,1},{4,6},{5,7},{6,4},{7,5},{8,10},{9,11},{10,... | collective-permute-start | bytes 344072 | tf_op jit(solution)/shard_map/ppermute | solution.py:234
  39.5 8.1 %collective-permute-start.11 = (bf16[2,64,1024]{2,1,0:T(8,128)(2,1)S(1)}, bf16[2,64,1024]{2,1,0:T(8,128)(2,1)S(1)}, u32[]{:S(2)}, u32[]{:S(2)}) collective-permute-start(bf16[2,64,1024]{2,1,0:T(8,128)(2,1)S(1)} %get-tuple-element.73), channel_id=1, source_target_pairs={{0,8},{8,0},{16,24},{24,16},{1,9},{9,1},{17,25},{25,17},{2,10},{10... | collective-permute-start | bytes 786440 | tf_op jit(solution)/shard_map/ppermute | solution.py:234
  41.0 10.5 %collective-permute-start.12 = (bf16[2,64,1024]{2,1,0:T(8,128)(2,1)S(1)}, bf16[2,64,1024]{2,1,0:T(8,128)(2,1)S(1)}, u32[]{:S(2)}, u32[]{:S(2)}) collective-permute-start(bf16[2,64,1024]{2,1,0:T(8,128)(2,1)S(1)} %get-tuple-element.74), channel_id=1, source_target_pairs={{0,16},{8,24},{16,0},{24,8},{1,17},{9,25},{17,1},{25,9},{2,18},{10... | collective-permute-start | bytes 786440 | tf_op jit(solution)/shard_map/ppermute | solution.py:234
  42.6 9.0 %collective-permute-start.13 = (bf16[2,64,1024]{2,1,0:T(8,128)(2,1)S(1)}, bf16[2,64,1024]{2,1,0:T(8,128)(2,1)S(1)}, u32[]{:S(2)}, u32[]{:S(2)}) collective-permute-start(bf16[2,64,1024]{2,1,0:T(8,128)(2,1)S(1)} %get-tuple-element.75), channel_id=1, source_target_pairs={{0,24},{8,16},{16,8},{24,0},{1,25},{9,17},{17,9},{25,1},{2,26},{10... | collective-permute-start | bytes 786440 | tf_op jit(solution)/shard_map/ppermute | solution.py:234
  52.3 3.9 %collective-permute-start.14 = (bf16[4,32,896]{2,1,0:T(8,128)(2,1)S(1)}, bf16[4,32,896]{2,1,0:T(8,128)(2,1)S(1)}, u32[]{:S(2)}, u32[]{:S(2)}) collective-permute-start(bf16[4,32,896]{2,1,0:T(8,128)(2,1)S(1)} %get-tuple-element.77), channel_id=1, source_target_pairs={{0,1},{1,0},{2,3},{3,2},{4,5},{5,4},{6,7},{7,6},{8,9},{9,8},{10,11... | collective-permute-start | bytes 688136 | tf_op jit(solution)/shard_map/ppermute | solution.py:234
  52.7 9.2 %collective-permute-start.15 = (bf16[2,64,1024]{2,1,0:T(8,128)(2,1)S(1)}, bf16[2,64,1024]{2,1,0:T(8,128)(2,1)S(1)}, u32[]{:S(2)}, u32[]{:S(2)}) collective-permute-start(bf16[2,64,1024]{2,1,0:T(8,128)(2,1)S(1)} %shard_map.118.refs_0_), channel_id=1, source_target_pairs={{0,8},{8,0},{16,24},{24,16},{1,9},{9,1},{17,25},{25,17},{2,10},{10... | collective-permute-start | bytes 786440 | tf_op jit(solution)/shard_map/ppermute | solution.py:234
  54.0 12.4 %collective-permute-start.16 = (bf16[2,64,1024]{2,1,0:T(8,128)(2,1)S(1)}, bf16[2,64,1024]{2,1,0:T(8,128)(2,1)S(1)}, u32[]{:S(2)}, u32[]{:S(2)}) collective-permute-start(bf16[2,64,1024]{2,1,0:T(8,128)(2,1)S(1)} %shard_map.118.refs_0_), channel_id=1, source_target_pairs={{0,16},{8,24},{16,0},{24,8},{1,17},{9,25},{17,1},{25,9},{2,18},{10... | collective-permute-start | bytes 786440 | tf_op jit(solution)/shard_map/ppermute | solution.py:234
  54.8 13.2 %collective-permute-start.17 = (bf16[2,64,1024]{2,1,0:T(8,128)(2,1)S(1)}, bf16[2,64,1024]{2,1,0:T(8,128)(2,1)S(1)}, u32[]{:S(2)}, u32[]{:S(2)}) collective-permute-start(bf16[2,64,1024]{2,1,0:T(8,128)(2,1)S(1)} %shard_map.118.refs_0_), channel_id=1, source_target_pairs={{0,24},{8,16},{16,8},{24,0},{1,25},{9,17},{17,9},{25,1},{2,26},{10... | collective-permute-start | bytes 786440 | tf_op jit(solution)/shard_map/ppermute | solution.py:234
  56.3 11.7 %collective-permute-start.18 = (bf16[2,32,896]{2,1,0:T(8,128)(2,1)S(1)}, bf16[2,32,896]{2,1,0:T(8,128)(2,1)S(1)}, u32[]{:S(2)}, u32[]{:S(2)}) collective-permute-start(bf16[2,32,896]{2,1,0:T(8,128)(2,1)S(1)} %get-tuple-element.78), channel_id=1, source_target_pairs={{0,4},{1,5},{2,6},{3,7},{4,0},{5,1},{6,2},{7,3},{8,12},{9,13},{10,... | collective-permute-start | bytes 344072 | tf_op jit(solution)/shard_map/ppermute | solution.py:234
  56.4 11.7 %collective-permute-start.19 = (bf16[2,32,896]{2,1,0:T(8,128)(2,1)S(1)}, bf16[2,32,896]{2,1,0:T(8,128)(2,1)S(1)}, u32[]{:S(2)}, u32[]{:S(2)}) collective-permute-start(bf16[2,32,896]{2,1,0:T(8,128)(2,1)S(1)} %get-tuple-element.79), channel_id=1, source_target_pairs={{0,6},{1,7},{2,4},{3,5},{4,2},{5,3},{6,0},{7,1},{8,14},{9,15},{10,... | collective-permute-start | bytes 344072 | tf_op jit(solution)/shard_map/ppermute | solution.py:234
  69.4 2.0 %collective-permute-start.21 = (bf16[4,32,896]{2,1,0:T(8,128)(2,1)S(1)}, bf16[4,32,896]{2,1,0:T(8,128)(2,1)S(1)}, u32[]{:S(2)}, u32[]{:S(2)}) collective-permute-start(bf16[4,32,896]{2,1,0:T(8,128)(2,1)S(1)} %get-tuple-element.88), channel_id=1, source_target_pairs={{0,1},{1,0},{2,3},{3,2},{4,5},{5,4},{6,7},{7,6},{8,9},{9,8},{10,11... | collective-permute-start | bytes 688136 | tf_op jit(solution)/shard_map/ppermute | solution.py:234
  69.5 8.4 %collective-permute-start.20 = (bf16[2,32,896]{2,1,0:T(8,128)(2,1)S(1)}, bf16[2,32,896]{2,1,0:T(8,128)(2,1)S(1)}, u32[]{:S(2)}, u32[]{:S(2)}) collective-permute-start(bf16[2,32,896]{2,1,0:T(8,128)(2,1)S(1)} %get-tuple-element.82), channel_id=1, source_target_pairs={{0,2},{1,3},{2,0},{3,1},{4,6},{5,7},{6,4},{7,5},{8,10},{9,11},{10,... | collective-permute-start | bytes 344072 | tf_op jit(solution)/shard_map/ppermute | solution.py:234
  71.4 10.3 %collective-permute-start.22 = (bf16[2,32,896]{2,1,0:T(8,128)(2,1)S(1)}, bf16[2,32,896]{2,1,0:T(8,128)(2,1)S(1)}, u32[]{:S(2)}, u32[]{:S(2)}) collective-permute-start(bf16[2,32,896]{2,1,0:T(8,128)(2,1)S(1)} %get-tuple-element.90), channel_id=1, source_target_pairs={{0,6},{1,7},{2,4},{3,5},{4,2},{5,3},{6,0},{7,1},{8,14},{9,15},{10,... | collective-permute-start | bytes 344072 | tf_op jit(solution)/shard_map/ppermute | solution.py:234
  73.5 11.4 %collective-permute-start.23 = (bf16[2,32,896]{2,1,0:T(8,128)(2,1)S(1)}, bf16[2,32,896]{2,1,0:T(8,128)(2,1)S(1)}, u32[]{:S(2)}, u32[]{:S(2)}) collective-permute-start(bf16[2,32,896]{2,1,0:T(8,128)(2,1)S(1)} %get-tuple-element.91), channel_id=1, source_target_pairs={{0,4},{1,5},{2,6},{3,7},{4,0},{5,1},{6,2},{7,3},{8,12},{9,13},{10,... | collective-permute-start | bytes 344072 | tf_op jit(solution)/shard_map/ppermute | solution.py:234
  74.4 10.5 %collective-permute-start.24 = (bf16[2,32,896]{2,1,0:T(8,128)(2,1)S(1)}, bf16[2,32,896]{2,1,0:T(8,128)(2,1)S(1)}, u32[]{:S(2)}, u32[]{:S(2)}) collective-permute-start(bf16[2,32,896]{2,1,0:T(8,128)(2,1)S(1)} %get-tuple-element.89.refs_5_.refs_2_), channel_id=1, source_target_pairs={{0,2},{1,3},{2,0},{3,1},{4,6},{5,7},{6,4},{7,5},{8,10},{9,11},{10,... | collective-permute-start | bytes 344072 | tf_op jit(solution)/shard_map/ppermute | solution.py:234
  (9 other events, 58.3 us)
